TPU v7x, 128 devices: a whole 4x4x4 slice. The times are simulated.
128 devices in a mesh: sample: 16 (over x, z_hi, core), tok: 8 (over z_lo, y).
Axes of the slice: x: 4, y: 4, z: 4 (z_hi: 2, z_lo: 2; z = z_hi * 2 + z_lo), core: 2. Of those that a mesh axis runs over, the one named last changes fastest.
Arguments:
- act: bfloat16 [32, 1024, 768], P('sample', 'tok'), may hold values from -500 to 500, as said below
- pair_bias: bfloat16 [16, 1024, 1024], P(None, 'tok'), may hold values from -12 to 260
- ln_gain: float32 [768], replicated, may hold values from 0.5 to 1.5
- w_in: bfloat16 [768, 3072], replicated, may hold values from -0.21875 to 0.21875
- w_out: bfloat16 [768, 768], replicated, may hold values from -0.21875 to 0.21875
- d_out: bfloat16 [32, 1024, 768], P('sample', 'tok'), may hold values from -6 to 6
Outputs:
- result: bfloat16 [32, 1024, 768], P('sample', 'tok')
- grad_act: bfloat16 [32, 1024, 768], P('sample', 'tok')
- grad_bias: float32 [16, 1024, 1024], P(None, 'tok', 'sample')
- grad_gain: float32 [768], replicated
- grad_win: float32 [768, 3072], P(None, ('sample', 'tok'))
- grad_wout: float32 [768, 768], P(None, ('sample', 'tok'))
Inputs may be any that keep to these rules, and one draw needn't show every extreme that they name: `act`: activations of order one to some hundreds; channels and tokens have scales of their own.
All inputs are finite; a program needn't handle non-finite values.
Results may differ from a plain program's by a relative error of at most 0.017.
Values may be sent and summed in bfloat16 or wider, within the bound.
No kernel may reach another device: no remote copies, remote signals or barrier semaphores. Data moves between devices by JAX's collectives and lax.ppermute only.
A program may use at most 192 MiB of HBM per device.

v0:
```python
import math

import jax
import jax.numpy as jnp
from jax import lax
from jax.sharding import PartitionSpec as P

EPS = 1e-05


def per_device(act, pair_bias, ln_gain, w_in, w_out, d_out):
    sample_count, row_count, channels = act.shape
    head_count = pair_bias.shape[0]
    head_dim = channels // head_count
    score_scale = 1.0 / math.sqrt(head_dim)
    flat_count = sample_count * row_count
    values_f = act.astype(jnp.float32)
    center = jnp.mean(values_f, -1, keepdims=True)
    spread = jnp.mean((values_f - center) ** 2, -1, keepdims=True)
    inv_std = lax.rsqrt(spread + EPS)
    normed = (values_f - center) * inv_std
    scaled = (normed * ln_gain).astype(jnp.bfloat16)
    flat_scaled = scaled.reshape(flat_count, channels)
    projected = jnp.dot(flat_scaled, w_in, preferred_element_type=jnp.float32)
    projected = projected.reshape(sample_count, row_count, 4 * channels)
    query_rows = projected[..., :channels].astype(jnp.bfloat16)
    key_part = projected[..., channels : 2 * channels].astype(jnp.bfloat16)
    value_part = projected[..., 2 * channels : 3 * channels].astype(jnp.bfloat16)
    gate_open = jax.nn.sigmoid(projected[..., 3 * channels :])
    all_keys, all_values = (
        lax.all_gather(key_part, "tok", axis=1, tiled=True),
        lax.all_gather(value_part, "tok", axis=1, tiled=True),
    )
    token_count = all_keys.shape[1]
    bias_float = pair_bias.astype(jnp.float32)
    prob_list = []
    attended_list = []
    for sample_index in range(sample_count):
        query_heads = query_rows[sample_index].reshape(row_count, head_count, head_dim)
        key_heads = all_keys[sample_index].reshape(token_count, head_count, head_dim)
        value_heads = all_values[sample_index].reshape(token_count, head_count, head_dim)
        scores = (
            jnp.einsum("qhd,khd->hqk", query_heads, key_heads, preferred_element_type=jnp.float32)
            * score_scale
            + bias_float
        )
        attn_probs = jax.nn.softmax(scores, axis=-1)
        probs_low = attn_probs.astype(jnp.bfloat16)
        attended = jnp.einsum(
            "hqk,khd->qhd", probs_low, value_heads, preferred_element_type=jnp.float32
        ).reshape(row_count, channels)
        prob_list.append(attn_probs)
        attended_list.append(attended)
    attended_all = jnp.stack(attended_list)
    gated = (attended_all * gate_open).astype(jnp.bfloat16)
    gated_flat = gated.reshape(flat_count, channels)
    output = jnp.dot(gated_flat, w_out, preferred_element_type=jnp.float32).astype(jnp.bfloat16)
    grad_rows = d_out.reshape(flat_count, channels)
    grad_gated = jnp.einsum(
        "rd,cd->rc", grad_rows, w_out, preferred_element_type=jnp.float32
    ).astype(jnp.bfloat16)
    wout_term = jnp.einsum("rc,rd->cd", gated_flat, grad_rows, preferred_element_type=jnp.float32)
    gated_float = grad_gated.astype(jnp.float32).reshape(sample_count, row_count, channels)
    grad_attended = (gated_float * gate_open).astype(jnp.bfloat16)
    grad_gatepre = gated_float * attended_all * gate_open * (1.0 - gate_open)
    bias_term = jnp.zeros((head_count, row_count, token_count), jnp.float32)
    low_scores = []
    low_probs = []
    query_grads = []
    for sample_index in range(sample_count):
        attn_probs = prob_list[sample_index]
        key_heads = all_keys[sample_index].reshape(token_count, head_count, head_dim)
        value_heads = all_values[sample_index].reshape(token_count, head_count, head_dim)
        attended_heads = grad_attended[sample_index].reshape(row_count, head_count, head_dim)
        grad_probs = jnp.einsum(
            "qhd,khd->hqk", attended_heads, value_heads, preferred_element_type=jnp.float32
        )
        delta_sum = jnp.sum(attn_probs * grad_probs, -1, keepdims=True)
        grad_scores = attn_probs * (grad_probs - delta_sum)
        bias_term = bias_term + grad_scores
        scores_low = grad_scores.astype(jnp.bfloat16)
        grad_query = (
            jnp.einsum(
                "hqk,khd->qhd", scores_low, key_heads, preferred_element_type=jnp.float32
            ).reshape(row_count, channels)
            * score_scale
        )
        low_scores.append(scores_low)
        low_probs.append(attn_probs.astype(jnp.bfloat16))
        query_grads.append(grad_query)
    grad_bias = lax.psum_scatter(
        bias_term.astype(jnp.bfloat16), "sample", scatter_dimension=2, tiled=True
    ).astype(jnp.float32)
    scores_all = jnp.stack(low_scores)
    probs_all = jnp.stack(low_probs)
    query_all = query_rows.reshape(sample_count, row_count, head_count, head_dim)
    attended_all_heads = grad_attended.reshape(sample_count, row_count, head_count, head_dim)
    count = lax.axis_size("tok") * row_count
    grad_key = (
        jnp.einsum("shqk,sqhd->kshd", scores_all, query_all, preferred_element_type=jnp.float32)
        * score_scale
    )
    grad_value = jnp.einsum(
        "shqk,sqhd->kshd", probs_all, attended_all_heads, preferred_element_type=jnp.float32
    )
    key_value_grad = lax.psum_scatter(
        jnp.concatenate(
            [
                grad_key.reshape(count, sample_count, channels),
                grad_value.reshape(count, sample_count, channels),
            ],
            -1,
        ).astype(jnp.bfloat16),
        "tok",
        scatter_dimension=0,
        tiled=True,
    ).astype(jnp.float32)
    grad_key_own = key_value_grad[:, :, :channels].transpose(1, 0, 2)
    grad_value_own = key_value_grad[:, :, channels:].transpose(1, 0, 2)
    grad_proj = jnp.concatenate(
        [jnp.stack(query_grads), grad_key_own, grad_value_own, grad_gatepre], -1
    ).astype(jnp.bfloat16)
    proj_flat = grad_proj.reshape(flat_count, 4 * channels)
    win_term = jnp.einsum("rc,rd->cd", flat_scaled, proj_flat, preferred_element_type=jnp.float32)
    grad_scaled = jnp.einsum("rd,cd->rc", proj_flat, w_in, preferred_element_type=jnp.float32)
    grad_scaled = grad_scaled.reshape(sample_count, row_count, channels)
    gain_term = jnp.sum(grad_scaled * normed, (0, 1))
    grad_normed = grad_scaled * ln_gain
    grad_act = inv_std * (
        grad_normed
        - jnp.mean(grad_normed, -1, keepdims=True)
        - normed * jnp.mean(grad_normed * normed, -1, keepdims=True)
    )
    grad_gain = lax.psum(gain_term, ("sample", "tok"))
    grad_win, grad_wout = (
        lax.psum_scatter(win_term, ("sample", "tok"), scatter_dimension=1, tiled=True),
        lax.psum_scatter(wout_term, ("sample", "tok"), scatter_dimension=1, tiled=True),
    )
    return (
        output.reshape(sample_count, row_count, channels),
        grad_act.astype(jnp.bfloat16),
        grad_bias,
        grad_gain,
        grad_win,
        grad_wout,
    )


def solution(mesh):
    return jax.shard_map(
        per_device,
        mesh=mesh,
        in_specs=(
            P("sample", "tok", None),
            P(None, "tok", None),
            P(),
            P(),
            P(),
            P("sample", "tok", None),
        ),
        out_specs=(
            P("sample", "tok", None),
            P("sample", "tok", None),
            P(None, "tok", "sample"),
            P(),
            P(None, ("sample", "tok")),
            P(None, ("sample", "tok")),
        ),
        check_vma=False,
    )
```

profile of v0, /device:TPU:103, one launch (start us, length us, event | category | flops | bytes accessed | tf_op | source)
XLA Modules:
  0.0 1023.9 jit_solution(8671369309967813274)
XLA Ops:
  9.7 5.6 fusion.67
  20.3 37.8 %all-gather.5.cloned.1.call-done = bf16[2,1024,768]{2,1,0:T(8,128)(2,1)} async-done(((bf16[2,128,768]{2,1,0:T(8,128)(2,1)}), bf16[2,1024,768]{2,1,0:T(8,128)(2,1)}) %all-gather.5.cloned.1.call-update) | async-done | bytes 3145744 | tf_op jit(solution)/shard_map/all_gather | solution.py:31
  58.1 3.7 fusion.62
  61.9 1.7 copy.56
  63.6 40.7 %all-gather.3.cloned.1.call-done = bf16[2,1024,768]{2,1,0:T(8,128)(2,1)} async-done(((bf16[2,128,768]{2,1,0:T(8,128)(2,1)}), bf16[2,1024,768]{2,1,0:T(8,128)(2,1)}) %all-gather.3.cloned.1.call-update) | async-done | bytes 3145744 | tf_op jit(solution)/shard_map/all_gather | solution.py:32
  104.3 3.8 fusion.63
  108.1 2.6 copy.54
  110.7 2.6 copy.57
  113.3 2.6 copy.59
  115.9 9.1 fusion.68
  124.9 6.2 fusion.26
  131.4 9.3 fusion.69
  140.7 5.7 fusion.28
  147.3 2.6 fusion.52
  151.5 8.7 multiply_reduce_fusion
  160.2 7.3 multiply_reduce_fusion.1
  167.5 1.5 slice-done.2
  171.4 12.4 %add_convert_fusion = (bf16[16,128,1024]{2,1,0:T(8,128)(2,1)}, bf16[16,128,1024]{2,1,0:T(8,128)(2,1)}, bf16[16,128,1024]{2,1,0:T(8,128)(2,1)}, bf16[1,16,128,102...) fusion(f32[16,128,1024]{2,1,0:T(8,128)} %get-tuple-element.55, f32[16,128]{1,0:T(8,128)S(1)} %get-tuple-element.54, ...), kind=kLoop, calls=%fused_computation.12 | loop fusion | flops 25165824 | bytes 54558720 | tf_op jit(solution)/shard_map/convert_element_type | solution.py:92
  183.8 5.3 fusion.23
  189.1 4.7 copy.69
  193.8 6.6 multiply_convert_fusion
  200.3 4.7 copy.68
  205.0 6.0 pad_maximum_fusion
  211.1 6.9 copy.70
  218.1 4.2 fusion.35
  222.5 4.4 fusion.34
  227.1 59.8 %reduce-scatter.6.cloned.1.call-done = bf16[128,2,1536]{2,0,1:T(8,128)(2,1)} async-done(((bf16[1024,2,1536]{2,0,1:T(8,128)(2,1)}), bf16[128,2,1536]{2,0,1:T(8,128)(2,1)}) %reduce-scatter.6.cloned.1.call-update) | async-done | bytes 786448 | tf_op jit(solution)/shard_map/reduce_scatter | solution.py:106
  288.9 6.2 convolution_bitcast_fusion
  295.1 1.6 convolution_bitcast_fusion.1
  296.8 326.4 %fusion = f32[768,8]{0,1:T(8,128)} fusion(f32[768,768]{0,1:T(8,128)S(1)} %convolution_bitcast_fusion.1), kind=kCustom, calls=%all-reduce-scatter | all-reduce-scatter fusion | flops 786433 | bytes 2383872
  623.2 1.4 collective-permute-start.30
  626.7 1.3 collective-permute-start.29
  633.2 3.5 collective-permute-done.29
  638.0 4.8 collective-permute-done.28
  644.0 2.0 collective-permute-done.27
  653.5 1.5 collective-permute-done.22
  656.3 1.4 collective-permute-done.21
  676.9 1.6 collective-permute-done.9
  681.2 2.2 collective-permute-start.2
  683.4 2.2 collective-permute-start.1
  685.6 1.9 collective-permute-start
  687.6 2.2 convolution_convert_fusion.1
  691.7 1.4 collective-permute-done
  693.1 22.7 %concatenate.12 = f32[768,262]{0,1:T(8,128)S(1)} concatenate(f32[768,6]{0,1:T(8,128)S(1)} %collective-permute-done.31, f32[768,8]{0,1:T(8,128)S(1)} %collective-permute-done.30, f32[768,8]{0,1:T(8,128)S(1)} %collective-permute-done.29, f32[768,8]{0,1:T(8,128)S(1)} %collective-permute-done.28, f32[768,8]{0,1:T(8,128)S(1)} %collective-permute-done.27, ...), dimensions={1} | concatenate | bytes 1609728
  716.5 1.8 copy.73
  718.3 4.2 fusion.47
  722.5 93.8 %psum.7 = f32[768]{0:T(1024)} all-reduce(f32[768]{0:T(1024)S(1)} %get-tuple-element.24), channel_id=1, replica_groups=mesh['sample'=16,'tok'=8] {'sample','tok'}, use_global_device_ids=true, to_apply=%region_13.0 | all-reduce | flops 768 | bytes 6144 | tf_op jit(solution)/shard_map/psum | solution.py:134
  817.3 200.1 %reduce-scatter.10.cloned.1.call-done = f32[768,24]{0,1:T(8,128)} async-done(((f32[768,3072]{0,1:T(8,128)}), f32[768,24]{0,1:T(8,128)}) %reduce-scatter.10.cloned.1.call-update) | async-done | bytes 73744 | tf_op jit(solution)/shard_map/reduce_scatter | solution.py:136
  (181 shorter events, 58.4 us)
Async XLA Ops:
  7.2 50.9 %all-gather.5.cloned.1.call-start = ((), (), s32[]{:S(2)}) async-start(), calls=%async_computation.4 | async-start | bytes 3538944 | tf_op jit(solution)/shard_map/all_gather | solution.py:31
  16.3 88.0 %all-gather.3.cloned.1.call-start = ((), (), s32[]{:S(2)}) async-start(), calls=%async_computation.3 | async-start | bytes 3538944 | tf_op jit(solution)/shard_map/all_gather | solution.py:32
  17.0 269.8 %reduce-scatter.6.cloned.1.call-start = ((), (), s32[]{:S(2)}) async-start(), calls=%async_computation.5 | async-start | bytes 7077888 | tf_op jit(solution)/shard_map/reduce_scatter | solution.py:106
  19.0 96.9 %copy-start.14 = (bf16[1,128,768]{1,2,0:T(8,128)(2,1)}, bf16[1,128,768]{1,2,0:T(8,128)(2,1)S(1)}, u32[]{:S(2)}) copy-start(bf16[1,128,768]{1,2,0:T(8,128)(2,1)S(1)} %copy.58) | copy-start | bytes 589828
  211.0 505.4 %reduce-scatter.8.cloned.1.call-start = ((), (), s32[]{:S(2)}) async-start(), calls=%async_computation.6 | async-start | bytes 4456448 | tf_op jit(solution)/shard_map/reduce_scatter | solution.py:91
  218.0 799.3 %reduce-scatter.10.cloned.1.call-start = ((), (), s32[]{:S(2)}) async-start(), calls=%async_computation.7 | async-start | bytes 9510912 | tf_op jit(solution)/shard_map/reduce_scatter | solution.py:136
  222.3 66.6 %copy-start.1 = (bf16[2,128,768]{2,1,0:T(8,128)(2,1)S(1)}, bf16[2,128,768]{2,1,0:T(8,128)(2,1)}, u32[]{:S(2)}) copy-start(bf16[2,128,768]{2,1,0:T(8,128)(2,1)} %param.6) | copy-start | bytes 1179652
  222.3 66.6 %copy-start.15 = (f32[768]{0:T(1024)S(1)}, f32[768]{0:T(1024)}, u32[]{:S(2)}) copy-start(f32[768]{0:T(1024)} %param.8) | copy-start | bytes 9220
  222.5 72.6 %copy-start.11 = (bf16[1,128,768]{2,1,0:T(8,128)(2,1)}, bf16[1,128,768]{2,1,0:T(8,128)(2,1)S(1)}, u32[]{:S(2)}) copy-start(bf16[1,128,768]{2,1,0:T(8,128)(2,1)S(1)} %copy.65) | copy-start | bytes 589828
  227.1 68.0 %copy-start.13 = (bf16[1,128,768]{2,1,0:T(8,128)(2,1)}, bf16[1,128,768]{2,1,0:T(8,128)(2,1)S(1)}, u32[]{:S(2)}) copy-start(bf16[1,128,768]{2,1,0:T(8,128)(2,1)S(1)} %copy.64) | copy-start | bytes 589828
  623.2 95.1 %copy-start.2 = (bf16[2,128,768]{2,1,0:T(8,128)(2,1)S(1)}, bf16[2,128,768]{2,1,0:T(8,128)(2,1)}, u32[]{:S(2)}) copy-start(bf16[2,128,768]{2,1,0:T(8,128)(2,1)} %param.6) | copy-start | bytes 1179652
  623.2 95.1 %copy-start.5 = (bf16[2,128,768]{2,1,0:T(8,128)(2,1)S(1)}, bf16[2,128,768]{2,1,0:T(8,128)(2,1)}, u32[]{:S(2)}) copy-start(bf16[2,128,768]{2,1,0:T(8,128)(2,1)} %get-tuple-element.32) | copy-start | bytes 1179652
  623.2 95.1 %copy-start.9 = (bf16[2,128,768]{2,1,0:T(8,128)(2,1)S(1)}, bf16[2,128,768]{2,1,0:T(8,128)(2,1)}, u32[]{:S(2)}) copy-start(bf16[2,128,768]{2,1,0:T(8,128)(2,1)} %copy-done.8) | copy-start | bytes 1179652
  623.2 95.1 %copy-start.12 = (bf16[1,128,768]{2,1,0:T(8,128)(2,1)S(1)}, bf16[1,128,768]{2,1,0:T(8,128)(2,1)}, u32[]{:S(2)}) copy-start(bf16[1,128,768]{2,1,0:T(8,128)(2,1)} %copy-done.11) | copy-start | bytes 589828
  623.2 8.7 collective-permute-start.30
  625.4 5.2 collective-permute-start.31
  626.7 10.0 collective-permute-start.29
  628.0 14.7 %collective-permute-start.28 = (f32[768,8]{0,1:T(8,128)}, f32[768,8]{0,1:T(8,128)S(1)}, u32[]{:S(2)}, u32[]{:S(2)}) collective-permute-start(f32[768,8]{0,1:T(8,128)} %fusion), channel_id=1, source_target_pairs={{0,29},{1,30},{2,31},{3,32},{4,33},{5,34},{6,35},{7,36},{8,37},{9,... | collective-permute-start | bytes 73736
  629.3 16.8 %collective-permute-start.27 = (f32[768,8]{0,1:T(8,128)}, f32[768,8]{0,1:T(8,128)S(1)}, u32[]{:S(2)}, u32[]{:S(2)}) collective-permute-start(f32[768,8]{0,1:T(8,128)} %fusion), channel_id=1, source_target_pairs={{0,28},{1,29},{2,30},{3,31},{4,32},{5,33},{6,34},{7,35},{8,36},{9,... | collective-permute-start | bytes 73736
  630.6 17.1 %collective-permute-start.26 = (f32[768,8]{0,1:T(8,128)}, f32[768,8]{0,1:T(8,128)S(1)}, u32[]{:S(2)}, u32[]{:S(2)}) collective-permute-start(f32[768,8]{0,1:T(8,128)} %fusion), channel_id=1, source_target_pairs={{0,27},{1,28},{2,29},{3,30},{4,31},{5,32},{6,33},{7,34},{8,35},{9,... | collective-permute-start | bytes 73736
  631.9 17.7 %collective-permute-start.25 = (f32[768,8]{0,1:T(8,128)}, f32[768,8]{0,1:T(8,128)S(1)}, u32[]{:S(2)}, u32[]{:S(2)}) collective-permute-start(f32[768,8]{0,1:T(8,128)} %fusion), channel_id=1, source_target_pairs={{0,26},{1,27},{2,28},{3,29},{4,30},{5,31},{6,32},{7,33},{8,34},{9,... | collective-permute-start | bytes 73736
  636.7 14.2 %collective-permute-start.24 = (f32[768,8]{0,1:T(8,128)}, f32[768,8]{0,1:T(8,128)S(1)}, u32[]{:S(2)}, u32[]{:S(2)}) collective-permute-start(f32[768,8]{0,1:T(8,128)} %fusion), channel_id=1, source_target_pairs={{0,25},{1,26},{2,27},{3,28},{4,29},{5,30},{6,31},{7,32},{8,33},{9,... | collective-permute-start | bytes 73736
  642.7 9.5 collective-permute-start.23
  646.0 9.0 collective-permute-start.22
  647.7 10.0 collective-permute-start.21
  649.6 9.4 collective-permute-start.20
  650.9 40.0 %copy-start.16 = (f32[768,8]{0,1:T(8,128)}, f32[768,8]{0,1:T(8,128)S(1)}, u32[]{:S(2)}) copy-start(f32[768,8]{0,1:T(8,128)S(1)} %collective-permute-done.24) | copy-start | bytes 73732
  650.9 9.4 collective-permute-start.19
  652.2 38.7 %copy-start.17 = (f32[768,8]{0,1:T(8,128)}, f32[768,8]{0,1:T(8,128)S(1)}, u32[]{:S(2)}) copy-start(f32[768,8]{0,1:T(8,128)S(1)} %collective-permute-done.23) | copy-start | bytes 73732
  652.2 9.4 collective-permute-start.18
  655.0 8.5 collective-permute-start.17
  657.7 8.3 collective-permute-start.16
  659.0 8.3 collective-permute-start.15
  660.3 8.3 collective-permute-start.14
  661.7 8.9 collective-permute-start.13
  663.5 8.4 collective-permute-start.12
  666.0 7.2 collective-permute-start.11
  667.3 8.3 collective-permute-start.10
  668.7 9.9 collective-permute-start.9
  670.5 9.3 collective-permute-start.8
  671.9 9.2 collective-permute-start.7
  673.2 10.2 collective-permute-start.6
  675.6 10.0 collective-permute-start.5
  678.5 11.3 %collective-permute-start.4 = (f32[768,8]{0,1:T(8,128)}, f32[768,8]{0,1:T(8,128)S(1)}, u32[]{:S(2)}, u32[]{:S(2)}) collective-permute-start(f32[768,8]{0,1:T(8,128)} %fusion), channel_id=1, source_target_pairs={{0,5},{1,6},{2,7},{3,8},{4,9},{5,10},{6,11},{7,12},{8,13},{9,14},{... | collective-permute-start | bytes 73736
  679.8 10.0 collective-permute-start.3
  681.2 8.7 collective-permute-start.2
  683.4 7.5 collective-permute-start.1
  685.6 7.5 collective-permute-start
  (36 other events, 489.7 us)
Sparse Core Ops, SparseCore 0:
  16.4 41.6 all-gather.4
  60.3 43.8 all-gather.2
  211.2 75.6 reduce-scatter.5
  290.8 77.5 reduce-scatter.7
  371.3 646.0 reduce-scatter.9
where the time goes:
time: 1040 us; the launch traced here: 1020 us
  blocking collectives  420 us (40%)
  waiting for transfers between devices  361 us (35%)
  matrix products  87.9 us (8%)
  local copies, waits for them, and re-layouts  71.8 us (7%)
  starting transfers between devices  44 us (4%)
  other arithmetic  24.5 us (2%)
  between operations  14.7 us (1%)
    unnamed x1, blocking collectives  326 us
    reduce_scatter x1, waiting for transfers between devices, per_device(): lax.psum_scatter(win_term, ('sample', 'tok'), scatter_dimension=1, tiled=...  200 us
    psum x1, blocking collectives, per_device(): grad_gain = lax.psum(gain_term, ('sample', 'tok'))  93.8 us
    reduce_scatter x1, waiting for transfers between devices, per_device(): lax.psum_scatter(jnp.concatenate([grad_key.reshape(count, sample_count, c...  59.8 us
    unnamed x32, starting transfers between devices  43.8 us
    all_gather x1, waiting for transfers between devices, per_device(): lax.all_gather(value_part, 'tok', axis=1, tiled=True)  40.7 us
    all_gather x1, waiting for transfers between devices, per_device(): lax.all_gather(key_part, 'tok', axis=1, tiled=True)  37.8 us
    unnamed x98, local copies, waits for them, and re-layouts  31.5 us
  transfers between devices with their start and end apart: 37, of which 19 were waited for; matrix products, arithmetic and copies ran while one was open for 38% of the time, Pallas kernels for 0%

commit v1 on v0

v1 whole, which is shorter than its diff:
```python
import functools
import math

import jax
import jax.numpy as jnp
from jax import lax
from jax.experimental import pallas as pl
from jax.experimental.pallas import tpu as pltpu
from jax.sharding import Mesh
from jax.sharding import PartitionSpec as P

EPS = 1e-05
LOG2E = math.log2(math.e)
BF = jnp.bfloat16
F32 = jnp.float32
HEADS = 16
DH = 48
TOK = 128
KEYS = 1024
PLANE = ("zh", "zl", "y")


def dot(a, b):
    return jnp.dot(a, b, preferred_element_type=F32)


def attention_kernel(
    x_ref, bias_ref, out_ref, gbias_ref, qa_s, ka_s, va_s, vt_s, kn_s, gn_s, qt_s, dk_s, dv_s, gb_s, *, rows
):
    sample = pl.program_id(0)
    block = pl.program_id(1)
    last_block = pl.num_programs(1) - 1
    half = sample // 2
    lane0 = pl.multiple_of((sample % 2) * TOK, TOK)
    scale = 1.0 / math.sqrt(DH)
    per_block = rows // TOK

    @pl.when(block == 0)
    def _():
        whole = jnp.concatenate(
            [x_ref[half * 8 + t, :, pl.ds(lane0, TOK)] for t in range(8)], axis=1
        )
        qt, kt, vt, gt = (whole[i * DH : (i + 1) * DH] for i in range(4))
        qs = qt.astype(F32) * (scale * LOG2E)
        q_hi = qs.astype(BF)
        q_lo = (qs - q_hi.astype(F32)).astype(BF)
        zeros32 = jnp.zeros((32, KEYS), BF)
        zeros64 = jnp.zeros((64, KEYS), BF)
        zeros80 = jnp.zeros((80, KEYS), BF)
        ones16 = jnp.ones((16, KEYS), BF)
        qa_s[...] = jnp.concatenate([q_hi, q_lo, zeros32], axis=0).T
        ka_s[...] = jnp.concatenate([kt, kt, zeros32], axis=0)
        v_one = jnp.concatenate([vt, ones16, zeros64], axis=0)
        va_s[...] = v_one
        vt_s[...] = v_one.T
        kn_s[...] = jnp.concatenate([kt, zeros80], axis=0).T
        gn_s[...] = jnp.concatenate([gt, zeros80], axis=0).T
        qt_s[...] = qt
        dk_s[...] = jnp.zeros_like(dk_s)
        dv_s[...] = jnp.zeros_like(dv_s)

    row0 = pl.multiple_of(block * rows, rows)
    these = pl.ds(row0, rows)
    scores = dot(qa_s[these, :], ka_s[...]) + bias_ref[these, :].astype(F32) * LOG2E
    top = jnp.max(scores, axis=1, keepdims=True)
    expd = jnp.exp2(scores - top)
    expd_low = expd.astype(BF)
    summed = dot(expd_low, vt_s[...])
    inv = 1.0 / summed[:, DH : DH + 1]
    out = summed * inv
    gscaled = (gn_s[these, :].astype(F32) * inv).astype(BF)
    gscaled_f = gscaled.astype(F32)
    delta = jnp.sum(out * gscaled_f, axis=1, keepdims=True)
    delta_hi = delta.astype(BF).astype(F32)
    delta_lo = delta - delta_hi
    lane = lax.broadcasted_iota(jnp.int32, (rows, 128), 1)
    left = jnp.where(
        lane == DH, -delta_hi, jnp.where(lane == DH + 1, -delta_lo, gscaled_f)
    ).astype(BF)
    dscores = expd * dot(left, va_s[...])
    dscores_low = dscores.astype(BF)

    @pl.when(sample == 0)
    def _():
        gb_s[these, :] = dscores

    @pl.when(sample > 0)
    def _():
        gb_s[these, :] = gb_s[these, :] + dscores

    @pl.when(sample == pl.num_programs(0) - 1)
    def _():
        gbias_ref[these, :] = gb_s[these, :].astype(BF)

    dquery = dot(dscores_low, kn_s[...]) * scale
    dk_s[...] += dot(qt_s[:, these], dscores_low)
    gscaled_t = gscaled_f.T.astype(BF)
    dv_s[...] += dot(gscaled_t[:DH], expd_low)
    out_t = out.T
    dquery_t = dquery.T
    for t in range(per_block):
        cols = slice(t * TOK, (t + 1) * TOK)
        where = half * 8 + block * per_block + t
        out_ref[where, 0:DH, pl.ds(lane0, TOK)] = out_t[:DH, cols].astype(BF)
        out_ref[where, DH : 2 * DH, pl.ds(lane0, TOK)] = dquery_t[:DH, cols].astype(BF)

    @pl.when(block == last_block)
    def _():
        for t in range(8):
            cols = slice(t * TOK, (t + 1) * TOK)
            out_ref[half * 8 + t, 2 * DH : 3 * DH, pl.ds(lane0, TOK)] = (
                dk_s[:, cols] * scale
            ).astype(BF)
            out_ref[half * 8 + t, 3 * DH : 4 * DH, pl.ds(lane0, TOK)] = dv_s[:, cols].astype(BF)


def attention(x, bias, rows=256):
    whole3 = pl.BlockSpec(x.shape, lambda s, b: (0, 0, 0))
    whole2 = pl.BlockSpec(bias.shape, lambda s, b: (0, 0))
    return pl.pallas_call(
        functools.partial(attention_kernel, rows=rows),
        grid=(4, KEYS // rows),
        in_specs=[whole3, whole2],
        out_specs=[whole3, whole2],
        out_shape=[
            jax.ShapeDtypeStruct(x.shape, BF),
            jax.ShapeDtypeStruct(bias.shape, BF),
        ],
        scratch_shapes=[
            pltpu.VMEM((KEYS, 128), BF),
            pltpu.VMEM((128, KEYS), BF),
            pltpu.VMEM((128, KEYS), BF),
            pltpu.VMEM((KEYS, 128), BF),
            pltpu.VMEM((KEYS, 128), BF),
            pltpu.VMEM((KEYS, 128), BF),
            pltpu.VMEM((DH, KEYS), BF),
            pltpu.VMEM((DH, KEYS), F32),
            pltpu.VMEM((DH, KEYS), F32),
            pltpu.VMEM((KEYS, KEYS), F32),
        ],
        compiler_params=pltpu.CompilerParams(vmem_limit_bytes=48 * 1024 * 1024),
        cost_estimate=pl.CostEstimate(
            flops=4 * 6 * 2 * KEYS * KEYS * 128, bytes_accessed=8 * 2**20, transcendentals=4 * KEYS * KEYS
        ),
        name="attention",
    )(x, bias)


def split_pair(values):
    high = lax.reduce_precision(values, 8, 7)
    return high.astype(BF), (values - high).astype(BF)


def per_device(act, pair_bias, ln_gain, w_in, w_out, d_out):
    sample_count, row_count, channels = act.shape
    flat = sample_count * row_count
    core = lax.axis_index("core")
    zh = lax.axis_index("zh")

    bias_own = lax.dynamic_slice(pair_bias, (zh * 8, core * 64, 0), (8, 64, KEYS))
    bias_own = lax.all_to_all(bias_own, ("zl", "y"), 0, 0, tiled=True)
    bias_other = lax.ppermute(bias_own, "core", [(0, 1), (1, 0)])
    first = core == 0
    bias_head = jnp.stack(
        [jnp.where(first, bias_own, bias_other), jnp.where(first, bias_other, bias_own)], axis=1
    ).reshape(KEYS, KEYS)

    values_f = act.reshape(flat, channels).astype(F32)
    center = jnp.mean(values_f, -1, keepdims=True)
    spread = jnp.mean((values_f - center) ** 2, -1, keepdims=True)
    inv_std = lax.rsqrt(spread + EPS)
    normed = (values_f - center) * inv_std
    scaled = (normed * ln_gain).astype(BF)
    rows_out = d_out.reshape(flat, channels)

    proj_t = jnp.einsum("cd,rc->dr", w_in, scaled, preferred_element_type=F32)
    gate_t = jax.nn.sigmoid(proj_t[3 * channels :])
    ggated_t = (
        jnp.einsum("cd,rd->cr", w_out, rows_out, preferred_element_type=F32).astype(BF).astype(F32)
    )
    gatt_t = (ggated_t * gate_t).astype(BF)
    send = jnp.concatenate(
        [
            proj_t[: 3 * channels].astype(BF).reshape(3, HEADS, DH, flat).transpose(1, 0, 2, 3).reshape(HEADS, 3 * DH, flat),
            gatt_t.reshape(HEADS, DH, flat),
        ],
        axis=1,
    )
    received = lax.all_to_all(send, PLANE, 0, 0, tiled=True)
    result, gbias = attention(received, bias_head)
    back = lax.all_to_all(result, PLANE, 0, 0, tiled=True)

    gb = gbias.reshape(KEYS, 4, 2, 2, 64).transpose(1, 3, 2, 0, 4).reshape(8 * 2 * KEYS, 64)
    gb = lax.psum_scatter(gb, ("x", "core"), scatter_dimension=0, tiled=True)
    gb = gb.reshape(2, 2, 4, TOK, 64).reshape(HEADS, TOK, 64)
    grad_bias = lax.all_to_all(gb, PLANE, 0, 0, tiled=True).astype(F32)

    att_t = back[:, :DH].reshape(channels, flat).astype(F32)
    gated_t = (att_t * gate_t).astype(BF)
    output = jnp.einsum("cr,cd->rd", gated_t, w_out, preferred_element_type=F32).astype(BF)
    gatepre_t = (ggated_t * att_t * gate_t * (1.0 - gate_t)).astype(BF)
    gproj_t = jnp.concatenate(
        [
            back[:, DH:].reshape(HEADS, 3, DH, flat).transpose(1, 0, 2, 3).reshape(3 * channels, flat),
            gatepre_t,
        ],
        axis=0,
    )
    win_t = dot(gproj_t, scaled).astype(BF)
    wout_t = jnp.einsum("rd,cr->dc", rows_out, gated_t, preferred_element_type=F32).astype(BF)
    grad_scaled = jnp.einsum("dr,cd->rc", gproj_t, w_in, preferred_element_type=F32)
    gain = jnp.sum(grad_scaled * normed, 0)
    grad_normed = grad_scaled * ln_gain
    grad_act = inv_std * (
        grad_normed
        - jnp.mean(grad_normed, -1, keepdims=True)
        - normed * jnp.mean(grad_normed * normed, -1, keepdims=True)
    )
    high, low = split_pair(gain)
    parts = jnp.concatenate(
        [
            win_t.reshape(128, 24, channels),
            wout_t.reshape(128, 6, channels),
            jnp.broadcast_to(high, (128, 1, channels)),
            jnp.broadcast_to(low, (128, 1, channels)),
        ],
        axis=1,
    )
    parts = parts.reshape(8, 2, 8, 32, channels).transpose(1, 0, 2, 3, 4).reshape(2, 64, 32, channels)
    parts = lax.all_to_all(parts, "core", 0, 0, tiled=True)
    pair = parts[0].astype(F32) + parts[1].astype(F32)
    high, low = split_pair(pair[:, 30:31] + pair[:, 31:32])
    parts = jnp.concatenate([pair[:, :30].astype(BF), high, low], axis=1)
    parts = lax.all_to_all(parts, ("x", "zh", "zl", "y"), 0, 0, tiled=True)
    total = jnp.sum(parts.astype(F32), axis=0)
    return (
        output.reshape(sample_count, row_count, channels),
        grad_act.astype(BF).reshape(sample_count, row_count, channels),
        grad_bias,
        total[30] + total[31],
        total[:24].T,
        total[24:30].T,
    )


def solution(mesh):
    fine = Mesh(mesh.devices.reshape(4, 2, 2, 2, 4), ("x", "zh", "core", "zl", "y"))
    sample = ("x", "zh", "core")
    tok = ("zl", "y")
    return jax.shard_map(
        per_device,
        mesh=fine,
        in_specs=(
            P(sample, tok, None),
            P(None, tok, None),
            P(),
            P(),
            P(),
            P(sample, tok, None),
        ),
        out_specs=(
            P(sample, tok, None),
            P(sample, tok, None),
            P(None, tok, sample),
            P(),
            P(None, sample + tok),
            P(None, sample + tok),
        ),
        check_vma=False,
    )
```

time: 1040 us -> 246 us (0.24); the launches traced: 1020 us -> 244 us
  blocking collectives: 420 us -> 11.7 us
  waiting for transfers between devices: 361 us -> 79.6 us
  matrix products: 87.9 us -> 17.8 us
  local copies, waits for them, and re-layouts: 71.8 us -> 39.9 us
  Pallas kernels: 0 us -> 28.5 us
  starting transfers between devices: 44 us -> 32.6 us
    unnamed x1 -> x0, blocking collectives: 326 us -> none
    reduce_scatter x3 -> x1, waiting for transfers between devices: 260 us -> 0.01 us  [per_device(): gb = lax.psum_scatter(gb, ('x', 'core'), scatter_dimension=0, tiled=True)]
    psum x1 -> x0, blocking collectives: 93.8 us -> none  [per_device(): grad_gain = lax.psum(gain_term, ('sample', 'tok'))]
    all_to_all x0 -> x5, waiting for transfers between devices: none -> 79.6 us  [the longest x1 42.9 us: per_device(): parts = lax.all_to_all(parts, ('x', 'zh', 'zl', 'y'), 0, 0, tiled=True)]
    all_gather x2 -> x0, waiting for transfers between devices: 78.5 us -> none  [the longest x1 40.7 us: per_device(): lax.all_gather(value_part, 'tok', axis=1, tiled=True)]
    dot_general x14 -> x6, matrix products: 69.5 us -> 17.8 us  [the longest x1 6.06 us: per_device(): jnp.einsum('dr,cd->rc', gproj_t, w_in, preferred_element_type=F32)]
    unnamed x32 -> x0, starting transfers between devices: 43.8 us -> none
    all_to_all x0 -> x5, starting transfers between devices: none -> 31.6 us  [the longest x1 10.1 us: per_device(): parts = lax.all_to_all(parts, ('x', 'zh', 'zl', 'y'), 0, 0, tiled=True)]
  transfers between devices with their start and end apart: 37 -> 7, of which waited for: 19 -> 4; matrix products, arithmetic and copies ran while one was open for 38% -> 26% of each run, Pallas kernels for 0% -> 0%
where the time goes in v1:
time: 246 us; the launch traced here: 244 us
  waiting for transfers between devices  79.6 us (32%)
  local copies, waits for them, and re-layouts  39.9 us (16%)
  starting transfers between devices  32.6 us (13%)
  Pallas kernels  28.5 us (12%)
  other arithmetic  19.7 us (8%)
  matrix products  17.8 us (7%)
  between operations  14.4 us (6%)
  blocking collectives  11.7 us (5%)
    all_to_all x1, waiting for transfers between devices, per_device(): parts = lax.all_to_all(parts, ('x', 'zh', 'zl', 'y'), 0, 0, tiled=True)  42.9 us
    pallas_call x1, Pallas kernels, attention(): pl.pallas_call(functools.partial(attention_kernel, rows=rows), grid=(4, K...  28.5 us
    all_to_all x1, waiting for transfers between devices, per_device(): received = lax.all_to_all(send, PLANE, 0, 0, tiled=True)  21 us
    all_to_all x1, blocking collectives, per_device(): parts = lax.all_to_all(parts, 'core', 0, 0, tiled=True)  11.7 us
    all_to_all x1, waiting for transfers between devices, per_device(): back = lax.all_to_all(result, PLANE, 0, 0, tiled=True)  10.9 us
    all_to_all x1, starting transfers between devices, per_device(): parts = lax.all_to_all(parts, ('x', 'zh', 'zl', 'y'), 0, 0, tiled=True)  10.1 us
    dot_general x1, matrix products, per_device(): jnp.einsum('dr,cd->rc', gproj_t, w_in, preferred_element_type=F32)  6.06 us
    all_to_all x1, starting transfers between devices, per_device(): back = lax.all_to_all(result, PLANE, 0, 0, tiled=True)  5.56 us
  transfers between devices with their start and end apart: 7, of which 4 were waited for; matrix products, arithmetic and copies ran while one was open for 26% of the time, Pallas kernels for 0%

profile of v1, /device:TPU:103, one launch (start us, length us, event | category | flops | bytes accessed | tf_op | source)
XLA Modules:
  0.0 244.3 jit_solution(18401579470549890669)
XLA Ops:
  7.2 2.4 constant_dynamic-slice_fusion
  9.6 5.4 %all-to-all-start.1 = ((bf16[8,64,1024]{2,1,0:T(8,128)(2,1)}), bf16[8,64,1024]{2,1,0:T(8,128)(2,1)}, u32[]{:S(2)}, u32[]{:S(2)}) async-start(bf16[8,64,1024]{2,1,0:T(8,128)(2,1)} %constant_dynamic-slice_fusion), calls=%async_computation.1 | async-start | bytes 2097152 | tf_op jit(solution)/shard_map/all_to_all | solution.py:161
  15.6 3.9 %convolution_bitcast_fusion = f32[3072,256]{0,1:T(8,128)S(1)} fusion(bf16[256,768]{1,0:T(8,128)(2,1)S(1)} %multiply_convert_fusion.4, bf16[768,3072]{1,0:T(8,128)(2,1)} %param.9), kind=kOutput, calls=%fused_computation.5 | convolution fusion | flops 1207959552 | bytes 8257536 | tf_op jit(solution)/shard_map/cd,rc->dr/dot_general | solution.py:176
  19.6 1.6 copy-done.6
  21.3 0.6 copy.62
  22.0 2.7 %multiply_convert_fusion.3 = (bf16[768,256]{0,1:T(8,128)(2,1)S(1)}, f32[768,256]{0,1:T(8,128)}) fusion(f32[3072,256]{0,1:T(8,128)} %copy-done.6, bf16[768,768]{1,0:T(8,128)(2,1)S(1)} %copy-done, bf16[256,768]{1,0:T(8,128)(2,1)} %bitcast.81), kind=kOutput, calls=%fused_computation.30 | convolution fusion | flops 303366144 | bytes 3538944 | tf_op jit(solution)/shard_map/cd,rd->cr/dot_general | solution.py:179
  24.9 4.8 %all-to-all-done.1 = bf16[8,64,1024]{2,1,0:T(8,128)(2,1)} async-done(((bf16[8,64,1024]{2,1,0:T(8,128)(2,1)}), bf16[8,64,1024]{2,1,0:T(8,128)(2,1)}, u32[]{:S(2)}, u32[]{:S(2)}) %all-to-all-start.1) | async-done | bytes 1048608 | tf_op jit(solution)/shard_map/all_to_all | solution.py:161
  29.7 0.8 collective-permute-start
  30.5 1.4 pad_maximum_fusion.3
  31.9 5.2 %all-to-all-start = ((bf16[16,192,256]{2,1,0:T(8,128)(2,1)}), bf16[16,192,256]{2,1,0:T(8,128)(2,1)S(1)}, u32[]{:S(2)}, u32[]{:S(2)}) async-start(bf16[16,192,256]{2,1,0:T(8,128)(2,1)} %pad_maximum_fusion.3), calls=%async_computation | async-start | bytes 3145728 | tf_op jit(solution)/shard_map/all_to_all | solution.py:189
  37.1 1.7 select_bitcast_fusion.1
  39.0 1.5 copy.66
  40.5 21.0 %all-to-all-done.x_ref = bf16[16,192,256]{2,1,0:T(8,128)(2,1)S(1)} async-done(((bf16[16,192,256]{2,1,0:T(8,128)(2,1)}), bf16[16,192,256]{2,1,0:T(8,128)(2,1)S(1)}, u32[]{:S(2)}, u32[]{:S(2)}) %all-to-all-start) | async-done | bytes 1572896 | tf_op jit(solution)/shard_map/all_to_all | solution.py:189
  61.5 1.2 copy-done.1
  62.7 1.4 copy-done.2
  64.1 28.5 %attention.1 = (bf16[16,192,256]{2,1,0:T(8,128)(2,1)S(1)}, bf16[1024,1024]{1,0:T(8,128)(2,1)S(1)}) custom-call(bf16[16,192,256]{2,1,0:T(8,128)(2,1)S(1)} %copy-done.2, bf16[1024,1024]{1,0:T(8,128)(2,1)} %bitcast.76), custom_call_target="tpu_custom_call" | custom-call | flops 6442450944 | bytes 8388608 | tf_op jit(solution)/shard_map/attention/pallas_call | solution.py:120
  92.7 1.1 copy-done.3
  93.8 5.6 %all-to-all-start.2 = ((bf16[16,192,256]{2,1,0:T(8,128)(2,1)}), bf16[16,192,256]{2,1,0:T(8,128)(2,1)}, u32[]{:S(2)}, u32[]{:S(2)}) async-start(bf16[16,192,256]{2,1,0:T(8,128)(2,1)} %copy-done.3), calls=%async_computation.2 | async-start | bytes 3145728 | tf_op jit(solution)/shard_map/all_to_all | solution.py:191
  99.6 2.6 %copy.71 = bf16[1024,1024]{0,1:T(8,128)(2,1)} copy(bf16[1024,1024]{1,0:T(8,128)(2,1)S(1)} %get-tuple-element.9) | data formatting | bytes 4194304 | tf_op jit(solution)/shard_map/attention/pallas_call | solution.py:120
  102.2 3.8 %copy.72 = bf16[4,2,2,1024,64]{3,2,1,0,4:T(2,128)(2,1)S(1)} copy(bf16[4,2,2,1024,64]{3,4,1,2,0:T(8,128)(2,1)} %bitcast.71) | data formatting | bytes 4194304 | tf_op jit(solution)/shard_map/transpose | solution.py:193
  105.9 2.8 %reshape.118 = bf16[16384,64]{0,1:T(8,128)(2,1)} reshape(bf16[4,2,2,1024,64]{3,2,1,0,4:T(2,128)(2,1)S(1)} %copy.72) | data formatting | bytes 4194304 | tf_op jit(solution)/shard_map/reshape | solution.py:193
  108.8 10.9 %all-to-all-done.2 = bf16[16,192,256]{2,1,0:T(8,128)(2,1)} async-done(((bf16[16,192,256]{2,1,0:T(8,128)(2,1)}), bf16[16,192,256]{2,1,0:T(8,128)(2,1)}, u32[]{:S(2)}, u32[]{:S(2)}) %all-to-all-start.2) | async-done | bytes 1572896 | tf_op jit(solution)/shard_map/all_to_all | solution.py:191
  119.7 1.4 slice.57
  121.0 1.1 copy.68
  122.2 1.0 slice.56
  123.6 1.7 multiply_convert_fusion.1
  125.2 0.9 copy.70
  126.2 2.6 %fusion = bf16[768,768]{1,0:T(8,128)(2,1)} fusion(bf16[768,256]{0,1:T(8,128)(2,1)S(1)} %get-tuple-element.22, bf16[256,768]{1,0:T(8,128)(2,1)} %bitcast.82), kind=kOutput, calls=%fused_computation.12 | convolution fusion | flops 302579712 | bytes 1966080 | tf_op jit(solution)/shard_map/rd,cr->dc/dot_general | solution.py:210
  128.7 2.2 concatenate.20
  131.0 6.1 %multiply_reduce_fusion = (f32[768]{0:T(1024)S(1)}, f32[256]{0:T(256)S(1)}, f32[256]{0:T(256)}, f32[256,768]{1,0:T(8,128)}) fusion(bf16[2,128,768]{2,1,0:T(8,128)(2,1)S(1)} %copy-done.5, f32[256]{0:T(256)S(1)} %rsqrt_bitcast_fusion, f32[256]{0:T(256)S(1)} %get-tuple-element.27, f32[768]{0:T(1024)S(1)} %copy-done.12, bf16[768,3072]{1,0:T(8,128)(2,1)} %param.9, ...), kind=kOutput, calls=%fused_computation.25 | convolution fusion | flops 1212873472 | bytes 7481344 | tf_op jit(solution)/shard_map/dr,cd->rc/dot_general | solution.py:211
  137.1 1.4 convolution_convert_fusion
  138.9 4.0 %pad_maximum_fusion = bf16[8,2,8,32,768]{4,3,2,0,1:T(8,128)(2,1)S(1)} fusion(bf16[8,2,8,1,768]{4,3,2,0,1:T(2,128)(2,1)S(1)} %broadcast_in_dim.5, bf16[8,2,8,1,768]{4,3,2,0,1:T(2,128)(2,1)S(1)} %broadcast_in_dim.4, bf16[8,2,8,24,768]{4,3,2,1,0:T(8,128)(2,1)S(1)} %bitcast.72, bf16[8,2,8,6,768]{4,3,2,1,0:T(8,128)(2,1)S(1)} %concatenate.20), kind=kLoop, calls=%fused_computation | loop fusion | flops 25165824 | bytes 12582912 | tf_op jit(solution)/shard_map/concatenate | solution.py:220
  143.0 3.6 %copy.76 = bf16[2,64,32,768]{3,1,2,0:T(8,128)(2,1)S(1)} copy(bf16[2,64,32,768]{3,2,1,0:T(8,128)(2,1)S(1)} %bitcast.70) | data formatting | bytes 12582912 | tf_op jit(solution)/shard_map/reshape | solution.py:229
  146.6 11.7 %all_to_all.30 = bf16[2,64,32,768]{3,1,2,0:T(8,128)(2,1)S(1)} all-to-all(bf16[2,64,32,768]{3,1,2,0:T(8,128)(2,1)S(1)} %copy.76), channel_id=1, replica_groups=mesh['x'=4,'zh'=2,'core'=2,'zl'=2,'y'=4] {'core'}, dimensions={0} | all-to-all | bytes 12582912 | tf_op jit(solution)/shard_map/all_to_all | solution.py:230
  158.3 3.8 %add_bitcast_fusion = f32[64,32,768]{2,0,1:T(8,128)} fusion(bf16[2,64,32,768]{3,1,2,0:T(8,128)(2,1)S(1)} %all_to_all.30), kind=kLoop, calls=%fused_computation.2 | loop fusion | flops 4718592 | bytes 12582912 | tf_op jit(solution)/shard_map/add | solution.py:231
  162.1 1.7 copy_bitcast_fusion
  163.8 5.3 %all-to-all-start.3 = ((bf16[16,128,64]{1,2,0:T(8,128)(2,1)}), bf16[16,128,64]{1,2,0:T(8,128)(2,1)S(1)}, u32[]{:S(2)}, u32[]{:S(2)}) async-start(bf16[16,128,64]{1,2,0:T(8,128)(2,1)} %copy_bitcast_fusion), calls=%async_computation.4 | async-start | bytes 524288 | tf_op jit(solution)/shard_map/all_to_all | solution.py:196
  169.2 1.1 reduce-precision_convert_fusion
  170.2 3.1 %slice.100 = bf16[64,30,768]{2,0,1:T(8,128)(2,1)S(1)} slice(f32[64,32,768]{2,0,1:T(8,128)} %add_bitcast_fusion), slice={[0:64], [0:30], [0:768]} | slice | bytes 5898240 | tf_op jit(solution)/shard_map/slice | solution.py:233
  173.7 3.4 %copy.77 = bf16[64,32,768]{2,1,0:T(8,128)(2,1)} copy(bf16[64,32,768]{2,0,1:T(8,128)(2,1)S(1)} %pad_maximum_fusion.1) | data formatting | bytes 6291456 | tf_op jit(solution)/shard_map/concatenate | solution.py:233
  177.1 10.1 %all-to-all-start.5 = ((bf16[64,32,768]{2,1,0:T(8,128)(2,1)}), bf16[64,32,768]{2,1,0:T(8,128)(2,1)}, u32[]{:S(2)}, u32[]{:S(2)}) async-start(bf16[64,32,768]{2,1,0:T(8,128)(2,1)} %copy.77), calls=%async_computation.6 | async-start | bytes 6291456 | tf_op jit(solution)/shard_map/all_to_all | solution.py:234
  187.3 1.0 multiply_convert_fusion
  188.3 1.2 convolution_convert_fusion.2
  189.6 0.8 convert_element_type.90
  190.4 42.9 %all-to-all-done.5 = bf16[64,32,768]{2,1,0:T(8,128)(2,1)} async-done(((bf16[64,32,768]{2,1,0:T(8,128)(2,1)}), bf16[64,32,768]{2,1,0:T(8,128)(2,1)}, u32[]{:S(2)}, u32[]{:S(2)}) %all-to-all-start.5) | async-done | bytes 3145760 | tf_op jit(solution)/shard_map/all_to_all | solution.py:234
  233.3 2.3 convert_reduce_fusion
  236.2 0.6 slice_bitcast_fusion.1
  236.8 0.6 slice_bitcast_fusion
  (46 shorter events, 3.2 us)
Async XLA Ops:
  7.2 14.9 %copy-start = (bf16[768,768]{1,0:T(8,128)(2,1)S(1)}, bf16[768,768]{1,0:T(8,128)(2,1)}, u32[]{:S(2)}) copy-start(bf16[768,768]{1,0:T(8,128)(2,1)} %param.10) | copy-start | bytes 3538948
  7.2 7.8 %copy-start.4 = (bf16[2,128,768]{2,1,0:T(8,128)(2,1)S(1)}, bf16[2,128,768]{2,1,0:T(8,128)(2,1)}, u32[]{:S(2)}) copy-start(bf16[2,128,768]{2,1,0:T(8,128)(2,1)} %param.6) | copy-start | bytes 1179652
  7.2 8.2 %copy-start.12 = (f32[768]{0:T(1024)S(1)}, f32[768]{0:T(1024)}, u32[]{:S(2)}) copy-start(f32[768]{0:T(1024)} %param.8) | copy-start | bytes 9220
  9.6 20.1 %all-to-all-start.1 = ((bf16[8,64,1024]{2,1,0:T(8,128)(2,1)}), bf16[8,64,1024]{2,1,0:T(8,128)(2,1)}, u32[]{:S(2)}, u32[]{:S(2)}) async-start(bf16[8,64,1024]{2,1,0:T(8,128)(2,1)} %constant_dynamic-slice_fusion), calls=%async_computation.1 | async-start | bytes 2097152 | tf_op jit(solution)/shard_map/all_to_all | solution.py:161
  15.6 4.0 %copy-start.9 = (bf16[256,768]{1,0:T(8,128)(2,1)}, bf16[256,768]{1,0:T(8,128)(2,1)S(1)}, u32[]{:S(2)}) copy-start(bf16[256,768]{1,0:T(8,128)(2,1)S(1)} %multiply_convert_fusion.4) | copy-start | bytes 1179652
  19.6 1.6 copy-start.6
  29.7 7.4 %collective-permute-start = (bf16[8,64,1024]{2,1,0:T(8,128)(2,1)}, bf16[8,64,1024]{2,1,0:T(8,128)(2,1)}, u32[]{:S(2)}, u32[]{:S(2)}) collective-permute-start(bf16[8,64,1024]{2,1,0:T(8,128)(2,1)} %all-to-all-done.1), channel_id=1, source_target_pairs={{0,8},{8,0},{1,9},{9,1},{2,10},{10,2},{3,11},{11,3},{4,12},{12,4},... | collective-permute-start | bytes 3145736 | tf_op jit(solution)/shard_map/ppermute | solution.py:162
  31.9 29.6 %all-to-all-start = ((bf16[16,192,256]{2,1,0:T(8,128)(2,1)}), bf16[16,192,256]{2,1,0:T(8,128)(2,1)S(1)}, u32[]{:S(2)}, u32[]{:S(2)}) async-start(bf16[16,192,256]{2,1,0:T(8,128)(2,1)} %pad_maximum_fusion.3), calls=%async_computation | async-start | bytes 3145728 | tf_op jit(solution)/shard_map/all_to_all | solution.py:189
  61.5 1.2 copy-start.1
  62.7 1.4 copy-start.2
  92.6 1.1 copy-start.3
  93.8 25.9 %all-to-all-start.2 = ((bf16[16,192,256]{2,1,0:T(8,128)(2,1)}), bf16[16,192,256]{2,1,0:T(8,128)(2,1)}, u32[]{:S(2)}, u32[]{:S(2)}) async-start(bf16[16,192,256]{2,1,0:T(8,128)(2,1)} %copy-done.3), calls=%async_computation.2 | async-start | bytes 3145728 | tf_op jit(solution)/shard_map/all_to_all | solution.py:191
  99.4 62.8 %reduce-scatter.2.cloned.1.call-start = ((), (), s32[]{:S(2)}) async-start(), calls=%async_computation.7 | async-start | bytes 2359296 | tf_op jit(solution)/shard_map/reduce_scatter | solution.py:194
  125.2 5.8 %copy-start.5 = (bf16[2,128,768]{2,1,0:T(8,128)(2,1)S(1)}, bf16[2,128,768]{2,1,0:T(8,128)(2,1)}, u32[]{:S(2)}) copy-start(bf16[2,128,768]{2,1,0:T(8,128)(2,1)} %param.6) | copy-start | bytes 1179652
  131.0 6.1 %copy-start.7 = (bf16[16,3,48,256]{3,2,0,1:T(8,128)(2,1)S(1)}, bf16[16,3,48,256]{3,2,0,1:T(8,128)(2,1)}, u32[]{:S(2)}) copy-start(bf16[16,3,48,256]{3,2,0,1:T(8,128)(2,1)} %copy.68) | copy-start | bytes 3538948
  131.0 6.1 %copy-start.10 = (bf16[256,768]{1,0:T(8,128)(2,1)S(1)}, bf16[256,768]{1,0:T(8,128)(2,1)}, u32[]{:S(2)}) copy-start(bf16[256,768]{1,0:T(8,128)(2,1)} %copy-done.9) | copy-start | bytes 1179652
  131.0 6.1 %copy-start.11 = (bf16[768,256]{1,0:T(8,128)(2,1)S(1)}, bf16[768,256]{1,0:T(8,128)(2,1)}, u32[]{:S(2)}) copy-start(bf16[768,256]{1,0:T(8,128)(2,1)} %copy.70) | copy-start | bytes 1179652
  163.8 13.3 %all-to-all-start.3 = ((bf16[16,128,64]{1,2,0:T(8,128)(2,1)}), bf16[16,128,64]{1,2,0:T(8,128)(2,1)S(1)}, u32[]{:S(2)}, u32[]{:S(2)}) async-start(bf16[16,128,64]{1,2,0:T(8,128)(2,1)} %copy_bitcast_fusion), calls=%async_computation.4 | async-start | bytes 524288 | tf_op jit(solution)/shard_map/all_to_all | solution.py:196
  177.1 10.2 %copy-start.13 = (f32[256]{0:T(256)S(1)}, f32[256]{0:T(256)}, u32[]{:S(2)}) copy-start(f32[256]{0:T(256)} %get-tuple-element.18) | copy-start | bytes 3076
  177.1 10.2 %copy-start.8 = (f32[256,768]{1,0:T(8,128)S(1)}, f32[256,768]{1,0:T(8,128)}, u32[]{:S(2)}) copy-start(f32[256,768]{1,0:T(8,128)} %get-tuple-element.31) | copy-start | bytes 2359300
  177.1 56.1 %all-to-all-start.5 = ((bf16[64,32,768]{2,1,0:T(8,128)(2,1)}), bf16[64,32,768]{2,1,0:T(8,128)(2,1)}, u32[]{:S(2)}, u32[]{:S(2)}) async-start(bf16[64,32,768]{2,1,0:T(8,128)(2,1)} %copy.77), calls=%async_computation.6 | async-start | bytes 6291456 | tf_op jit(solution)/shard_map/all_to_all | solution.py:234
Sparse Core Ops, SparseCore 0:
  108.9 34.2 reduce-scatter.1

commit v2 on v1

v2 whole, which is shorter than its diff:
```python
import functools
import math

import jax
import jax.numpy as jnp
from jax import lax
from jax.experimental import pallas as pl
from jax.experimental.pallas import tpu as pltpu
from jax.sharding import Mesh
from jax.sharding import PartitionSpec as P

EPS = 1e-05
LOG2E = math.log2(math.e)
BF = jnp.bfloat16
F32 = jnp.float32
C = 768
HEADS = 16
DH = 48
TOK = 128
KEYS = 1024
PLANE = ("zh", "zl", "y")
SWAP = [(0, 1), (1, 0)]
SCALE = 1.0 / math.sqrt(DH)
VMEM_LIMIT = 48 * 1024 * 1024


def dot(a, b):
    return jnp.dot(a, b, preferred_element_type=F32)


def dot_nt(a, b):
    return lax.dot_general(a, b, (((1,), (1,)), ((), ())), preferred_element_type=F32)


def params():
    return pltpu.CompilerParams(vmem_limit_bytes=VMEM_LIMIT)


def front_kernel(
    act_ref, gain_ref, w_ref, wout_ref, dout_ref,
    scaled_ref, normed_ref, inv_ref, send0_ref, send1_ref, gate0_ref, gate1_ref, gg0_ref, gg1_ref,
):
    step = pl.program_id(0)
    sends = (send0_ref, send1_ref)

    @pl.when(step == 0)
    def _():
        values = act_ref[...].astype(F32)
        center = jnp.mean(values, -1, keepdims=True)
        shifted = values - center
        spread = jnp.mean(shifted * shifted, -1, keepdims=True)
        inv_std = lax.rsqrt(spread + EPS)
        normed = shifted * inv_std
        normed_ref[...] = normed
        inv_ref[...] = inv_std
        scaled_ref[...] = (normed * gain_ref[...]).astype(BF)

    block = dot(scaled_ref[...], w_ref[...])

    for kind in range(3):

        @pl.when(step == kind)
        def _(kind=kind):
            low = block.astype(BF).T
            for j in range(2):
                sends[j][:, kind * DH : (kind + 1) * DH, :] = low[:, j * TOK : (j + 1) * TOK].reshape(
                    HEADS, DH, TOK
                )

    @pl.when(step == 3)
    def _():
        gate = jax.nn.sigmoid(block.T)
        ggated = dot_nt(wout_ref[...], dout_ref[...]).astype(BF)
        gatt = (ggated.astype(F32) * gate).astype(BF)
        for j, gate_ref, gg_ref in ((0, gate0_ref, gg0_ref), (1, gate1_ref, gg1_ref)):
            cols = slice(j * TOK, (j + 1) * TOK)
            gate_ref[...] = gate[:, cols]
            gg_ref[...] = ggated[:, cols]
            sends[j][:, 3 * DH : 4 * DH, :] = gatt[:, cols].reshape(HEADS, DH, TOK)


def front(act, ln_gain, w_in, w_out, d_out):
    flat = act.shape[0]
    shapes = [
        ((flat, C), BF),
        ((flat, C), F32),
        ((flat, 1), F32),
        ((HEADS, 4 * DH, TOK), BF),
        ((HEADS, 4 * DH, TOK), BF),
        ((C, TOK), F32),
        ((C, TOK), F32),
        ((C, TOK), BF),
        ((C, TOK), BF),
    ]

    def whole(shape):
        return pl.BlockSpec(shape, lambda t: (0,) * len(shape))

    return pl.pallas_call(
        front_kernel,
        grid=(4,),
        in_specs=[
            whole((flat, C)),
            whole((1, C)),
            pl.BlockSpec((C, C), lambda t: (0, t)),
            whole((C, C)),
            whole((flat, C)),
        ],
        out_specs=[whole(s) for s, _ in shapes],
        out_shape=[jax.ShapeDtypeStruct(s, d) for s, d in shapes],
        compiler_params=params(),
        cost_estimate=pl.CostEstimate(
            flops=2 * flat * C * 5 * C, bytes_accessed=11 * 2**20, transcendentals=flat * C
        ),
        name="front",
    )(act, ln_gain, w_in, w_out, d_out)


def attention_kernel(*refs, rows, first):
    if first:
        x_ref, bias_ref, out_ref, gsum_ref = refs[:4]
        gin_ref = None
    else:
        x_ref, bias_ref, gin_ref, out_ref, gsum_ref = refs[:5]
    qa_s, ka_s, va_s, vt_s, kn_s, gn_s, qt_s, dk_s, dv_s, gb_s = refs[-10:]
    half = pl.program_id(0)
    block = pl.program_id(1)
    last_block = pl.num_programs(1) - 1
    per_block = rows // TOK

    @pl.when(block == 0)
    def _():
        whole = jnp.concatenate([x_ref[half * 8 + t] for t in range(8)], axis=1)
        qt, kt, vt, gt = (whole[i * DH : (i + 1) * DH] for i in range(4))
        qs = qt.astype(F32) * (SCALE * LOG2E)
        q_hi = qs.astype(BF)
        q_lo = (qs - q_hi.astype(F32)).astype(BF)
        zeros32 = jnp.zeros((32, KEYS), BF)
        zeros64 = jnp.zeros((64, KEYS), BF)
        zeros80 = jnp.zeros((80, KEYS), BF)
        ones16 = jnp.ones((16, KEYS), BF)
        qa_s[...] = jnp.concatenate([q_hi, q_lo, zeros32], axis=0).T
        ka_s[...] = jnp.concatenate([kt, kt, zeros32], axis=0)
        v_one = jnp.concatenate([vt, ones16, zeros64], axis=0)
        va_s[...] = v_one
        vt_s[...] = v_one.T
        kn_s[...] = jnp.concatenate([kt, zeros80], axis=0).T
        gn_s[...] = jnp.concatenate([gt, zeros80], axis=0).T
        qt_s[...] = qt
        dk_s[...] = jnp.zeros_like(dk_s)
        dv_s[...] = jnp.zeros_like(dv_s)

    row0 = pl.multiple_of(block * rows, rows)
    these = pl.ds(row0, rows)
    scores = dot(qa_s[these, :], ka_s[...]) + bias_ref[these, :].astype(F32) * LOG2E
    top = jnp.max(scores, axis=1, keepdims=True)
    expd = jnp.exp2(scores - top)
    expd_low = expd.astype(BF)
    summed = dot(expd_low, vt_s[...])
    inv = 1.0 / summed[:, DH : DH + 1]
    out = summed * inv
    gscaled = (gn_s[these, :].astype(F32) * inv).astype(BF)
    gscaled_f = gscaled.astype(F32)
    delta = jnp.sum(out * gscaled_f, axis=1, keepdims=True)
    delta_hi = delta.astype(BF).astype(F32)
    delta_lo = delta - delta_hi
    lane = lax.broadcasted_iota(jnp.int32, (rows, 128), 1)
    left = jnp.where(
        lane == DH, -delta_hi, jnp.where(lane == DH + 1, -delta_lo, gscaled_f)
    ).astype(BF)
    dscores = expd * dot(left, va_s[...])
    dscores_low = dscores.astype(BF)

    if first:

        @pl.when(half == 0)
        def _():
            gsum_ref[these, :] = dscores

        @pl.when(half == 1)
        def _():
            gsum_ref[these, :] = gsum_ref[these, :] + dscores

    else:

        @pl.when(half == 0)
        def _():
            gb_s[these, :] = gin_ref[these, :] + dscores

        @pl.when(half == 1)
        def _():
            total = (gb_s[these, :] + dscores).astype(BF)
            for x in range(4):
                even = total[:, x * 256 : x * 256 + 128]
                odd = total[:, x * 256 + 128 : x * 256 + 256]
                gsum_ref[2 * x, these, :] = jnp.concatenate([even[:, :64], odd[:, :64]], axis=1)
                gsum_ref[2 * x + 1, these, :] = jnp.concatenate([even[:, 64:], odd[:, 64:]], axis=1)

    dquery = dot(dscores_low, kn_s[...]) * SCALE
    dk_s[...] += dot(qt_s[:, these], dscores_low)
    gscaled_t = gscaled_f.T.astype(BF)
    dv_s[...] += dot(gscaled_t[:DH], expd_low)
    out_t = out.T
    dquery_t = dquery.T
    for t in range(per_block):
        cols = slice(t * TOK, (t + 1) * TOK)
        where = half * 8 + block * per_block + t
        out_ref[where, 0:DH, :] = out_t[:DH, cols].astype(BF)
        out_ref[where, DH : 2 * DH, :] = dquery_t[:DH, cols].astype(BF)

    @pl.when(block == last_block)
    def _():
        for t in range(8):
            cols = slice(t * TOK, (t + 1) * TOK)
            out_ref[half * 8 + t, 2 * DH : 3 * DH, :] = (dk_s[:, cols] * SCALE).astype(BF)
            out_ref[half * 8 + t, 3 * DH : 4 * DH, :] = dv_s[:, cols].astype(BF)


def attention(x, bias, gsum=None, rows=256):
    first = gsum is None

    def whole(shape):
        return pl.BlockSpec(shape, lambda s, b: (0,) * len(shape))

    sum_shape, sum_type = ((KEYS, KEYS), F32) if first else ((8, KEYS, 128), BF)
    operands = [x, bias] + ([] if first else [gsum])
    return pl.pallas_call(
        functools.partial(attention_kernel, rows=rows, first=first),
        grid=(2, KEYS // rows),
        in_specs=[whole(o.shape) for o in operands],
        out_specs=[whole(x.shape), whole(sum_shape)],
        out_shape=[jax.ShapeDtypeStruct(x.shape, BF), jax.ShapeDtypeStruct(sum_shape, sum_type)],
        scratch_shapes=[
            pltpu.VMEM((KEYS, 128), BF),
            pltpu.VMEM((128, KEYS), BF),
            pltpu.VMEM((128, KEYS), BF),
            pltpu.VMEM((KEYS, 128), BF),
            pltpu.VMEM((KEYS, 128), BF),
            pltpu.VMEM((KEYS, 128), BF),
            pltpu.VMEM((DH, KEYS), BF),
            pltpu.VMEM((DH, KEYS), F32),
            pltpu.VMEM((DH, KEYS), F32),
            pltpu.VMEM((8, 128) if first else (KEYS, KEYS), F32),
        ],
        compiler_params=params(),
        cost_estimate=pl.CostEstimate(
            flops=2 * 6 * 2 * KEYS * KEYS * 256, bytes_accessed=8 * 2**20, transcendentals=2 * KEYS * KEYS
        ),
        name="attention",
    )(*operands)


def gate_kernel(core_ref, back_ref, gate_ref, gg_ref, gproj_ref, gated_ref, send_ref):
    other = 1 - core_ref[0]
    att = back_ref[:, :DH, :].astype(F32).reshape(C, TOK)
    gate = gate_ref[...]
    opened = att * gate
    gated = opened.astype(BF)
    gated_ref[...] = gated
    send_ref[8] = gated[: C // 4]
    send_ref[9] = gated[C // 4 : C // 2]
    send_ref[10] = gated[C // 2 : 3 * C // 4]
    send_ref[11] = gated[3 * C // 4 :]
    for kind in range(3):
        gproj_ref[kind * 4 : kind * 4 + 4] = back_ref[:, (kind + 1) * DH : (kind + 2) * DH, :].reshape(
            4, 4 * DH, TOK
        )
    gproj_ref[12:16] = (gg_ref[...].astype(F32) * opened * (1.0 - gate)).astype(BF).reshape(4, 4 * DH, TOK)
    for n in range(8):
        send_ref[n] = gproj_ref[2 * n + other]


def gate_step(core, back, gate, ggated):
    def whole(shape):
        return pl.BlockSpec(shape, lambda t, core: (0,) * len(shape))

    shapes = [(16, 4 * DH, TOK), (C, TOK), (12, 4 * DH, TOK)]
    return pl.pallas_call(
        gate_kernel,
        grid_spec=pltpu.PrefetchScalarGridSpec(
            num_scalar_prefetch=1,
            grid=(1,),
            in_specs=[whole(back.shape), whole(gate.shape), whole(ggated.shape)],
            out_specs=[whole(s) for s in shapes],
        ),
        out_shape=[jax.ShapeDtypeStruct(s, BF) for s in shapes],
        compiler_params=params(),
        cost_estimate=pl.CostEstimate(flops=6 * C * TOK, bytes_accessed=4 * 2**20, transcendentals=0),
        name="gate",
    )(core, back, gate, ggated)


def weight_kernel(
    core_ref, g0_ref, g1_ref, o0_ref, o1_ref, gated0_ref, gated1_ref, sc_ref, sco_ref, do_ref, doo_ref,
    a_ref, b_ref, c_ref, scaled_s, gated_s,
):
    core = core_ref[0]
    n = pl.program_id(0)
    x = n // 2
    zh = n % 2

    @pl.when(n == 0)
    def _():
        scaled_s[: 2 * TOK] = sc_ref[...]
        scaled_s[2 * TOK :] = sco_ref[...]
        gated_s[:TOK] = gated0_ref[...].T
        gated_s[TOK : 2 * TOK] = gated1_ref[...].T
        for q in range(4):
            lanes = slice(q * 192, (q + 1) * 192)
            gated_s[2 * TOK : 3 * TOK, lanes] = o0_ref[8 + q].T
            gated_s[3 * TOK :, lanes] = o1_ref[8 + q].T

    mine = 2 * n + core
    left = jnp.concatenate([g0_ref[mine], g1_ref[mine], o0_ref[n], o1_ref[n]], axis=1)
    win = dot(left, scaled_s[...])
    wout = dot(jnp.concatenate([do_ref[n], doo_ref[n]], axis=1), gated_s[...])
    for k in range(8):
        zl, y = k // 4, k % 4
        z = zh * 2 + zl
        chunk = jnp.concatenate([win[k * 24 : k * 24 + 24], wout[k * 8 : k * 8 + 8]], axis=0).astype(BF)
        a_ref[y, z, x] = chunk[:, :256]
        b_ref[z, x, y] = chunk[:, 256:512]
        c_ref[x, y, z] = chunk[:, 512:]


def weight_grads(core, operands):
    def whole(shape):
        return pl.BlockSpec(shape, lambda t, core: (0,) * len(shape))

    shape = (4, 4, 4, 32, 256)
    return pl.pallas_call(
        weight_kernel,
        grid_spec=pltpu.PrefetchScalarGridSpec(
            num_scalar_prefetch=1,
            grid=(8,),
            in_specs=[whole(o.shape) for o in operands],
            out_specs=[whole(shape)] * 3,
            scratch_shapes=[pltpu.VMEM((4 * TOK, C), BF), pltpu.VMEM((4 * TOK, C), BF)],
        ),
        out_shape=[jax.ShapeDtypeStruct(shape, BF)] * 3,
        compiler_params=params(),
        cost_estimate=pl.CostEstimate(
            flops=2 * 4 * TOK * C * 2048, bytes_accessed=8 * 2**20, transcendentals=0
        ),
        name="weight_grads",
    )(core, *operands)


def reduce_parts(parts):
    axes = {"x": "x", "y": "y", "z": ("zh", "zl")}
    orders = ("yzx", "zxy", "xyz")
    for stage in range(3):
        sent = [
            lax.all_to_all(p, axes[order[stage]], 0, 0, tiled=True) for p, order in zip(parts, orders)
        ]
        parts = [jnp.sum(p.astype(F32), axis=0) for p in sent]
        if stage < 2:
            parts = [p.astype(BF) for p in parts]
    return jnp.concatenate(parts, axis=-1)


def sum_everywhere(vector):
    tile = jnp.pad(vector, (0, 1024 - C)).reshape(8, 128)
    tile = jnp.sum(
        lax.all_to_all(jnp.broadcast_to(tile, (8, 8, 128)), ("x", "core"), 0, 0, tiled=True), axis=0
    )
    tile = jnp.sum(
        lax.all_to_all(jnp.broadcast_to(tile, (16, 8, 128)), PLANE, 0, 0, tiled=True), axis=0
    )
    return tile.reshape(1024)[:C]


def per_device(act, pair_bias, ln_gain, w_in, w_out, d_out):
    sample_count, row_count, channels = act.shape
    flat = sample_count * row_count
    core = lax.axis_index("core")
    core_arg = jnp.full((1,), core, jnp.int32)
    zh = lax.axis_index("zh")

    bias_own = lax.dynamic_slice(pair_bias, (zh * 8, core * 64, 0), (8, 64, KEYS))
    bias_own = lax.all_to_all(bias_own, ("zl", "y"), 0, 0, tiled=True)
    bias_other = lax.ppermute(bias_own, "core", SWAP)
    is_first = core == 0
    bias_head = jnp.stack(
        [jnp.where(is_first, bias_own, bias_other), jnp.where(is_first, bias_other, bias_own)], axis=1
    ).reshape(KEYS, KEYS)

    rows_out = d_out.reshape(flat, channels)
    scaled, normed, inv_std, send0, send1, gate0, gate1, gg0, gg1 = front(
        act.reshape(flat, channels), ln_gain.reshape(1, C), w_in, w_out, rows_out
    )
    in0 = lax.all_to_all(send0, PLANE, 0, 0, tiled=True)
    send1, in0 = lax.optimization_barrier((send1, in0))
    in1 = lax.all_to_all(send1, PLANE, 0, 0, tiled=True)

    dout_t = jnp.pad(rows_out.T.reshape(128, 6, flat), ((0, 0), (0, 2), (0, 0)))
    dout_t = dout_t.reshape(8, 2, 64, flat)
    dout_mine = lax.dynamic_index_in_dim(dout_t, core, 1, keepdims=False)
    dout_send = lax.dynamic_index_in_dim(dout_t, 1 - core, 1, keepdims=False)
    dout_other = lax.ppermute(dout_send, "core", SWAP)
    scaled_other = lax.ppermute(scaled, "core", SWAP)

    result0, gsum = attention(in0, bias_head)
    back0 = lax.all_to_all(result0, PLANE, 0, 0, tiled=True)
    result1, gsum = attention(in1, bias_head, gsum)
    back1 = lax.all_to_all(result1, PLANE, 0, 0, tiled=True)

    gb = lax.psum_scatter(gsum, ("x", "core"), scatter_dimension=0, tiled=False)
    gb = gb.reshape(8, TOK, 2, 64).transpose(2, 0, 1, 3).reshape(HEADS, TOK, 64)
    grad_bias = lax.all_to_all(gb, PLANE, 0, 0, tiled=True).astype(F32)

    gproj0, gated0, half0 = gate_step(core_arg, back0, gate0, gg0)
    other0 = lax.ppermute(half0, "core", SWAP)
    gproj1, gated1, half1 = gate_step(core_arg, back1, gate1, gg1)
    other1 = lax.ppermute(half1, "core", SWAP)
    parts = weight_grads(
        core_arg,
        (gproj0, gproj1, other0, other1, gated0, gated1, scaled, scaled_other, dout_mine, dout_other),
    )
    total = reduce_parts(parts)

    outputs = []
    grad_acts = []
    gain = jnp.zeros((C,), F32)
    for j, gproj, gated in ((0, gproj0, gated0), (1, gproj1, gated1)):
        rows = slice(j * TOK, (j + 1) * TOK)
        outputs.append(jnp.einsum("cr,cd->rd", gated, w_out, preferred_element_type=F32).astype(BF))
        grad_scaled = jnp.einsum(
            "dr,cd->rc", gproj.reshape(4 * C, TOK), w_in, preferred_element_type=F32
        )
        gain = gain + jnp.sum(grad_scaled * normed[rows], 0)
        grad_normed = grad_scaled * ln_gain
        grad_acts.append(
            (
                inv_std[rows]
                * (
                    grad_normed
                    - jnp.mean(grad_normed, -1, keepdims=True)
                    - normed[rows] * jnp.mean(grad_normed * normed[rows], -1, keepdims=True)
                )
            ).astype(BF)
        )
    return (
        jnp.stack(outputs),
        jnp.stack(grad_acts),
        grad_bias,
        sum_everywhere(gain),
        total[:24].T,
        total[24:30].T,
    )


def solution(mesh):
    fine = Mesh(mesh.devices.reshape(4, 2, 2, 2, 4), ("x", "zh", "core", "zl", "y"))
    sample = ("x", "zh", "core")
    tok = ("zl", "y")
    return jax.shard_map(
        per_device,
        mesh=fine,
        in_specs=(
            P(sample, tok, None),
            P(None, tok, None),
            P(),
            P(),
            P(),
            P(sample, tok, None),
        ),
        out_specs=(
            P(sample, tok, None),
            P(sample, tok, None),
            P(None, tok, sample),
            P(),
            P(None, sample + tok),
            P(None, sample + tok),
        ),
        check_vma=False,
    )
```

time: 246 us -> 309 us (1.26)
  the two profiles are of different devices: /device:TPU:103 before, /device:TPU:0 now
where the time goes in v2:
time: 309 us; the launch traced here: 307 us
  blocking collectives  68.4 us (22%)
  starting transfers between devices  59.8 us (19%)
  waiting for transfers between devices  55.6 us (18%)
  Pallas kernels  46.7 us (15%)
  local copies, waits for them, and re-layouts  32.7 us (11%)
  other arithmetic  17.1 us (6%)
  between operations  14.5 us (5%)
  matrix products  11.7 us (4%)
    all_to_all x2, blocking collectives, reduce_parts(): lax.all_to_all(p, axes[order[stage]], 0, 0, tiled=True)  37.1 us
    all_to_all x7, waiting for transfers between devices, reduce_parts(): lax.all_to_all(p, axes[order[stage]], 0, 0, tiled=True)  33 us
    pallas_call x2, Pallas kernels, attention(): pl.pallas_call(functools.partial(attention_kernel, rows=rows, first=first...  31.2 us
    all_to_all x7, starting transfers between devices, reduce_parts(): lax.all_to_all(p, axes[order[stage]], 0, 0, tiled=True)  24.3 us
    all_to_all x1, blocking collectives, per_device(): bias_own = lax.all_to_all(bias_own, ('zl', 'y'), 0, 0, tiled=True)  21.5 us
    unnamed x77, local copies, waits for them, and re-layouts  19.6 us
    all_to_all x1, waiting for transfers between devices, per_device(): in0 = lax.all_to_all(send0, PLANE, 0, 0, tiled=True)  15 us
    all_to_all x1, blocking collectives, sum_everywhere(): lax.all_to_all(jnp.broadcast_to(tile, (8, 8, 128)), ('x', 'core'), 0, 0,...  9.75 us
  transfers between devices with their start and end apart: 19, of which 10 were waited for; matrix products, arithmetic and copies ran while one was open for 12% of the time, Pallas kernels for 15%

profile of v2, /device:TPU:0, one launch (start us, length us, event | category | flops | bytes accessed | tf_op | source)
XLA Modules:
  0.0 306.5 jit_solution(13929516485992069854)
XLA Ops:
  7.2 1.4 constant_dynamic-slice_fusion
  8.7 21.5 %all_to_all.85 = bf16[8,64,1024]{2,1,0:T(8,128)(2,1)} all-to-all(bf16[8,64,1024]{2,1,0:T(8,128)(2,1)S(1)} %constant_dynamic-slice_fusion), channel_id=1, replica_groups=mesh['x'=4,'zh'=2,'core'=2,'zl'=2,'y'=4] {'zl','y'}, dimensions={0} | all-to-all | bytes 2097152 | tf_op jit(solution)/shard_map/all_to_all | solution.py:381
  30.2 6.4 %front.1 = (bf16[256,768]{1,0:T(8,128)(2,1)S(1)}, f32[256,768]{1,0:T(8,128)S(1)}, f32[256,1]{1,0:T(8,128)S(1)}, bf16[16,192,128]{2,1,0:T(8,128)(2,1)}, bf16[16,1...) custom-call(bf16[256,768]{1,0:T(8,128)(2,1)S(1)} %bitcast.56, ...), custom_call_target="tpu_custom_call" | custom-call | flops 1509949440 | bytes 11534336 | tf_op jit(solution)/shard_map/front/pallas_call | solution.py:99
  40.9 5.6 %all-to-all-start = ((bf16[16,192,128]{2,1,0:T(8,128)(2,1)}), bf16[16,192,128]{2,1,0:T(8,128)(2,1)S(1)}, u32[]{:S(2)}, u32[]{:S(2)}) async-start(bf16[16,192,128]{2,1,0:T(8,128)(2,1)} %get-tuple-element.31), calls=%async_computation | async-start | bytes 1572864 | tf_op jit(solution)/shard_map/all_to_all | solution.py:392
  46.5 15.0 %all-to-all-done.refs_0_ = bf16[16,192,128]{2,1,0:T(8,128)(2,1)S(1)} async-done(((bf16[16,192,128]{2,1,0:T(8,128)(2,1)}), bf16[16,192,128]{2,1,0:T(8,128)(2,1)S(1)}, u32[]{:S(2)}, u32[]{:S(2)}) %all-to-all-start) | async-done | bytes 786464 | tf_op jit(solution)/shard_map/all_to_all | solution.py:392
  61.6 3.6 %all-to-all-start.3 = ((bf16[16,192,128]{2,1,0:T(8,128)(2,1)}), bf16[16,192,128]{2,1,0:T(8,128)(2,1)S(1)}, u32[]{:S(2)}, u32[]{:S(2)}) async-start(bf16[16,192,128]{2,1,0:T(8,128)(2,1)} %get-tuple-element.37), calls=%async_computation.3 | async-start | bytes 1572864 | tf_op jit(solution)/shard_map/all_to_all | solution.py:394
  65.2 1.7 select_bitcast_fusion.1
  67.3 15.1 %attention.2 = (bf16[16,192,128]{2,1,0:T(8,128)(2,1)S(1)}, f32[1024,1024]{1,0:T(8,128)}) custom-call(bf16[16,192,128]{2,1,0:T(8,128)(2,1)S(1)} %all-to-all-done.refs_0_, bf16[1024,1024]{1,0:T(8,128)(2,1)S(1)} %bitcast.50), custom_call_target="tpu_custom_call" | custom-call | flops 6442450944 | bytes 8388608 | tf_op jit(solution)/shard_map/attention/pallas_call | solution.py:227
  82.4 1.3 copy-done.2
  84.7 7.2 %all-to-all-start.2 = ((bf16[16,192,128]{2,1,0:T(8,128)(2,1)}), bf16[16,192,128]{2,1,0:T(8,128)(2,1)S(1)}, u32[]{:S(2)}, u32[]{:S(2)}) async-start(bf16[16,192,128]{2,1,0:T(8,128)(2,1)} %copy-done.6), calls=%async_computation.2 | async-start | bytes 1572864 | tf_op jit(solution)/shard_map/all_to_all | solution.py:404
  91.8 1.6 copy-done.3
  93.4 16.1 %attention.3 = (bf16[16,192,128]{2,1,0:T(8,128)(2,1)S(1)}, bf16[8,1024,128]{2,1,0:T(8,128)(2,1)S(1)}) custom-call(bf16[16,192,128]{2,1,0:T(8,128)(2,1)S(1)} %all-to-all-done.3.refs_0_, bf16[1024,1024]{1,0:T(8,128)(2,1)S(1)} %bitcast.51, f32[1024,1024]{1,0:T(8,128)} %get-tuple-element.38.refs_2_), custom_call_target="tpu_custom_call" | custom-call | flops 6442450944 | bytes 8388608 | tf_op jit(solution)/shard_map/attention/pallas_call | solution.py:227
  109.5 1.3 copy-done.1
  111.7 7.2 %all-to-all-start.4 = ((bf16[16,192,128]{2,1,0:T(8,128)(2,1)}), bf16[16,192,128]{2,1,0:T(8,128)(2,1)S(1)}, u32[]{:S(2)}, u32[]{:S(2)}) async-start(bf16[16,192,128]{2,1,0:T(8,128)(2,1)} %copy-done.5), calls=%async_computation.4 | async-start | bytes 1572864 | tf_op jit(solution)/shard_map/all_to_all | solution.py:406
  119.1 1.9 copy.24
  121.0 1.9 reshape.69
  122.9 1.9 pad.9
  124.8 1.9 dynamic-slice_bitcast_fusion
  129.2 1.1 gate.2
  133.8 1.1 gate.3
  135.3 4.1 %fusion.4 = f32[128,768]{1,0:T(8,128)S(1)} fusion(bf16[3072,128]{1,0:T(8,128)(2,1)S(1)} %bitcast.55, bf16[768,3072]{1,0:T(8,128)(2,1)} %w_ref.1), kind=kOutput, calls=%fused_computation.36 | convolution fusion | flops 603979776 | bytes 5898240 | tf_op jit(solution)/shard_map/dr,cd->rc/dot_general | solution.py:428
  139.5 5.5 %multiply_reduce_fusion.1 = (f32[768]{0:T(1024)S(1)}, f32[128]{0:T(128)}, f32[128]{0:T(128)S(1)}, f32[768]{0:T(1024)S(1)}, f32[128]{0:T(128)S(1)}, /*index=5*/f32[128]{0:T(128)}, f32[128,768]{1,0:T(8,128)}) fusion(f32[256,768]{1,0:T(8,128)S(1)} %get-tuple-element.45, f32[768]{0:T(1024)S(1)} %copy-done.35, f32[128,768]{1,0:T(8,128)S(1)} %fusion.4, ...), kind=kOutput, calls=%fused_computation.10 | convolution fusion | flops 605157376 | bytes 7089152 | tf_op jit(solution)/shard_map/dr,cd->rc/dot_general | solution.py:428
  145.0 9.8 %all_to_all.86 = f32[8,8,128]{2,1,0:T(8,128)} all-to-all(f32[8,8,128]{2,1,0:T(8,128)S(1)} %broadcast_in_dim.7), channel_id=1, replica_groups=mesh['x'=4,'zh'=2,'core'=2,'zl'=2,'y'=4] {'x','core'}, dimensions={0} | all-to-all | bytes 65536 | tf_op jit(solution)/shard_map/all_to_all | solution.py:365
  156.1 7.3 %all-to-all-start.7 = ((f32[16,8,128]{2,1,0:T(8,128)}), f32[16,8,128]{2,1,0:T(8,128)}, u32[]{:S(2)}, u32[]{:S(2)}) async-start(f32[16,8,128]{2,1,0:T(8,128)} %broadcast_in_dim.8), calls=%async_computation.8 | async-start | bytes 131072 | tf_op jit(solution)/shard_map/all_to_all | solution.py:368
  167.3 7.0 %weight_grads.1 = (bf16[4,4,4,32,256]{4,3,2,1,0:T(8,128)(2,1)}, bf16[4,4,4,32,256]{4,3,2,1,0:T(8,128)(2,1)}, bf16[4,4,4,32,256]{4,3,2,1,0:T(8,128)(2,1)}) custom-call(s32[1]{0:T(128)} %bitcast.core_ref, bf16[16,192,128]{2,1,0:T(8,128)(2,1)S(1)} %copy-done.8, bf16[16,192,128]{2,1,0:T(8,128)(2,1)S(1)} %copy-done.10, ...), custom_call_target="tpu_custom_call" | custom-call | flops 1610612736 | bytes 8388608 | tf_op jit(solution)/shard_map/weight_grads/pallas_call | solution.py:331
  174.4 19.5 %all_to_all.87 = bf16[4,4,4,32,256]{4,3,2,1,0:T(8,128)(2,1)} all-to-all(bf16[4,4,4,32,256]{4,3,2,1,0:T(8,128)(2,1)} %get-tuple-element.53), channel_id=1, replica_groups=mesh['x'=4,'zh'=2,'core'=2,'zl'=2,'y'=4] {'x'}, dimensions={0} | all-to-all | bytes 2097152 | tf_op jit(solution)/shard_map/all_to_all | solution.py:354
  193.9 17.6 %all_to_all.88 = bf16[4,4,4,32,256]{4,3,2,1,0:T(8,128)(2,1)} all-to-all(bf16[4,4,4,32,256]{4,3,2,1,0:T(8,128)(2,1)S(1)} %copy-done.32), channel_id=1, replica_groups=mesh['x'=4,'zh'=2,'core'=2,'zl'=2,'y'=4] {'zh','zl'}, dimensions={0} | all-to-all | bytes 2097152 | tf_op jit(solution)/shard_map/all_to_all | solution.py:354
  211.5 4.2 %all-to-all-start.8 = ((bf16[4,4,4,32,256]{4,3,2,1,0:T(8,128)(2,1)}), bf16[4,4,4,32,256]{4,3,2,1,0:T(8,128)(2,1)S(1)}, u32[]{:S(2)}, u32[]{:S(2)}) async-start(bf16[4,4,4,32,256]{4,3,2,1,0:T(8,128)(2,1)} %get-tuple-element.51), calls=%async_computation.9 | async-start | bytes 2097152 | tf_op jit(solution)/shard_map/all_to_all | solution.py:354
  215.9 2.2 reduce_sum.185
  218.1 9.4 %all-to-all-done.8 = bf16[4,4,4,32,256]{4,3,2,1,0:T(8,128)(2,1)S(1)} async-done(((bf16[4,4,4,32,256]{4,3,2,1,0:T(8,128)(2,1)}), bf16[4,4,4,32,256]{4,3,2,1,0:T(8,128)(2,1)S(1)}, u32[]{:S(2)}, u32[]{:S(2)}) %all-to-all-start.8) | async-done | bytes 1048608 | tf_op jit(solution)/shard_map/all_to_all | solution.py:354
  227.5 3.4 %all-to-all-start.15 = ((bf16[4,4,32,256]{3,2,1,0:T(8,128)(2,1)}), bf16[4,4,32,256]{3,2,1,0:T(8,128)(2,1)S(1)}, u32[]{:S(2)}, u32[]{:S(2)}) async-start(bf16[4,4,32,256]{3,2,1,0:T(8,128)(2,1)} %reduce_sum.185), calls=%async_computation.16 | async-start | bytes 524288 | tf_op jit(solution)/shard_map/all_to_all | solution.py:354
  230.9 2.1 fusion.2
  233.0 2.2 reduce_sum.182
  235.3 2.3 all-to-all-done.15
  237.6 3.4 %all-to-all-start.12 = ((bf16[4,4,32,256]{3,2,1,0:T(8,128)(2,1)}), bf16[4,4,32,256]{3,2,1,0:T(8,128)(2,1)S(1)}, u32[]{:S(2)}, u32[]{:S(2)}) async-start(bf16[4,4,32,256]{3,2,1,0:T(8,128)(2,1)} %reduce_sum.182), calls=%async_computation.13 | async-start | bytes 524288 | tf_op jit(solution)/shard_map/all_to_all | solution.py:354
  244.0 3.6 %all-to-all-done.12 = bf16[4,4,32,256]{3,2,1,0:T(8,128)(2,1)S(1)} async-done(((bf16[4,4,32,256]{3,2,1,0:T(8,128)(2,1)}), bf16[4,4,32,256]{3,2,1,0:T(8,128)(2,1)S(1)}, u32[]{:S(2)}, u32[]{:S(2)}) %all-to-all-start.12) | async-done | bytes 262176 | tf_op jit(solution)/shard_map/all_to_all | solution.py:354
  247.6 3.4 %all-to-all-start.9 = ((bf16[4,4,32,256]{3,2,1,0:T(8,128)(2,1)}), bf16[4,4,32,256]{3,2,1,0:T(8,128)(2,1)S(1)}, u32[]{:S(2)}, u32[]{:S(2)}) async-start(bf16[4,4,32,256]{3,2,1,0:T(8,128)(2,1)} %reduce_sum.179), calls=%async_computation.10 | async-start | bytes 524288 | tf_op jit(solution)/shard_map/all_to_all | solution.py:354
  251.1 1.8 pad_maximum_fusion.1
  255.2 2.9 all-to-all-done.9
  258.1 3.3 %all-to-all-start.16 = ((bf16[4,32,256]{2,1,0:T(8,128)(2,1)}), bf16[4,32,256]{2,1,0:T(8,128)(2,1)S(1)}, u32[]{:S(2)}, u32[]{:S(2)}) async-start(bf16[4,32,256]{2,1,0:T(8,128)(2,1)} %reduce_sum.186), calls=%async_computation.17 | async-start | bytes 131072 | tf_op jit(solution)/shard_map/all_to_all | solution.py:354
  263.3 3.7 %all-to-all-done.16 = bf16[4,32,256]{2,1,0:T(8,128)(2,1)S(1)} async-done(((bf16[4,32,256]{2,1,0:T(8,128)(2,1)}), bf16[4,32,256]{2,1,0:T(8,128)(2,1)S(1)}, u32[]{:S(2)}, u32[]{:S(2)}) %all-to-all-start.16) | async-done | bytes 65568 | tf_op jit(solution)/shard_map/all_to_all | solution.py:354
  266.9 3.3 %all-to-all-start.13 = ((bf16[4,32,256]{2,1,0:T(8,128)(2,1)}), bf16[4,32,256]{2,1,0:T(8,128)(2,1)S(1)}, u32[]{:S(2)}, u32[]{:S(2)}) async-start(bf16[4,32,256]{2,1,0:T(8,128)(2,1)} %reduce_sum.183), calls=%async_computation.14 | async-start | bytes 131072 | tf_op jit(solution)/shard_map/all_to_all | solution.py:354
  270.2 5.6 %all-to-all-done.13 = bf16[4,32,256]{2,1,0:T(8,128)(2,1)S(1)} async-done(((bf16[4,32,256]{2,1,0:T(8,128)(2,1)}), bf16[4,32,256]{2,1,0:T(8,128)(2,1)S(1)}, u32[]{:S(2)}, u32[]{:S(2)}) %all-to-all-start.13) | async-done | bytes 65568 | tf_op jit(solution)/shard_map/all_to_all | solution.py:354
  275.8 3.3 %all-to-all-start.10 = ((bf16[4,32,256]{2,1,0:T(8,128)(2,1)}), bf16[4,32,256]{2,1,0:T(8,128)(2,1)S(1)}, u32[]{:S(2)}, u32[]{:S(2)}) async-start(bf16[4,32,256]{2,1,0:T(8,128)(2,1)} %reduce_sum.180), calls=%async_computation.11 | async-start | bytes 131072 | tf_op jit(solution)/shard_map/all_to_all | solution.py:354
  279.1 5.6 %all-to-all-done.10 = bf16[4,32,256]{2,1,0:T(8,128)(2,1)S(1)} async-done(((bf16[4,32,256]{2,1,0:T(8,128)(2,1)}), bf16[4,32,256]{2,1,0:T(8,128)(2,1)S(1)}, u32[]{:S(2)}, u32[]{:S(2)}) %all-to-all-start.10) | async-done | bytes 65568 | tf_op jit(solution)/shard_map/all_to_all | solution.py:354
  284.8 1.1 copy.22
  286.7 3.5 %all-to-all-start.5 = ((bf16[16,128,64]{1,2,0:T(8,128)(2,1)}), bf16[16,128,64]{1,2,0:T(8,128)(2,1)S(1)}, u32[]{:S(2)}, u32[]{:S(2)}) async-start(bf16[16,128,64]{1,2,0:T(8,128)(2,1)} %bitcast.13), calls=%async_computation.6 | async-start | bytes 524288 | tf_op jit(solution)/shard_map/all_to_all | solution.py:410
  291.4 7.4 %all-to-all-done.5 = bf16[16,128,64]{1,2,0:T(8,128)(2,1)S(1)} async-done(((bf16[16,128,64]{1,2,0:T(8,128)(2,1)}), bf16[16,128,64]{1,2,0:T(8,128)(2,1)S(1)}, u32[]{:S(2)}, u32[]{:S(2)}) %all-to-all-start.5) | async-done | bytes 262176 | tf_op jit(solution)/shard_map/all_to_all | solution.py:410
  (119 shorter events, 28.7 us)
Async XLA Ops:
  7.2 23.0 %copy-start.35 = (f32[768]{0:T(1024)S(1)}, f32[768]{0:T(1024)}, u32[]{:S(2)}) copy-start(f32[768]{0:T(1024)} %param.8) | copy-start | bytes 9220
  7.2 23.0 %copy-start = (bf16[768,768]{1,0:T(8,128)(2,1)S(1)}, bf16[768,768]{1,0:T(8,128)(2,1)}, u32[]{:S(2)}) copy-start(bf16[768,768]{1,0:T(8,128)(2,1)} %wout_ref.1) | copy-start | bytes 3538948
  7.2 23.0 %copy-start.4 = (bf16[2,128,768]{2,1,0:T(8,128)(2,1)S(1)}, bf16[2,128,768]{2,1,0:T(8,128)(2,1)}, u32[]{:S(2)}) copy-start(bf16[2,128,768]{2,1,0:T(8,128)(2,1)} %param.11) | copy-start | bytes 1179652
  7.2 23.0 %copy-start.15 = (bf16[2,128,768]{2,1,0:T(8,128)(2,1)S(1)}, bf16[2,128,768]{2,1,0:T(8,128)(2,1)}, u32[]{:S(2)}) copy-start(bf16[2,128,768]{2,1,0:T(8,128)(2,1)} %param.6) | copy-start | bytes 1179652
  30.2 35.0 %collective-permute-start = (bf16[8,64,1024]{2,1,0:T(8,128)(2,1)}, bf16[8,64,1024]{2,1,0:T(8,128)(2,1)}, u32[]{:S(2)}, u32[]{:S(2)}) collective-permute-start(bf16[8,64,1024]{2,1,0:T(8,128)(2,1)} %all_to_all.85), channel_id=1, source_target_pairs={{0,8},{8,0},{1,9},{9,1},{2,10},{10,2},{3,11},{11,3},{4,12},{12,4},... | collective-permute-start | bytes 3145736 | tf_op jit(solution)/shard_map/ppermute | solution.py:382
  40.9 20.6 %all-to-all-start = ((bf16[16,192,128]{2,1,0:T(8,128)(2,1)}), bf16[16,192,128]{2,1,0:T(8,128)(2,1)S(1)}, u32[]{:S(2)}, u32[]{:S(2)}) async-start(bf16[16,192,128]{2,1,0:T(8,128)(2,1)} %get-tuple-element.31), calls=%async_computation | async-start | bytes 1572864 | tf_op jit(solution)/shard_map/all_to_all | solution.py:392
  61.6 23.1 %all-to-all-start.3 = ((bf16[16,192,128]{2,1,0:T(8,128)(2,1)}), bf16[16,192,128]{2,1,0:T(8,128)(2,1)S(1)}, u32[]{:S(2)}, u32[]{:S(2)}) async-start(bf16[16,192,128]{2,1,0:T(8,128)(2,1)} %get-tuple-element.37), calls=%async_computation.3 | async-start | bytes 1572864 | tf_op jit(solution)/shard_map/all_to_all | solution.py:394
  82.4 1.3 copy-start.2
  84.7 27.0 %all-to-all-start.2 = ((bf16[16,192,128]{2,1,0:T(8,128)(2,1)}), bf16[16,192,128]{2,1,0:T(8,128)(2,1)S(1)}, u32[]{:S(2)}, u32[]{:S(2)}) async-start(bf16[16,192,128]{2,1,0:T(8,128)(2,1)} %copy-done.6), calls=%async_computation.2 | async-start | bytes 1572864 | tf_op jit(solution)/shard_map/all_to_all | solution.py:404
  91.8 1.6 copy-start.3
  109.5 1.3 copy-start.1
  111.7 20.2 %all-to-all-start.4 = ((bf16[16,192,128]{2,1,0:T(8,128)(2,1)}), bf16[16,192,128]{2,1,0:T(8,128)(2,1)S(1)}, u32[]{:S(2)}, u32[]{:S(2)}) async-start(bf16[16,192,128]{2,1,0:T(8,128)(2,1)} %copy-done.5), calls=%async_computation.4 | async-start | bytes 1572864 | tf_op jit(solution)/shard_map/all_to_all | solution.py:406
  118.9 165.8 %reduce-scatter.2.cloned.1.call-start = ((), (), s32[]{:S(2)}) async-start(), calls=%async_computation.18 | async-start | bytes 2359296 | tf_op jit(solution)/shard_map/reduce_scatter | solution.py:408
  119.0 44.5 %collective-permute-start.3 = (bf16[256,768]{1,0:T(8,128)(2,1)}, bf16[256,768]{1,0:T(8,128)(2,1)}, u32[]{:S(2)}, u32[]{:S(2)}) collective-permute-start(bf16[256,768]{1,0:T(8,128)(2,1)} %copy-done.29), channel_id=1, source_target_pairs={{0,8},{8,0},{1,9},{9,1},{2,10},{10,2},{3,11},{11,3},{4,12},{12,4},... | collective-permute-start | bytes 1179656 | tf_op jit(solution)/shard_map/ppermute | solution.py:401
  126.7 36.8 %collective-permute-start.4 = (bf16[8,64,256]{2,1,0:T(8,128)(2,1)}, bf16[8,64,256]{2,1,0:T(8,128)(2,1)}, u32[]{:S(2)}, u32[]{:S(2)}) collective-permute-start(bf16[8,64,256]{2,1,0:T(8,128)(2,1)} %get-tuple-element.68), channel_id=1, source_target_pairs={{0,8},{8,0},{1,9},{9,1},{2,10},{10,2},{3,11},{11,3},{4,12},{12,4},... | collective-permute-start | bytes 786440 | tf_op jit(solution)/shard_map/ppermute | solution.py:400
  127.2 1.0 copy-start.14
  128.2 0.9 copy-start.26
  130.2 0.9 copy-start.7
  131.8 31.7 %collective-permute-start.1 = (bf16[12,192,128]{2,1,0:T(8,128)(2,1)}, bf16[12,192,128]{2,1,0:T(8,128)(2,1)}, u32[]{:S(2)}, u32[]{:S(2)}) collective-permute-start(bf16[12,192,128]{2,1,0:T(8,128)(2,1)} %get-tuple-element.48), channel_id=1, source_target_pairs={{0,8},{8,0},{1,9},{9,1},{2,10},{10,2},{3,11},{11,3},{4,12},{12,4},... | collective-permute-start | bytes 1769480 | tf_op jit(solution)/shard_map/ppermute | solution.py:413
  131.9 1.0 copy-start.12
  132.9 0.9 copy-start.24
  134.9 4.5 %copy-start.9 = (bf16[16,192,128]{2,1,0:T(8,128)(2,1)}, bf16[16,192,128]{2,1,0:T(8,128)(2,1)S(1)}, u32[]{:S(2)}) copy-start(bf16[16,192,128]{2,1,0:T(8,128)(2,1)S(1)} %get-tuple-element.46.g1_ref) | copy-start | bytes 2359300
  134.9 4.6 %copy-start.20 = (bf16[768,128]{1,0:T(8,128)(2,1)}, bf16[768,128]{1,0:T(8,128)(2,1)S(1)}, u32[]{:S(2)}) copy-start(bf16[768,128]{1,0:T(8,128)(2,1)S(1)} %get-tuple-element.42.gated1_ref) | copy-start | bytes 589828
  134.9 28.6 %collective-permute-start.2 = (bf16[12,192,128]{2,1,0:T(8,128)(2,1)}, bf16[12,192,128]{2,1,0:T(8,128)(2,1)}, u32[]{:S(2)}, u32[]{:S(2)}) collective-permute-start(bf16[12,192,128]{2,1,0:T(8,128)(2,1)} %get-tuple-element.49), channel_id=1, source_target_pairs={{0,8},{8,0},{1,9},{9,1},{2,10},{10,2},{3,11},{11,3},{4,12},{12,4},... | collective-permute-start | bytes 1769480 | tf_op jit(solution)/shard_map/ppermute | solution.py:415
  135.3 4.2 %copy-start.8 = (bf16[16,192,128]{2,1,0:T(8,128)(2,1)S(1)}, bf16[16,192,128]{2,1,0:T(8,128)(2,1)}, u32[]{:S(2)}) copy-start(bf16[16,192,128]{2,1,0:T(8,128)(2,1)} %copy-done.7) | copy-start | bytes 2359300
  139.4 5.5 %copy-start.31 = (f32[128,768]{1,0:T(8,128)}, f32[128,768]{1,0:T(8,128)S(1)}, u32[]{:S(2)}) copy-start(f32[128,768]{1,0:T(8,128)S(1)} %fusion.4) | copy-start | bytes 1179652
  139.5 24.0 %copy-start.10 = (bf16[16,192,128]{2,1,0:T(8,128)(2,1)S(1)}, bf16[16,192,128]{2,1,0:T(8,128)(2,1)}, u32[]{:S(2)}) copy-start(bf16[16,192,128]{2,1,0:T(8,128)(2,1)} %copy-done.9) | copy-start | bytes 2359300
  156.1 18.2 %all-to-all-start.7 = ((f32[16,8,128]{2,1,0:T(8,128)}), f32[16,8,128]{2,1,0:T(8,128)}, u32[]{:S(2)}, u32[]{:S(2)}) async-start(f32[16,8,128]{2,1,0:T(8,128)} %broadcast_in_dim.8), calls=%async_computation.8 | async-start | bytes 131072 | tf_op jit(solution)/shard_map/all_to_all | solution.py:368
  163.5 1.0 copy-start.16
  164.5 0.9 copy-start.18
  165.4 0.9 copy-start.21
  166.3 1.0 copy-start.30
  174.4 19.5 %copy-start.32 = (bf16[4,4,4,32,256]{4,3,2,1,0:T(8,128)(2,1)S(1)}, bf16[4,4,4,32,256]{4,3,2,1,0:T(8,128)(2,1)}, u32[]{:S(2)}) copy-start(bf16[4,4,4,32,256]{4,3,2,1,0:T(8,128)(2,1)} %get-tuple-element.52) | copy-start | bytes 3145732
  193.9 21.9 %copy-start.28 = (f32[256,1]{1,0:T(8,128)S(1)}, f32[256,1]{1,0:T(8,128)}, u32[]{:S(2)}) copy-start(f32[256,1]{1,0:T(8,128)} %copy-done.27) | copy-start | bytes 3076
  193.9 22.0 %copy-start.36 = (f32[128]{0:T(128)S(1)}, f32[128]{0:T(128)}, u32[]{:S(2)}) copy-start(f32[128]{0:T(128)} %get-tuple-element.57) | copy-start | bytes 1540
  193.9 22.0 %copy-start.37 = (f32[128]{0:T(128)S(1)}, f32[128]{0:T(128)}, u32[]{:S(2)}) copy-start(f32[128]{0:T(128)} %get-tuple-element.61) | copy-start | bytes 1540
  211.5 16.0 %all-to-all-start.8 = ((bf16[4,4,4,32,256]{4,3,2,1,0:T(8,128)(2,1)}), bf16[4,4,4,32,256]{4,3,2,1,0:T(8,128)(2,1)S(1)}, u32[]{:S(2)}, u32[]{:S(2)}) async-start(bf16[4,4,4,32,256]{4,3,2,1,0:T(8,128)(2,1)} %get-tuple-element.51), calls=%async_computation.9 | async-start | bytes 2097152 | tf_op jit(solution)/shard_map/all_to_all | solution.py:354
  218.1 22.9 %copy-start.22 = (bf16[768,128]{1,0:T(8,128)(2,1)S(1)}, bf16[768,128]{1,0:T(8,128)(2,1)}, u32[]{:S(2)}) copy-start(bf16[768,128]{1,0:T(8,128)(2,1)} %copy-done.20) | copy-start | bytes 589828
  227.5 10.1 %all-to-all-start.15 = ((bf16[4,4,32,256]{3,2,1,0:T(8,128)(2,1)}), bf16[4,4,32,256]{3,2,1,0:T(8,128)(2,1)S(1)}, u32[]{:S(2)}, u32[]{:S(2)}) async-start(bf16[4,4,32,256]{3,2,1,0:T(8,128)(2,1)} %reduce_sum.185), calls=%async_computation.16 | async-start | bytes 524288 | tf_op jit(solution)/shard_map/all_to_all | solution.py:354
  233.0 9.0 %copy-start.19 = (bf16[768,128]{1,0:T(8,128)(2,1)S(1)}, bf16[768,128]{1,0:T(8,128)(2,1)}, u32[]{:S(2)}) copy-start(bf16[768,128]{1,0:T(8,128)(2,1)} %copy-done.17) | copy-start | bytes 589828
  237.6 10.1 %all-to-all-start.12 = ((bf16[4,4,32,256]{3,2,1,0:T(8,128)(2,1)}), bf16[4,4,32,256]{3,2,1,0:T(8,128)(2,1)S(1)}, u32[]{:S(2)}, u32[]{:S(2)}) async-start(bf16[4,4,32,256]{3,2,1,0:T(8,128)(2,1)} %reduce_sum.182), calls=%async_computation.13 | async-start | bytes 524288 | tf_op jit(solution)/shard_map/all_to_all | solution.py:354
  242.1 10.8 %copy-start.33 = (bf16[1,128,768]{2,1,0:T(8,128)(2,1)S(1)}, bf16[1,128,768]{2,1,0:T(8,128)(2,1)}, u32[]{:S(2)}) copy-start(bf16[1,128,768]{2,1,0:T(8,128)(2,1)} %get-tuple-element.66) | copy-start | bytes 589828
  243.1 9.8 %copy-start.34 = (bf16[1,128,768]{2,1,0:T(8,128)(2,1)S(1)}, bf16[1,128,768]{2,1,0:T(8,128)(2,1)}, u32[]{:S(2)}) copy-start(bf16[1,128,768]{2,1,0:T(8,128)(2,1)} %get-tuple-element.67) | copy-start | bytes 589828
  247.6 10.4 %all-to-all-start.9 = ((bf16[4,4,32,256]{3,2,1,0:T(8,128)(2,1)}), bf16[4,4,32,256]{3,2,1,0:T(8,128)(2,1)S(1)}, u32[]{:S(2)}, u32[]{:S(2)}) async-start(bf16[4,4,32,256]{3,2,1,0:T(8,128)(2,1)} %reduce_sum.179), calls=%async_computation.10 | async-start | bytes 524288 | tf_op jit(solution)/shard_map/all_to_all | solution.py:354
  258.1 8.9 %all-to-all-start.16 = ((bf16[4,32,256]{2,1,0:T(8,128)(2,1)}), bf16[4,32,256]{2,1,0:T(8,128)(2,1)S(1)}, u32[]{:S(2)}, u32[]{:S(2)}) async-start(bf16[4,32,256]{2,1,0:T(8,128)(2,1)} %reduce_sum.186), calls=%async_computation.17 | async-start | bytes 131072 | tf_op jit(solution)/shard_map/all_to_all | solution.py:354
  266.9 8.9 %all-to-all-start.13 = ((bf16[4,32,256]{2,1,0:T(8,128)(2,1)}), bf16[4,32,256]{2,1,0:T(8,128)(2,1)S(1)}, u32[]{:S(2)}, u32[]{:S(2)}) async-start(bf16[4,32,256]{2,1,0:T(8,128)(2,1)} %reduce_sum.183), calls=%async_computation.14 | async-start | bytes 131072 | tf_op jit(solution)/shard_map/all_to_all | solution.py:354
  275.8 8.9 %all-to-all-start.10 = ((bf16[4,32,256]{2,1,0:T(8,128)(2,1)}), bf16[4,32,256]{2,1,0:T(8,128)(2,1)S(1)}, u32[]{:S(2)}, u32[]{:S(2)}) async-start(bf16[4,32,256]{2,1,0:T(8,128)(2,1)} %reduce_sum.180), calls=%async_computation.11 | async-start | bytes 131072 | tf_op jit(solution)/shard_map/all_to_all | solution.py:354
  286.7 12.2 %all-to-all-start.5 = ((bf16[16,128,64]{1,2,0:T(8,128)(2,1)}), bf16[16,128,64]{1,2,0:T(8,128)(2,1)S(1)}, u32[]{:S(2)}, u32[]{:S(2)}) async-start(bf16[16,128,64]{1,2,0:T(8,128)(2,1)} %bitcast.13), calls=%async_computation.6 | async-start | bytes 524288 | tf_op jit(solution)/shard_map/all_to_all | solution.py:410
  (9 other events, 6.7 us)
Sparse Core Ops, SparseCore 0:
  127.4 35.3 reduce-scatter.1

commit v3 on v2

v3 whole, which is shorter than its diff:
```python
import functools
import math

import jax
import jax.numpy as jnp
from jax import lax
from jax.experimental import pallas as pl
from jax.experimental.pallas import tpu as pltpu
from jax.sharding import Mesh
from jax.sharding import PartitionSpec as P

EPS = 1e-05
LOG2E = math.log2(math.e)
BF = jnp.bfloat16
F32 = jnp.float32
C = 768
HEADS = 16
DH = 48
TOK = 128
KEYS = 1024
PLANE = ("zh", "zl", "y")
SWAP = [(0, 1), (1, 0)]
SCALE = 1.0 / math.sqrt(DH)
VMEM_LIMIT = 48 * 1024 * 1024


def dot(a, b):
    return jnp.dot(a, b, preferred_element_type=F32)


def dot_nt(a, b):
    return lax.dot_general(a, b, (((1,), (1,)), ((), ())), preferred_element_type=F32)


def params():
    return pltpu.CompilerParams(vmem_limit_bytes=VMEM_LIMIT)


def front_kernel(
    act_ref, gain_ref, w_ref, wout_ref, dout_ref, scaled_ref, normed_ref, inv_ref, send_ref, gate_ref, gg_ref
):
    step = pl.program_id(0)
    flat = act_ref.shape[0]

    @pl.when(step == 0)
    def _():
        values = act_ref[...].astype(F32)
        center = jnp.mean(values, -1, keepdims=True)
        shifted = values - center
        spread = jnp.mean(shifted * shifted, -1, keepdims=True)
        inv_std = lax.rsqrt(spread + EPS)
        normed = shifted * inv_std
        normed_ref[...] = normed
        inv_ref[...] = inv_std
        scaled_ref[...] = (normed * gain_ref[...]).astype(BF)

    block = dot(scaled_ref[...], w_ref[...])

    for kind in range(3):

        @pl.when(step == kind)
        def _(kind=kind):
            send_ref[:, kind * DH : (kind + 1) * DH, :] = block.astype(BF).T.reshape(HEADS, DH, flat)

    @pl.when(step == 3)
    def _():
        gate = jax.nn.sigmoid(block.T)
        ggated = dot_nt(wout_ref[...], dout_ref[...]).astype(BF)
        gate_ref[...] = gate
        gg_ref[...] = ggated
        send_ref[:, 3 * DH : 4 * DH, :] = (ggated.astype(F32) * gate).astype(BF).reshape(HEADS, DH, flat)


def front(act, ln_gain, w_in, w_out, d_out):
    flat = act.shape[0]
    shapes = [
        ((flat, C), BF),
        ((flat, C), F32),
        ((flat, 1), F32),
        ((HEADS, 4 * DH, flat), BF),
        ((C, flat), F32),
        ((C, flat), BF),
    ]

    def whole(shape):
        return pl.BlockSpec(shape, lambda t: (0,) * len(shape))

    return pl.pallas_call(
        front_kernel,
        grid=(4,),
        in_specs=[
            whole((flat, C)),
            whole((1, C)),
            pl.BlockSpec((C, C), lambda t: (0, t)),
            whole((C, C)),
            whole((flat, C)),
        ],
        out_specs=[whole(s) for s, _ in shapes],
        out_shape=[jax.ShapeDtypeStruct(s, d) for s, d in shapes],
        compiler_params=params(),
        cost_estimate=pl.CostEstimate(
            flops=2 * flat * C * 5 * C, bytes_accessed=11 * 2**20, transcendentals=flat * C
        ),
        name="front",
    )(act, ln_gain, w_in, w_out, d_out)


def attention_kernel(
    core_ref, x_ref, bias_ref, out_ref, keep_ref, give_ref,
    qa_s, ka_s, va_s, vt_s, kn_s, gn_s, qt_s, dk_s, dv_s, gb_s, bias_s, *, rows,
):
    core = core_ref[0]
    sample = pl.program_id(0)
    block = pl.program_id(1)
    last_block = pl.num_programs(1) - 1
    half = sample // 2
    lane0 = pl.multiple_of((sample % 2) * TOK, TOK)
    per_block = rows // TOK

    @pl.when(block == 0)
    def _():
        whole = jnp.concatenate([x_ref[half * 8 + t, :, pl.ds(lane0, TOK)] for t in range(8)], axis=1)
        qt, kt, vt, gt = (whole[i * DH : (i + 1) * DH] for i in range(4))
        qs = qt.astype(F32) * (SCALE * LOG2E)
        q_hi = qs.astype(BF)
        q_lo = (qs - q_hi.astype(F32)).astype(BF)
        zeros32 = jnp.zeros((32, KEYS), BF)
        zeros64 = jnp.zeros((64, KEYS), BF)
        zeros80 = jnp.zeros((80, KEYS), BF)
        ones16 = jnp.ones((16, KEYS), BF)
        qa_s[...] = jnp.concatenate([q_hi, q_lo, zeros32], axis=0).T
        ka_s[...] = jnp.concatenate([kt, kt, zeros32], axis=0)
        v_one = jnp.concatenate([vt, ones16, zeros64], axis=0)
        va_s[...] = v_one
        vt_s[...] = v_one.T
        kn_s[...] = jnp.concatenate([kt, zeros80], axis=0).T
        gn_s[...] = jnp.concatenate([gt, zeros80], axis=0).T
        qt_s[...] = qt
        dk_s[...] = jnp.zeros_like(dk_s)
        dv_s[...] = jnp.zeros_like(dv_s)

    row0 = pl.multiple_of(block * rows, rows)
    these = pl.ds(row0, rows)

    @pl.when(sample == 0)
    def _():
        pieces = [bias_ref[p, block * per_block + t] for t in range(per_block) for p in range(8)]
        bias_s[these, :] = jnp.concatenate(pieces, axis=0).astype(F32) * LOG2E

    scores = dot(qa_s[these, :], ka_s[...]) + bias_s[these, :]
    top = jnp.max(scores, axis=1, keepdims=True)
    expd = jnp.exp2(scores - top)
    expd_low = expd.astype(BF)
    summed = dot(expd_low, vt_s[...])
    inv = 1.0 / summed[:, DH : DH + 1]
    out = summed * inv
    gscaled = (gn_s[these, :].astype(F32) * inv).astype(BF)
    gscaled_f = gscaled.astype(F32)
    delta = jnp.sum(out * gscaled_f, axis=1, keepdims=True)
    delta_hi = delta.astype(BF).astype(F32)
    delta_lo = delta - delta_hi
    lane = lax.broadcasted_iota(jnp.int32, (rows, 128), 1)
    left = jnp.where(
        lane == DH, -delta_hi, jnp.where(lane == DH + 1, -delta_lo, gscaled_f)
    ).astype(BF)
    dscores = expd * dot(left, va_s[...])
    dscores_low = dscores.astype(BF)

    @pl.when(sample == 0)
    def _():
        gb_s[these, :] = dscores

    @pl.when((sample > 0) & (sample < 3))
    def _():
        gb_s[these, :] = gb_s[these, :] + dscores

    @pl.when(sample == 3)
    def _():
        total = (gb_s[these, :] + dscores).astype(BF)
        for x in range(4):
            even = total[:, x * 256 : x * 256 + 128]
            odd = total[:, x * 256 + 128 : x * 256 + 256]
            low = jnp.concatenate([even[:, :64], odd[:, :64]], axis=1)
            high = jnp.concatenate([even[:, 64:], odd[:, 64:]], axis=1)
            keep_ref[x, these, :] = jnp.where(core == 0, low, high)
            give_ref[x, these, :] = jnp.where(core == 0, high, low)

    dquery = dot(dscores_low, kn_s[...]) * SCALE
    dk_s[...] += dot(qt_s[:, these], dscores_low)
    gscaled_t = gscaled_f.T.astype(BF)
    dv_s[...] += dot(gscaled_t[:DH], expd_low)
    out_t = out.T
    dquery_t = dquery.T
    for t in range(per_block):
        cols = slice(t * TOK, (t + 1) * TOK)
        where = half * 8 + block * per_block + t
        out_ref[where, 0:DH, pl.ds(lane0, TOK)] = out_t[:DH, cols].astype(BF)
        out_ref[where, DH : 2 * DH, pl.ds(lane0, TOK)] = dquery_t[:DH, cols].astype(BF)

    @pl.when(block == last_block)
    def _():
        for t in range(8):
            cols = slice(t * TOK, (t + 1) * TOK)
            out_ref[half * 8 + t, 2 * DH : 3 * DH, pl.ds(lane0, TOK)] = (dk_s[:, cols] * SCALE).astype(BF)
            out_ref[half * 8 + t, 3 * DH : 4 * DH, pl.ds(lane0, TOK)] = dv_s[:, cols].astype(BF)


def attention(core, x, bias, rows=256):
    def whole(shape):
        return pl.BlockSpec(shape, lambda s, b, core: (0,) * len(shape))

    half_sum = (4, KEYS, 128)
    return pl.pallas_call(
        functools.partial(attention_kernel, rows=rows),
        grid_spec=pltpu.PrefetchScalarGridSpec(
            num_scalar_prefetch=1,
            grid=(4, KEYS // rows),
            in_specs=[whole(x.shape), whole(bias.shape)],
            out_specs=[whole(x.shape), whole(half_sum), whole(half_sum)],
            scratch_shapes=[
                pltpu.VMEM((KEYS, 128), BF),
                pltpu.VMEM((128, KEYS), BF),
                pltpu.VMEM((128, KEYS), BF),
                pltpu.VMEM((KEYS, 128), BF),
                pltpu.VMEM((KEYS, 128), BF),
                pltpu.VMEM((KEYS, 128), BF),
                pltpu.VMEM((DH, KEYS), BF),
                pltpu.VMEM((DH, KEYS), F32),
                pltpu.VMEM((DH, KEYS), F32),
                pltpu.VMEM((KEYS, KEYS), F32),
                pltpu.VMEM((KEYS, KEYS), F32),
            ],
        ),
        out_shape=[
            jax.ShapeDtypeStruct(x.shape, BF),
            jax.ShapeDtypeStruct(half_sum, BF),
            jax.ShapeDtypeStruct(half_sum, BF),
        ],
        compiler_params=params(),
        cost_estimate=pl.CostEstimate(
            flops=4 * 6 * 2 * KEYS * KEYS * 256, bytes_accessed=8 * 2**20, transcendentals=4 * KEYS * KEYS
        ),
        name="attention",
    )(core, x, bias)


def gate_kernel(core_ref, back_ref, gate_ref, gg_ref, gproj_ref, gated_ref, send_ref):
    other = 1 - core_ref[0]
    flat = gate_ref.shape[1]
    att = back_ref[:, :DH, :].astype(F32).reshape(C, flat)
    gate = gate_ref[...]
    opened = att * gate
    gated = opened.astype(BF)
    gated_ref[...] = gated
    for q in range(4):
        send_ref[8 + q] = gated[q * 192 : (q + 1) * 192]
    for kind in range(3):
        gproj_ref[kind * 4 : kind * 4 + 4] = back_ref[:, (kind + 1) * DH : (kind + 2) * DH, :].reshape(
            4, 4 * DH, flat
        )
    gproj_ref[12:16] = (gg_ref[...].astype(F32) * opened * (1.0 - gate)).astype(BF).reshape(4, 4 * DH, flat)
    for n in range(8):
        send_ref[n] = gproj_ref[2 * n + other]


def gate_step(core, back, gate, ggated):
    def whole(shape):
        return pl.BlockSpec(shape, lambda t, core: (0,) * len(shape))

    flat = gate.shape[1]
    shapes = [(16, 4 * DH, flat), (C, flat), (12, 4 * DH, flat)]
    return pl.pallas_call(
        gate_kernel,
        grid_spec=pltpu.PrefetchScalarGridSpec(
            num_scalar_prefetch=1,
            grid=(1,),
            in_specs=[whole(back.shape), whole(gate.shape), whole(ggated.shape)],
            out_specs=[whole(s) for s in shapes],
        ),
        out_shape=[jax.ShapeDtypeStruct(s, BF) for s in shapes],
        compiler_params=params(),
        cost_estimate=pl.CostEstimate(flops=6 * C * flat, bytes_accessed=6 * 2**20, transcendentals=0),
        name="gate",
    )(core, back, gate, ggated)


def input_grad_kernel(g_ref, w_ref, normed_ref, inv_ref, gain_ref, grad_ref, ggain_ref, total_s):
    step = pl.program_id(0)
    flat = normed_ref.shape[0]
    part = dot(w_ref[...], g_ref[...].reshape(C, flat))

    @pl.when(step == 0)
    def _():
        total_s[...] = part

    @pl.when(step > 0)
    def _():
        total_s[...] += part

    @pl.when(step == 3)
    def _():
        grad_scaled = total_s[...].T
        normed = normed_ref[...]
        ggain_ref[...] = jnp.sum(grad_scaled * normed, axis=0, keepdims=True)
        grad_normed = grad_scaled * gain_ref[...]
        grad_ref[...] = (
            inv_ref[...]
            * (
                grad_normed
                - jnp.mean(grad_normed, -1, keepdims=True)
                - normed * jnp.mean(grad_normed * normed, -1, keepdims=True)
            )
        ).astype(BF)


def input_grad(gproj, w_in, normed, inv_std, ln_gain):
    flat = normed.shape[0]

    def whole(shape):
        return pl.BlockSpec(shape, lambda t: (0,) * len(shape))

    return pl.pallas_call(
        input_grad_kernel,
        grid=(4,),
        in_specs=[
            pl.BlockSpec((4, 4 * DH, flat), lambda t: (t, 0, 0)),
            pl.BlockSpec((C, C), lambda t: (0, t)),
            whole((flat, C)),
            whole((flat, 1)),
            whole((1, C)),
        ],
        out_specs=[whole((flat, C)), whole((1, C))],
        out_shape=[jax.ShapeDtypeStruct((flat, C), BF), jax.ShapeDtypeStruct((1, C), F32)],
        scratch_shapes=[pltpu.VMEM((C, flat), F32)],
        compiler_params=params(),
        cost_estimate=pl.CostEstimate(
            flops=2 * flat * C * 4 * C, bytes_accessed=8 * 2**20, transcendentals=0
        ),
        name="input_grad",
    )(gproj, w_in, normed, inv_std, ln_gain)


def weight_kernel(
    core_ref, g_ref, o_ref, gated_ref, sc_ref, sco_ref, do_ref, doo_ref, gain_ref, out_ref, scaled_s, gated_s
):
    core = core_ref[0]
    n = pl.program_id(0)
    flat = sc_ref.shape[0]

    @pl.when(n == 0)
    def _():
        scaled_s[:flat] = sc_ref[...]
        scaled_s[flat:] = sco_ref[...]
        gated_s[:flat] = gated_ref[...].T
        gated_s[flat:] = o_ref[8:12].reshape(C, flat).T

    left = jnp.concatenate([g_ref[2 * n + core], o_ref[n]], axis=1)
    win = dot(left, scaled_s[...])
    wout = dot(jnp.concatenate([do_ref[n], doo_ref[n]], axis=1), gated_s[...])
    gain = gain_ref[...]
    gain_hi = gain.astype(BF).astype(F32)
    gain_lo = gain - gain_hi
    row = lax.broadcasted_iota(jnp.int32, (8, C), 0)
    for k in range(8):
        tail = jnp.where(row == 6, gain_hi, jnp.where(row == 7, gain_lo, wout[k * 8 : k * 8 + 8]))
        out_ref[k] = jnp.concatenate([win[k * 24 : k * 24 + 24], tail], axis=0).astype(BF)


def weight_grads(core, operands):
    def whole(shape):
        return pl.BlockSpec(shape, lambda t, core: (0,) * len(shape))

    flat = operands[3].shape[0]
    return pl.pallas_call(
        weight_kernel,
        grid_spec=pltpu.PrefetchScalarGridSpec(
            num_scalar_prefetch=1,
            grid=(8,),
            in_specs=[whole(o.shape) for o in operands],
            out_specs=pl.BlockSpec((8, 32, C), lambda t, core: (t, 0, 0)),
            scratch_shapes=[pltpu.VMEM((2 * flat, C), BF), pltpu.VMEM((2 * flat, C), BF)],
        ),
        out_shape=jax.ShapeDtypeStruct((64, 32, C), BF),
        compiler_params=params(),
        cost_estimate=pl.CostEstimate(
            flops=2 * 2 * flat * C * 2048, bytes_accessed=8 * 2**20, transcendentals=0
        ),
        name="weight_grads",
    )(core, *operands)


def per_device(act, pair_bias, ln_gain, w_in, w_out, d_out):
    sample_count, row_count, channels = act.shape
    flat = sample_count * row_count
    core = lax.axis_index("core")
    core_arg = jnp.full((1,), core, jnp.int32)
    place = lax.axis_index("x") * 2 + core
    zh = lax.axis_index("zh")

    bias = lax.dynamic_slice(pair_bias, (zh * 8, place * 16, 0), (8, 16, KEYS))
    bias = lax.all_to_all(bias, ("zl", "y"), 0, 0, tiled=True)
    bias = lax.all_gather(bias, ("x", "core"))

    rows_out = d_out.reshape(flat, channels)
    scaled, normed, inv_std, send, gate, ggated = front(
        act.reshape(flat, channels), ln_gain.reshape(1, C), w_in, w_out, rows_out
    )
    received = lax.all_to_all(send, PLANE, 0, 0, tiled=True)

    dout_t = jnp.pad(rows_out.T.reshape(128, 6, flat), ((0, 0), (0, 2), (0, 0)))
    dout_t = dout_t.reshape(8, 2, 64, flat)
    dout_mine = lax.dynamic_index_in_dim(dout_t, core, 1, keepdims=False)
    dout_send = lax.dynamic_index_in_dim(dout_t, 1 - core, 1, keepdims=False)
    dout_other = lax.ppermute(dout_send, "core", SWAP)
    scaled_other = lax.ppermute(scaled, "core", SWAP)

    result, keep, give = attention(core_arg, received, bias)
    back = lax.all_to_all(result, PLANE, 0, 0, tiled=True)

    got = lax.ppermute(give, "core", SWAP)
    gb = (keep.astype(F32) + got.astype(F32)).astype(BF)
    gb = lax.psum_scatter(gb, "x", scatter_dimension=0, tiled=False)
    gb = gb.reshape(8, TOK, 2, 64).transpose(2, 0, 1, 3).reshape(HEADS, TOK, 64)
    grad_bias = lax.all_to_all(gb, PLANE, 0, 0, tiled=True).astype(F32)

    gproj, gated, half = gate_step(core_arg, back, gate, ggated)
    other = lax.ppermute(half, "core", SWAP)
    grad_act, gain = input_grad(gproj, w_in, normed, inv_std, ln_gain.reshape(1, C))
    chunks = weight_grads(
        core_arg, (gproj, other, gated, scaled, scaled_other, dout_mine, dout_other, gain)
    )
    chunks, gated = lax.optimization_barrier((chunks, gated))
    output = jnp.einsum("cr,cd->rd", gated, w_out, preferred_element_type=F32).astype(BF)
    chunks = lax.all_to_all(chunks, ("x", "zh", "zl", "y"), 0, 0, tiled=True)
    total = jnp.sum(chunks.astype(F32), axis=0)
    gain = total[30] + total[31]
    return (
        output.reshape(sample_count, row_count, channels),
        grad_act.reshape(sample_count, row_count, channels),
        grad_bias,
        gain + lax.ppermute(gain, "core", SWAP),
        total[:24].T,
        total[24:30].T,
    )


def solution(mesh):
    fine = Mesh(mesh.devices.reshape(4, 2, 2, 2, 4), ("x", "zh", "core", "zl", "y"))
    sample = ("x", "zh", "core")
    tok = ("zl", "y")
    return jax.shard_map(
        per_device,
        mesh=fine,
        in_specs=(
            P(sample, tok, None),
            P(None, tok, None),
            P(),
            P(),
            P(),
            P(sample, tok, None),
        ),
        out_specs=(
            P(sample, tok, None),
            P(sample, tok, None),
            P(None, tok, sample),
            P(),
            P(None, sample + tok),
            P(None, sample + tok),
        ),
        check_vma=False,
    )
```

time: 309 us -> 219 us (0.71)
  the two profiles are of different devices: /device:TPU:0 before, /device:TPU:103 now
where the time goes in v3:
time: 219 us; the launch traced here: 218 us
  waiting for transfers between devices  66.5 us (30%)
  Pallas kernels  49.5 us (23%)
  blocking collectives  35.4 us (16%)
  starting transfers between devices  25.8 us (12%)
  local copies, waits for them, and re-layouts  17.9 us (8%)
  between operations  14.2 us (6%)
  other arithmetic  7.23 us (3%)
    all_to_all x1, waiting for transfers between devices, per_device(): chunks = lax.all_to_all(chunks, ('x', 'zh', 'zl', 'y'), 0, 0, tiled=True)  43.4 us
    pallas_call x1, Pallas kernels, attention(): pl.pallas_call(functools.partial(attention_kernel, rows=rows), grid_spec=...  30.4 us
    all_to_all x1, blocking collectives, per_device(): received = lax.all_to_all(send, PLANE, 0, 0, tiled=True)  25 us
    all_to_all x1, waiting for transfers between devices, per_device(): back = lax.all_to_all(result, PLANE, 0, 0, tiled=True)  22.8 us
    all_to_all x1, blocking collectives, per_device(): bias = lax.all_to_all(bias, ('zl', 'y'), 0, 0, tiled=True)  10.4 us
    all_to_all x1, starting transfers between devices, per_device(): chunks = lax.all_to_all(chunks, ('x', 'zh', 'zl', 'y'), 0, 0, tiled=True)  10.1 us
    unnamed x35, local copies, waits for them, and re-layouts  10 us
    pallas_call x1, Pallas kernels, weight_grads(): pl.pallas_call(weight_kernel, grid_spec=pltpu.PrefetchScalarGridSpec(num_...  6.61 us
  transfers between devices with their start and end apart: 10, of which 3 were waited for; matrix products, arithmetic and copies ran while one was open for 5% of the time, Pallas kernels for 9%

profile of v3, /device:TPU:103, one launch (start us, length us, event | category | flops | bytes accessed | tf_op | source)
XLA Modules:
  0.0 217.7 jit_solution(15003395956227643878)
XLA Ops:
  7.2 0.0 copy-start.2
  7.2 0.0 all-gather.3.cloned.1.call-start
  7.2 1.1 constant_dynamic-slice_fusion
  8.3 10.4 %all_to_all.25 = bf16[8,16,1024]{2,1,0:T(8,128)(2,1)} all-to-all(bf16[8,16,1024]{2,1,0:T(8,128)(2,1)S(1)} %constant_dynamic-slice_fusion), channel_id=1, replica_groups=mesh['x'=4,'zh'=2,'core'=2,'zl'=2,'y'=4] {'zl','y'}, dimensions={0} | all-to-all | bytes 524288 | tf_op jit(solution)/shard_map/all_to_all | solution.py:401
  18.7 0.0 all-gather.3.cloned.1.call-update
  18.7 0.7 reshape.39.gain_ref
  19.4 1.0 copy-done
  20.4 1.0 copy-done.14
  21.4 5.3 %front.1 = (bf16[256,768]{1,0:T(8,128)(2,1)S(1)}, f32[256,768]{1,0:T(8,128)S(1)}, f32[256,1]{1,0:T(8,128)S(1)}, bf16[16,192,256]{2,1,0:T(8,128)(2,1)S(1)}, f32[7...) custom-call(bf16[256,768]{1,0:T(8,128)(2,1)S(1)} %bitcast.30, f32[1,768]{1,0:T(1,128)S(1)} %reshape.39.gain_ref, ...), custom_call_target="tpu_custom_call" | custom-call | flops 1509949440 | bytes 11534336 | tf_op jit(solution)/shard_map/front/pallas_call | solution.py:88
  26.7 0.9 copy-done.4
  27.6 0.9 copy-done.6
  28.5 0.8 copy-done.8
  29.3 0.7 copy-done.12
  30.0 0.6 copy-done.15
  30.6 25.0 %all_to_all.26.x_ref = bf16[16,192,256]{2,1,0:T(8,128)(2,1)S(1)} all-to-all(bf16[16,192,256]{2,1,0:T(8,128)(2,1)S(1)} %get-tuple-element.22), channel_id=1, replica_groups=mesh['x'=4,'zh'=2,'core'=2,'zl'=2,'y'=4] {'zh','zl','y'}, dimensions={0} | all-to-all | bytes 3145728 | tf_op jit(solution)/shard_map/all_to_all | solution.py:408
  55.6 30.4 %attention.1 = (bf16[16,192,256]{2,1,0:T(8,128)(2,1)}, bf16[4,1024,128]{2,1,0:T(8,128)(2,1)S(1)}, bf16[4,1024,128]{2,1,0:T(8,128)(2,1)}) custom-call(s32[1]{0:T(128)} %bitcast.core_ref, bf16[16,192,256]{2,1,0:T(8,128)(2,1)S(1)} %all_to_all.26.x_ref, bf16[8,8,16,1024]{3,2,1,0:T(8,128)(2,1)} %bitcast.34), custom_call_target="tpu_custom_call" | custom-call | flops 12884901888 | bytes 8388608 | tf_op jit(solution)/shard_map/attention/pallas_call | solution.py:213
  86.0 2.8 %collective-permute-start.3 = (bf16[4,1024,128]{2,1,0:T(8,128)(2,1)}, bf16[4,1024,128]{2,1,0:T(8,128)(2,1)}, u32[]{:S(2)}, u32[]{:S(2)}) collective-permute-start(bf16[4,1024,128]{2,1,0:T(8,128)(2,1)} %get-tuple-element.36), channel_id=1, source_target_pairs={{0,8},{8,0},{1,9},{9,1},{2,10},{10,2},{3,11},{11,3},{4,12},{12,4},... | collective-permute-start | bytes 3145736 | tf_op jit(solution)/shard_map/ppermute | solution.py:420
  88.8 5.5 %all-to-all-start.2 = ((bf16[16,192,256]{2,1,0:T(8,128)(2,1)}), bf16[16,192,256]{2,1,0:T(8,128)(2,1)S(1)}, u32[]{:S(2)}, u32[]{:S(2)}) async-start(bf16[16,192,256]{2,1,0:T(8,128)(2,1)} %get-tuple-element.23), calls=%async_computation.2 | async-start | bytes 3145728 | tf_op jit(solution)/shard_map/all_to_all | solution.py:418
  94.3 0.0 reduce-scatter.2.cloned.1.call-start
  94.4 2.5 %add_convert_fusion = bf16[4,1024,128]{2,1,0:T(8,128)(2,1)} fusion(bf16[4,1024,128]{2,1,0:T(8,128)(2,1)} %collective-permute-done.3, bf16[4,1024,128]{2,1,0:T(8,128)(2,1)S(1)} %get-tuple-element.35), kind=kLoop, calls=%fused_computation.1 | loop fusion | flops 2097152 | bytes 3145728 | tf_op jit(solution)/shard_map/convert_element_type | solution.py:421
  96.9 0.0 reduce-scatter.2.cloned.1.call-update
  96.9 22.8 %all-to-all-done.2.back_ref = bf16[16,192,256]{2,1,0:T(8,128)(2,1)S(1)} async-done(((bf16[16,192,256]{2,1,0:T(8,128)(2,1)}), bf16[16,192,256]{2,1,0:T(8,128)(2,1)S(1)}, u32[]{:S(2)}, u32[]{:S(2)}) %all-to-all-start.2) | async-done | bytes 1572896 | tf_op jit(solution)/shard_map/all_to_all | solution.py:418
  119.7 1.1 copy-done.5
  120.9 1.0 copy-done.13
  121.8 1.6 gate.1
  123.4 0.7 copy-done.10
  124.2 0.8 collective-permute-start
  125.0 0.2 copy.18
  125.1 0.9 reshape.41
  126.1 1.2 pad.4
  127.2 0.8 dynamic-slice_bitcast_fusion
  128.0 0.5 collective-permute-start.2
  128.5 1.1 copy.19
  129.6 0.8 copy.20
  130.4 5.5 %all-to-all-start.3 = ((bf16[16,128,64]{1,2,0:T(8,128)(2,1)}), bf16[16,128,64]{1,2,0:T(8,128)(2,1)}, u32[]{:S(2)}, u32[]{:S(2)}) async-start(bf16[16,128,64]{1,2,0:T(8,128)(2,1)} %bitcast.11), calls=%async_computation.4 | async-start | bytes 524288 | tf_op jit(solution)/shard_map/all_to_all | solution.py:424
  135.9 1.1 copy-done.7
  137.0 5.7 %input_grad.1 = (bf16[256,768]{1,0:T(8,128)(2,1)}, f32[1,768]{1,0:T(1,128)S(1)}) custom-call(bf16[16,192,256]{2,1,0:T(8,128)(2,1)S(1)} %get-tuple-element.26.g_ref, bf16[768,3072]{1,0:T(8,128)(2,1)} %w_ref.3, f32[256,768]{1,0:T(8,128)S(1)} %copy-done.7, f32[256,1]{1,0:T(8,128)S(1)} %copy-done.16, f32[1,768]{1,0:T(1,128)S(1)} %reshape.39.gain_ref), custom_call_target="tpu_custom_call" | custom-call | flops 1207959552 | bytes 8388608 | tf_op jit(solution)/shard_map/input_grad/pallas_call | solution.py:322
  142.7 6.6 %weight_grads.1 = bf16[64,32,768]{2,1,0:T(8,128)(2,1)} custom-call(s32[1]{0:T(128)} %bitcast.core_ref, bf16[16,192,256]{2,1,0:T(8,128)(2,1)S(1)} %get-tuple-element.26.g_ref, bf16[12,192,256]{2,1,0:T(8,128)(2,1)S(1)} %collective-permute-done.o_ref, bf16[768,256]{1,0:T(8,128)(2,1)S(1)} %copy-done.11, bf16[256,768]{1,0:T(8,128)(2,1)S(1)} %copy-done.9, ...), custom_call_target="tpu_custom_call" | custom-call | flops 1610612736 | bytes 8388608 | tf_op jit(solution)/shard_map/weight_grads/pallas_call | solution.py:374
  149.4 10.1 %all-to-all-start.4 = ((bf16[64,32,768]{2,1,0:T(8,128)(2,1)}), bf16[64,32,768]{2,1,0:T(8,128)(2,1)}, u32[]{:S(2)}, u32[]{:S(2)}) async-start(bf16[64,32,768]{2,1,0:T(8,128)(2,1)} %weight_grads.1), calls=%async_computation.5 | async-start | bytes 6291456 | tf_op jit(solution)/shard_map/all_to_all | solution.py:434
  159.5 1.3 convolution_convert_fusion
  160.8 1.8 convert_element_type.24
  162.5 43.4 %all-to-all-done.4 = bf16[64,32,768]{2,1,0:T(8,128)(2,1)} async-done(((bf16[64,32,768]{2,1,0:T(8,128)(2,1)}), bf16[64,32,768]{2,1,0:T(8,128)(2,1)}, u32[]{:S(2)}, u32[]{:S(2)}) %all-to-all-start.4) | async-done | bytes 3145760 | tf_op jit(solution)/shard_map/all_to_all | solution.py:434
  206.0 2.3 %convert_reduce_fusion = f32[32,768]{1,0:T(8,128)S(1)} fusion(bf16[64,32,768]{2,1,0:T(8,128)(2,1)} %all-to-all-done.4), kind=kLoop, calls=%fused_computation | loop fusion | flops 3121152 | bytes 3244032 | tf_op jit(solution)/shard_map/reduce_sum | solution.py:435
  208.3 0.6 slice_bitcast_fusion
  209.0 0.5 collective-permute-start.4
  209.5 0.6 slice_bitcast_fusion.1
  210.1 0.2 collective-permute-done.4
  210.3 0.6 add.41
  (32 shorter events, 0.1 us)
Async XLA Ops:
  7.2 12.2 %copy-start.2 = (bf16[768,768]{1,0:T(8,128)(2,1)S(1)}, bf16[768,768]{1,0:T(8,128)(2,1)}, u32[]{:S(2)}) copy-start(bf16[768,768]{1,0:T(8,128)(2,1)} %wout_ref.1) | copy-start | bytes 3538948
  7.2 48.5 %all-gather.3.cloned.1.call-start = ((), (), s32[]{:S(2)}) async-start(), calls=%async_computation.7 | async-start | bytes 2359296 | tf_op jit(solution)/shard_map/all_gather | solution.py:402
  19.4 1.0 copy-start
  20.4 1.0 copy-start.14
  26.7 0.9 copy-start.4
  27.6 0.9 copy-start.6
  28.5 0.8 copy-start.8
  29.3 0.7 copy-start.12
  30.0 0.6 copy-start.15
  86.0 8.4 %collective-permute-start.3 = (bf16[4,1024,128]{2,1,0:T(8,128)(2,1)}, bf16[4,1024,128]{2,1,0:T(8,128)(2,1)}, u32[]{:S(2)}, u32[]{:S(2)}) collective-permute-start(bf16[4,1024,128]{2,1,0:T(8,128)(2,1)} %get-tuple-element.36), channel_id=1, source_target_pairs={{0,8},{8,0},{1,9},{9,1},{2,10},{10,2},{3,11},{11,3},{4,12},{12,4},... | collective-permute-start | bytes 3145736 | tf_op jit(solution)/shard_map/ppermute | solution.py:420
  88.8 30.9 %all-to-all-start.2 = ((bf16[16,192,256]{2,1,0:T(8,128)(2,1)}), bf16[16,192,256]{2,1,0:T(8,128)(2,1)S(1)}, u32[]{:S(2)}, u32[]{:S(2)}) async-start(bf16[16,192,256]{2,1,0:T(8,128)(2,1)} %get-tuple-element.23), calls=%async_computation.2 | async-start | bytes 3145728 | tf_op jit(solution)/shard_map/all_to_all | solution.py:418
  94.3 34.2 %reduce-scatter.2.cloned.1.call-start = ((), (), s32[]{:S(2)}) async-start(), calls=%async_computation.6 | async-start | bytes 1310720 | tf_op jit(solution)/shard_map/reduce_scatter | solution.py:422
  96.9 28.1 %copy-start.1 = (bf16[2,128,768]{2,1,0:T(8,128)(2,1)S(1)}, bf16[2,128,768]{2,1,0:T(8,128)(2,1)}, u32[]{:S(2)}) copy-start(bf16[2,128,768]{2,1,0:T(8,128)(2,1)} %param.11) | copy-start | bytes 1179652
  119.7 1.1 copy-start.5
  120.9 1.0 copy-start.13
  123.4 0.7 copy-start.10
  124.2 18.6 %collective-permute-start = (bf16[12,192,256]{2,1,0:T(8,128)(2,1)}, bf16[12,192,256]{2,1,0:T(8,128)(2,1)S(1)}, u32[]{:S(2)}, u32[]{:S(2)}) collective-permute-start(bf16[12,192,256]{2,1,0:T(8,128)(2,1)} %get-tuple-element.27), channel_id=1, source_target_pairs={{0,8},{8,0},{1,9},{9,1},{2,10},{10,2},{3,11},{11,3},{4,12},{12,4},... | collective-permute-start | bytes 3538952 | tf_op jit(solution)/shard_map/ppermute | solution.py:427
  124.9 17.8 %collective-permute-start.1 = (bf16[256,768]{1,0:T(8,128)(2,1)}, bf16[256,768]{1,0:T(8,128)(2,1)}, u32[]{:S(2)}, u32[]{:S(2)}) collective-permute-start(bf16[256,768]{1,0:T(8,128)(2,1)} %copy-done.8), channel_id=1, source_target_pairs={{0,8},{8,0},{1,9},{9,1},{2,10},{10,2},{3,11},{11,3},{4,12},{12,4},... | collective-permute-start | bytes 1179656 | tf_op jit(solution)/shard_map/ppermute | solution.py:415
  126.1 9.8 %copy-start.16 = (f32[256,1]{1,0:T(8,128)S(1)}, f32[256,1]{1,0:T(8,128)}, u32[]{:S(2)}) copy-start(f32[256,1]{1,0:T(8,128)} %copy-done.15) | copy-start | bytes 3076
  128.0 14.7 %collective-permute-start.2 = (bf16[8,64,256]{2,1,0:T(8,128)(2,1)}, bf16[8,64,256]{2,1,0:T(8,128)(2,1)}, u32[]{:S(2)}, u32[]{:S(2)}) collective-permute-start(bf16[8,64,256]{2,1,0:T(8,128)(2,1)} %get-tuple-element.38), channel_id=1, source_target_pairs={{0,8},{8,0},{1,9},{9,1},{2,10},{10,2},{3,11},{11,3},{4,12},{12,4},... | collective-permute-start | bytes 786440 | tf_op jit(solution)/shard_map/ppermute | solution.py:414
  130.4 19.0 %all-to-all-start.3 = ((bf16[16,128,64]{1,2,0:T(8,128)(2,1)}), bf16[16,128,64]{1,2,0:T(8,128)(2,1)}, u32[]{:S(2)}, u32[]{:S(2)}) async-start(bf16[16,128,64]{1,2,0:T(8,128)(2,1)} %bitcast.11), calls=%async_computation.4 | async-start | bytes 524288 | tf_op jit(solution)/shard_map/all_to_all | solution.py:424
  135.9 1.1 copy-start.7
  137.0 5.7 %copy-start.9 = (bf16[256,768]{1,0:T(8,128)(2,1)S(1)}, bf16[256,768]{1,0:T(8,128)(2,1)}, u32[]{:S(2)}) copy-start(bf16[256,768]{1,0:T(8,128)(2,1)} %copy-done.8) | copy-start | bytes 1179652
  137.0 5.7 %copy-start.11 = (bf16[768,256]{1,0:T(8,128)(2,1)S(1)}, bf16[768,256]{1,0:T(8,128)(2,1)}, u32[]{:S(2)}) copy-start(bf16[768,256]{1,0:T(8,128)(2,1)} %copy-done.10) | copy-start | bytes 1179652
  149.4 10.1 %copy-start.3 = (bf16[768,768]{1,0:T(8,128)(2,1)S(1)}, bf16[768,768]{1,0:T(8,128)(2,1)}, u32[]{:S(2)}) copy-start(bf16[768,768]{1,0:T(8,128)(2,1)} %wout_ref.1) | copy-start | bytes 3538948
  149.4 56.6 %all-to-all-start.4 = ((bf16[64,32,768]{2,1,0:T(8,128)(2,1)}), bf16[64,32,768]{2,1,0:T(8,128)(2,1)}, u32[]{:S(2)}, u32[]{:S(2)}) async-start(bf16[64,32,768]{2,1,0:T(8,128)(2,1)} %weight_grads.1), calls=%async_computation.5 | async-start | bytes 6291456 | tf_op jit(solution)/shard_map/all_to_all | solution.py:434
  209.0 1.3 collective-permute-start.4
Sparse Core Ops, SparseCore 0:
  18.8 25.8 all-gather.2
  97.6 21.0 reduce-scatter.1

commit v4 on v3

--- a/solution.py
+++ b/solution.py
@@ -21,7 +21,7 @@
 PLANE = ("zh", "zl", "y")
 SWAP = [(0, 1), (1, 0)]
 SCALE = 1.0 / math.sqrt(DH)
-VMEM_LIMIT = 48 * 1024 * 1024
+VMEM_LIMIT = 60 * 1024 * 1024
 
 
 def dot(a, b):
@@ -107,114 +107,100 @@
 
 def attention_kernel(
     core_ref, x_ref, bias_ref, out_ref, keep_ref, give_ref,
-    qa_s, ka_s, va_s, vt_s, kn_s, gn_s, qt_s, dk_s, dv_s, gb_s, bias_s, *, rows,
+    qa_s, ka_s, va_s, vt_s, kn_s, gn_s, gb_s, bias_s, *, blocks,
 ):
     core = core_ref[0]
     sample = pl.program_id(0)
-    block = pl.program_id(1)
-    last_block = pl.num_programs(1) - 1
     half = sample // 2
     lane0 = pl.multiple_of((sample % 2) * TOK, TOK)
-    per_block = rows // TOK
-
-    @pl.when(block == 0)
-    def _():
-        whole = jnp.concatenate([x_ref[half * 8 + t, :, pl.ds(lane0, TOK)] for t in range(8)], axis=1)
-        qt, kt, vt, gt = (whole[i * DH : (i + 1) * DH] for i in range(4))
-        qs = qt.astype(F32) * (SCALE * LOG2E)
-        q_hi = qs.astype(BF)
-        q_lo = (qs - q_hi.astype(F32)).astype(BF)
-        zeros32 = jnp.zeros((32, KEYS), BF)
-        zeros64 = jnp.zeros((64, KEYS), BF)
-        zeros80 = jnp.zeros((80, KEYS), BF)
-        ones16 = jnp.ones((16, KEYS), BF)
-        qa_s[...] = jnp.concatenate([q_hi, q_lo, zeros32], axis=0).T
-        ka_s[...] = jnp.concatenate([kt, kt, zeros32], axis=0)
-        v_one = jnp.concatenate([vt, ones16, zeros64], axis=0)
-        va_s[...] = v_one
-        vt_s[...] = v_one.T
-        kn_s[...] = jnp.concatenate([kt, zeros80], axis=0).T
-        gn_s[...] = jnp.concatenate([gt, zeros80], axis=0).T
-        qt_s[...] = qt
-        dk_s[...] = jnp.zeros_like(dk_s)
-        dv_s[...] = jnp.zeros_like(dv_s)
-
-    row0 = pl.multiple_of(block * rows, rows)
-    these = pl.ds(row0, rows)
 
     @pl.when(sample == 0)
     def _():
-        pieces = [bias_ref[p, block * per_block + t] for t in range(per_block) for p in range(8)]
-        bias_s[these, :] = jnp.concatenate(pieces, axis=0).astype(F32) * LOG2E
-
-    scores = dot(qa_s[these, :], ka_s[...]) + bias_s[these, :]
-    top = jnp.max(scores, axis=1, keepdims=True)
-    expd = jnp.exp2(scores - top)
-    expd_low = expd.astype(BF)
-    summed = dot(expd_low, vt_s[...])
-    inv = 1.0 / summed[:, DH : DH + 1]
-    out = summed * inv
-    gscaled = (gn_s[these, :].astype(F32) * inv).astype(BF)
-    gscaled_f = gscaled.astype(F32)
-    delta = jnp.sum(out * gscaled_f, axis=1, keepdims=True)
-    delta_hi = delta.astype(BF).astype(F32)
-    delta_lo = delta - delta_hi
+        for t in range(8):
+            tile = jnp.concatenate([bias_ref[p, t] for p in range(8)], axis=0)
+            bias_s[t * TOK : (t + 1) * TOK] = tile.astype(F32) * LOG2E
+
+    whole = jnp.concatenate([x_ref[half * 8 + t, :, pl.ds(lane0, TOK)] for t in range(8)], axis=1)
+    qt, kt, vt, gt = (whole[i * DH : (i + 1) * DH] for i in range(4))
+    qs = qt.astype(F32) * (SCALE * LOG2E)
+    q_hi = qs.astype(BF)
+    q_lo = (qs - q_hi.astype(F32)).astype(BF)
+    zeros32 = jnp.zeros((32, KEYS), BF)
+    zeros64 = jnp.zeros((64, KEYS), BF)
+    zeros80 = jnp.zeros((80, KEYS), BF)
+    ones16 = jnp.ones((16, KEYS), BF)
+    qa_s[...] = jnp.concatenate([q_hi, q_lo, zeros32], axis=0).T
+    ka_s[...] = jnp.concatenate([kt, kt, zeros32], axis=0)
+    v_one = jnp.concatenate([vt, ones16, zeros64], axis=0)
+    va_s[...] = v_one
+    vt_s[...] = v_one.T
+    kn_s[...] = jnp.concatenate([kt, zeros80], axis=0).T
+    gn_s[...] = jnp.concatenate([gt, zeros80], axis=0).T
+
+    rows = KEYS // blocks
+    every = [slice(i * rows, (i + 1) * rows) for i in range(blocks)]
     lane = lax.broadcasted_iota(jnp.int32, (rows, 128), 1)
-    left = jnp.where(
-        lane == DH, -delta_hi, jnp.where(lane == DH + 1, -delta_lo, gscaled_f)
-    ).astype(BF)
-    dscores = expd * dot(left, va_s[...])
-    dscores_low = dscores.astype(BF)
+    scores = [dot(qa_s[p], ka_s[...]) + bias_s[p] for p in every]
+    expd = [jnp.exp2(s - jnp.max(s, axis=1, keepdims=True)) for s in scores]
+    expd_low = [e.astype(BF) for e in expd]
+    summed = [dot(e, vt_s[...]) for e in expd_low]
+    inv = [1.0 / s[:, DH : DH + 1] for s in summed]
+    out = [s * i for s, i in zip(summed, inv)]
+    gscaled = [(gn_s[p].astype(F32) * i).astype(BF).astype(F32) for p, i in zip(every, inv)]
+    left = []
+    for o, g in zip(out, gscaled):
+        delta = jnp.sum(o * g, axis=1, keepdims=True)
+        delta_hi = delta.astype(BF).astype(F32)
+        left.append(
+            jnp.where(lane == DH, -delta_hi, jnp.where(lane == DH + 1, delta_hi - delta, g)).astype(BF)
+        )
+    dscores = [e * dot(l, va_s[...]) for e, l in zip(expd, left)]
+    dscores_low = [d.astype(BF) for d in dscores]
 
     @pl.when(sample == 0)
     def _():
-        gb_s[these, :] = dscores
+        for p, d in zip(every, dscores):
+            gb_s[p] = d
 
     @pl.when((sample > 0) & (sample < 3))
     def _():
-        gb_s[these, :] = gb_s[these, :] + dscores
+        for p, d in zip(every, dscores):
+            gb_s[p] = gb_s[p] + d
 
     @pl.when(sample == 3)
     def _():
-        total = (gb_s[these, :] + dscores).astype(BF)
-        for x in range(4):
-            even = total[:, x * 256 : x * 256 + 128]
-            odd = total[:, x * 256 + 128 : x * 256 + 256]
-            low = jnp.concatenate([even[:, :64], odd[:, :64]], axis=1)
-            high = jnp.concatenate([even[:, 64:], odd[:, 64:]], axis=1)
-            keep_ref[x, these, :] = jnp.where(core == 0, low, high)
-            give_ref[x, these, :] = jnp.where(core == 0, high, low)
-
-    dquery = dot(dscores_low, kn_s[...]) * SCALE
-    dk_s[...] += dot(qt_s[:, these], dscores_low)
-    gscaled_t = gscaled_f.T.astype(BF)
-    dv_s[...] += dot(gscaled_t[:DH], expd_low)
-    out_t = out.T
-    dquery_t = dquery.T
-    for t in range(per_block):
+        for p, d in zip(every, dscores):
+            total = (gb_s[p] + d).astype(BF)
+            for x in range(4):
+                even = total[:, x * 256 : x * 256 + 128]
+                odd = total[:, x * 256 + 128 : x * 256 + 256]
+                low = jnp.concatenate([even[:, :64], odd[:, :64]], axis=1)
+                high = jnp.concatenate([even[:, 64:], odd[:, 64:]], axis=1)
+                keep_ref[x, p] = jnp.where(core == 0, low, high)
+                give_ref[x, p] = jnp.where(core == 0, high, low)
+
+    all_low = jnp.concatenate(dscores_low, axis=0)
+    gscaled_t = jnp.concatenate(gscaled, axis=0).T.astype(BF)
+    out_t = jnp.concatenate(out, axis=0).T[:DH].astype(BF)
+    dquery_t = (dot(all_low, kn_s[...]) * SCALE).T[:DH].astype(BF)
+    dkey_t = (dot(qt, all_low) * SCALE).astype(BF)
+    dvalue_t = dot(gscaled_t[:DH], jnp.concatenate(expd_low, axis=0)).astype(BF)
+    for t in range(8):
         cols = slice(t * TOK, (t + 1) * TOK)
-        where = half * 8 + block * per_block + t
-        out_ref[where, 0:DH, pl.ds(lane0, TOK)] = out_t[:DH, cols].astype(BF)
-        out_ref[where, DH : 2 * DH, pl.ds(lane0, TOK)] = dquery_t[:DH, cols].astype(BF)
-
-    @pl.when(block == last_block)
-    def _():
-        for t in range(8):
-            cols = slice(t * TOK, (t + 1) * TOK)
-            out_ref[half * 8 + t, 2 * DH : 3 * DH, pl.ds(lane0, TOK)] = (dk_s[:, cols] * SCALE).astype(BF)
-            out_ref[half * 8 + t, 3 * DH : 4 * DH, pl.ds(lane0, TOK)] = dv_s[:, cols].astype(BF)
-
-
-def attention(core, x, bias, rows=256):
+        for i, part in enumerate((out_t, dquery_t, dkey_t, dvalue_t)):
+            out_ref[half * 8 + t, i * DH : (i + 1) * DH, pl.ds(lane0, TOK)] = part[:, cols]
+
+
+def attention(core, x, bias, blocks=4):
     def whole(shape):
-        return pl.BlockSpec(shape, lambda s, b, core: (0,) * len(shape))
+        return pl.BlockSpec(shape, lambda s, core: (0,) * len(shape))
 
     half_sum = (4, KEYS, 128)
     return pl.pallas_call(
-        functools.partial(attention_kernel, rows=rows),
+        functools.partial(attention_kernel, blocks=blocks),
         grid_spec=pltpu.PrefetchScalarGridSpec(
             num_scalar_prefetch=1,
-            grid=(4, KEYS // rows),
+            grid=(4,),
             in_specs=[whole(x.shape), whole(bias.shape)],
             out_specs=[whole(x.shape), whole(half_sum), whole(half_sum)],
             scratch_shapes=[
@@ -224,9 +210,6 @@
                 pltpu.VMEM((KEYS, 128), BF),
                 pltpu.VMEM((KEYS, 128), BF),
                 pltpu.VMEM((KEYS, 128), BF),
-                pltpu.VMEM((DH, KEYS), BF),
-                pltpu.VMEM((DH, KEYS), F32),
-                pltpu.VMEM((DH, KEYS), F32),
                 pltpu.VMEM((KEYS, KEYS), F32),
                 pltpu.VMEM((KEYS, KEYS), F32),
             ],
@@ -399,12 +382,13 @@
 
     bias = lax.dynamic_slice(pair_bias, (zh * 8, place * 16, 0), (8, 16, KEYS))
     bias = lax.all_to_all(bias, ("zl", "y"), 0, 0, tiled=True)
-    bias = lax.all_gather(bias, ("x", "core"))
 
     rows_out = d_out.reshape(flat, channels)
     scaled, normed, inv_std, send, gate, ggated = front(
         act.reshape(flat, channels), ln_gain.reshape(1, C), w_in, w_out, rows_out
     )
+    bias, send = lax.optimization_barrier((bias, send))
+    bias = lax.all_gather(bias, ("x", "core"))
     received = lax.all_to_all(send, PLANE, 0, 0, tiled=True)
 
     dout_t = jnp.pad(rows_out.T.reshape(128, 6, flat), ((0, 0), (0, 2), (0, 0)))
@@ -414,6 +398,9 @@
     dout_other = lax.ppermute(dout_send, "core", SWAP)
     scaled_other = lax.ppermute(scaled, "core", SWAP)
 
+    received, dout_mine, dout_other, scaled_other = lax.optimization_barrier(
+        (received, dout_mine, dout_other, scaled_other)
+    )
     result, keep, give = attention(core_arg, received, bias)
     back = lax.all_to_all(result, PLANE, 0, 0, tiled=True)
 

time: 219 us -> 200 us (0.913)
  blocking collectives: 35.4 us -> 0 us
  waiting for transfers between devices: 66.5 us -> 82.5 us
  starting transfers between devices: 25.8 us -> 38.8 us
  local copies, waits for them, and re-layouts: 17.9 us -> 11.4 us
  Pallas kernels: 49.5 us -> 45.6 us
  other arithmetic: 7.23 us -> 4.39 us
    all_to_all x2 -> x0, blocking collectives: 35.4 us -> none  [the longest x1 25 us: per_device(): received = lax.all_to_all(send, PLANE, 0, 0, tiled=True)]
    all_to_all x0 -> x2, waiting for transfers between devices: none -> 15.2 us  [the longest x1 15.2 us: per_device(): received = lax.all_to_all(send, PLANE, 0, 0, tiled=True)]
    all_to_all x0 -> x2, starting transfers between devices: none -> 11.8 us  [the longest x1 6.4 us: per_device(): received = lax.all_to_all(send, PLANE, 0, 0, tiled=True)]
    pallas_call x1, Pallas kernels: 30.4 us -> 20.1 us  [attention(): pl.pallas_call(functools.partial(attention_kernel, blocks=blocks), grid_s...]
    unnamed x35 -> x19, local copies, waits for them, and re-layouts: 10 us -> 4.15 us
    pallas_call x1, Pallas kernels: 5.28 us -> 7.82 us  [front(): pl.pallas_call(front_kernel, grid=(4,), in_specs=[whole((flat, C)), whole...]
  transfers between devices with their start and end apart: 10 -> 12, of which waited for: 3 -> 5; matrix products, arithmetic and copies ran while one was open for 5% -> 5% of each run, Pallas kernels for 9% -> 13%
where the time goes in v4:
time: 200 us; the launch traced here: 199 us
  waiting for transfers between devices  82.5 us (41%)
  Pallas kernels  45.6 us (23%)
  starting transfers between devices  38.8 us (19%)
  between operations  14.2 us (7%)
  local copies, waits for them, and re-layouts  11.4 us (6%)
  other arithmetic  4.39 us (2%)
  matrix products  2.65 us (1%)
    all_to_all x1, waiting for transfers between devices, per_device(): chunks = lax.all_to_all(chunks, ('x', 'zh', 'zl', 'y'), 0, 0, tiled=True)  43.1 us
    all_to_all x1, waiting for transfers between devices, per_device(): back = lax.all_to_all(result, PLANE, 0, 0, tiled=True)  22.4 us
    pallas_call x1, Pallas kernels, attention(): pl.pallas_call(functools.partial(attention_kernel, blocks=blocks), grid_s...  20.1 us
    all_to_all x1, waiting for transfers between devices, per_device(): received = lax.all_to_all(send, PLANE, 0, 0, tiled=True)  15.2 us
    all_to_all x1, starting transfers between devices, per_device(): chunks = lax.all_to_all(chunks, ('x', 'zh', 'zl', 'y'), 0, 0, tiled=True)  9.86 us
    pallas_call x1, Pallas kernels, front(): pl.pallas_call(front_kernel, grid=(4,), in_specs=[whole((flat, C)), whole...  7.82 us
    pallas_call x1, Pallas kernels, weight_grads(): pl.pallas_call(weight_kernel, grid_spec=pltpu.PrefetchScalarGridSpec(num_...  7.73 us
    all_to_all x1, starting transfers between devices, per_device(): received = lax.all_to_all(send, PLANE, 0, 0, tiled=True)  6.4 us
  transfers between devices with their start and end apart: 12, of which 5 were waited for; matrix products, arithmetic and copies ran while one was open for 5% of the time, Pallas kernels for 13%

profile of v4, /device:TPU:103, one launch (start us, length us, event | category | flops | bytes accessed | tf_op | source)
XLA Modules:
  0.0 199.5 jit_solution(2731467049525539276)
XLA Ops:
  7.2 1.7 constant_dynamic-slice_fusion
  8.9 5.4 %all-to-all-start = ((bf16[8,16,1024]{2,1,0:T(8,128)(2,1)}), bf16[8,16,1024]{2,1,0:T(8,128)(2,1)S(1)}, u32[]{:S(2)}, u32[]{:S(2)}) async-start(bf16[8,16,1024]{2,1,0:T(8,128)(2,1)} %constant_dynamic-slice_fusion), calls=%async_computation | async-start | bytes 524288 | tf_op jit(solution)/shard_map/all_to_all | solution.py:384
  14.2 1.3 reshape.39.gain_ref
  15.5 7.8 %front.1 = (bf16[256,768]{1,0:T(8,128)(2,1)}, f32[256,768]{1,0:T(8,128)}, f32[256,1]{1,0:T(8,128)}, bf16[16,192,256]{2,1,0:T(8,128)(2,1)}, f32[768,256]{1,0:T(8,128)}, /*index=5*/bf16[768,256]{1,0:T(8,128)(2,1)}) custom-call(bf16[256,768]{1,0:T(8,128)(2,1)} %bitcast.33, f32[1,768]{1,0:T(1,128)} %reshape.39.gain_ref, bf16[768,3072]{1,0:T(8,128)(2,1)} %w_ref.3, ...), custom_call_target="tpu_custom_call" | custom-call | flops 1509949440 | bytes 11534336 | tf_op jit(solution)/shard_map/front/pallas_call | solution.py:88
  23.3 0.0 all-to-all-done
  23.3 0.0 copy-start.5
  23.3 0.7 copy-done.5
  24.0 0.0 all-gather.3.cloned.1.call-update
  24.1 6.4 %all-to-all-start.1 = ((bf16[16,192,256]{2,1,0:T(8,128)(2,1)}), bf16[16,192,256]{2,1,0:T(8,128)(2,1)S(1)}, u32[]{:S(2)}, u32[]{:S(2)}) async-start(bf16[16,192,256]{2,1,0:T(8,128)(2,1)} %get-tuple-element.29), calls=%async_computation.1 | async-start | bytes 3145728 | tf_op jit(solution)/shard_map/all_to_all | solution.py:392
  30.5 1.9 collective-permute-start.1
  32.3 0.2 copy.18
  32.5 0.1 reshape.41
  32.7 0.1 pad.4
  32.8 0.8 dynamic-slice_bitcast_fusion
  33.5 0.0 collective-permute-start
  33.5 1.5 collective-permute-done.doo_ref
  35.1 0.0 collective-permute-done.1.sco_ref
  35.1 15.2 %all-to-all-done.1.x_ref = bf16[16,192,256]{2,1,0:T(8,128)(2,1)S(1)} async-done(((bf16[16,192,256]{2,1,0:T(8,128)(2,1)}), bf16[16,192,256]{2,1,0:T(8,128)(2,1)S(1)}, u32[]{:S(2)}, u32[]{:S(2)}) %all-to-all-start.1) | async-done | bytes 1572896 | tf_op jit(solution)/shard_map/all_to_all | solution.py:392
  50.3 1.2 copy-done.1
  51.5 20.1 %attention.1 = (bf16[16,192,256]{2,1,0:T(8,128)(2,1)}, bf16[4,1024,128]{2,1,0:T(8,128)(2,1)}, bf16[4,1024,128]{2,1,0:T(8,128)(2,1)}) custom-call(s32[1]{0:T(128)} %bitcast.core_ref, bf16[16,192,256]{2,1,0:T(8,128)(2,1)} %copy-done.1, bf16[8,8,16,1024]{3,2,1,0:T(8,128)(2,1)} %bitcast.34), custom_call_target="tpu_custom_call" | custom-call | flops 12884901888 | bytes 8388608 | tf_op jit(solution)/shard_map/attention/pallas_call | solution.py:199
  71.6 3.3 %collective-permute-start.3 = (bf16[4,1024,128]{2,1,0:T(8,128)(2,1)}, bf16[4,1024,128]{2,1,0:T(8,128)(2,1)}, u32[]{:S(2)}, u32[]{:S(2)}) collective-permute-start(bf16[4,1024,128]{2,1,0:T(8,128)(2,1)} %get-tuple-element.48), channel_id=1, source_target_pairs={{0,8},{8,0},{1,9},{9,1},{2,10},{10,2},{3,11},{11,3},{4,12},{12,4},... | collective-permute-start | bytes 3145736 | tf_op jit(solution)/shard_map/ppermute | solution.py:407
  74.9 5.5 %all-to-all-start.2 = ((bf16[16,192,256]{2,1,0:T(8,128)(2,1)}), bf16[16,192,256]{2,1,0:T(8,128)(2,1)S(1)}, u32[]{:S(2)}, u32[]{:S(2)}) async-start(bf16[16,192,256]{2,1,0:T(8,128)(2,1)} %get-tuple-element.33), calls=%async_computation.2 | async-start | bytes 3145728 | tf_op jit(solution)/shard_map/all_to_all | solution.py:405
  80.4 0.0 reduce-scatter.2.cloned.1.call-start
  80.5 0.0 collective-permute-done.3
  80.5 2.5 %add_convert_fusion = bf16[4,1024,128]{2,1,0:T(8,128)(2,1)} fusion(bf16[4,1024,128]{2,1,0:T(8,128)(2,1)} %collective-permute-done.3, bf16[4,1024,128]{2,1,0:T(8,128)(2,1)S(1)} %copy-done.4), kind=kLoop, calls=%fused_computation.1 | loop fusion | flops 2097152 | bytes 3145728 | tf_op jit(solution)/shard_map/convert_element_type | solution.py:408
  83.0 0.0 reduce-scatter.2.cloned.1.call-update
  83.0 22.4 %all-to-all-done.2.back_ref = bf16[16,192,256]{2,1,0:T(8,128)(2,1)S(1)} async-done(((bf16[16,192,256]{2,1,0:T(8,128)(2,1)}), bf16[16,192,256]{2,1,0:T(8,128)(2,1)S(1)}, u32[]{:S(2)}, u32[]{:S(2)}) %all-to-all-start.2) | async-done | bytes 1572896 | tf_op jit(solution)/shard_map/all_to_all | solution.py:405
  105.4 1.2 copy-done
  106.6 3.7 %gate.1 = (bf16[16,192,256]{2,1,0:T(8,128)(2,1)}, bf16[768,256]{1,0:T(8,128)(2,1)}, bf16[12,192,256]{2,1,0:T(8,128)(2,1)}) custom-call(s32[1]{0:T(128)} %bitcast.core_ref, bf16[16,192,256]{2,1,0:T(8,128)(2,1)} %copy-done, f32[768,256]{1,0:T(8,128)} %get-tuple-element.34.gate_ref, bf16[768,256]{1,0:T(8,128)(2,1)} %get-tuple-element.35.gg_ref), custom_call_target="tpu_custom_call" | custom-call | flops 1179648 | bytes 6291456 | tf_op jit(solution)/shard_map/gate/pallas_call | solution.py:255
  110.3 1.0 collective-permute-start.2
  111.3 1.1 copy.19
  112.4 0.8 copy.20
  113.2 5.0 %all-to-all-start.3 = ((bf16[16,128,64]{1,2,0:T(8,128)(2,1)}), bf16[16,128,64]{1,2,0:T(8,128)(2,1)S(1)}, u32[]{:S(2)}, u32[]{:S(2)}) async-start(bf16[16,128,64]{1,2,0:T(8,128)(2,1)} %bitcast.11), calls=%async_computation.4 | async-start | bytes 524288 | tf_op jit(solution)/shard_map/all_to_all | solution.py:411
  118.2 6.2 %input_grad.1 = (bf16[256,768]{1,0:T(8,128)(2,1)}, f32[1,768]{1,0:T(1,128)}) custom-call(bf16[16,192,256]{2,1,0:T(8,128)(2,1)} %get-tuple-element.36.g_ref, bf16[768,3072]{1,0:T(8,128)(2,1)} %w_ref.3, f32[256,768]{1,0:T(8,128)} %get-tuple-element.42.normed_ref, f32[256,1]{1,0:T(8,128)} %get-tuple-element.43.inv_ref, f32[1,768]{1,0:T(1,128)} %reshape.39.gain_ref), custom_call_target="tpu_custom_call" | custom-call | flops 1207959552 | bytes 8388608 | tf_op jit(solution)/shard_map/input_grad/pallas_call | solution.py:305
  124.4 0.0 collective-permute-done.2.o_ref
  124.4 1.0 copy-done.3
  125.4 7.7 %weight_grads.1 = bf16[64,32,768]{2,1,0:T(8,128)(2,1)} custom-call(s32[1]{0:T(128)} %bitcast.core_ref, bf16[16,192,256]{2,1,0:T(8,128)(2,1)} %get-tuple-element.36.g_ref, bf16[12,192,256]{2,1,0:T(8,128)(2,1)} %copy-done.3, bf16[768,256]{1,0:T(8,128)(2,1)} %get-tuple-element.45.gated_ref, bf16[256,768]{1,0:T(8,128)(2,1)} %get-tuple-element.30.sc_ref, ...), custom_call_target="tpu_custom_call" | custom-call | flops 1610612736 | bytes 8388608 | tf_op jit(solution)/shard_map/weight_grads/pallas_call | solution.py:357
  133.2 0.0 all-to-all-done.3
  133.2 9.9 %all-to-all-start.4 = ((bf16[64,32,768]{2,1,0:T(8,128)(2,1)}), bf16[64,32,768]{2,1,0:T(8,128)(2,1)S(1)}, u32[]{:S(2)}, u32[]{:S(2)}) async-start(bf16[64,32,768]{2,1,0:T(8,128)(2,1)} %weight_grads.1), calls=%async_computation.5 | async-start | bytes 6291456 | tf_op jit(solution)/shard_map/all_to_all | solution.py:421
  143.0 2.7 %convolution_convert_fusion = bf16[256,768]{1,0:T(8,128)(2,1)} fusion(bf16[768,256]{1,0:T(8,128)(2,1)} %get-tuple-element.45.gated_ref, bf16[768,768]{1,0:T(8,128)(2,1)} %wout_ref.1), kind=kOutput, calls=%fused_computation.2 | convolution fusion | flops 302186496 | bytes 1966080 | tf_op jit(solution)/shard_map/cr,cd->rd/dot_general | solution.py:420
  145.7 0.8 convert_element_type.24
  146.5 43.1 %all-to-all-done.4 = bf16[64,32,768]{2,1,0:T(8,128)(2,1)S(1)} async-done(((bf16[64,32,768]{2,1,0:T(8,128)(2,1)}), bf16[64,32,768]{2,1,0:T(8,128)(2,1)S(1)}, u32[]{:S(2)}, u32[]{:S(2)}) %all-to-all-start.4) | async-done | bytes 3145760 | tf_op jit(solution)/shard_map/all_to_all | solution.py:421
  189.6 0.5 convert_reduce_fusion
  190.1 0.6 slice_bitcast_fusion
  190.7 0.5 collective-permute-start.4
  191.2 0.6 slice_bitcast_fusion.1
  191.9 0.2 collective-permute-done.4
  192.1 0.6 add.41
  (18 shorter events, 0.1 us)
Async XLA Ops:
  8.9 14.5 %all-to-all-start = ((bf16[8,16,1024]{2,1,0:T(8,128)(2,1)}), bf16[8,16,1024]{2,1,0:T(8,128)(2,1)S(1)}, u32[]{:S(2)}, u32[]{:S(2)}) async-start(bf16[8,16,1024]{2,1,0:T(8,128)(2,1)} %constant_dynamic-slice_fusion), calls=%async_computation | async-start | bytes 524288 | tf_op jit(solution)/shard_map/all_to_all | solution.py:384
  14.2 36.1 %all-gather.3.cloned.1.call-start = ((), (), s32[]{:S(2)}) async-start(), calls=%async_computation.7 | async-start | bytes 2359296 | tf_op jit(solution)/shard_map/all_gather | solution.py:391
  23.3 7.1 %copy-start.6 = (bf16[256,768]{1,0:T(8,128)(2,1)S(1)}, bf16[256,768]{1,0:T(8,128)(2,1)}, u32[]{:S(2)}) copy-start(bf16[256,768]{1,0:T(8,128)(2,1)} %get-tuple-element.30.sc_ref) | copy-start | bytes 1179652
  23.3 9.0 %copy-start.2 = (bf16[2,128,768]{2,1,0:T(8,128)(2,1)S(1)}, bf16[2,128,768]{2,1,0:T(8,128)(2,1)}, u32[]{:S(2)}) copy-start(bf16[2,128,768]{2,1,0:T(8,128)(2,1)} %param.11) | copy-start | bytes 1179652
  23.3 0.7 copy-start.5
  24.1 26.2 %all-to-all-start.1 = ((bf16[16,192,256]{2,1,0:T(8,128)(2,1)}), bf16[16,192,256]{2,1,0:T(8,128)(2,1)S(1)}, u32[]{:S(2)}, u32[]{:S(2)}) async-start(bf16[16,192,256]{2,1,0:T(8,128)(2,1)} %get-tuple-element.29), calls=%async_computation.1 | async-start | bytes 3145728 | tf_op jit(solution)/shard_map/all_to_all | solution.py:392
  30.5 4.6 %collective-permute-start.1 = (bf16[256,768]{1,0:T(8,128)(2,1)S(1)}, bf16[256,768]{1,0:T(8,128)(2,1)S(1)}, u32[]{:S(2)}, u32[]{:S(2)}) collective-permute-start(bf16[256,768]{1,0:T(8,128)(2,1)S(1)} %copy-done.6), channel_id=1, source_target_pairs={{0,8},{8,0},{1,9},{9,1},{2,10},{10,2},{3,11},{11,3},{4,12},{12,4},... | collective-permute-start | bytes 1179656 | tf_op jit(solution)/shard_map/ppermute | solution.py:399
  33.5 1.5 collective-permute-start
  35.1 15.2 %copy-start.8 = (bf16[8,64,256]{2,1,0:T(8,128)(2,1)}, bf16[8,64,256]{2,1,0:T(8,128)(2,1)S(1)}, u32[]{:S(2)}) copy-start(bf16[8,64,256]{2,1,0:T(8,128)(2,1)S(1)} %collective-permute-done.doo_ref) | copy-start | bytes 786436
  35.1 36.5 %copy-start.7 = (bf16[256,768]{1,0:T(8,128)(2,1)}, bf16[256,768]{1,0:T(8,128)(2,1)S(1)}, u32[]{:S(2)}) copy-start(bf16[256,768]{1,0:T(8,128)(2,1)S(1)} %collective-permute-done.1.sco_ref) | copy-start | bytes 1179652
  50.3 1.2 copy-start.1
  71.6 8.9 %copy-start.4 = (bf16[4,1024,128]{2,1,0:T(8,128)(2,1)S(1)}, bf16[4,1024,128]{2,1,0:T(8,128)(2,1)}, u32[]{:S(2)}) copy-start(bf16[4,1024,128]{2,1,0:T(8,128)(2,1)} %get-tuple-element.47) | copy-start | bytes 3145732
  71.6 8.9 %collective-permute-start.3 = (bf16[4,1024,128]{2,1,0:T(8,128)(2,1)}, bf16[4,1024,128]{2,1,0:T(8,128)(2,1)}, u32[]{:S(2)}, u32[]{:S(2)}) collective-permute-start(bf16[4,1024,128]{2,1,0:T(8,128)(2,1)} %get-tuple-element.48), channel_id=1, source_target_pairs={{0,8},{8,0},{1,9},{9,1},{2,10},{10,2},{3,11},{11,3},{4,12},{12,4},... | collective-permute-start | bytes 3145736 | tf_op jit(solution)/shard_map/ppermute | solution.py:407
  74.9 30.5 %all-to-all-start.2 = ((bf16[16,192,256]{2,1,0:T(8,128)(2,1)}), bf16[16,192,256]{2,1,0:T(8,128)(2,1)S(1)}, u32[]{:S(2)}, u32[]{:S(2)}) async-start(bf16[16,192,256]{2,1,0:T(8,128)(2,1)} %get-tuple-element.33), calls=%async_computation.2 | async-start | bytes 3145728 | tf_op jit(solution)/shard_map/all_to_all | solution.py:405
  80.4 30.9 %reduce-scatter.2.cloned.1.call-start = ((), (), s32[]{:S(2)}) async-start(), calls=%async_computation.6 | async-start | bytes 1310720 | tf_op jit(solution)/shard_map/reduce_scatter | solution.py:409
  105.4 1.2 copy-start
  110.3 14.1 %collective-permute-start.2 = (bf16[12,192,256]{2,1,0:T(8,128)(2,1)}, bf16[12,192,256]{2,1,0:T(8,128)(2,1)S(1)}, u32[]{:S(2)}, u32[]{:S(2)}) collective-permute-start(bf16[12,192,256]{2,1,0:T(8,128)(2,1)} %get-tuple-element.37), channel_id=1, source_target_pairs={{0,8},{8,0},{1,9},{9,1},{2,10},{10,2},{3,11},{11,3},{4,12},{12,4},... | collective-permute-start | bytes 3538952 | tf_op jit(solution)/shard_map/ppermute | solution.py:414
  113.2 19.9 %all-to-all-start.3 = ((bf16[16,128,64]{1,2,0:T(8,128)(2,1)}), bf16[16,128,64]{1,2,0:T(8,128)(2,1)S(1)}, u32[]{:S(2)}, u32[]{:S(2)}) async-start(bf16[16,128,64]{1,2,0:T(8,128)(2,1)} %bitcast.11), calls=%async_computation.4 | async-start | bytes 524288 | tf_op jit(solution)/shard_map/all_to_all | solution.py:411
  124.4 1.0 copy-start.3
  133.2 56.5 %all-to-all-start.4 = ((bf16[64,32,768]{2,1,0:T(8,128)(2,1)}), bf16[64,32,768]{2,1,0:T(8,128)(2,1)S(1)}, u32[]{:S(2)}, u32[]{:S(2)}) async-start(bf16[64,32,768]{2,1,0:T(8,128)(2,1)} %weight_grads.1), calls=%async_computation.5 | async-start | bytes 6291456 | tf_op jit(solution)/shard_map/all_to_all | solution.py:421
  190.7 1.3 collective-permute-start.4
Sparse Core Ops, SparseCore 0:
  24.2 25.7 all-gather.2
  83.7 21.4 reduce-scatter.1

commit v5 on v4

--- a/solution.py
+++ b/solution.py
@@ -52,7 +52,7 @@
         normed = shifted * inv_std
         normed_ref[...] = normed
         inv_ref[...] = inv_std
-        scaled_ref[...] = (normed * gain_ref[...]).astype(BF)
+        scaled_ref[...] = (normed * gain_ref[...].reshape(1, C)).astype(BF)
 
     block = dot(scaled_ref[...], w_ref[...])
 
@@ -90,7 +90,7 @@
         grid=(4,),
         in_specs=[
             whole((flat, C)),
-            whole((1, C)),
+            whole((C,)),
             pl.BlockSpec((C, C), lambda t: (0, t)),
             whole((C, C)),
             whole((flat, C)),
@@ -171,13 +171,14 @@
     def _():
         for p, d in zip(every, dscores):
             total = (gb_s[p] + d).astype(BF)
-            for x in range(4):
-                even = total[:, x * 256 : x * 256 + 128]
-                odd = total[:, x * 256 + 128 : x * 256 + 256]
-                low = jnp.concatenate([even[:, :64], odd[:, :64]], axis=1)
-                high = jnp.concatenate([even[:, 64:], odd[:, 64:]], axis=1)
-                keep_ref[x, p] = jnp.where(core == 0, low, high)
-                give_ref[x, p] = jnp.where(core == 0, high, low)
+            for t in range(rows // TOK):
+                for n in range(8):
+                    tile = total[t * TOK : (t + 1) * TOK, n * TOK : (n + 1) * TOK]
+                    low = jnp.concatenate([tile[:64, :64], tile[64:, :64]], axis=1)
+                    high = jnp.concatenate([tile[:64, 64:], tile[64:, 64:]], axis=1)
+                    where = (n % 2) * 8 + p.start // TOK + t
+                    keep_ref[n // 2, where] = jnp.where(core == 0, low, high)
+                    give_ref[n // 2, where] = jnp.where(core == 0, high, low)
 
     all_low = jnp.concatenate(dscores_low, axis=0)
     gscaled_t = jnp.concatenate(gscaled, axis=0).T.astype(BF)
@@ -195,7 +196,7 @@
     def whole(shape):
         return pl.BlockSpec(shape, lambda s, core: (0,) * len(shape))
 
-    half_sum = (4, KEYS, 128)
+    half_sum = (4, HEADS, 64, 128)
     return pl.pallas_call(
         functools.partial(attention_kernel, blocks=blocks),
         grid_spec=pltpu.PrefetchScalarGridSpec(
@@ -227,7 +228,7 @@
     )(core, x, bias)
 
 
-def gate_kernel(core_ref, back_ref, gate_ref, gg_ref, gproj_ref, gated_ref, send_ref):
+def gate_kernel(core_ref, back_ref, gate_ref, gg_ref, ggate_ref, gated_ref, send_ref):
     other = 1 - core_ref[0]
     flat = gate_ref.shape[1]
     att = back_ref[:, :DH, :].astype(F32).reshape(C, flat)
@@ -237,13 +238,18 @@
     gated_ref[...] = gated
     for q in range(4):
         send_ref[8 + q] = gated[q * 192 : (q + 1) * 192]
-    for kind in range(3):
-        gproj_ref[kind * 4 : kind * 4 + 4] = back_ref[:, (kind + 1) * DH : (kind + 2) * DH, :].reshape(
-            4, 4 * DH, flat
-        )
-    gproj_ref[12:16] = (gg_ref[...].astype(F32) * opened * (1.0 - gate)).astype(BF).reshape(4, 4 * DH, flat)
+    ggate_ref[...] = (gg_ref[...].astype(F32) * opened * (1.0 - gate)).astype(BF).reshape(4, 4 * DH, flat)
     for n in range(8):
-        send_ref[n] = gproj_ref[2 * n + other]
+        send_ref[n] = head_rows(back_ref, ggate_ref, n, other)
+
+
+def head_rows(back_ref, ggate_ref, n, core):
+    kind = n // 2
+    group = (n % 2) * 2 + core
+    if kind == 3:
+        return ggate_ref[group]
+    flat = back_ref.shape[2]
+    return back_ref[pl.ds(group * 4, 4), (kind + 1) * DH : (kind + 2) * DH, :].reshape(4 * DH, flat)
 
 
 def gate_step(core, back, gate, ggated):
@@ -251,7 +257,7 @@
         return pl.BlockSpec(shape, lambda t, core: (0,) * len(shape))
 
     flat = gate.shape[1]
-    shapes = [(16, 4 * DH, flat), (C, flat), (12, 4 * DH, flat)]
+    shapes = [(4, 4 * DH, flat), (C, flat), (12, 4 * DH, flat)]
     return pl.pallas_call(
         gate_kernel,
         grid_spec=pltpu.PrefetchScalarGridSpec(
@@ -267,25 +273,28 @@
     )(core, back, gate, ggated)
 
 
-def input_grad_kernel(g_ref, w_ref, normed_ref, inv_ref, gain_ref, grad_ref, ggain_ref, total_s):
+def input_grad_kernel(back_ref, ggate_ref, w_ref, normed_ref, inv_ref, gain_ref, grad_ref, total_s):
     step = pl.program_id(0)
     flat = normed_ref.shape[0]
-    part = dot(w_ref[...], g_ref[...].reshape(C, flat))
-
-    @pl.when(step == 0)
-    def _():
-        total_s[...] = part
-
-    @pl.when(step > 0)
-    def _():
-        total_s[...] += part
+
+    for kind in range(4):
+
+        @pl.when(step == kind)
+        def _(kind=kind):
+            if kind == 3:
+                total_s[...] += dot(w_ref[...], ggate_ref[...].reshape(C, flat))
+            else:
+                rows = back_ref[:, (kind + 1) * DH : (kind + 2) * DH, :].reshape(C, flat)
+                part = dot(w_ref[...], rows)
+                if kind == 0:
+                    total_s[...] = part
+                else:
+                    total_s[...] += part
 
     @pl.when(step == 3)
     def _():
-        grad_scaled = total_s[...].T
         normed = normed_ref[...]
-        ggain_ref[...] = jnp.sum(grad_scaled * normed, axis=0, keepdims=True)
-        grad_normed = grad_scaled * gain_ref[...]
+        grad_normed = total_s[...].T * gain_ref[...].reshape(1, C)
         grad_ref[...] = (
             inv_ref[...]
             * (
@@ -296,7 +305,7 @@
         ).astype(BF)
 
 
-def input_grad(gproj, w_in, normed, inv_std, ln_gain):
+def input_grad(back, ggate, w_in, normed, inv_std, ln_gain):
     flat = normed.shape[0]
 
     def whole(shape):
@@ -306,62 +315,92 @@
         input_grad_kernel,
         grid=(4,),
         in_specs=[
-            pl.BlockSpec((4, 4 * DH, flat), lambda t: (t, 0, 0)),
+            whole(back.shape),
+            whole(ggate.shape),
             pl.BlockSpec((C, C), lambda t: (0, t)),
             whole((flat, C)),
             whole((flat, 1)),
-            whole((1, C)),
+            whole((C,)),
         ],
-        out_specs=[whole((flat, C)), whole((1, C))],
-        out_shape=[jax.ShapeDtypeStruct((flat, C), BF), jax.ShapeDtypeStruct((1, C), F32)],
+        out_specs=whole((flat, C)),
+        out_shape=jax.ShapeDtypeStruct((flat, C), BF),
         scratch_shapes=[pltpu.VMEM((C, flat), F32)],
         compiler_params=params(),
         cost_estimate=pl.CostEstimate(
             flops=2 * flat * C * 4 * C, bytes_accessed=8 * 2**20, transcendentals=0
         ),
         name="input_grad",
-    )(gproj, w_in, normed, inv_std, ln_gain)
+    )(back, ggate, w_in, normed, inv_std, ln_gain)
 
 
 def weight_kernel(
-    core_ref, g_ref, o_ref, gated_ref, sc_ref, sco_ref, do_ref, doo_ref, gain_ref, out_ref, scaled_s, gated_s
+    core_ref, back_ref, ggate_ref, o_ref, gated_ref, sc_ref, sco_ref, do_ref, doo_ref, wt_ref, gain_ref,
+    out_ref, scaled_s, gated_s, sum_s,
 ):
     core = core_ref[0]
-    n = pl.program_id(0)
+    step = pl.program_id(0)
     flat = sc_ref.shape[0]
-
-    @pl.when(n == 0)
+    last = pl.num_programs(0) - 1
+
+    @pl.when(step == 0)
     def _():
         scaled_s[:flat] = sc_ref[...]
         scaled_s[flat:] = sco_ref[...]
         gated_s[:flat] = gated_ref[...].T
         gated_s[flat:] = o_ref[8:12].reshape(C, flat).T
-
-    left = jnp.concatenate([g_ref[2 * n + core], o_ref[n]], axis=1)
-    win = dot(left, scaled_s[...])
-    wout = dot(jnp.concatenate([do_ref[n], doo_ref[n]], axis=1), gated_s[...])
-    gain = gain_ref[...]
-    gain_hi = gain.astype(BF).astype(F32)
-    gain_lo = gain - gain_hi
-    row = lax.broadcasted_iota(jnp.int32, (8, C), 0)
-    for k in range(8):
-        tail = jnp.where(row == 6, gain_hi, jnp.where(row == 7, gain_lo, wout[k * 8 : k * 8 + 8]))
-        out_ref[k] = jnp.concatenate([win[k * 24 : k * 24 + 24], tail], axis=0).astype(BF)
+        sum_s[...] = jnp.zeros_like(sum_s)
+
+    for kind in range(4):
+
+        @pl.when(step == kind)
+        def _(kind=kind):
+            blocks = [
+                jnp.concatenate([head_rows(back_ref, ggate_ref, n, core), o_ref[n]], axis=1)
+                for n in (2 * kind, 2 * kind + 1)
+            ]
+            win = dot(jnp.concatenate(blocks, axis=0), scaled_s[...])
+            tails = jnp.concatenate(
+                [
+                    jnp.concatenate([do_ref[n], doo_ref[n]], axis=1)
+                    for n in (2 * kind, 2 * kind + 1)
+                ],
+                axis=0,
+            )
+            wout = dot(tails, gated_s[...])
+            weights = wt_ref[2 * kind : 2 * kind + 2].reshape(8 * DH, C).astype(F32)
+            sum_s[...] += jnp.sum((win * weights).reshape(DH, 8, C), axis=0)
+            for k in range(16):
+                out_ref[kind * 16 + k] = jnp.concatenate(
+                    [win[k * 24 : k * 24 + 24], wout[k * 8 : k * 8 + 8]], axis=0
+                ).astype(BF)
+
+    @pl.when(step == last)
+    def _():
+        gain = jnp.sum(sum_s[...], axis=0, keepdims=True) / gain_ref[...].reshape(1, C)
+        gain_hi = gain.astype(BF).astype(F32)
+        row = lax.broadcasted_iota(jnp.int32, (16, C), 0)
+        extra = jnp.where(row == 14, gain_hi, gain - gain_hi).astype(BF)
+        for k in range(64):
+            out_ref[k, 16:] = jnp.where(row >= 14, extra, out_ref[k, 16:])
 
 
 def weight_grads(core, operands):
     def whole(shape):
         return pl.BlockSpec(shape, lambda t, core: (0,) * len(shape))
 
-    flat = operands[3].shape[0]
+    flat = operands[4].shape[0]
     return pl.pallas_call(
         weight_kernel,
         grid_spec=pltpu.PrefetchScalarGridSpec(
             num_scalar_prefetch=1,
-            grid=(8,),
+            grid=(4,),
             in_specs=[whole(o.shape) for o in operands],
-            out_specs=pl.BlockSpec((8, 32, C), lambda t, core: (t, 0, 0)),
-            scratch_shapes=[pltpu.VMEM((2 * flat, C), BF), pltpu.VMEM((2 * flat, C), BF)],
+            out_specs=whole((64, 32, C)),
+            scratch_shapes=[
+                pltpu.VMEM((2 * flat, C), BF),
+                pltpu.VMEM((2 * flat, C), BF),
+                pltpu.VMEM((8, C), F32),
+            ],
         ),
         out_shape=jax.ShapeDtypeStruct((64, 32, C), BF),
         compiler_params=params(),
@@ -385,7 +424,7 @@
 
     rows_out = d_out.reshape(flat, channels)
     scaled, normed, inv_std, send, gate, ggated = front(
-        act.reshape(flat, channels), ln_gain.reshape(1, C), w_in, w_out, rows_out
+        act.reshape(flat, channels), ln_gain, w_in, w_out, rows_out
     )
     bias, send = lax.optimization_barrier((bias, send))
     bias = lax.all_gather(bias, ("x", "core"))
@@ -398,8 +437,9 @@
     dout_other = lax.ppermute(dout_send, "core", SWAP)
     scaled_other = lax.ppermute(scaled, "core", SWAP)
 
-    received, dout_mine, dout_other, scaled_other = lax.optimization_barrier(
-        (received, dout_mine, dout_other, scaled_other)
+    w_rows = lax.dynamic_index_in_dim(w_in.T.reshape(8, 2, 4 * DH, C), core, 1, keepdims=False)
+    received, dout_mine, dout_other, scaled_other, w_rows = lax.optimization_barrier(
+        (received, dout_mine, dout_other, scaled_other, w_rows)
     )
     result, keep, give = attention(core_arg, received, bias)
     back = lax.all_to_all(result, PLANE, 0, 0, tiled=True)
@@ -407,16 +447,18 @@
     got = lax.ppermute(give, "core", SWAP)
     gb = (keep.astype(F32) + got.astype(F32)).astype(BF)
     gb = lax.psum_scatter(gb, "x", scatter_dimension=0, tiled=False)
-    gb = gb.reshape(8, TOK, 2, 64).transpose(2, 0, 1, 3).reshape(HEADS, TOK, 64)
-    grad_bias = lax.all_to_all(gb, PLANE, 0, 0, tiled=True).astype(F32)
-
-    gproj, gated, half = gate_step(core_arg, back, gate, ggated)
+    gb = lax.all_to_all(gb, PLANE, 0, 0, tiled=True)
+
+    ggate, gated, half = gate_step(core_arg, back, gate, ggated)
     other = lax.ppermute(half, "core", SWAP)
-    grad_act, gain = input_grad(gproj, w_in, normed, inv_std, ln_gain.reshape(1, C))
     chunks = weight_grads(
-        core_arg, (gproj, other, gated, scaled, scaled_other, dout_mine, dout_other, gain)
+        core_arg,
+        (back, ggate, other, gated, scaled, scaled_other, dout_mine, dout_other, w_rows, ln_gain),
     )
-    chunks, gated = lax.optimization_barrier((chunks, gated))
+    chunks, gated, ggate, gb = lax.optimization_barrier((chunks, gated, ggate, gb))
+    grad_act = input_grad(back, ggate, w_in, normed, inv_std, ln_gain)
+    gb = gb.astype(F32)
+    grad_bias = jnp.concatenate([gb[:, :, :64], gb[:, :, 64:]], axis=1)
     output = jnp.einsum("cr,cd->rd", gated, w_out, preferred_element_type=F32).astype(BF)
     chunks = lax.all_to_all(chunks, ("x", "zh", "zl", "y"), 0, 0, tiled=True)
     total = jnp.sum(chunks.astype(F32), axis=0)

time: 200 us -> 190 us (0.950)
  waiting for transfers between devices: 82.5 us -> 63.7 us
  local copies, waits for them, and re-layouts: 11.4 us -> 20.6 us
    unnamed x19 -> x22, local copies, waits for them, and re-layouts: 4.15 us -> 13.1 us
    all_to_all x1, waiting for transfers between devices: 43.1 us -> 34.4 us  [per_device(): chunks = lax.all_to_all(chunks, ('x', 'zh', 'zl', 'y'), 0, 0, tiled=True)]
    all_to_all x1, waiting for transfers between devices: 15.2 us -> 6.8 us  [per_device(): received = lax.all_to_all(send, PLANE, 0, 0, tiled=True)]
    squeeze x0 -> x1, local copies, waits for them, and re-layouts: none -> 3.3 us  [per_device(): lax.dynamic_index_in_dim(w_in.T.reshape(8, 2, 4 * DH, C), core, 1, keepdi...]
  transfers between devices with their start and end apart: 12 -> 12, of which waited for: 5 -> 4; matrix products, arithmetic and copies ran while one was open for 5% -> 11% of each run, Pallas kernels for 13% -> 13%
where the time goes in v5:
time: 190 us; the launch traced here: 189 us
  waiting for transfers between devices  63.7 us (34%)
  Pallas kernels  44.7 us (24%)
  starting transfers between devices  38.8 us (20%)
  local copies, waits for them, and re-layouts  20.6 us (11%)
  between operations  14.2 us (7%)
  other arithmetic  4.77 us (3%)
  matrix products  2.52 us (1%)
    all_to_all x1, waiting for transfers between devices, per_device(): chunks = lax.all_to_all(chunks, ('x', 'zh', 'zl', 'y'), 0, 0, tiled=True)  34.4 us
    all_to_all x1, waiting for transfers between devices, per_device(): back = lax.all_to_all(result, PLANE, 0, 0, tiled=True)  22.3 us
    pallas_call x1, Pallas kernels, attention(): pl.pallas_call(functools.partial(attention_kernel, blocks=blocks), grid_s...  20.1 us
    unnamed x22, local copies, waits for them, and re-layouts  13.1 us
    all_to_all x1, starting transfers between devices, per_device(): chunks = lax.all_to_all(chunks, ('x', 'zh', 'zl', 'y'), 0, 0, tiled=True)  9.87 us
    pallas_call x1, Pallas kernels, front(): pl.pallas_call(front_kernel, grid=(4,), in_specs=[whole((flat, C)), whole...  7.83 us
    pallas_call x1, Pallas kernels, weight_grads(): pl.pallas_call(weight_kernel, grid_spec=pltpu.PrefetchScalarGridSpec(num_...  7.43 us
    all_to_all x1, waiting for transfers between devices, per_device(): received = lax.all_to_all(send, PLANE, 0, 0, tiled=True)  6.8 us
  transfers between devices with their start and end apart: 12, of which 4 were waited for; matrix products, arithmetic and copies ran while one was open for 11% of the time, Pallas kernels for 13%

profile of v5, /device:TPU:103, one launch (start us, length us, event | category | flops | bytes accessed | tf_op | source)
XLA Modules:
  0.0 189.3 jit_solution(734971270432126266)
XLA Ops:
  7.2 1.7 constant_dynamic-slice_fusion
  8.9 5.4 %all-to-all-start = ((bf16[8,16,1024]{2,1,0:T(8,128)(2,1)}), bf16[8,16,1024]{2,1,0:T(8,128)(2,1)S(1)}, u32[]{:S(2)}, u32[]{:S(2)}) async-start(bf16[8,16,1024]{2,1,0:T(8,128)(2,1)} %constant_dynamic-slice_fusion), calls=%async_computation | async-start | bytes 524288 | tf_op jit(solution)/shard_map/all_to_all | solution.py:423
  14.2 7.8 %front.1 = (bf16[256,768]{1,0:T(8,128)(2,1)}, f32[256,768]{1,0:T(8,128)}, f32[256,1]{1,0:T(8,128)}, bf16[16,192,256]{2,1,0:T(8,128)(2,1)}, f32[768,256]{1,0:T(8,128)}, /*index=5*/bf16[768,256]{1,0:T(8,128)(2,1)}) custom-call(bf16[256,768]{1,0:T(8,128)(2,1)} %bitcast.30, f32[768]{0:T(1024)} %gain_ref.5, bf16[768,3072]{1,0:T(8,128)(2,1)} %w_ref.3, ...), custom_call_target="tpu_custom_call" | custom-call | flops 1509949440 | bytes 11534336 | tf_op jit(solution)/shard_map/front/pallas_call | solution.py:88
  22.1 0.0 all-to-all-done
  22.1 0.7 copy-done.5
  22.8 0.0 all-gather.3.cloned.1.call-update
  22.8 6.4 %all-to-all-start.1 = ((bf16[16,192,256]{2,1,0:T(8,128)(2,1)}), bf16[16,192,256]{2,1,0:T(8,128)(2,1)S(1)}, u32[]{:S(2)}, u32[]{:S(2)}) async-start(bf16[16,192,256]{2,1,0:T(8,128)(2,1)} %get-tuple-element.30), calls=%async_computation.1 | async-start | bytes 3145728 | tf_op jit(solution)/shard_map/all_to_all | solution.py:431
  29.2 1.9 collective-permute-start.1
  31.1 0.2 copy.17
  31.3 0.1 reshape.36
  31.4 0.1 pad.4
  31.5 0.8 dynamic-slice_bitcast_fusion.1
  32.3 0.0 collective-permute-start
  32.3 6.6 %copy.18 = bf16[768,3072]{0,1:T(8,128)(2,1)} copy(bf16[768,3072]{1,0:T(8,128)(2,1)} %w_ref.3) | data formatting | bytes 9437184 | tf_op args[3]
  38.9 3.3 %dynamic-slice_bitcast_fusion.wt_ref = bf16[8,192,768]{2,1,0:T(8,128)(2,1)} fusion(bf16[8,2,192,768]{3,2,1,0:T(8,128)(2,1)} %bitcast.25, s32[]{:T(128)S(6)} %select_n.17), kind=kLoop, calls=%fused_computation.1 | loop fusion | bytes 4718596 | tf_op jit(solution)/shard_map/jit(dynamic_index_in_dim)/squeeze | solution.py:440
  42.2 0.0 collective-permute-done.doo_ref
  42.2 0.0 collective-permute-done.1.sco_ref
  42.2 0.0 copy-start.7
  42.2 6.8 %all-to-all-done.1.x_ref = bf16[16,192,256]{2,1,0:T(8,128)(2,1)S(1)} async-done(((bf16[16,192,256]{2,1,0:T(8,128)(2,1)}), bf16[16,192,256]{2,1,0:T(8,128)(2,1)S(1)}, u32[]{:S(2)}, u32[]{:S(2)}) %all-to-all-start.1) | async-done | bytes 1572896 | tf_op jit(solution)/shard_map/all_to_all | solution.py:431
  49.0 1.1 copy-done.1
  50.2 20.1 %attention.1 = (bf16[16,192,256]{2,1,0:T(8,128)(2,1)}, bf16[4,16,64,128]{3,2,1,0:T(8,128)(2,1)}, bf16[4,16,64,128]{3,2,1,0:T(8,128)(2,1)}) custom-call(s32[1]{0:T(128)} %bitcast.core_ref, bf16[16,192,256]{2,1,0:T(8,128)(2,1)} %copy-done.1, bf16[8,8,16,1024]{3,2,1,0:T(8,128)(2,1)} %bitcast.32), custom_call_target="tpu_custom_call" | custom-call | flops 12884901888 | bytes 8388608 | tf_op jit(solution)/shard_map/attention/pallas_call | solution.py:200
  70.3 3.3 %collective-permute-start.3 = (bf16[4,16,64,128]{3,2,1,0:T(8,128)(2,1)}, bf16[4,16,64,128]{3,2,1,0:T(8,128)(2,1)}, u32[]{:S(2)}, u32[]{:S(2)}) collective-permute-start(bf16[4,16,64,128]{3,2,1,0:T(8,128)(2,1)} %get-tuple-element.45), channel_id=1, source_target_pairs={{0,8},{8,0},{1,9},{9,1},{2,10},{10,2},{3,11},{11,3},{4,12},{12,4},... | collective-permute-start | bytes 3145736 | tf_op jit(solution)/shard_map/ppermute | solution.py:447
  73.6 5.5 %all-to-all-start.2 = ((bf16[16,192,256]{2,1,0:T(8,128)(2,1)}), bf16[16,192,256]{2,1,0:T(8,128)(2,1)S(1)}, u32[]{:S(2)}, u32[]{:S(2)}) async-start(bf16[16,192,256]{2,1,0:T(8,128)(2,1)} %get-tuple-element.34), calls=%async_computation.2 | async-start | bytes 3145728 | tf_op jit(solution)/shard_map/all_to_all | solution.py:445
  79.1 0.0 reduce-scatter.2.cloned.1.call-start
  79.1 0.0 collective-permute-done.3
  79.2 2.6 %add_convert_fusion = bf16[4,16,64,128]{3,2,1,0:T(8,128)(2,1)} fusion(bf16[4,16,64,128]{3,2,1,0:T(8,128)(2,1)} %collective-permute-done.3, bf16[4,16,64,128]{3,2,1,0:T(8,128)(2,1)S(1)} %copy-done.4), kind=kLoop, calls=%fused_computation.2 | loop fusion | flops 2097152 | bytes 3145728 | tf_op jit(solution)/shard_map/convert_element_type | solution.py:448
  81.8 0.0 reduce-scatter.2.cloned.1.call-update
  81.8 22.3 %all-to-all-done.2.back_ref = bf16[16,192,256]{2,1,0:T(8,128)(2,1)S(1)} async-done(((bf16[16,192,256]{2,1,0:T(8,128)(2,1)}), bf16[16,192,256]{2,1,0:T(8,128)(2,1)S(1)}, u32[]{:S(2)}, u32[]{:S(2)}) %all-to-all-start.2) | async-done | bytes 1572896 | tf_op jit(solution)/shard_map/all_to_all | solution.py:445
  104.1 1.2 copy-done
  105.2 3.3 %gate.1 = (bf16[4,192,256]{2,1,0:T(8,128)(2,1)}, bf16[768,256]{1,0:T(8,128)(2,1)}, bf16[12,192,256]{2,1,0:T(8,128)(2,1)}) custom-call(s32[1]{0:T(128)} %bitcast.core_ref, bf16[16,192,256]{2,1,0:T(8,128)(2,1)} %copy-done, f32[768,256]{1,0:T(8,128)} %get-tuple-element.35.gate_ref, bf16[768,256]{1,0:T(8,128)(2,1)} %get-tuple-element.36.gg_ref), custom_call_target="tpu_custom_call" | custom-call | flops 1179648 | bytes 6291456 | tf_op jit(solution)/shard_map/gate/pallas_call | solution.py:261
  108.5 1.0 collective-permute-start.2
  109.5 5.0 %all-to-all-start.3 = ((bf16[16,64,128]{2,1,0:T(8,128)(2,1)}), bf16[16,64,128]{2,1,0:T(8,128)(2,1)S(1)}, u32[]{:S(2)}, u32[]{:S(2)}) async-start(bf16[16,64,128]{2,1,0:T(8,128)(2,1)} %bitcast.31), calls=%async_computation.4 | async-start | bytes 524288 | tf_op jit(solution)/shard_map/all_to_all | solution.py:450
  114.5 0.0 collective-permute-done.2.o_ref
  114.5 1.1 copy-done.3
  115.6 7.4 %weight_grads.1 = bf16[64,32,768]{2,1,0:T(8,128)(2,1)} custom-call(s32[1]{0:T(128)} %bitcast.core_ref, bf16[16,192,256]{2,1,0:T(8,128)(2,1)} %copy-done, bf16[4,192,256]{2,1,0:T(8,128)(2,1)} %get-tuple-element.47.ggate_ref, bf16[12,192,256]{2,1,0:T(8,128)(2,1)} %copy-done.3, bf16[768,256]{1,0:T(8,128)(2,1)} %get-tuple-element.46.gated_ref, ...), custom_call_target="tpu_custom_call" | custom-call | flops 1610612736 | bytes 8388608 | tf_op jit(solution)/shard_map/weight_grads/pallas_call | solution.py:392
  123.0 9.9 %all-to-all-start.4 = ((bf16[64,32,768]{2,1,0:T(8,128)(2,1)}), bf16[64,32,768]{2,1,0:T(8,128)(2,1)S(1)}, u32[]{:S(2)}, u32[]{:S(2)}) async-start(bf16[64,32,768]{2,1,0:T(8,128)(2,1)} %weight_grads.1), calls=%async_computation.5 | async-start | bytes 6291456 | tf_op jit(solution)/shard_map/all_to_all | solution.py:463
  132.9 0.2 fusion.1
  133.1 1.1 pad_maximum_fusion
  134.1 2.3 %copy.19 = f32[16,128,64]{1,2,0:T(8,128)} copy(f32[16,128,64]{2,1,0:T(8,128)} %pad_maximum_fusion) | data formatting | bytes 1048576
  136.5 6.0 %input_grad.1 = bf16[256,768]{1,0:T(8,128)(2,1)} custom-call(bf16[16,192,256]{2,1,0:T(8,128)(2,1)} %copy-done, bf16[4,192,256]{2,1,0:T(8,128)(2,1)} %get-tuple-element.47.ggate_ref, bf16[768,3072]{1,0:T(8,128)(2,1)} %w_ref.3, f32[256,768]{1,0:T(8,128)} %get-tuple-element.48.normed_ref, f32[256,1]{1,0:T(8,128)} %get-tuple-element.49.inv_ref, f32[768]{0:T(1024)} %gain_ref.5), custom_call_target="tpu_custom_call" | custom-call | flops 1207959552 | bytes 8388608 | tf_op jit(solution)/shard_map/input_grad/pallas_call | solution.py:314
  142.5 2.5 %convolution_convert_fusion = bf16[256,768]{1,0:T(8,128)(2,1)} fusion(bf16[768,256]{1,0:T(8,128)(2,1)S(1)} %copy-done.8, bf16[768,768]{1,0:T(8,128)(2,1)} %wout_ref.1), kind=kOutput, calls=%fused_computation.3 | convolution fusion | flops 302186496 | bytes 1966080 | tf_op jit(solution)/shard_map/cr,cd->rd/dot_general | solution.py:462
  145.0 34.4 %all-to-all-done.4 = bf16[64,32,768]{2,1,0:T(8,128)(2,1)S(1)} async-done(((bf16[64,32,768]{2,1,0:T(8,128)(2,1)}), bf16[64,32,768]{2,1,0:T(8,128)(2,1)S(1)}, u32[]{:S(2)}, u32[]{:S(2)}) %all-to-all-start.4) | async-done | bytes 3145760 | tf_op jit(solution)/shard_map/all_to_all | solution.py:463
  179.4 0.5 convert_reduce_fusion
  179.9 0.6 slice_bitcast_fusion
  180.6 0.5 collective-permute-start.4
  181.1 0.6 slice_bitcast_fusion.1
  181.7 0.2 collective-permute-done.4
  181.9 0.6 add.43
  (20 shorter events, 0.1 us)
Async XLA Ops:
  8.9 13.2 %all-to-all-start = ((bf16[8,16,1024]{2,1,0:T(8,128)(2,1)}), bf16[8,16,1024]{2,1,0:T(8,128)(2,1)S(1)}, u32[]{:S(2)}, u32[]{:S(2)}) async-start(bf16[8,16,1024]{2,1,0:T(8,128)(2,1)} %constant_dynamic-slice_fusion), calls=%async_computation | async-start | bytes 524288 | tf_op jit(solution)/shard_map/all_to_all | solution.py:423
  14.2 34.8 %all-gather.3.cloned.1.call-start = ((), (), s32[]{:S(2)}) async-start(), calls=%async_computation.7 | async-start | bytes 2359296 | tf_op jit(solution)/shard_map/all_gather | solution.py:430
  22.1 7.2 %copy-start.6 = (bf16[256,768]{1,0:T(8,128)(2,1)S(1)}, bf16[256,768]{1,0:T(8,128)(2,1)}, u32[]{:S(2)}) copy-start(bf16[256,768]{1,0:T(8,128)(2,1)} %get-tuple-element.31.sc_ref) | copy-start | bytes 1179652
  22.1 9.0 %copy-start.2 = (bf16[2,128,768]{2,1,0:T(8,128)(2,1)S(1)}, bf16[2,128,768]{2,1,0:T(8,128)(2,1)}, u32[]{:S(2)}) copy-start(bf16[2,128,768]{2,1,0:T(8,128)(2,1)} %param.11) | copy-start | bytes 1179652
  22.1 0.7 copy-start.5
  22.8 26.2 %all-to-all-start.1 = ((bf16[16,192,256]{2,1,0:T(8,128)(2,1)}), bf16[16,192,256]{2,1,0:T(8,128)(2,1)S(1)}, u32[]{:S(2)}, u32[]{:S(2)}) async-start(bf16[16,192,256]{2,1,0:T(8,128)(2,1)} %get-tuple-element.30), calls=%async_computation.1 | async-start | bytes 3145728 | tf_op jit(solution)/shard_map/all_to_all | solution.py:431
  29.2 13.0 %collective-permute-start.1 = (bf16[256,768]{1,0:T(8,128)(2,1)S(1)}, bf16[256,768]{1,0:T(8,128)(2,1)S(1)}, u32[]{:S(2)}, u32[]{:S(2)}) collective-permute-start(bf16[256,768]{1,0:T(8,128)(2,1)S(1)} %copy-done.6), channel_id=1, source_target_pairs={{0,8},{8,0},{1,9},{9,1},{2,10},{10,2},{3,11},{11,3},{4,12},{12,4},... | collective-permute-start | bytes 1179656 | tf_op jit(solution)/shard_map/ppermute | solution.py:438
  32.3 10.0 %collective-permute-start = (bf16[8,64,256]{2,1,0:T(8,128)(2,1)S(1)}, bf16[8,64,256]{2,1,0:T(8,128)(2,1)S(1)}, u32[]{:S(2)}, u32[]{:S(2)}) collective-permute-start(bf16[8,64,256]{2,1,0:T(8,128)(2,1)S(1)} %get-tuple-element.70), channel_id=1, source_target_pairs={{0,8},{8,0},{1,9},{9,1},{2,10},{10,2},{3,11},{11,3},{4,12},{12,4},... | collective-permute-start | bytes 786440 | tf_op jit(solution)/shard_map/ppermute | solution.py:437
  42.2 28.0 %copy-start.9 = (bf16[8,64,256]{2,1,0:T(8,128)(2,1)}, bf16[8,64,256]{2,1,0:T(8,128)(2,1)S(1)}, u32[]{:S(2)}) copy-start(bf16[8,64,256]{2,1,0:T(8,128)(2,1)S(1)} %collective-permute-done.doo_ref) | copy-start | bytes 786436
  42.2 28.0 %copy-start.7 = (bf16[256,768]{1,0:T(8,128)(2,1)}, bf16[256,768]{1,0:T(8,128)(2,1)S(1)}, u32[]{:S(2)}) copy-start(bf16[256,768]{1,0:T(8,128)(2,1)S(1)} %collective-permute-done.1.sco_ref) | copy-start | bytes 1179652
  49.0 1.2 copy-start.1
  70.3 8.9 %copy-start.4 = (bf16[4,16,64,128]{3,2,1,0:T(8,128)(2,1)S(1)}, bf16[4,16,64,128]{3,2,1,0:T(8,128)(2,1)}, u32[]{:S(2)}) copy-start(bf16[4,16,64,128]{3,2,1,0:T(8,128)(2,1)} %get-tuple-element.44) | copy-start | bytes 3145732
  70.3 8.9 %collective-permute-start.3 = (bf16[4,16,64,128]{3,2,1,0:T(8,128)(2,1)}, bf16[4,16,64,128]{3,2,1,0:T(8,128)(2,1)}, u32[]{:S(2)}, u32[]{:S(2)}) collective-permute-start(bf16[4,16,64,128]{3,2,1,0:T(8,128)(2,1)} %get-tuple-element.45), channel_id=1, source_target_pairs={{0,8},{8,0},{1,9},{9,1},{2,10},{10,2},{3,11},{11,3},{4,12},{12,4},... | collective-permute-start | bytes 3145736 | tf_op jit(solution)/shard_map/ppermute | solution.py:447
  73.6 30.5 %all-to-all-start.2 = ((bf16[16,192,256]{2,1,0:T(8,128)(2,1)}), bf16[16,192,256]{2,1,0:T(8,128)(2,1)S(1)}, u32[]{:S(2)}, u32[]{:S(2)}) async-start(bf16[16,192,256]{2,1,0:T(8,128)(2,1)} %get-tuple-element.34), calls=%async_computation.2 | async-start | bytes 3145728 | tf_op jit(solution)/shard_map/all_to_all | solution.py:445
  79.1 30.4 %reduce-scatter.2.cloned.1.call-start = ((), (), s32[]{:S(2)}) async-start(), calls=%async_computation.6 | async-start | bytes 1310720 | tf_op jit(solution)/shard_map/reduce_scatter | solution.py:449
  104.1 1.2 copy-start
  108.5 5.9 %collective-permute-start.2 = (bf16[12,192,256]{2,1,0:T(8,128)(2,1)}, bf16[12,192,256]{2,1,0:T(8,128)(2,1)S(1)}, u32[]{:S(2)}, u32[]{:S(2)}) collective-permute-start(bf16[12,192,256]{2,1,0:T(8,128)(2,1)} %get-tuple-element.38), channel_id=1, source_target_pairs={{0,8},{8,0},{1,9},{9,1},{2,10},{10,2},{3,11},{11,3},{4,12},{12,4},... | collective-permute-start | bytes 3538952 | tf_op jit(solution)/shard_map/ppermute | solution.py:453
  109.5 13.5 %all-to-all-start.3 = ((bf16[16,64,128]{2,1,0:T(8,128)(2,1)}), bf16[16,64,128]{2,1,0:T(8,128)(2,1)S(1)}, u32[]{:S(2)}, u32[]{:S(2)}) async-start(bf16[16,64,128]{2,1,0:T(8,128)(2,1)} %bitcast.31), calls=%async_computation.4 | async-start | bytes 524288 | tf_op jit(solution)/shard_map/all_to_all | solution.py:450
  114.5 1.1 copy-start.3
  123.0 56.4 %all-to-all-start.4 = ((bf16[64,32,768]{2,1,0:T(8,128)(2,1)}), bf16[64,32,768]{2,1,0:T(8,128)(2,1)S(1)}, u32[]{:S(2)}, u32[]{:S(2)}) async-start(bf16[64,32,768]{2,1,0:T(8,128)(2,1)} %weight_grads.1), calls=%async_computation.5 | async-start | bytes 6291456 | tf_op jit(solution)/shard_map/all_to_all | solution.py:463
  136.5 6.0 %copy-start.8 = (bf16[768,256]{1,0:T(8,128)(2,1)S(1)}, bf16[768,256]{1,0:T(8,128)(2,1)}, u32[]{:S(2)}) copy-start(bf16[768,256]{1,0:T(8,128)(2,1)} %get-tuple-element.46.gated_ref) | copy-start | bytes 1179652
  180.6 1.3 collective-permute-start.4
Sparse Core Ops, SparseCore 0:
  22.9 25.8 all-gather.2
  82.3 21.1 reduce-scatter.1

commit v6 on v5

--- a/solution.py
+++ b/solution.py
@@ -30,6 +30,10 @@
 
 def dot_nt(a, b):
     return lax.dot_general(a, b, (((1,), (1,)), ((), ())), preferred_element_type=F32)
+
+
+def turn(shift):
+    return [(i, (i + shift) % 4) for i in range(4)]
 
 
 def params():
@@ -106,10 +110,11 @@
 
 
 def attention_kernel(
-    core_ref, x_ref, bias_ref, out_ref, keep_ref, give_ref,
+    place_ref, x_ref, mine_ref, other_ref, out_ref, keep_ref, give_ref,
     qa_s, ka_s, va_s, vt_s, kn_s, gn_s, gb_s, bias_s, *, blocks,
 ):
-    core = core_ref[0]
+    core = place_ref[0]
+    own_x = place_ref[1]
     sample = pl.program_id(0)
     half = sample // 2
     lane0 = pl.multiple_of((sample % 2) * TOK, TOK)
@@ -117,8 +122,12 @@
     @pl.when(sample == 0)
     def _():
         for t in range(8):
-            tile = jnp.concatenate([bias_ref[p, t] for p in range(8)], axis=0)
-            bias_s[t * TOK : (t + 1) * TOK] = tile.astype(F32) * LOG2E
+            pieces = []
+            for x in range(4):
+                mine = mine_ref[(own_x - x + 4) % 4, t]
+                other = other_ref[(own_x - x + 4) % 4, t]
+                pieces += [jnp.where(core == 0, mine, other), jnp.where(core == 0, other, mine)]
+            bias_s[t * TOK : (t + 1) * TOK] = jnp.concatenate(pieces, axis=0).astype(F32) * LOG2E
 
     whole = jnp.concatenate([x_ref[half * 8 + t, :, pl.ds(lane0, TOK)] for t in range(8)], axis=1)
     qt, kt, vt, gt = (whole[i * DH : (i + 1) * DH] for i in range(4))
@@ -177,8 +186,9 @@
                     low = jnp.concatenate([tile[:64, :64], tile[64:, :64]], axis=1)
                     high = jnp.concatenate([tile[:64, 64:], tile[64:, 64:]], axis=1)
                     where = (n % 2) * 8 + p.start // TOK + t
-                    keep_ref[n // 2, where] = jnp.where(core == 0, low, high)
-                    give_ref[n // 2, where] = jnp.where(core == 0, high, low)
+                    ahead = (n // 2 - own_x + 4) % 4
+                    keep_ref[ahead, where] = jnp.where(core == 0, low, high)
+                    give_ref[ahead, where] = jnp.where(core == 0, high, low)
 
     all_low = jnp.concatenate(dscores_low, axis=0)
     gscaled_t = jnp.concatenate(gscaled, axis=0).T.astype(BF)
@@ -192,9 +202,9 @@
             out_ref[half * 8 + t, i * DH : (i + 1) * DH, pl.ds(lane0, TOK)] = part[:, cols]
 
 
-def attention(core, x, bias, blocks=4):
+def attention(place, x, mine, other, blocks=4):
     def whole(shape):
-        return pl.BlockSpec(shape, lambda s, core: (0,) * len(shape))
+        return pl.BlockSpec(shape, lambda s, place: (0,) * len(shape))
 
     half_sum = (4, HEADS, 64, 128)
     return pl.pallas_call(
@@ -202,7 +212,7 @@
         grid_spec=pltpu.PrefetchScalarGridSpec(
             num_scalar_prefetch=1,
             grid=(4,),
-            in_specs=[whole(x.shape), whole(bias.shape)],
+            in_specs=[whole(x.shape), whole(mine.shape), whole(other.shape)],
             out_specs=[whole(x.shape), whole(half_sum), whole(half_sum)],
             scratch_shapes=[
                 pltpu.VMEM((KEYS, 128), BF),
@@ -225,7 +235,7 @@
             flops=4 * 6 * 2 * KEYS * KEYS * 256, bytes_accessed=8 * 2**20, transcendentals=4 * KEYS * KEYS
         ),
         name="attention",
-    )(core, x, bias)
+    )(place, x, mine, other)
 
 
 def gate_kernel(core_ref, back_ref, gate_ref, gg_ref, ggate_ref, gated_ref, send_ref):
@@ -416,10 +426,11 @@
     flat = sample_count * row_count
     core = lax.axis_index("core")
     core_arg = jnp.full((1,), core, jnp.int32)
-    place = lax.axis_index("x") * 2 + core
+    own_x = lax.axis_index("x")
+    place = jnp.stack([core, own_x]).astype(jnp.int32)
     zh = lax.axis_index("zh")
 
-    bias = lax.dynamic_slice(pair_bias, (zh * 8, place * 16, 0), (8, 16, KEYS))
+    bias = lax.dynamic_slice(pair_bias, (zh * 8, (own_x * 2 + core) * 16, 0), (8, 16, KEYS))
     bias = lax.all_to_all(bias, ("zl", "y"), 0, 0, tiled=True)
 
     rows_out = d_out.reshape(flat, channels)
@@ -427,7 +438,8 @@
         act.reshape(flat, channels), ln_gain, w_in, w_out, rows_out
     )
     bias, send = lax.optimization_barrier((bias, send))
-    bias = lax.all_gather(bias, ("x", "core"))
+    bias = jnp.stack([bias] + [lax.ppermute(bias, "x", turn(s)) for s in (1, 2, 3)])
+    bias_other = lax.ppermute(bias, "core", SWAP)
     received = lax.all_to_all(send, PLANE, 0, 0, tiled=True)
 
     dout_t = jnp.pad(rows_out.T.reshape(128, 6, flat), ((0, 0), (0, 2), (0, 0)))
@@ -441,12 +453,15 @@
     received, dout_mine, dout_other, scaled_other, w_rows = lax.optimization_barrier(
         (received, dout_mine, dout_other, scaled_other, w_rows)
     )
-    result, keep, give = attention(core_arg, received, bias)
+    result, keep, give = attention(place, received, bias, bias_other)
     back = lax.all_to_all(result, PLANE, 0, 0, tiled=True)
 
     got = lax.ppermute(give, "core", SWAP)
-    gb = (keep.astype(F32) + got.astype(F32)).astype(BF)
-    gb = lax.psum_scatter(gb, "x", scatter_dimension=0, tiled=False)
+    sums = [(keep[s].astype(F32) + got[s].astype(F32)).astype(BF) for s in range(4)]
+    gb = sums[0].astype(F32)
+    for s in (1, 2, 3):
+        gb = gb + lax.ppermute(sums[s], "x", turn(s)).astype(F32)
+    back, gb = lax.optimization_barrier((back, gb.astype(BF)))
     gb = lax.all_to_all(gb, PLANE, 0, 0, tiled=True)
 
     ggate, gated, half = gate_step(core_arg, back, gate, ggated)

time: 190 us -> 184 us (0.968)
  between operations: 14.2 us -> 0.8 us
  starting transfers between devices: 38.8 us -> 44.6 us
  other arithmetic: 4.77 us -> 7.11 us
    ppermute x0 -> x7, waiting for transfers between devices: none -> 22.5 us  [the longest x3 11.4 us: per_device(): lax.ppermute(bias, 'x', turn(s))]
    all_to_all x1, waiting for transfers between devices: 22.3 us -> 4.59 us  [per_device(): back = lax.all_to_all(result, PLANE, 0, 0, tiled=True)]
    ppermute x0 -> x7, starting transfers between devices: none -> 8.35 us  [the longest x3 3.6 us: per_device(): gb = gb + lax.ppermute(sums[s], 'x', turn(s)).astype(F32)]
    all_to_all x1, waiting for transfers between devices: 6.8 us -> 0.01 us  [per_device(): received = lax.all_to_all(send, PLANE, 0, 0, tiled=True)]
    ppermute x1, starting transfers between devices: 3.34 us -> 0.09 us  [per_device(): got = lax.ppermute(give, 'core', SWAP)]
    unnamed x22 -> x18, local copies, waits for them, and re-layouts: 13.1 us -> 12.4 us
  transfers between devices with their start and end apart: 12 -> 17, of which waited for: 4 -> 8; matrix products, arithmetic and copies ran while one was open for 11% -> 12% of each run, Pallas kernels for 13% -> 12%
where the time goes in v6:
time: 184 us; the launch traced here: 183 us
  waiting for transfers between devices  62.3 us (34%)
  Pallas kernels  45.4 us (25%)
  starting transfers between devices  44.6 us (24%)
  local copies, waits for them, and re-layouts  20 us (11%)
  other arithmetic  7.11 us (4%)
  matrix products  2.52 us (1%)
    all_to_all x1, waiting for transfers between devices, per_device(): chunks = lax.all_to_all(chunks, ('x', 'zh', 'zl', 'y'), 0, 0, tiled=True)  35 us
    pallas_call x1, Pallas kernels, attention(): pl.pallas_call(functools.partial(attention_kernel, blocks=blocks), grid_s...  20.8 us
    unnamed x18, local copies, waits for them, and re-layouts  12.4 us
    ppermute x3, waiting for transfers between devices, per_device(): lax.ppermute(bias, 'x', turn(s))  11.4 us
    ppermute x3, waiting for transfers between devices, per_device(): gb = gb + lax.ppermute(sums[s], 'x', turn(s)).astype(F32)  11.1 us
    all_to_all x1, starting transfers between devices, per_device(): chunks = lax.all_to_all(chunks, ('x', 'zh', 'zl', 'y'), 0, 0, tiled=True)  9.8 us
    pallas_call x1, Pallas kernels, front(): pl.pallas_call(front_kernel, grid=(4,), in_specs=[whole((flat, C)), whole...  7.83 us
    pallas_call x1, Pallas kernels, weight_grads(): pl.pallas_call(weight_kernel, grid_spec=pltpu.PrefetchScalarGridSpec(num_...  7.43 us
  transfers between devices with their start and end apart: 17, of which 8 were waited for; matrix products, arithmetic and copies ran while one was open for 12% of the time, Pallas kernels for 12%

profile of v6, /device:TPU:103, one launch (start us, length us, event | category | flops | bytes accessed | tf_op | source)
XLA Modules:
  0.0 182.7 jit_solution(14146469117006341983)
XLA Ops:
  0.6 1.7 constant_dynamic-slice_fusion
  2.3 5.4 %all-to-all-start = ((bf16[8,16,1024]{2,1,0:T(8,128)(2,1)}), bf16[8,16,1024]{2,1,0:T(8,128)(2,1)S(1)}, u32[]{:S(2)}, u32[]{:S(2)}) async-start(bf16[8,16,1024]{2,1,0:T(8,128)(2,1)} %constant_dynamic-slice_fusion), calls=%async_computation | async-start | bytes 524288 | tf_op jit(solution)/shard_map/all_to_all | solution.py:434
  7.7 7.8 %front.1 = (bf16[256,768]{1,0:T(8,128)(2,1)}, f32[256,768]{1,0:T(8,128)}, f32[256,1]{1,0:T(8,128)}, bf16[16,192,256]{2,1,0:T(8,128)(2,1)}, f32[768,256]{1,0:T(8,128)}, /*index=5*/bf16[768,256]{1,0:T(8,128)(2,1)}) custom-call(bf16[256,768]{1,0:T(8,128)(2,1)} %bitcast.45, f32[768]{0:T(1024)} %gain_ref.5, bf16[768,3072]{1,0:T(8,128)(2,1)} %w_ref.3, ...), custom_call_target="tpu_custom_call" | custom-call | flops 1509949440 | bytes 11534336 | tf_op jit(solution)/shard_map/front/pallas_call | solution.py:92
  15.6 6.5 %all-to-all-start.1 = ((bf16[16,192,256]{2,1,0:T(8,128)(2,1)}), bf16[16,192,256]{2,1,0:T(8,128)(2,1)S(1)}, u32[]{:S(2)}, u32[]{:S(2)}) async-start(bf16[16,192,256]{2,1,0:T(8,128)(2,1)} %get-tuple-element.32), calls=%async_computation.1 | async-start | bytes 3145728 | tf_op jit(solution)/shard_map/all_to_all | solution.py:443
  22.1 0.5 collective-permute-start.4
  22.6 0.8 collective-permute-start.3
  23.5 1.8 %collective-permute-start.2 = (bf16[8,16,1024]{2,1,0:T(8,128)(2,1)S(1)}, bf16[8,16,1024]{2,1,0:T(8,128)(2,1)S(1)}, u32[]{:S(2)}, u32[]{:S(2)}) collective-permute-start(bf16[8,16,1024]{2,1,0:T(8,128)(2,1)S(1)} %all-to-all-done), channel_id=1, source_target_pairs={{0,32},{32,64},{64,96},{96,0},{1,33},{33,65},{65,97},{97,1},{2,34}... | collective-permute-start | bytes 786440 | tf_op jit(solution)/shard_map/ppermute | solution.py:441
  25.3 5.6 %collective-permute-done.4 = bf16[8,16,1024]{2,1,0:T(8,128)(2,1)S(1)} collective-permute-done((bf16[8,16,1024]{2,1,0:T(8,128)(2,1)S(1)}, bf16[8,16,1024]{2,1,0:T(8,128)(2,1)S(1)}, u32[]{:S(2)}, u32[]{:S(2)}) %collective-permute-start.4) | collective-permute-done | bytes 262176 | tf_op jit(solution)/shard_map/ppermute | solution.py:441
  30.9 2.8 %collective-permute-done.3 = bf16[8,16,1024]{2,1,0:T(8,128)(2,1)S(1)} collective-permute-done((bf16[8,16,1024]{2,1,0:T(8,128)(2,1)S(1)}, bf16[8,16,1024]{2,1,0:T(8,128)(2,1)S(1)}, u32[]{:S(2)}, u32[]{:S(2)}) %collective-permute-start.3) | collective-permute-done | bytes 262176 | tf_op jit(solution)/shard_map/ppermute | solution.py:441
  33.7 3.0 %collective-permute-done.2 = bf16[8,16,1024]{2,1,0:T(8,128)(2,1)S(1)} collective-permute-done((bf16[8,16,1024]{2,1,0:T(8,128)(2,1)S(1)}, bf16[8,16,1024]{2,1,0:T(8,128)(2,1)S(1)}, u32[]{:S(2)}, u32[]{:S(2)}) %collective-permute-start.2) | collective-permute-done | bytes 262176 | tf_op jit(solution)/shard_map/ppermute | solution.py:441
  36.7 1.1 pad_maximum_fusion.mine_ref
  37.8 1.6 collective-permute-start.5
  39.4 0.2 copy.14
  39.5 0.1 reshape.54
  39.8 0.8 dynamic-slice_bitcast_fusion.1
  40.6 0.5 collective-permute-start
  41.1 6.6 %copy.15 = bf16[768,3072]{0,1:T(8,128)(2,1)} copy(bf16[768,3072]{1,0:T(8,128)(2,1)} %w_ref.3) | data formatting | bytes 9437184 | tf_op args[3]
  47.7 0.6 pad_add_fusion.place_ref
  48.3 3.3 %dynamic-slice_bitcast_fusion.wt_ref = bf16[8,192,768]{2,1,0:T(8,128)(2,1)} fusion(bf16[8,2,192,768]{3,2,1,0:T(8,128)(2,1)} %bitcast.39, s32[]{:T(128)S(6)} %select_n.17), kind=kLoop, calls=%fused_computation.1 | loop fusion | bytes 4718596 | tf_op jit(solution)/shard_map/jit(dynamic_index_in_dim)/squeeze | solution.py:452
  51.6 1.2 copy-done.1
  52.8 20.8 %attention.1 = (bf16[16,192,256]{2,1,0:T(8,128)(2,1)}, bf16[4,16,64,128]{3,2,1,0:T(8,128)(2,1)}, bf16[4,16,64,128]{3,2,1,0:T(8,128)(2,1)}) custom-call(s32[2]{0:T(128)} %pad_add_fusion.place_ref, bf16[16,192,256]{2,1,0:T(8,128)(2,1)} %copy-done.1, bf16[4,8,16,1024]{3,2,1,0:T(8,128)(2,1)} %pad_maximum_fusion.mine_ref, ...), custom_call_target="tpu_custom_call" | custom-call | flops 12884901888 | bytes 8388608 | tf_op jit(solution)/shard_map/attention/pallas_call | solution.py:210
  73.7 6.8 %all-to-all-start.2 = ((bf16[16,192,256]{2,1,0:T(8,128)(2,1)}), bf16[16,192,256]{2,1,0:T(8,128)(2,1)S(1)}, u32[]{:S(2)}, u32[]{:S(2)}) async-start(bf16[16,192,256]{2,1,0:T(8,128)(2,1)} %get-tuple-element.36), calls=%async_computation.2 | async-start | bytes 3145728 | tf_op jit(solution)/shard_map/all_to_all | solution.py:457
  80.5 1.4 fusion.4
  81.9 0.5 collective-permute-start.9
  82.4 3.1 %collective-permute-start.8 = (bf16[16,64,128]{2,1,0:T(8,128)(2,1)S(1)}, bf16[16,64,128]{2,1,0:T(8,128)(2,1)S(1)}, u32[]{:S(2)}, u32[]{:S(2)}) collective-permute-start(bf16[16,64,128]{2,1,0:T(8,128)(2,1)S(1)} %get-tuple-element.70), channel_id=1, source_target_pairs={{0,64},{32,96},{64,0},{96,32},{1,65},{33,97},{65,1},{97,33},{2,66}... | collective-permute-start | bytes 786440 | tf_op jit(solution)/shard_map/ppermute | solution.py:463
  85.5 4.6 %collective-permute-done.9 = bf16[16,64,128]{2,1,0:T(8,128)(2,1)S(1)} collective-permute-done((bf16[16,64,128]{2,1,0:T(8,128)(2,1)S(1)}, bf16[16,64,128]{2,1,0:T(8,128)(2,1)S(1)}, u32[]{:S(2)}, u32[]{:S(2)}) %collective-permute-start.9) | collective-permute-done | bytes 262176 | tf_op jit(solution)/shard_map/ppermute | solution.py:463
  90.1 6.5 %collective-permute-done.8 = bf16[16,64,128]{2,1,0:T(8,128)(2,1)S(1)} collective-permute-done((bf16[16,64,128]{2,1,0:T(8,128)(2,1)S(1)}, bf16[16,64,128]{2,1,0:T(8,128)(2,1)S(1)}, u32[]{:S(2)}, u32[]{:S(2)}) %collective-permute-start.8) | collective-permute-done | bytes 262176 | tf_op jit(solution)/shard_map/ppermute | solution.py:463
  96.6 1.9 %fusion.2 = bf16[16,64,128]{2,1,0:T(8,128)(2,1)} fusion(bf16[16,64,128]{2,1,0:T(8,128)(2,1)S(1)} %collective-permute-done.9, bf16[16,64,128]{2,1,0:T(8,128)(2,1)S(1)} %collective-permute-done.8, bf16[16,64,128]{2,1,0:T(8,128)(2,1)S(1)} %collective-permute-done.7, bf16[4,16,64,128]{3,2,1,0:T(8,128)(2,1)} %collective-permute-done.6, ...), kind=kLoop, calls=%fused_computation.8 | loop fusion | flops 1572864 | bytes 1572864 | tf_op jit(solution)/shard_map/convert_element_type | solution.py:464
  98.5 4.6 %all-to-all-done.2.back_ref = bf16[16,192,256]{2,1,0:T(8,128)(2,1)S(1)} async-done(((bf16[16,192,256]{2,1,0:T(8,128)(2,1)}), bf16[16,192,256]{2,1,0:T(8,128)(2,1)S(1)}, u32[]{:S(2)}, u32[]{:S(2)}) %all-to-all-start.2) | async-done | bytes 1572896 | tf_op jit(solution)/shard_map/all_to_all | solution.py:457
  103.1 1.2 copy-done
  104.2 3.3 %gate.1 = (bf16[4,192,256]{2,1,0:T(8,128)(2,1)}, bf16[768,256]{1,0:T(8,128)(2,1)}, bf16[12,192,256]{2,1,0:T(8,128)(2,1)}) custom-call(s32[1]{0:T(128)} %bitcast.core_ref, bf16[16,192,256]{2,1,0:T(8,128)(2,1)} %copy-done, f32[768,256]{1,0:T(8,128)} %get-tuple-element.40.gate_ref, bf16[768,256]{1,0:T(8,128)(2,1)} %get-tuple-element.41.gg_ref), custom_call_target="tpu_custom_call" | custom-call | flops 1179648 | bytes 6291456 | tf_op jit(solution)/shard_map/gate/pallas_call | solution.py:271
  107.5 1.8 collective-permute-start.10
  109.3 4.9 %all-to-all-start.3 = ((bf16[16,64,128]{2,1,0:T(8,128)(2,1)}), bf16[16,64,128]{2,1,0:T(8,128)(2,1)S(1)}, u32[]{:S(2)}, u32[]{:S(2)}) async-start(bf16[16,64,128]{2,1,0:T(8,128)(2,1)} %fusion.2), calls=%async_computation.3 | async-start | bytes 524288 | tf_op jit(solution)/shard_map/all_to_all | solution.py:465
  114.2 1.1 copy-done.3
  115.3 7.4 %weight_grads.1 = bf16[64,32,768]{2,1,0:T(8,128)(2,1)} custom-call(s32[1]{0:T(128)} %bitcast.core_ref, bf16[16,192,256]{2,1,0:T(8,128)(2,1)} %copy-done, bf16[4,192,256]{2,1,0:T(8,128)(2,1)} %get-tuple-element.51.ggate_ref, bf16[12,192,256]{2,1,0:T(8,128)(2,1)} %copy-done.3, bf16[768,256]{1,0:T(8,128)(2,1)} %get-tuple-element.50.gated_ref, ...), custom_call_target="tpu_custom_call" | custom-call | flops 1610612736 | bytes 8388608 | tf_op jit(solution)/shard_map/weight_grads/pallas_call | solution.py:402
  122.7 9.8 %all-to-all-start.4 = ((bf16[64,32,768]{2,1,0:T(8,128)(2,1)}), bf16[64,32,768]{2,1,0:T(8,128)(2,1)S(1)}, u32[]{:S(2)}, u32[]{:S(2)}) async-start(bf16[64,32,768]{2,1,0:T(8,128)(2,1)} %weight_grads.1), calls=%async_computation.4 | async-start | bytes 6291456 | tf_op jit(solution)/shard_map/all_to_all | solution.py:478
  132.5 0.2 fusion.8
  132.7 1.1 pad_maximum_fusion.1
  133.8 2.3 %copy.16 = f32[16,128,64]{1,2,0:T(8,128)} copy(f32[16,128,64]{2,1,0:T(8,128)} %pad_maximum_fusion.1) | data formatting | bytes 1048576
  136.1 6.0 %input_grad.1 = bf16[256,768]{1,0:T(8,128)(2,1)} custom-call(bf16[16,192,256]{2,1,0:T(8,128)(2,1)} %copy-done, bf16[4,192,256]{2,1,0:T(8,128)(2,1)} %get-tuple-element.51.ggate_ref, bf16[768,3072]{1,0:T(8,128)(2,1)} %w_ref.3, f32[256,768]{1,0:T(8,128)} %get-tuple-element.52.normed_ref, f32[256,1]{1,0:T(8,128)} %get-tuple-element.53.inv_ref, f32[768]{0:T(1024)} %gain_ref.5), custom_call_target="tpu_custom_call" | custom-call | flops 1207959552 | bytes 8388608 | tf_op jit(solution)/shard_map/input_grad/pallas_call | solution.py:324
  142.2 2.5 %convolution_convert_fusion = bf16[256,768]{1,0:T(8,128)(2,1)} fusion(bf16[768,256]{1,0:T(8,128)(2,1)S(1)} %copy-done.6, bf16[768,768]{1,0:T(8,128)(2,1)} %wout_ref.1), kind=kOutput, calls=%fused_computation.2 | convolution fusion | flops 302186496 | bytes 1966080 | tf_op jit(solution)/shard_map/cr,cd->rd/dot_general | solution.py:477
  144.7 35.0 %all-to-all-done.4 = bf16[64,32,768]{2,1,0:T(8,128)(2,1)S(1)} async-done(((bf16[64,32,768]{2,1,0:T(8,128)(2,1)}), bf16[64,32,768]{2,1,0:T(8,128)(2,1)S(1)}, u32[]{:S(2)}, u32[]{:S(2)}) %all-to-all-start.4) | async-done | bytes 3145760 | tf_op jit(solution)/shard_map/all_to_all | solution.py:478
  179.7 0.5 convert_reduce_fusion
  180.2 0.6 slice_bitcast_fusion
  180.8 0.5 collective-permute-start.11
  181.3 0.6 slice_bitcast_fusion.1
  181.9 0.2 collective-permute-done.11
  182.1 0.6 add.69
  (27 shorter events, 0.3 us)
Async XLA Ops:
  2.3 13.2 %all-to-all-start = ((bf16[8,16,1024]{2,1,0:T(8,128)(2,1)}), bf16[8,16,1024]{2,1,0:T(8,128)(2,1)S(1)}, u32[]{:S(2)}, u32[]{:S(2)}) async-start(bf16[8,16,1024]{2,1,0:T(8,128)(2,1)} %constant_dynamic-slice_fusion), calls=%async_computation | async-start | bytes 524288 | tf_op jit(solution)/shard_map/all_to_all | solution.py:434
  15.5 23.8 %copy-start.5 = (bf16[256,768]{1,0:T(8,128)(2,1)S(1)}, bf16[256,768]{1,0:T(8,128)(2,1)}, u32[]{:S(2)}) copy-start(bf16[256,768]{1,0:T(8,128)(2,1)} %get-tuple-element.33.sc_ref) | copy-start | bytes 1179652
  15.5 23.8 %copy-start.2 = (bf16[2,128,768]{2,1,0:T(8,128)(2,1)S(1)}, bf16[2,128,768]{2,1,0:T(8,128)(2,1)}, u32[]{:S(2)}) copy-start(bf16[2,128,768]{2,1,0:T(8,128)(2,1)} %param.11) | copy-start | bytes 1179652
  15.6 36.0 %all-to-all-start.1 = ((bf16[16,192,256]{2,1,0:T(8,128)(2,1)}), bf16[16,192,256]{2,1,0:T(8,128)(2,1)S(1)}, u32[]{:S(2)}, u32[]{:S(2)}) async-start(bf16[16,192,256]{2,1,0:T(8,128)(2,1)} %get-tuple-element.32), calls=%async_computation.1 | async-start | bytes 3145728 | tf_op jit(solution)/shard_map/all_to_all | solution.py:443
  22.1 8.8 %collective-permute-start.4 = (bf16[8,16,1024]{2,1,0:T(8,128)(2,1)S(1)}, bf16[8,16,1024]{2,1,0:T(8,128)(2,1)S(1)}, u32[]{:S(2)}, u32[]{:S(2)}) collective-permute-start(bf16[8,16,1024]{2,1,0:T(8,128)(2,1)S(1)} %all-to-all-done), channel_id=1, source_target_pairs={{0,96},{32,0},{64,32},{96,64},{1,97},{33,1},{65,33},{97,65},{2,98}... | collective-permute-start | bytes 786440 | tf_op jit(solution)/shard_map/ppermute | solution.py:441
  22.6 11.0 %collective-permute-start.3 = (bf16[8,16,1024]{2,1,0:T(8,128)(2,1)S(1)}, bf16[8,16,1024]{2,1,0:T(8,128)(2,1)S(1)}, u32[]{:S(2)}, u32[]{:S(2)}) collective-permute-start(bf16[8,16,1024]{2,1,0:T(8,128)(2,1)S(1)} %all-to-all-done), channel_id=1, source_target_pairs={{0,64},{32,96},{64,0},{96,32},{1,65},{33,97},{65,1},{97,33},{2,66}... | collective-permute-start | bytes 786440 | tf_op jit(solution)/shard_map/ppermute | solution.py:441
  23.5 13.2 %collective-permute-start.2 = (bf16[8,16,1024]{2,1,0:T(8,128)(2,1)S(1)}, bf16[8,16,1024]{2,1,0:T(8,128)(2,1)S(1)}, u32[]{:S(2)}, u32[]{:S(2)}) collective-permute-start(bf16[8,16,1024]{2,1,0:T(8,128)(2,1)S(1)} %all-to-all-done), channel_id=1, source_target_pairs={{0,32},{32,64},{64,96},{96,0},{1,33},{33,65},{65,97},{97,1},{2,34}... | collective-permute-start | bytes 786440 | tf_op jit(solution)/shard_map/ppermute | solution.py:441
  37.8 13.8 %collective-permute-start.5 = (bf16[4,8,16,1024]{3,2,1,0:T(8,128)(2,1)}, bf16[4,8,16,1024]{3,2,1,0:T(8,128)(2,1)}, u32[]{:S(2)}, u32[]{:S(2)}) collective-permute-start(bf16[4,8,16,1024]{3,2,1,0:T(8,128)(2,1)} %pad_maximum_fusion.mine_ref), channel_id=1, source_target_pairs={{0,8},{8,0},{1,9},{9,1},{2,10},{10,2},{3,11},{11,3},{4,12},{12,4},... | collective-permute-start | bytes 3145736 | tf_op jit(solution)/shard_map/ppermute | solution.py:442
  39.4 12.2 %collective-permute-start.1 = (bf16[256,768]{1,0:T(8,128)(2,1)S(1)}, bf16[256,768]{1,0:T(8,128)(2,1)}, u32[]{:S(2)}, u32[]{:S(2)}) collective-permute-start(bf16[256,768]{1,0:T(8,128)(2,1)S(1)} %copy-done.5), channel_id=1, source_target_pairs={{0,8},{8,0},{1,9},{9,1},{2,10},{10,2},{3,11},{11,3},{4,12},{12,4},... | collective-permute-start | bytes 1179656 | tf_op jit(solution)/shard_map/ppermute | solution.py:450
  40.6 11.0 %collective-permute-start = (bf16[8,64,256]{2,1,0:T(8,128)(2,1)S(1)}, bf16[8,64,256]{2,1,0:T(8,128)(2,1)S(1)}, u32[]{:S(2)}, u32[]{:S(2)}) collective-permute-start(bf16[8,64,256]{2,1,0:T(8,128)(2,1)S(1)} %get-tuple-element.71), channel_id=1, source_target_pairs={{0,8},{8,0},{1,9},{9,1},{2,10},{10,2},{3,11},{11,3},{4,12},{12,4},... | collective-permute-start | bytes 786440 | tf_op jit(solution)/shard_map/ppermute | solution.py:449
  51.6 22.0 %copy-start.7 = (bf16[8,64,256]{2,1,0:T(8,128)(2,1)}, bf16[8,64,256]{2,1,0:T(8,128)(2,1)S(1)}, u32[]{:S(2)}) copy-start(bf16[8,64,256]{2,1,0:T(8,128)(2,1)S(1)} %collective-permute-done.doo_ref) | copy-start | bytes 786436
  51.6 1.2 copy-start.1
  73.6 6.9 %copy-start.4 = (bf16[4,16,64,128]{3,2,1,0:T(8,128)(2,1)S(1)}, bf16[4,16,64,128]{3,2,1,0:T(8,128)(2,1)}, u32[]{:S(2)}) copy-start(bf16[4,16,64,128]{3,2,1,0:T(8,128)(2,1)} %get-tuple-element.37) | copy-start | bytes 3145732
  73.6 6.9 %collective-permute-start.6 = (bf16[4,16,64,128]{3,2,1,0:T(8,128)(2,1)}, bf16[4,16,64,128]{3,2,1,0:T(8,128)(2,1)}, u32[]{:S(2)}, u32[]{:S(2)}) collective-permute-start(bf16[4,16,64,128]{3,2,1,0:T(8,128)(2,1)} %get-tuple-element.38), channel_id=1, source_target_pairs={{0,8},{8,0},{1,9},{9,1},{2,10},{10,2},{3,11},{11,3},{4,12},{12,4},... | collective-permute-start | bytes 3145736 | tf_op jit(solution)/shard_map/ppermute | solution.py:459
  73.7 29.4 %all-to-all-start.2 = ((bf16[16,192,256]{2,1,0:T(8,128)(2,1)}), bf16[16,192,256]{2,1,0:T(8,128)(2,1)S(1)}, u32[]{:S(2)}, u32[]{:S(2)}) async-start(bf16[16,192,256]{2,1,0:T(8,128)(2,1)} %get-tuple-element.36), calls=%async_computation.2 | async-start | bytes 3145728 | tf_op jit(solution)/shard_map/all_to_all | solution.py:457
  81.9 8.2 %collective-permute-start.9 = (bf16[16,64,128]{2,1,0:T(8,128)(2,1)S(1)}, bf16[16,64,128]{2,1,0:T(8,128)(2,1)S(1)}, u32[]{:S(2)}, u32[]{:S(2)}) collective-permute-start(bf16[16,64,128]{2,1,0:T(8,128)(2,1)S(1)} %get-tuple-element.69), channel_id=1, source_target_pairs={{0,96},{32,0},{64,32},{96,64},{1,97},{33,1},{65,33},{97,65},{2,98}... | collective-permute-start | bytes 786440 | tf_op jit(solution)/shard_map/ppermute | solution.py:463
  82.4 14.1 %collective-permute-start.8 = (bf16[16,64,128]{2,1,0:T(8,128)(2,1)S(1)}, bf16[16,64,128]{2,1,0:T(8,128)(2,1)S(1)}, u32[]{:S(2)}, u32[]{:S(2)}) collective-permute-start(bf16[16,64,128]{2,1,0:T(8,128)(2,1)S(1)} %get-tuple-element.70), channel_id=1, source_target_pairs={{0,64},{32,96},{64,0},{96,32},{1,65},{33,97},{65,1},{97,33},{2,66}... | collective-permute-start | bytes 786440 | tf_op jit(solution)/shard_map/ppermute | solution.py:463
  85.5 11.1 %collective-permute-start.7 = (bf16[16,64,128]{2,1,0:T(8,128)(2,1)S(1)}, bf16[16,64,128]{2,1,0:T(8,128)(2,1)S(1)}, u32[]{:S(2)}, u32[]{:S(2)}) collective-permute-start(bf16[16,64,128]{2,1,0:T(8,128)(2,1)S(1)} %get-tuple-element.68), channel_id=1, source_target_pairs={{0,32},{32,64},{64,96},{96,0},{1,33},{33,65},{65,97},{97,1},{2,34}... | collective-permute-start | bytes 786440 | tf_op jit(solution)/shard_map/ppermute | solution.py:463
  103.1 1.2 copy-start
  107.5 6.7 %collective-permute-start.10 = (bf16[12,192,256]{2,1,0:T(8,128)(2,1)}, bf16[12,192,256]{2,1,0:T(8,128)(2,1)S(1)}, u32[]{:S(2)}, u32[]{:S(2)}) collective-permute-start(bf16[12,192,256]{2,1,0:T(8,128)(2,1)} %get-tuple-element.43), channel_id=1, source_target_pairs={{0,8},{8,0},{1,9},{9,1},{2,10},{10,2},{3,11},{11,3},{4,12},{12,4},... | collective-permute-start | bytes 3538952 | tf_op jit(solution)/shard_map/ppermute | solution.py:468
  109.3 13.4 %all-to-all-start.3 = ((bf16[16,64,128]{2,1,0:T(8,128)(2,1)}), bf16[16,64,128]{2,1,0:T(8,128)(2,1)S(1)}, u32[]{:S(2)}, u32[]{:S(2)}) async-start(bf16[16,64,128]{2,1,0:T(8,128)(2,1)} %fusion.2), calls=%async_computation.3 | async-start | bytes 524288 | tf_op jit(solution)/shard_map/all_to_all | solution.py:465
  114.2 1.1 copy-start.3
  122.7 57.0 %all-to-all-start.4 = ((bf16[64,32,768]{2,1,0:T(8,128)(2,1)}), bf16[64,32,768]{2,1,0:T(8,128)(2,1)S(1)}, u32[]{:S(2)}, u32[]{:S(2)}) async-start(bf16[64,32,768]{2,1,0:T(8,128)(2,1)} %weight_grads.1), calls=%async_computation.4 | async-start | bytes 6291456 | tf_op jit(solution)/shard_map/all_to_all | solution.py:478
  136.1 6.0 %copy-start.6 = (bf16[768,256]{1,0:T(8,128)(2,1)S(1)}, bf16[768,256]{1,0:T(8,128)(2,1)}, u32[]{:S(2)}) copy-start(bf16[768,256]{1,0:T(8,128)(2,1)} %get-tuple-element.50.gated_ref) | copy-start | bytes 1179652
  180.8 1.3 collective-permute-start.11

commit v7 on v6

--- a/solution.py
+++ b/solution.py
@@ -238,19 +238,48 @@
     )(place, x, mine, other)
 
 
+def turn_kernel(core_ref, w_ref, out_ref, turned_s):
+    turned_s[...] = w_ref[...].T
+    out_ref[0] = turned_s[pl.ds(pl.multiple_of(core_ref[0] * 4 * DH, 4 * DH), 4 * DH), :]
+
+
+def turn_half(core, w_in):
+    return pl.pallas_call(
+        turn_kernel,
+        grid_spec=pltpu.PrefetchScalarGridSpec(
+            num_scalar_prefetch=1,
+            grid=(8,),
+            in_specs=[pl.BlockSpec((C, 8 * DH), lambda n, core: (0, n))],
+            out_specs=pl.BlockSpec((1, 4 * DH, C), lambda n, core: (n, 0, 0)),
+            scratch_shapes=[pltpu.VMEM((8 * DH, C), BF)],
+        ),
+        out_shape=jax.ShapeDtypeStruct((8, 4 * DH, C), BF),
+        compiler_params=params(),
+        cost_estimate=pl.CostEstimate(flops=8 * C * C, bytes_accessed=7 * 2**20, transcendentals=0),
+        name="turn_half",
+    )(core, w_in)
+
+
 def gate_kernel(core_ref, back_ref, gate_ref, gg_ref, ggate_ref, gated_ref, send_ref):
     other = 1 - core_ref[0]
+    group = pl.program_id(0)
     flat = gate_ref.shape[1]
-    att = back_ref[:, :DH, :].astype(F32).reshape(C, flat)
+    att = back_ref[:, :DH, :].astype(F32).reshape(4 * DH, flat)
     gate = gate_ref[...]
     opened = att * gate
     gated = opened.astype(BF)
+    ggate = (gg_ref[...].astype(F32) * opened * (1.0 - gate)).astype(BF)
     gated_ref[...] = gated
-    for q in range(4):
-        send_ref[8 + q] = gated[q * 192 : (q + 1) * 192]
-    ggate_ref[...] = (gg_ref[...].astype(F32) * opened * (1.0 - gate)).astype(BF).reshape(4, 4 * DH, flat)
-    for n in range(8):
-        send_ref[n] = head_rows(back_ref, ggate_ref, n, other)
+    ggate_ref[0] = ggate
+    send_ref[8 + group] = gated
+
+    @pl.when(group % 2 == other)
+    def _():
+        for kind in range(3):
+            send_ref[2 * kind + group // 2] = back_ref[:, (kind + 1) * DH : (kind + 2) * DH, :].reshape(
+                4 * DH, flat
+            )
+        send_ref[6 + group // 2] = ggate
 
 
 def head_rows(back_ref, ggate_ref, n, core):
@@ -263,18 +292,20 @@
 
 
 def gate_step(core, back, gate, ggated):
-    def whole(shape):
-        return pl.BlockSpec(shape, lambda t, core: (0,) * len(shape))
-
     flat = gate.shape[1]
+    rows = pl.BlockSpec((4 * DH, flat), lambda t, core: (t, 0))
     shapes = [(4, 4 * DH, flat), (C, flat), (12, 4 * DH, flat)]
     return pl.pallas_call(
         gate_kernel,
         grid_spec=pltpu.PrefetchScalarGridSpec(
             num_scalar_prefetch=1,
-            grid=(1,),
-            in_specs=[whole(back.shape), whole(gate.shape), whole(ggated.shape)],
-            out_specs=[whole(s) for s in shapes],
+            grid=(4,),
+            in_specs=[pl.BlockSpec((4, 4 * DH, flat), lambda t, core: (t, 0, 0)), rows, rows],
+            out_specs=[
+                pl.BlockSpec((1, 4 * DH, flat), lambda t, core: (t, 0, 0)),
+                rows,
+                pl.BlockSpec(shapes[2], lambda t, core: (0, 0, 0)),
+            ],
         ),
         out_shape=[jax.ShapeDtypeStruct(s, BF) for s in shapes],
         compiler_params=params(),
@@ -377,7 +408,7 @@
                 axis=0,
             )
             wout = dot(tails, gated_s[...])
-            weights = wt_ref[2 * kind : 2 * kind + 2].reshape(8 * DH, C).astype(F32)
+            weights = wt_ref[...].reshape(8 * DH, C).astype(F32)
             sum_s[...] += jnp.sum((win * weights).reshape(DH, 8, C), axis=0)
             for k in range(16):
                 out_ref[kind * 16 + k] = jnp.concatenate(
@@ -404,7 +435,8 @@
         grid_spec=pltpu.PrefetchScalarGridSpec(
             num_scalar_prefetch=1,
             grid=(4,),
-            in_specs=[whole(o.shape) for o in operands],
+            in_specs=[whole(o.shape) for o in operands[:8]]
+            + [pl.BlockSpec((2, 4 * DH, C), lambda t, core: (t, 0, 0)), whole(operands[9].shape)],
             out_specs=whole((64, 32, C)),
             scratch_shapes=[
                 pltpu.VMEM((2 * flat, C), BF),
@@ -438,20 +470,22 @@
         act.reshape(flat, channels), ln_gain, w_in, w_out, rows_out
     )
     bias, send = lax.optimization_barrier((bias, send))
-    bias = jnp.stack([bias] + [lax.ppermute(bias, "x", turn(s)) for s in (1, 2, 3)])
-    bias_other = lax.ppermute(bias, "core", SWAP)
+    pieces = [bias] + [lax.ppermute(bias, "x", turn(s)) for s in (1, 2, 3)]
     received = lax.all_to_all(send, PLANE, 0, 0, tiled=True)
 
     dout_t = jnp.pad(rows_out.T.reshape(128, 6, flat), ((0, 0), (0, 2), (0, 0)))
     dout_t = dout_t.reshape(8, 2, 64, flat)
     dout_mine = lax.dynamic_index_in_dim(dout_t, core, 1, keepdims=False)
     dout_send = lax.dynamic_index_in_dim(dout_t, 1 - core, 1, keepdims=False)
+    scaled_other = lax.ppermute(scaled, "core", SWAP)
+
+    w_rows = turn_half(core_arg, w_in)
+    pieces, dout_mine, dout_send, w_rows = lax.optimization_barrier((pieces, dout_mine, dout_send, w_rows))
+    bias = jnp.stack(pieces)
+    bias_other = lax.ppermute(bias, "core", SWAP)
     dout_other = lax.ppermute(dout_send, "core", SWAP)
-    scaled_other = lax.ppermute(scaled, "core", SWAP)
-
-    w_rows = lax.dynamic_index_in_dim(w_in.T.reshape(8, 2, 4 * DH, C), core, 1, keepdims=False)
-    received, dout_mine, dout_other, scaled_other, w_rows = lax.optimization_barrier(
-        (received, dout_mine, dout_other, scaled_other, w_rows)
+    received, dout_other, scaled_other, bias_other = lax.optimization_barrier(
+        (received, dout_other, scaled_other, bias_other)
     )
     result, keep, give = attention(place, received, bias, bias_other)
     back = lax.all_to_all(result, PLANE, 0, 0, tiled=True)

time: 184 us -> 178 us (0.967)
  local copies, waits for them, and re-layouts: 20 us -> 10.7 us
  Pallas kernels: 45.4 us -> 53.1 us
  waiting for transfers between devices: 62.3 us -> 58.1 us
    ppermute x3, waiting for transfers between devices: 11.4 us -> 3.2 us  [per_device(): pieces = [bias] + [lax.ppermute(bias, 'x', turn(s)) for s in (1, 2, 3)]]
    pallas_call x0 -> x1, Pallas kernels: none -> 7.05 us  [turn_half(): pl.pallas_call(turn_kernel, grid_spec=pltpu.PrefetchScalarGridSpec(num_sc...]
    unnamed x18 -> x21, local copies, waits for them, and re-layouts: 12.4 us -> 6.45 us
    squeeze x1 -> x0, local copies, waits for them, and re-layouts: 3.27 us -> none  [per_device(): lax.dynamic_index_in_dim(w_in.T.reshape(8, 2, 4 * DH, C), core, 1, keepdi...]
  transfers between devices with their start and end apart: 17 -> 17, of which waited for: 8 -> 10; matrix products, arithmetic and copies ran while one was open for 12% -> 7% of each run, Pallas kernels for 12% -> 16%
where the time goes in v7:
time: 178 us; the launch traced here: 177 us
  waiting for transfers between devices  58.1 us (33%)
  Pallas kernels  53.1 us (30%)
  starting transfers between devices  44.8 us (25%)
  local copies, waits for them, and re-layouts  10.7 us (6%)
  other arithmetic  7.05 us (4%)
  matrix products  2.52 us (1%)
    all_to_all x1, waiting for transfers between devices, per_device(): chunks = lax.all_to_all(chunks, ('x', 'zh', 'zl', 'y'), 0, 0, tiled=True)  35 us
    pallas_call x1, Pallas kernels, attention(): pl.pallas_call(functools.partial(attention_kernel, blocks=blocks), grid_s...  20.8 us
    ppermute x3, waiting for transfers between devices, per_device(): gb = gb + lax.ppermute(sums[s], 'x', turn(s)).astype(F32)  11.3 us
    all_to_all x1, starting transfers between devices, per_device(): chunks = lax.all_to_all(chunks, ('x', 'zh', 'zl', 'y'), 0, 0, tiled=True)  10.2 us
    pallas_call x1, Pallas kernels, front(): pl.pallas_call(front_kernel, grid=(4,), in_specs=[whole((flat, C)), whole...  7.83 us
    pallas_call x1, Pallas kernels, weight_grads(): pl.pallas_call(weight_kernel, grid_spec=pltpu.PrefetchScalarGridSpec(num_...  7.25 us
    pallas_call x1, Pallas kernels, turn_half(): pl.pallas_call(turn_kernel, grid_spec=pltpu.PrefetchScalarGridSpec(num_sc...  7.05 us
    all_to_all x1, starting transfers between devices, per_device(): received = lax.all_to_all(send, PLANE, 0, 0, tiled=True)  6.53 us
  transfers between devices with their start and end apart: 17, of which 10 were waited for; matrix products, arithmetic and copies ran while one was open for 7% of the time, Pallas kernels for 16%

profile of v7, /device:TPU:103, one launch (start us, length us, event | category | flops | bytes accessed | tf_op | source)
XLA Modules:
  0.0 177.1 jit_solution(12248040541805086321)
XLA Ops:
  0.6 1.7 constant_dynamic-slice_fusion
  2.3 5.4 %all-to-all-start = ((bf16[8,16,1024]{2,1,0:T(8,128)(2,1)}), bf16[8,16,1024]{2,1,0:T(8,128)(2,1)S(1)}, u32[]{:S(2)}, u32[]{:S(2)}) async-start(bf16[8,16,1024]{2,1,0:T(8,128)(2,1)} %constant_dynamic-slice_fusion), calls=%async_computation | async-start | bytes 524288 | tf_op jit(solution)/shard_map/all_to_all | solution.py:466
  7.7 7.8 %front.1 = (bf16[256,768]{1,0:T(8,128)(2,1)}, f32[256,768]{1,0:T(8,128)}, f32[256,1]{1,0:T(8,128)}, bf16[16,192,256]{2,1,0:T(8,128)(2,1)}, f32[768,256]{1,0:T(8,128)}, /*index=5*/bf16[768,256]{1,0:T(8,128)(2,1)}) custom-call(bf16[256,768]{1,0:T(8,128)(2,1)} %bitcast.39, f32[768]{0:T(1024)} %gain_ref.5, bf16[768,3072]{1,0:T(8,128)(2,1)} %w_ref.5, ...), custom_call_target="tpu_custom_call" | custom-call | flops 1509949440 | bytes 11534336 | tf_op jit(solution)/shard_map/front/pallas_call | solution.py:92
  15.5 6.5 %all-to-all-start.1 = ((bf16[16,192,256]{2,1,0:T(8,128)(2,1)}), bf16[16,192,256]{2,1,0:T(8,128)(2,1)S(1)}, u32[]{:S(2)}, u32[]{:S(2)}) async-start(bf16[16,192,256]{2,1,0:T(8,128)(2,1)} %get-tuple-element.38), calls=%async_computation.1 | async-start | bytes 3145728 | tf_op jit(solution)/shard_map/all_to_all | solution.py:474
  22.1 0.5 collective-permute-start.2
  22.6 0.8 collective-permute-start.1
  23.4 1.8 %collective-permute-start = (bf16[8,16,1024]{2,1,0:T(8,128)(2,1)S(1)}, bf16[8,16,1024]{2,1,0:T(8,128)(2,1)}, u32[]{:S(2)}, u32[]{:S(2)}) collective-permute-start(bf16[8,16,1024]{2,1,0:T(8,128)(2,1)S(1)} %all-to-all-done), channel_id=1, source_target_pairs={{0,32},{32,64},{64,96},{96,0},{1,33},{33,65},{65,97},{97,1},{2,34}... | collective-permute-start | bytes 786440 | tf_op jit(solution)/shard_map/ppermute | solution.py:473
  25.3 0.2 copy.13
  25.7 7.0 %turn_half.1.wt_ref = bf16[8,192,768]{2,1,0:T(8,128)(2,1)} custom-call(s32[1]{0:T(128)} %bitcast.core_ref, bf16[768,3072]{1,0:T(8,128)(2,1)} %w_ref.5), custom_call_target="tpu_custom_call" | custom-call | flops 4718592 | bytes 7340032 | tf_op jit(solution)/shard_map/turn_half/pallas_call | solution.py:247
  32.7 0.7 dynamic-slice_bitcast_fusion
  33.6 3.0 %collective-permute-done = bf16[8,16,1024]{2,1,0:T(8,128)(2,1)} collective-permute-done((bf16[8,16,1024]{2,1,0:T(8,128)(2,1)S(1)}, bf16[8,16,1024]{2,1,0:T(8,128)(2,1)}, u32[]{:S(2)}, u32[]{:S(2)}) %collective-permute-start) | collective-permute-done | bytes 262176 | tf_op jit(solution)/shard_map/ppermute | solution.py:473
  36.7 1.1 pad_maximum_fusion.mine_ref
  37.8 1.7 collective-permute-start.5
  39.6 0.4 collective-permute-start.3
  40.0 0.6 pad_add_fusion.place_ref
  40.6 1.8 collective-permute-done.4.sco_ref
  42.4 0.4 collective-permute-done.3.doo_ref
  42.7 0.7 copy-done.9
  43.5 1.1 copy-done.1
  44.6 20.8 %attention.1 = (bf16[16,192,256]{2,1,0:T(8,128)(2,1)}, bf16[4,16,64,128]{3,2,1,0:T(8,128)(2,1)}, bf16[4,16,64,128]{3,2,1,0:T(8,128)(2,1)}) custom-call(s32[2]{0:T(128)} %pad_add_fusion.place_ref, bf16[16,192,256]{2,1,0:T(8,128)(2,1)} %copy-done.1, bf16[4,8,16,1024]{3,2,1,0:T(8,128)(2,1)} %copy-done.4, bf16[4,8,16,1024]{3,2,1,0:T(8,128)(2,1)} %collective-permute-done.5.other_ref), custom_call_target="tpu_custom_call" | custom-call | flops 12884901888 | bytes 8388608 | tf_op jit(solution)/shard_map/attention/pallas_call | solution.py:210
  65.4 1.7 collective-permute-start.6
  67.1 5.6 %all-to-all-start.2 = ((bf16[16,192,256]{2,1,0:T(8,128)(2,1)}), bf16[16,192,256]{2,1,0:T(8,128)(2,1)S(1)}, u32[]{:S(2)}, u32[]{:S(2)}) async-start(bf16[16,192,256]{2,1,0:T(8,128)(2,1)} %get-tuple-element.48), calls=%async_computation.2 | async-start | bytes 3145728 | tf_op jit(solution)/shard_map/all_to_all | solution.py:491
  72.7 1.4 fusion.4
  74.1 2.3 %collective-permute-start.7 = (bf16[16,64,128]{2,1,0:T(8,128)(2,1)S(1)}, bf16[16,64,128]{2,1,0:T(8,128)(2,1)S(1)}, u32[]{:S(2)}, u32[]{:S(2)}) collective-permute-start(bf16[16,64,128]{2,1,0:T(8,128)(2,1)S(1)} %get-tuple-element.80), channel_id=1, source_target_pairs={{0,32},{32,64},{64,96},{96,0},{1,33},{33,65},{65,97},{97,1},{2,34}... | collective-permute-start | bytes 786440 | tf_op jit(solution)/shard_map/ppermute | solution.py:497
  76.4 1.3 collective-permute-start.8
  77.7 4.0 %collective-permute-done.7 = bf16[16,64,128]{2,1,0:T(8,128)(2,1)S(1)} collective-permute-done((bf16[16,64,128]{2,1,0:T(8,128)(2,1)S(1)}, bf16[16,64,128]{2,1,0:T(8,128)(2,1)S(1)}, u32[]{:S(2)}, u32[]{:S(2)}) %collective-permute-start.7) | collective-permute-done | bytes 262176 | tf_op jit(solution)/shard_map/ppermute | solution.py:497
  81.7 3.8 %collective-permute-done.9 = bf16[16,64,128]{2,1,0:T(8,128)(2,1)S(1)} collective-permute-done((bf16[16,64,128]{2,1,0:T(8,128)(2,1)S(1)}, bf16[16,64,128]{2,1,0:T(8,128)(2,1)S(1)}, u32[]{:S(2)}, u32[]{:S(2)}) %collective-permute-start.9) | collective-permute-done | bytes 262176 | tf_op jit(solution)/shard_map/ppermute | solution.py:497
  85.5 3.5 %collective-permute-done.8 = bf16[16,64,128]{2,1,0:T(8,128)(2,1)S(1)} collective-permute-done((bf16[16,64,128]{2,1,0:T(8,128)(2,1)S(1)}, bf16[16,64,128]{2,1,0:T(8,128)(2,1)S(1)}, u32[]{:S(2)}, u32[]{:S(2)}) %collective-permute-start.8) | collective-permute-done | bytes 262176 | tf_op jit(solution)/shard_map/ppermute | solution.py:497
  89.0 1.9 %fusion.2 = bf16[16,64,128]{2,1,0:T(8,128)(2,1)} fusion(bf16[16,64,128]{2,1,0:T(8,128)(2,1)S(1)} %collective-permute-done.9, bf16[16,64,128]{2,1,0:T(8,128)(2,1)S(1)} %collective-permute-done.8, bf16[16,64,128]{2,1,0:T(8,128)(2,1)S(1)} %collective-permute-done.7, bf16[4,16,64,128]{3,2,1,0:T(8,128)(2,1)} %collective-permute-done.6, ...), kind=kLoop, calls=%fused_computation.7 | loop fusion | flops 1572864 | bytes 1572864 | tf_op jit(solution)/shard_map/convert_element_type | solution.py:498
  90.8 6.3 %all-to-all-done.2.back_ref = bf16[16,192,256]{2,1,0:T(8,128)(2,1)S(1)} async-done(((bf16[16,192,256]{2,1,0:T(8,128)(2,1)}), bf16[16,192,256]{2,1,0:T(8,128)(2,1)S(1)}, u32[]{:S(2)}, u32[]{:S(2)}) %all-to-all-start.2) | async-done | bytes 1572896 | tf_op jit(solution)/shard_map/all_to_all | solution.py:491
  97.1 1.2 copy-done
  98.3 4.2 %gate.1 = (bf16[4,192,256]{2,1,0:T(8,128)(2,1)}, bf16[768,256]{1,0:T(8,128)(2,1)}, bf16[12,192,256]{2,1,0:T(8,128)(2,1)}) custom-call(s32[1]{0:T(128)} %bitcast.core_ref, bf16[16,192,256]{2,1,0:T(8,128)(2,1)} %copy-done, f32[768,256]{1,0:T(8,128)} %get-tuple-element.52.gate_ref, bf16[768,256]{1,0:T(8,128)(2,1)} %get-tuple-element.53.gg_ref), custom_call_target="tpu_custom_call" | custom-call | flops 1179648 | bytes 6291456 | tf_op jit(solution)/shard_map/gate/pallas_call | solution.py:298
  102.4 1.2 collective-permute-start.10
  103.7 4.7 %all-to-all-start.3 = ((bf16[16,64,128]{2,1,0:T(8,128)(2,1)}), bf16[16,64,128]{2,1,0:T(8,128)(2,1)S(1)}, u32[]{:S(2)}, u32[]{:S(2)}) async-start(bf16[16,64,128]{2,1,0:T(8,128)(2,1)} %fusion.2), calls=%async_computation.3 | async-start | bytes 524288 | tf_op jit(solution)/shard_map/all_to_all | solution.py:499
  108.4 1.1 copy-done.3
  109.5 7.3 %weight_grads.1 = bf16[64,32,768]{2,1,0:T(8,128)(2,1)} custom-call(s32[1]{0:T(128)} %bitcast.core_ref, bf16[16,192,256]{2,1,0:T(8,128)(2,1)} %copy-done, bf16[4,192,256]{2,1,0:T(8,128)(2,1)} %get-tuple-element.63.ggate_ref, bf16[12,192,256]{2,1,0:T(8,128)(2,1)} %copy-done.3, bf16[768,256]{1,0:T(8,128)(2,1)} %get-tuple-element.62.gated_ref, ...), custom_call_target="tpu_custom_call" | custom-call | flops 1610612736 | bytes 8388608 | tf_op jit(solution)/shard_map/weight_grads/pallas_call | solution.py:433
  116.7 10.2 %all-to-all-start.4 = ((bf16[64,32,768]{2,1,0:T(8,128)(2,1)}), bf16[64,32,768]{2,1,0:T(8,128)(2,1)S(1)}, u32[]{:S(2)}, u32[]{:S(2)}) async-start(bf16[64,32,768]{2,1,0:T(8,128)(2,1)} %weight_grads.1), calls=%async_computation.4 | async-start | bytes 6291456 | tf_op jit(solution)/shard_map/all_to_all | solution.py:512
  127.1 1.1 pad_maximum_fusion.1
  128.1 2.3 %copy.14 = f32[16,128,64]{1,2,0:T(8,128)} copy(f32[16,128,64]{2,1,0:T(8,128)} %pad_maximum_fusion.1) | data formatting | bytes 1048576
  130.5 6.0 %input_grad.1 = bf16[256,768]{1,0:T(8,128)(2,1)} custom-call(bf16[16,192,256]{2,1,0:T(8,128)(2,1)} %copy-done, bf16[4,192,256]{2,1,0:T(8,128)(2,1)} %get-tuple-element.63.ggate_ref, bf16[768,3072]{1,0:T(8,128)(2,1)} %w_ref.5, f32[256,768]{1,0:T(8,128)} %get-tuple-element.64.normed_ref, f32[256,1]{1,0:T(8,128)} %get-tuple-element.65.inv_ref, f32[768]{0:T(1024)} %gain_ref.5), custom_call_target="tpu_custom_call" | custom-call | flops 1207959552 | bytes 8388608 | tf_op jit(solution)/shard_map/input_grad/pallas_call | solution.py:355
  136.5 2.5 %convolution_convert_fusion = bf16[256,768]{1,0:T(8,128)(2,1)} fusion(bf16[768,256]{1,0:T(8,128)(2,1)S(1)} %copy-done.8, bf16[768,768]{1,0:T(8,128)(2,1)} %wout_ref.1), kind=kOutput, calls=%fused_computation.1 | convolution fusion | flops 302186496 | bytes 1966080 | tf_op jit(solution)/shard_map/cr,cd->rd/dot_general | solution.py:511
  139.0 35.0 %all-to-all-done.4 = bf16[64,32,768]{2,1,0:T(8,128)(2,1)S(1)} async-done(((bf16[64,32,768]{2,1,0:T(8,128)(2,1)}), bf16[64,32,768]{2,1,0:T(8,128)(2,1)S(1)}, u32[]{:S(2)}, u32[]{:S(2)}) %all-to-all-start.4) | async-done | bytes 3145760 | tf_op jit(solution)/shard_map/all_to_all | solution.py:512
  174.0 0.5 convert_reduce_fusion
  174.5 0.6 slice_bitcast_fusion
  175.1 0.5 collective-permute-start.11
  175.6 0.6 slice_bitcast_fusion.1
  176.2 0.2 collective-permute-done.11
  176.5 0.6 add.67
  (30 shorter events, 0.7 us)
Async XLA Ops:
  2.3 13.2 %all-to-all-start = ((bf16[8,16,1024]{2,1,0:T(8,128)(2,1)}), bf16[8,16,1024]{2,1,0:T(8,128)(2,1)S(1)}, u32[]{:S(2)}, u32[]{:S(2)}) async-start(bf16[8,16,1024]{2,1,0:T(8,128)(2,1)} %constant_dynamic-slice_fusion), calls=%async_computation | async-start | bytes 524288 | tf_op jit(solution)/shard_map/all_to_all | solution.py:466
  15.5 9.7 %copy-start.2 = (bf16[2,128,768]{2,1,0:T(8,128)(2,1)S(1)}, bf16[2,128,768]{2,1,0:T(8,128)(2,1)}, u32[]{:S(2)}) copy-start(bf16[2,128,768]{2,1,0:T(8,128)(2,1)} %param.11) | copy-start | bytes 1179652
  15.5 27.9 %all-to-all-start.1 = ((bf16[16,192,256]{2,1,0:T(8,128)(2,1)}), bf16[16,192,256]{2,1,0:T(8,128)(2,1)S(1)}, u32[]{:S(2)}, u32[]{:S(2)}) async-start(bf16[16,192,256]{2,1,0:T(8,128)(2,1)} %get-tuple-element.38), calls=%async_computation.1 | async-start | bytes 3145728 | tf_op jit(solution)/shard_map/all_to_all | solution.py:474
  22.1 11.4 %collective-permute-start.2 = (bf16[8,16,1024]{2,1,0:T(8,128)(2,1)S(1)}, bf16[8,16,1024]{2,1,0:T(8,128)(2,1)S(1)}, u32[]{:S(2)}, u32[]{:S(2)}) collective-permute-start(bf16[8,16,1024]{2,1,0:T(8,128)(2,1)S(1)} %all-to-all-done), channel_id=1, source_target_pairs={{0,96},{32,0},{64,32},{96,64},{1,97},{33,1},{65,33},{97,65},{2,98}... | collective-permute-start | bytes 786440 | tf_op jit(solution)/shard_map/ppermute | solution.py:473
  22.6 11.0 %collective-permute-start.1 = (bf16[8,16,1024]{2,1,0:T(8,128)(2,1)S(1)}, bf16[8,16,1024]{2,1,0:T(8,128)(2,1)S(1)}, u32[]{:S(2)}, u32[]{:S(2)}) collective-permute-start(bf16[8,16,1024]{2,1,0:T(8,128)(2,1)S(1)} %all-to-all-done), channel_id=1, source_target_pairs={{0,64},{32,96},{64,0},{96,32},{1,65},{33,97},{65,1},{97,33},{2,66}... | collective-permute-start | bytes 786440 | tf_op jit(solution)/shard_map/ppermute | solution.py:473
  23.4 13.2 %collective-permute-start = (bf16[8,16,1024]{2,1,0:T(8,128)(2,1)S(1)}, bf16[8,16,1024]{2,1,0:T(8,128)(2,1)}, u32[]{:S(2)}, u32[]{:S(2)}) collective-permute-start(bf16[8,16,1024]{2,1,0:T(8,128)(2,1)S(1)} %all-to-all-done), channel_id=1, source_target_pairs={{0,32},{32,64},{64,96},{96,0},{1,33},{33,65},{65,97},{97,1},{2,34}... | collective-permute-start | bytes 786440 | tf_op jit(solution)/shard_map/ppermute | solution.py:473
  32.7 6.8 %copy-start.6 = (bf16[256,768]{1,0:T(8,128)(2,1)S(1)}, bf16[256,768]{1,0:T(8,128)(2,1)}, u32[]{:S(2)}) copy-start(bf16[256,768]{1,0:T(8,128)(2,1)} %get-tuple-element.41.sc_ref) | copy-start | bytes 1179652
  37.8 5.7 %copy-start.4 = (bf16[4,8,16,1024]{3,2,1,0:T(8,128)(2,1)}, bf16[4,8,16,1024]{3,2,1,0:T(8,128)(2,1)S(1)}, u32[]{:S(2)}) copy-start(bf16[4,8,16,1024]{3,2,1,0:T(8,128)(2,1)S(1)} %pad_maximum_fusion.mine_ref) | copy-start | bytes 3145732
  37.8 5.7 %collective-permute-start.5 = (bf16[4,8,16,1024]{3,2,1,0:T(8,128)(2,1)S(1)}, bf16[4,8,16,1024]{3,2,1,0:T(8,128)(2,1)}, u32[]{:S(2)}, u32[]{:S(2)}) collective-permute-start(bf16[4,8,16,1024]{3,2,1,0:T(8,128)(2,1)S(1)} %pad_maximum_fusion.mine_ref), channel_id=1, source_target_pairs={{0,8},{8,0},{1,9},{9,1},{2,10},{10,2},{3,11},{11,3},{4,12},{12,4},... | collective-permute-start | bytes 3145736 | tf_op jit(solution)/shard_map/ppermute | solution.py:485
  39.5 2.8 %collective-permute-start.4 = (bf16[256,768]{1,0:T(8,128)(2,1)S(1)}, bf16[256,768]{1,0:T(8,128)(2,1)S(1)}, u32[]{:S(2)}, u32[]{:S(2)}) collective-permute-start(bf16[256,768]{1,0:T(8,128)(2,1)S(1)} %copy-done.6), channel_id=1, source_target_pairs={{0,8},{8,0},{1,9},{9,1},{2,10},{10,2},{3,11},{11,3},{4,12},{12,4},... | collective-permute-start | bytes 1179656 | tf_op jit(solution)/shard_map/ppermute | solution.py:480
  39.6 3.1 %collective-permute-start.3 = (bf16[8,64,256]{2,1,0:T(8,128)(2,1)S(1)}, bf16[8,64,256]{2,1,0:T(8,128)(2,1)S(1)}, u32[]{:S(2)}, u32[]{:S(2)}) collective-permute-start(bf16[8,64,256]{2,1,0:T(8,128)(2,1)S(1)} %get-tuple-element.40), channel_id=1, source_target_pairs={{0,8},{8,0},{1,9},{9,1},{2,10},{10,2},{3,11},{11,3},{4,12},{12,4},... | collective-permute-start | bytes 786440 | tf_op jit(solution)/shard_map/ppermute | solution.py:486
  42.4 23.0 %copy-start.7 = (bf16[256,768]{1,0:T(8,128)(2,1)}, bf16[256,768]{1,0:T(8,128)(2,1)S(1)}, u32[]{:S(2)}) copy-start(bf16[256,768]{1,0:T(8,128)(2,1)S(1)} %collective-permute-done.4.sco_ref) | copy-start | bytes 1179652
  42.7 0.7 copy-start.9
  43.5 1.1 copy-start.1
  65.4 7.3 %collective-permute-start.6 = (bf16[4,16,64,128]{3,2,1,0:T(8,128)(2,1)}, bf16[4,16,64,128]{3,2,1,0:T(8,128)(2,1)}, u32[]{:S(2)}, u32[]{:S(2)}) collective-permute-start(bf16[4,16,64,128]{3,2,1,0:T(8,128)(2,1)} %get-tuple-element.50), channel_id=1, source_target_pairs={{0,8},{8,0},{1,9},{9,1},{2,10},{10,2},{3,11},{11,3},{4,12},{12,4},... | collective-permute-start | bytes 3145736 | tf_op jit(solution)/shard_map/ppermute | solution.py:493
  67.1 5.6 %copy-start.5 = (bf16[4,16,64,128]{3,2,1,0:T(8,128)(2,1)S(1)}, bf16[4,16,64,128]{3,2,1,0:T(8,128)(2,1)}, u32[]{:S(2)}) copy-start(bf16[4,16,64,128]{3,2,1,0:T(8,128)(2,1)} %get-tuple-element.49) | copy-start | bytes 3145732
  67.1 30.0 %all-to-all-start.2 = ((bf16[16,192,256]{2,1,0:T(8,128)(2,1)}), bf16[16,192,256]{2,1,0:T(8,128)(2,1)S(1)}, u32[]{:S(2)}, u32[]{:S(2)}) async-start(bf16[16,192,256]{2,1,0:T(8,128)(2,1)} %get-tuple-element.48), calls=%async_computation.2 | async-start | bytes 3145728 | tf_op jit(solution)/shard_map/all_to_all | solution.py:491
  74.1 7.6 %collective-permute-start.7 = (bf16[16,64,128]{2,1,0:T(8,128)(2,1)S(1)}, bf16[16,64,128]{2,1,0:T(8,128)(2,1)S(1)}, u32[]{:S(2)}, u32[]{:S(2)}) collective-permute-start(bf16[16,64,128]{2,1,0:T(8,128)(2,1)S(1)} %get-tuple-element.80), channel_id=1, source_target_pairs={{0,32},{32,64},{64,96},{96,0},{1,33},{33,65},{65,97},{97,1},{2,34}... | collective-permute-start | bytes 786440 | tf_op jit(solution)/shard_map/ppermute | solution.py:497
  76.4 9.1 %collective-permute-start.9 = (bf16[16,64,128]{2,1,0:T(8,128)(2,1)S(1)}, bf16[16,64,128]{2,1,0:T(8,128)(2,1)S(1)}, u32[]{:S(2)}, u32[]{:S(2)}) collective-permute-start(bf16[16,64,128]{2,1,0:T(8,128)(2,1)S(1)} %get-tuple-element.81), channel_id=1, source_target_pairs={{0,96},{32,0},{64,32},{96,64},{1,97},{33,1},{65,33},{97,65},{2,98}... | collective-permute-start | bytes 786440 | tf_op jit(solution)/shard_map/ppermute | solution.py:497
  76.4 12.6 %collective-permute-start.8 = (bf16[16,64,128]{2,1,0:T(8,128)(2,1)S(1)}, bf16[16,64,128]{2,1,0:T(8,128)(2,1)S(1)}, u32[]{:S(2)}, u32[]{:S(2)}) collective-permute-start(bf16[16,64,128]{2,1,0:T(8,128)(2,1)S(1)} %get-tuple-element.82), channel_id=1, source_target_pairs={{0,64},{32,96},{64,0},{96,32},{1,65},{33,97},{65,1},{97,33},{2,66}... | collective-permute-start | bytes 786440 | tf_op jit(solution)/shard_map/ppermute | solution.py:497
  97.1 1.2 copy-start
  102.4 5.9 %collective-permute-start.10 = (bf16[12,192,256]{2,1,0:T(8,128)(2,1)}, bf16[12,192,256]{2,1,0:T(8,128)(2,1)S(1)}, u32[]{:S(2)}, u32[]{:S(2)}) collective-permute-start(bf16[12,192,256]{2,1,0:T(8,128)(2,1)} %get-tuple-element.55), channel_id=1, source_target_pairs={{0,8},{8,0},{1,9},{9,1},{2,10},{10,2},{3,11},{11,3},{4,12},{12,4},... | collective-permute-start | bytes 3538952 | tf_op jit(solution)/shard_map/ppermute | solution.py:502
  103.7 13.1 %all-to-all-start.3 = ((bf16[16,64,128]{2,1,0:T(8,128)(2,1)}), bf16[16,64,128]{2,1,0:T(8,128)(2,1)S(1)}, u32[]{:S(2)}, u32[]{:S(2)}) async-start(bf16[16,64,128]{2,1,0:T(8,128)(2,1)} %fusion.2), calls=%async_computation.3 | async-start | bytes 524288 | tf_op jit(solution)/shard_map/all_to_all | solution.py:499
  108.4 1.1 copy-start.3
  116.7 57.3 %all-to-all-start.4 = ((bf16[64,32,768]{2,1,0:T(8,128)(2,1)}), bf16[64,32,768]{2,1,0:T(8,128)(2,1)S(1)}, u32[]{:S(2)}, u32[]{:S(2)}) async-start(bf16[64,32,768]{2,1,0:T(8,128)(2,1)} %weight_grads.1), calls=%async_computation.4 | async-start | bytes 6291456 | tf_op jit(solution)/shard_map/all_to_all | solution.py:512
  130.5 6.0 %copy-start.8 = (bf16[768,256]{1,0:T(8,128)(2,1)S(1)}, bf16[768,256]{1,0:T(8,128)(2,1)}, u32[]{:S(2)}) copy-start(bf16[768,256]{1,0:T(8,128)(2,1)} %get-tuple-element.62.gated_ref) | copy-start | bytes 1179652
  175.1 1.3 collective-permute-start.11

commit v8 on v6

--- a/solution.py
+++ b/solution.py
@@ -21,7 +21,11 @@
 PLANE = ("zh", "zl", "y")
 SWAP = [(0, 1), (1, 0)]
 SCALE = 1.0 / math.sqrt(DH)
-VMEM_LIMIT = 60 * 1024 * 1024
+MIB = 1024 * 1024
+
+
+def in_vmem(x):
+    return pltpu.with_memory_space_constraint(x, pltpu.VMEM)
 
 
 def dot(a, b):
@@ -36,12 +40,12 @@
     return [(i, (i + shift) % 4) for i in range(4)]
 
 
-def params():
-    return pltpu.CompilerParams(vmem_limit_bytes=VMEM_LIMIT)
+def params(mib=20):
+    return pltpu.CompilerParams(vmem_limit_bytes=mib * MIB)
 
 
 def front_kernel(
-    act_ref, gain_ref, w_ref, wout_ref, dout_ref, scaled_ref, normed_ref, inv_ref, send_ref, gate_ref, gg_ref
+    act_ref, gain_ref, w_ref, wout_ref, dout_ref, scaled_ref, mean_ref, inv_ref, send_ref, gate_ref, gg_ref
 ):
     step = pl.program_id(0)
     flat = act_ref.shape[0]
@@ -53,42 +57,39 @@
         shifted = values - center
         spread = jnp.mean(shifted * shifted, -1, keepdims=True)
         inv_std = lax.rsqrt(spread + EPS)
-        normed = shifted * inv_std
-        normed_ref[...] = normed
+        mean_ref[...] = center
         inv_ref[...] = inv_std
-        scaled_ref[...] = (normed * gain_ref[...].reshape(1, C)).astype(BF)
+        scaled_ref[...] = (shifted * inv_std * gain_ref[...].reshape(1, C)).astype(BF)
 
     block = dot(scaled_ref[...], w_ref[...])
-
-    for kind in range(3):
-
-        @pl.when(step == kind)
-        def _(kind=kind):
-            send_ref[:, kind * DH : (kind + 1) * DH, :] = block.astype(BF).T.reshape(HEADS, DH, flat)
+    rows = pl.ds(pl.multiple_of(step * 4 * DH, 4 * DH), 4 * DH)
+    gg_ref[rows, :] = dot_nt(wout_ref[...], dout_ref[...]).astype(BF)
+
+    @pl.when(step < 3)
+    def _():
+        send_ref[...] = block.astype(BF).T.reshape(HEADS, DH, flat)
 
     @pl.when(step == 3)
     def _():
         gate = jax.nn.sigmoid(block.T)
-        ggated = dot_nt(wout_ref[...], dout_ref[...]).astype(BF)
         gate_ref[...] = gate
-        gg_ref[...] = ggated
-        send_ref[:, 3 * DH : 4 * DH, :] = (ggated.astype(F32) * gate).astype(BF).reshape(HEADS, DH, flat)
+        send_ref[...] = (gg_ref[...].astype(F32) * gate).astype(BF).reshape(HEADS, DH, flat)
 
 
 def front(act, ln_gain, w_in, w_out, d_out):
     flat = act.shape[0]
-    shapes = [
-        ((flat, C), BF),
-        ((flat, C), F32),
-        ((flat, 1), F32),
-        ((HEADS, 4 * DH, flat), BF),
-        ((C, flat), F32),
-        ((C, flat), BF),
-    ]
 
     def whole(shape):
         return pl.BlockSpec(shape, lambda t: (0,) * len(shape))
 
+    outs = [
+        ((flat, C), BF, whole((flat, C))),
+        ((flat, 1), F32, whole((flat, 1))),
+        ((flat, 1), F32, whole((flat, 1))),
+        ((HEADS, 4 * DH, flat), BF, pl.BlockSpec((HEADS, DH, flat), lambda t: (0, t, 0))),
+        ((C, flat), F32, whole((C, flat))),
+        ((C, flat), BF, whole((C, flat))),
+    ]
     return pl.pallas_call(
         front_kernel,
         grid=(4,),
@@ -96,12 +97,12 @@
             whole((flat, C)),
             whole((C,)),
             pl.BlockSpec((C, C), lambda t: (0, t)),
-            whole((C, C)),
+            pl.BlockSpec((4 * DH, C), lambda t: (t, 0)),
             whole((flat, C)),
         ],
-        out_specs=[whole(s) for s, _ in shapes],
-        out_shape=[jax.ShapeDtypeStruct(s, d) for s, d in shapes],
-        compiler_params=params(),
+        out_specs=[spec for _, _, spec in outs],
+        out_shape=[jax.ShapeDtypeStruct(shape, kind) for shape, kind, _ in outs],
+        compiler_params=params(60),
         cost_estimate=pl.CostEstimate(
             flops=2 * flat * C * 5 * C, bytes_accessed=11 * 2**20, transcendentals=flat * C
         ),
@@ -116,8 +117,6 @@
     core = place_ref[0]
     own_x = place_ref[1]
     sample = pl.program_id(0)
-    half = sample // 2
-    lane0 = pl.multiple_of((sample % 2) * TOK, TOK)
 
     @pl.when(sample == 0)
     def _():
@@ -129,7 +128,7 @@
                 pieces += [jnp.where(core == 0, mine, other), jnp.where(core == 0, other, mine)]
             bias_s[t * TOK : (t + 1) * TOK] = jnp.concatenate(pieces, axis=0).astype(F32) * LOG2E
 
-    whole = jnp.concatenate([x_ref[half * 8 + t, :, pl.ds(lane0, TOK)] for t in range(8)], axis=1)
+    whole = jnp.concatenate([x_ref[t] for t in range(8)], axis=1)
     qt, kt, vt, gt = (whole[i * DH : (i + 1) * DH] for i in range(4))
     qs = qt.astype(F32) * (SCALE * LOG2E)
     q_hi = qs.astype(BF)
@@ -199,21 +198,22 @@
     for t in range(8):
         cols = slice(t * TOK, (t + 1) * TOK)
         for i, part in enumerate((out_t, dquery_t, dkey_t, dvalue_t)):
-            out_ref[half * 8 + t, i * DH : (i + 1) * DH, pl.ds(lane0, TOK)] = part[:, cols]
+            out_ref[t, i * DH : (i + 1) * DH, :] = part[:, cols]
 
 
 def attention(place, x, mine, other, blocks=4):
     def whole(shape):
         return pl.BlockSpec(shape, lambda s, place: (0,) * len(shape))
 
+    one = pl.BlockSpec((8, 4 * DH, TOK), lambda s, place: (s // 2, 0, s % 2))
     half_sum = (4, HEADS, 64, 128)
     return pl.pallas_call(
         functools.partial(attention_kernel, blocks=blocks),
         grid_spec=pltpu.PrefetchScalarGridSpec(
             num_scalar_prefetch=1,
             grid=(4,),
-            in_specs=[whole(x.shape), whole(mine.shape), whole(other.shape)],
-            out_specs=[whole(x.shape), whole(half_sum), whole(half_sum)],
+            in_specs=[one, whole(mine.shape), whole(other.shape)],
+            out_specs=[one, whole(half_sum), whole(half_sum)],
             scratch_shapes=[
                 pltpu.VMEM((KEYS, 128), BF),
                 pltpu.VMEM((128, KEYS), BF),
@@ -230,12 +230,49 @@
             jax.ShapeDtypeStruct(half_sum, BF),
             jax.ShapeDtypeStruct(half_sum, BF),
         ],
-        compiler_params=params(),
+        compiler_params=params(60),
         cost_estimate=pl.CostEstimate(
             flops=4 * 6 * 2 * KEYS * KEYS * 256, bytes_accessed=8 * 2**20, transcendentals=4 * KEYS * KEYS
         ),
         name="attention",
     )(place, x, mine, other)
+
+
+def stage_kernel(core_ref, w_ref, sc_ref, sco_ref, do_ref, doo_ref, wt_ref, scaled_ref, dout_ref, turned_s):
+    n = pl.program_id(0)
+    flat = sc_ref.shape[0]
+
+    @pl.when(n == 0)
+    def _():
+        scaled_ref[:flat] = sc_ref[...]
+        scaled_ref[flat:] = sco_ref[...]
+        dout_ref[:, :, :flat] = do_ref[...]
+        dout_ref[:, :, flat:] = doo_ref[...]
+
+    turned_s[...] = w_ref[...].T
+    wt_ref[n] = turned_s[pl.ds(pl.multiple_of(core_ref[0] * 4 * DH, 4 * DH), 4 * DH), :]
+
+
+def stage(core, w_in, *early):
+    def whole(shape):
+        return pl.BlockSpec(shape, lambda t, core: (0,) * len(shape))
+
+    flat = early[0].shape[0]
+    shapes = [(8, 4 * DH, C), (2 * flat, C), (8, 64, 2 * flat)]
+    return pl.pallas_call(
+        stage_kernel,
+        grid_spec=pltpu.PrefetchScalarGridSpec(
+            num_scalar_prefetch=1,
+            grid=(8,),
+            in_specs=[pl.BlockSpec((C, 8 * DH), lambda n, core: (0, n))] + [whole(e.shape) for e in early],
+            out_specs=[whole(s) for s in shapes],
+            scratch_shapes=[pltpu.VMEM((8 * DH, C), BF)],
+        ),
+        out_shape=[pltpu.VMEM(s, BF) for s in shapes],
+        compiler_params=params(24),
+        cost_estimate=pl.CostEstimate(flops=8 * C * C, bytes_accessed=7 * 2**20, transcendentals=0),
+        name="stage",
+    )(core, w_in, *early)
 
 
 def gate_kernel(core_ref, back_ref, gate_ref, gg_ref, ggate_ref, gated_ref, send_ref):
@@ -277,15 +314,15 @@
             out_specs=[whole(s) for s in shapes],
         ),
         out_shape=[jax.ShapeDtypeStruct(s, BF) for s in shapes],
-        compiler_params=params(),
+        compiler_params=params(20),
         cost_estimate=pl.CostEstimate(flops=6 * C * flat, bytes_accessed=6 * 2**20, transcendentals=0),
         name="gate",
     )(core, back, gate, ggated)
 
 
-def input_grad_kernel(back_ref, ggate_ref, w_ref, normed_ref, inv_ref, gain_ref, grad_ref, total_s):
+def input_grad_kernel(back_ref, ggate_ref, w_ref, act_ref, mean_ref, inv_ref, gain_ref, grad_ref, total_s):
     step = pl.program_id(0)
-    flat = normed_ref.shape[0]
+    flat = act_ref.shape[0]
 
     for kind in range(4):
 
@@ -303,7 +340,7 @@
 
     @pl.when(step == 3)
     def _():
-        normed = normed_ref[...]
+        normed = (act_ref[...].astype(F32) - mean_ref[...]) * inv_ref[...]
         grad_normed = total_s[...].T * gain_ref[...].reshape(1, C)
         grad_ref[...] = (
             inv_ref[...]
@@ -315,8 +352,8 @@
         ).astype(BF)
 
 
-def input_grad(back, ggate, w_in, normed, inv_std, ln_gain):
-    flat = normed.shape[0]
+def input_grad(back, ggate, w_in, act, mean, inv_std, ln_gain):
+    flat = act.shape[0]
 
     def whole(shape):
         return pl.BlockSpec(shape, lambda t: (0,) * len(shape))
@@ -330,32 +367,30 @@
             pl.BlockSpec((C, C), lambda t: (0, t)),
             whole((flat, C)),
             whole((flat, 1)),
+            whole((flat, 1)),
             whole((C,)),
         ],
         out_specs=whole((flat, C)),
         out_shape=jax.ShapeDtypeStruct((flat, C), BF),
         scratch_shapes=[pltpu.VMEM((C, flat), F32)],
-        compiler_params=params(),
+        compiler_params=params(60),
         cost_estimate=pl.CostEstimate(
             flops=2 * flat * C * 4 * C, bytes_accessed=8 * 2**20, transcendentals=0
         ),
         name="input_grad",
-    )(back, ggate, w_in, normed, inv_std, ln_gain)
+    )(back, ggate, w_in, act, mean, inv_std, ln_gain)
 
 
 def weight_kernel(
-    core_ref, back_ref, ggate_ref, o_ref, gated_ref, sc_ref, sco_ref, do_ref, doo_ref, wt_ref, gain_ref,
-    out_ref, scaled_s, gated_s, sum_s,
+    core_ref, back_ref, ggate_ref, o_ref, gated_ref, scaled_ref, dout_ref, wt_ref, gain_ref, out_ref, gated_s, sum_s
 ):
     core = core_ref[0]
     step = pl.program_id(0)
-    flat = sc_ref.shape[0]
+    flat = gated_ref.shape[1]
     last = pl.num_programs(0) - 1
 
     @pl.when(step == 0)
     def _():
-        scaled_s[:flat] = sc_ref[...]
-        scaled_s[flat:] = sco_ref[...]
         gated_s[:flat] = gated_ref[...].T
         gated_s[flat:] = o_ref[8:12].reshape(C, flat).T
         sum_s[...] = jnp.zeros_like(sum_s)
@@ -368,15 +403,8 @@
                 jnp.concatenate([head_rows(back_ref, ggate_ref, n, core), o_ref[n]], axis=1)
                 for n in (2 * kind, 2 * kind + 1)
             ]
-            win = dot(jnp.concatenate(blocks, axis=0), scaled_s[...])
-            tails = jnp.concatenate(
-                [
-                    jnp.concatenate([do_ref[n], doo_ref[n]], axis=1)
-                    for n in (2 * kind, 2 * kind + 1)
-                ],
-                axis=0,
-            )
-            wout = dot(tails, gated_s[...])
+            win = dot(jnp.concatenate(blocks, axis=0), scaled_ref[...])
+            wout = dot(dout_ref[2 * kind : 2 * kind + 2].reshape(128, 2 * flat), gated_s[...])
             weights = wt_ref[2 * kind : 2 * kind + 2].reshape(8 * DH, C).astype(F32)
             sum_s[...] += jnp.sum((win * weights).reshape(DH, 8, C), axis=0)
             for k in range(16):
@@ -398,7 +426,7 @@
     def whole(shape):
         return pl.BlockSpec(shape, lambda t, core: (0,) * len(shape))
 
-    flat = operands[4].shape[0]
+    flat = operands[3].shape[1]
     return pl.pallas_call(
         weight_kernel,
         grid_spec=pltpu.PrefetchScalarGridSpec(
@@ -408,12 +436,11 @@
             out_specs=whole((64, 32, C)),
             scratch_shapes=[
                 pltpu.VMEM((2 * flat, C), BF),
-                pltpu.VMEM((2 * flat, C), BF),
                 pltpu.VMEM((8, C), F32),
             ],
         ),
         out_shape=jax.ShapeDtypeStruct((64, 32, C), BF),
-        compiler_params=params(),
+        compiler_params=params(24),
         cost_estimate=pl.CostEstimate(
             flops=2 * 2 * flat * C * 2048, bytes_accessed=8 * 2**20, transcendentals=0
         ),
@@ -434,44 +461,50 @@
     bias = lax.all_to_all(bias, ("zl", "y"), 0, 0, tiled=True)
 
     rows_out = d_out.reshape(flat, channels)
-    scaled, normed, inv_std, send, gate, ggated = front(
-        act.reshape(flat, channels), ln_gain, w_in, w_out, rows_out
+    act = act.reshape(flat, channels)
+    scaled, mean, inv_std, send, gate, ggated = front(
+        act, ln_gain, w_in, w_out, rows_out
     )
     bias, send = lax.optimization_barrier((bias, send))
-    bias = jnp.stack([bias] + [lax.ppermute(bias, "x", turn(s)) for s in (1, 2, 3)])
-    bias_other = lax.ppermute(bias, "core", SWAP)
+    pieces = [bias] + [lax.ppermute(bias, "x", turn(s)) for s in (1, 2, 3)]
     received = lax.all_to_all(send, PLANE, 0, 0, tiled=True)
 
     dout_t = jnp.pad(rows_out.T.reshape(128, 6, flat), ((0, 0), (0, 2), (0, 0)))
     dout_t = dout_t.reshape(8, 2, 64, flat)
     dout_mine = lax.dynamic_index_in_dim(dout_t, core, 1, keepdims=False)
     dout_send = lax.dynamic_index_in_dim(dout_t, 1 - core, 1, keepdims=False)
+    scaled_other = lax.ppermute(scaled, "core", SWAP)
+
+    pieces, dout_mine, dout_send = lax.optimization_barrier((pieces, dout_mine, dout_send))
+    bias = jnp.stack(pieces)
+    bias_other = lax.ppermute(bias, "core", SWAP)
     dout_other = lax.ppermute(dout_send, "core", SWAP)
-    scaled_other = lax.ppermute(scaled, "core", SWAP)
-
-    w_rows = lax.dynamic_index_in_dim(w_in.T.reshape(8, 2, 4 * DH, C), core, 1, keepdims=False)
-    received, dout_mine, dout_other, scaled_other, w_rows = lax.optimization_barrier(
-        (received, dout_mine, dout_other, scaled_other, w_rows)
+    received, dout_other, scaled_other, bias_other = lax.optimization_barrier(
+        (received, dout_other, scaled_other, bias_other)
     )
     result, keep, give = attention(place, received, bias, bias_other)
     back = lax.all_to_all(result, PLANE, 0, 0, tiled=True)
 
+    keep, scaled, scaled_other, dout_mine, dout_other = lax.optimization_barrier(
+        (keep, scaled, scaled_other, dout_mine, dout_other)
+    )
     got = lax.ppermute(give, "core", SWAP)
     sums = [(keep[s].astype(F32) + got[s].astype(F32)).astype(BF) for s in range(4)]
     gb = sums[0].astype(F32)
     for s in (1, 2, 3):
         gb = gb + lax.ppermute(sums[s], "x", turn(s)).astype(F32)
-    back, gb = lax.optimization_barrier((back, gb.astype(BF)))
+    staged = stage(core_arg, w_in, scaled, scaled_other, dout_mine, dout_other)
+    back, gb, staged = lax.optimization_barrier((back, gb.astype(BF), staged))
     gb = lax.all_to_all(gb, PLANE, 0, 0, tiled=True)
 
     ggate, gated, half = gate_step(core_arg, back, gate, ggated)
     other = lax.ppermute(half, "core", SWAP)
     chunks = weight_grads(
         core_arg,
-        (back, ggate, other, gated, scaled, scaled_other, dout_mine, dout_other, w_rows, ln_gain),
+        (back, ggate, other, gated, in_vmem(staged[1]), in_vmem(staged[2]), in_vmem(staged[0]), ln_gain),
     )
     chunks, gated, ggate, gb = lax.optimization_barrier((chunks, gated, ggate, gb))
-    grad_act = input_grad(back, ggate, w_in, normed, inv_std, ln_gain)
+    grad_act = input_grad(back, ggate, w_in, act, mean, inv_std, ln_gain)
     gb = gb.astype(F32)
     grad_bias = jnp.concatenate([gb[:, :, :64], gb[:, :, 64:]], axis=1)
     output = jnp.einsum("cr,cd->rd", gated, w_out, preferred_element_type=F32).astype(BF)

time: 184 us -> 172 us (0.935)
  Pallas kernels: 45.4 us -> 39.8 us
  waiting for transfers between devices: 62.3 us -> 58.7 us
  local copies, waits for them, and re-layouts: 20 us -> 17.9 us
    ppermute x3, waiting for transfers between devices: 11.1 us -> 3.41 us  [per_device(): gb = gb + lax.ppermute(sums[s], 'x', turn(s)).astype(F32)]
    pallas_call x1, Pallas kernels: 7.43 us -> 2.53 us  [weight_grads(): pl.pallas_call(weight_kernel, grid_spec=pltpu.PrefetchScalarGridSpec(num_...]
    squeeze x1 -> x0, local copies, waits for them, and re-layouts: 3.27 us -> none  [per_device(): lax.dynamic_index_in_dim(w_in.T.reshape(8, 2, 4 * DH, C), core, 1, keepdi...]
    ppermute x1, starting transfers between devices: 0.09 us -> 3.24 us  [per_device(): got = lax.ppermute(give, 'core', SWAP)]
    all_to_all x1, waiting for transfers between devices: 4.59 us -> 7.59 us  [per_device(): back = lax.all_to_all(result, PLANE, 0, 0, tiled=True)]
    pallas_call x0 -> x1, Pallas kernels: none -> 2.59 us  [stage(): pl.pallas_call(stage_kernel, grid_spec=pltpu.PrefetchScalarGridSpec(num_s...]
    unnamed x18 -> x33, local copies, waits for them, and re-layouts: 12.4 us -> 13.3 us
  transfers between devices with their start and end apart: 17 -> 17, of which waited for: 8 -> 10; matrix products, arithmetic and copies ran while one was open for 12% -> 7% of each run, Pallas kernels for 12% -> 11%
where the time goes in v8:
time: 172 us; the launch traced here: 171 us
  waiting for transfers between devices  58.7 us (34%)
  starting transfers between devices  45.2 us (26%)
  Pallas kernels  39.8 us (23%)
  local copies, waits for them, and re-layouts  17.9 us (10%)
  other arithmetic  6.48 us (4%)
  matrix products  2.52 us (1%)
    all_to_all x1, waiting for transfers between devices, per_device(): chunks = lax.all_to_all(chunks, ('x', 'zh', 'zl', 'y'), 0, 0, tiled=True)  34.1 us
    pallas_call x1, Pallas kernels, attention(): pl.pallas_call(functools.partial(attention_kernel, blocks=blocks), grid_s...  20 us
    unnamed x33, local copies, waits for them, and re-layouts  13.3 us
    ppermute x3, waiting for transfers between devices, per_device(): pieces = [bias] + [lax.ppermute(bias, 'x', turn(s)) for s in (1, 2, 3)]  10.9 us
    all_to_all x1, starting transfers between devices, per_device(): chunks = lax.all_to_all(chunks, ('x', 'zh', 'zl', 'y'), 0, 0, tiled=True)  9.85 us
    all_to_all x1, waiting for transfers between devices, per_device(): back = lax.all_to_all(result, PLANE, 0, 0, tiled=True)  7.59 us
    pallas_call x1, Pallas kernels, front(): pl.pallas_call(front_kernel, grid=(4,), in_specs=[whole((flat, C)), whole...  7.25 us
    all_to_all x1, starting transfers between devices, per_device(): received = lax.all_to_all(send, PLANE, 0, 0, tiled=True)  6.52 us
  transfers between devices with their start and end apart: 17, of which 10 were waited for; matrix products, arithmetic and copies ran while one was open for 7% of the time, Pallas kernels for 11%

profile of v8, /device:TPU:103, one launch (start us, length us, event | category | flops | bytes accessed | tf_op | source)
XLA Modules:
  0.0 171.5 jit_solution(492281081421109706)
XLA Ops:
  0.6 1.7 constant_dynamic-slice_fusion
  2.3 5.4 %all-to-all-start = ((bf16[8,16,1024]{2,1,0:T(8,128)(2,1)}), bf16[8,16,1024]{2,1,0:T(8,128)(2,1)S(1)}, u32[]{:S(2)}, u32[]{:S(2)}) async-start(bf16[8,16,1024]{2,1,0:T(8,128)(2,1)} %constant_dynamic-slice_fusion), calls=%async_computation | async-start | bytes 524288 | tf_op jit(solution)/shard_map/all_to_all | solution.py:461
  7.7 7.2 %front.1 = (bf16[256,768]{1,0:T(8,128)(2,1)}, f32[256,1]{1,0:T(8,128)}, f32[256,1]{1,0:T(8,128)}, bf16[16,192,256]{2,1,0:T(8,128)(2,1)}, f32[768,256]{1,0:T(8,128)}, /*index=5*/bf16[768,256]{1,0:T(8,128)(2,1)}) custom-call(bf16[256,768]{1,0:T(8,128)(2,1)} %bitcast.35, f32[768]{0:T(1024)} %gain_ref.5, bf16[768,3072]{1,0:T(8,128)(2,1)} %w_ref.5, ...), custom_call_target="tpu_custom_call" | custom-call | flops 1509949440 | bytes 11534336 | tf_op jit(solution)/shard_map/front/pallas_call | solution.py:93
  15.0 6.5 %all-to-all-start.1 = ((bf16[16,192,256]{2,1,0:T(8,128)(2,1)}), bf16[16,192,256]{2,1,0:T(8,128)(2,1)}, u32[]{:S(2)}, u32[]{:S(2)}) async-start(bf16[16,192,256]{2,1,0:T(8,128)(2,1)} %get-tuple-element.48), calls=%async_computation.1 | async-start | bytes 3145728 | tf_op jit(solution)/shard_map/all_to_all | solution.py:470
  21.5 0.5 collective-permute-start.2
  22.0 0.8 collective-permute-start.1
  22.9 1.8 %collective-permute-start = (bf16[8,16,1024]{2,1,0:T(8,128)(2,1)S(1)}, bf16[8,16,1024]{2,1,0:T(8,128)(2,1)S(1)}, u32[]{:S(2)}, u32[]{:S(2)}) collective-permute-start(bf16[8,16,1024]{2,1,0:T(8,128)(2,1)S(1)} %all-to-all-done), channel_id=1, source_target_pairs={{0,32},{32,64},{64,96},{96,0},{1,33},{33,65},{65,97},{97,1},{2,34}... | collective-permute-start | bytes 786440 | tf_op jit(solution)/shard_map/ppermute | solution.py:469
  25.2 5.2 %collective-permute-done.2 = bf16[8,16,1024]{2,1,0:T(8,128)(2,1)S(1)} collective-permute-done((bf16[8,16,1024]{2,1,0:T(8,128)(2,1)S(1)}, bf16[8,16,1024]{2,1,0:T(8,128)(2,1)S(1)}, u32[]{:S(2)}, u32[]{:S(2)}) %collective-permute-start.2) | collective-permute-done | bytes 262176 | tf_op jit(solution)/shard_map/ppermute | solution.py:469
  30.3 2.8 %collective-permute-done.1 = bf16[8,16,1024]{2,1,0:T(8,128)(2,1)S(1)} collective-permute-done((bf16[8,16,1024]{2,1,0:T(8,128)(2,1)S(1)}, bf16[8,16,1024]{2,1,0:T(8,128)(2,1)S(1)}, u32[]{:S(2)}, u32[]{:S(2)}) %collective-permute-start.1) | collective-permute-done | bytes 262176 | tf_op jit(solution)/shard_map/ppermute | solution.py:469
  33.2 2.9 %collective-permute-done = bf16[8,16,1024]{2,1,0:T(8,128)(2,1)S(1)} collective-permute-done((bf16[8,16,1024]{2,1,0:T(8,128)(2,1)S(1)}, bf16[8,16,1024]{2,1,0:T(8,128)(2,1)S(1)}, u32[]{:S(2)}, u32[]{:S(2)}) %collective-permute-start) | collective-permute-done | bytes 262176 | tf_op jit(solution)/shard_map/ppermute | solution.py:469
  36.2 1.6 collective-permute-start.5
  38.4 0.6 pad_add_fusion.place_ref
  39.0 1.8 %collective-permute-done.4.sco_ref = bf16[256,768]{1,0:T(8,128)(2,1)S(1)} collective-permute-done((bf16[256,768]{1,0:T(8,128)(2,1)S(1)}, bf16[256,768]{1,0:T(8,128)(2,1)S(1)}, u32[]{:S(2)}, u32[]{:S(2)}) %collective-permute-start.4) | collective-permute-done | bytes 393248 | tf_op jit(solution)/shard_map/ppermute | solution.py:476
  41.4 20.0 %attention.1 = (bf16[16,192,256]{2,1,0:T(8,128)(2,1)}, bf16[4,16,64,128]{3,2,1,0:T(8,128)(2,1)}, bf16[4,16,64,128]{3,2,1,0:T(8,128)(2,1)}) custom-call(s32[2]{0:T(128)} %pad_add_fusion.place_ref, bf16[16,192,256]{2,1,0:T(8,128)(2,1)} %all-to-all-done.1.x_ref, bf16[4,8,16,1024]{3,2,1,0:T(8,128)(2,1)} %copy-done.15, ...), custom_call_target="tpu_custom_call" | custom-call | flops 12884901888 | bytes 8388608 | tf_op jit(solution)/shard_map/attention/pallas_call | solution.py:210
  61.4 3.2 %collective-permute-start.6 = (bf16[4,16,64,128]{3,2,1,0:T(8,128)(2,1)}, bf16[4,16,64,128]{3,2,1,0:T(8,128)(2,1)}, u32[]{:S(2)}, u32[]{:S(2)}) collective-permute-start(bf16[4,16,64,128]{3,2,1,0:T(8,128)(2,1)} %get-tuple-element.64), channel_id=1, source_target_pairs={{0,8},{8,0},{1,9},{9,1},{2,10},{10,2},{3,11},{11,3},{4,12},{12,4},... | collective-permute-start | bytes 3145736 | tf_op jit(solution)/shard_map/ppermute | solution.py:491
  64.7 5.5 %all-to-all-start.2 = ((bf16[16,192,256]{2,1,0:T(8,128)(2,1)}), bf16[16,192,256]{2,1,0:T(8,128)(2,1)S(1)}, u32[]{:S(2)}, u32[]{:S(2)}) async-start(bf16[16,192,256]{2,1,0:T(8,128)(2,1)} %get-tuple-element.58), calls=%async_computation.2 | async-start | bytes 3145728 | tf_op jit(solution)/shard_map/all_to_all | solution.py:486
  70.2 1.7 fusion.4
  71.8 0.4 collective-permute-start.7
  72.3 1.1 collective-permute-start.9
  73.4 1.1 collective-permute-start.8
  74.5 2.3 %copy-done = bf16[768,3072]{1,0:T(8,128)(2,1)S(1)} copy-done((bf16[768,3072]{1,0:T(8,128)(2,1)S(1)}, bf16[768,3072]{1,0:T(8,128)(2,1)}, u32[]{:S(2)}) %copy-start) | copy-done | bytes 4718616
  76.8 2.6 %stage.1 = (bf16[8,192,768]{2,1,0:T(8,128)(2,1)S(1)}, bf16[512,768]{1,0:T(8,128)(2,1)S(1)}, bf16[8,64,512]{2,1,0:T(8,128)(2,1)S(1)}) custom-call(s32[1]{0:T(128)} %bitcast.core_ref, bf16[768,3072]{1,0:T(8,128)(2,1)S(1)} %copy-done, bf16[256,768]{1,0:T(8,128)(2,1)S(1)} %copy-done.11, bf16[256,768]{1,0:T(8,128)(2,1)S(1)} %collective-permute-done.4.sco_ref, ...), custom_call_target="tpu_custom_call" | custom-call | flops 4718592 | bytes 7340032 | tf_op jit(solution)/shard_map/stage/pallas_call | solution.py:262
  79.4 1.4 copy-done.3
  80.9 0.9 copy-done.6
  81.8 0.8 copy-done.9
  82.6 3.4 %collective-permute-done.8 = bf16[16,64,128]{2,1,0:T(8,128)(2,1)S(1)} collective-permute-done((bf16[16,64,128]{2,1,0:T(8,128)(2,1)S(1)}, bf16[16,64,128]{2,1,0:T(8,128)(2,1)S(1)}, u32[]{:S(2)}, u32[]{:S(2)}) %collective-permute-start.8) | collective-permute-done | bytes 262176 | tf_op jit(solution)/shard_map/ppermute | solution.py:495
  86.0 1.9 %fusion.2 = bf16[16,64,128]{2,1,0:T(8,128)(2,1)} fusion(bf16[16,64,128]{2,1,0:T(8,128)(2,1)S(1)} %collective-permute-done.9, bf16[16,64,128]{2,1,0:T(8,128)(2,1)S(1)} %collective-permute-done.8, bf16[16,64,128]{2,1,0:T(8,128)(2,1)S(1)} %collective-permute-done.7, bf16[4,16,64,128]{3,2,1,0:T(8,128)(2,1)} %collective-permute-done.6, ...), kind=kLoop, calls=%fused_computation.7 | loop fusion | flops 1572864 | bytes 1572864 | tf_op jit(solution)/shard_map/convert_element_type | solution.py:497
  87.9 7.6 %all-to-all-done.2.back_ref = bf16[16,192,256]{2,1,0:T(8,128)(2,1)S(1)} async-done(((bf16[16,192,256]{2,1,0:T(8,128)(2,1)}), bf16[16,192,256]{2,1,0:T(8,128)(2,1)S(1)}, u32[]{:S(2)}, u32[]{:S(2)}) %all-to-all-start.2) | async-done | bytes 1572896 | tf_op jit(solution)/shard_map/all_to_all | solution.py:486
  95.5 1.5 gate.1
  97.1 0.8 collective-permute-start.10
  97.8 5.5 %all-to-all-start.3 = ((bf16[16,64,128]{2,1,0:T(8,128)(2,1)}), bf16[16,64,128]{2,1,0:T(8,128)(2,1)}, u32[]{:S(2)}, u32[]{:S(2)}) async-start(bf16[16,64,128]{2,1,0:T(8,128)(2,1)} %fusion.2), calls=%async_computation.3 | async-start | bytes 524288 | tf_op jit(solution)/shard_map/all_to_all | solution.py:498
  103.3 1.7 copy-done.4
  105.0 1.1 copy-done.7
  106.1 1.0 copy-done.10
  107.2 2.5 %weight_grads.1 = bf16[64,32,768]{2,1,0:T(8,128)(2,1)S(1)} custom-call(s32[1]{0:T(128)} %bitcast.core_ref, bf16[16,192,256]{2,1,0:T(8,128)(2,1)S(1)} %all-to-all-done.2.back_ref, bf16[4,192,256]{2,1,0:T(8,128)(2,1)S(1)} %get-tuple-element.83.ggate_ref, bf16[12,192,256]{2,1,0:T(8,128)(2,1)S(1)} %collective-permute-done.10.o_ref, ...), custom_call_target="tpu_custom_call" | custom-call | flops 1610612736 | bytes 8388608 | tf_op jit(solution)/shard_map/weight_grads/pallas_call | solution.py:430
  109.7 1.7 copy-done.2
  111.4 9.9 %all-to-all-start.4 = ((bf16[64,32,768]{2,1,0:T(8,128)(2,1)}), bf16[64,32,768]{2,1,0:T(8,128)(2,1)S(1)}, u32[]{:S(2)}, u32[]{:S(2)}) async-start(bf16[64,32,768]{2,1,0:T(8,128)(2,1)} %copy-done.2), calls=%async_computation.4 | async-start | bytes 6291456 | tf_op jit(solution)/shard_map/all_to_all | solution.py:511
  121.3 1.2 fusion.8
  122.5 1.1 pad_maximum_fusion.1
  123.5 2.3 %copy.14 = f32[16,128,64]{1,2,0:T(8,128)} copy(f32[16,128,64]{2,1,0:T(8,128)} %pad_maximum_fusion.1) | data formatting | bytes 1048576
  125.9 5.9 %input_grad.1 = bf16[256,768]{1,0:T(8,128)(2,1)} custom-call(bf16[16,192,256]{2,1,0:T(8,128)(2,1)} %copy-done.1, bf16[4,192,256]{2,1,0:T(8,128)(2,1)} %copy-done.5, bf16[768,3072]{1,0:T(8,128)(2,1)} %w_ref.5, bf16[256,768]{1,0:T(8,128)(2,1)} %bitcast.36, f32[256,1]{1,0:T(8,128)} %get-tuple-element.84.mean_ref, f32[256,1]{1,0:T(8,128)} %get-tuple-element.85.inv_ref, ...), custom_call_target="tpu_custom_call" | custom-call | flops 1207959552 | bytes 8388608 | tf_op jit(solution)/shard_map/input_grad/pallas_call | solution.py:361
  131.8 2.5 %convolution_convert_fusion = bf16[256,768]{1,0:T(8,128)(2,1)} fusion(bf16[768,256]{1,0:T(8,128)(2,1)S(1)} %get-tuple-element.82.gated_ref, bf16[768,768]{1,0:T(8,128)(2,1)} %wout_ref.1), kind=kOutput, calls=%fused_computation.1 | convolution fusion | flops 302186496 | bytes 1966080 | tf_op jit(solution)/shard_map/cr,cd->rd/dot_general | solution.py:510
  134.3 34.1 %all-to-all-done.4 = bf16[64,32,768]{2,1,0:T(8,128)(2,1)S(1)} async-done(((bf16[64,32,768]{2,1,0:T(8,128)(2,1)}), bf16[64,32,768]{2,1,0:T(8,128)(2,1)S(1)}, u32[]{:S(2)}, u32[]{:S(2)}) %all-to-all-start.4) | async-done | bytes 3145760 | tf_op jit(solution)/shard_map/all_to_all | solution.py:511
  168.4 0.5 convert_reduce_fusion
  168.9 0.6 slice_bitcast_fusion
  169.5 0.5 collective-permute-start.11
  170.0 0.6 slice_bitcast_fusion.1
  170.9 0.6 add.67
  (42 shorter events, 2.1 us)
Async XLA Ops:
  2.3 12.6 %all-to-all-start = ((bf16[8,16,1024]{2,1,0:T(8,128)(2,1)}), bf16[8,16,1024]{2,1,0:T(8,128)(2,1)S(1)}, u32[]{:S(2)}, u32[]{:S(2)}) async-start(bf16[8,16,1024]{2,1,0:T(8,128)(2,1)} %constant_dynamic-slice_fusion), calls=%async_computation | async-start | bytes 524288 | tf_op jit(solution)/shard_map/all_to_all | solution.py:461
  14.9 9.7 %copy-start.14 = (bf16[2,128,768]{2,1,0:T(8,128)(2,1)S(1)}, bf16[2,128,768]{2,1,0:T(8,128)(2,1)}, u32[]{:S(2)}) copy-start(bf16[2,128,768]{2,1,0:T(8,128)(2,1)} %param.11) | copy-start | bytes 1179652
  15.0 26.4 %all-to-all-start.1 = ((bf16[16,192,256]{2,1,0:T(8,128)(2,1)}), bf16[16,192,256]{2,1,0:T(8,128)(2,1)}, u32[]{:S(2)}, u32[]{:S(2)}) async-start(bf16[16,192,256]{2,1,0:T(8,128)(2,1)} %get-tuple-element.48), calls=%async_computation.1 | async-start | bytes 3145728 | tf_op jit(solution)/shard_map/all_to_all | solution.py:470
  21.5 8.9 %collective-permute-start.2 = (bf16[8,16,1024]{2,1,0:T(8,128)(2,1)S(1)}, bf16[8,16,1024]{2,1,0:T(8,128)(2,1)S(1)}, u32[]{:S(2)}, u32[]{:S(2)}) collective-permute-start(bf16[8,16,1024]{2,1,0:T(8,128)(2,1)S(1)} %all-to-all-done), channel_id=1, source_target_pairs={{0,96},{32,0},{64,32},{96,64},{1,97},{33,1},{65,33},{97,65},{2,98}... | collective-permute-start | bytes 786440 | tf_op jit(solution)/shard_map/ppermute | solution.py:469
  22.0 11.1 %collective-permute-start.1 = (bf16[8,16,1024]{2,1,0:T(8,128)(2,1)S(1)}, bf16[8,16,1024]{2,1,0:T(8,128)(2,1)S(1)}, u32[]{:S(2)}, u32[]{:S(2)}) collective-permute-start(bf16[8,16,1024]{2,1,0:T(8,128)(2,1)S(1)} %all-to-all-done), channel_id=1, source_target_pairs={{0,64},{32,96},{64,0},{96,32},{1,65},{33,97},{65,1},{97,33},{2,66}... | collective-permute-start | bytes 786440 | tf_op jit(solution)/shard_map/ppermute | solution.py:469
  22.9 13.2 %collective-permute-start = (bf16[8,16,1024]{2,1,0:T(8,128)(2,1)S(1)}, bf16[8,16,1024]{2,1,0:T(8,128)(2,1)S(1)}, u32[]{:S(2)}, u32[]{:S(2)}) collective-permute-start(bf16[8,16,1024]{2,1,0:T(8,128)(2,1)S(1)} %all-to-all-done), channel_id=1, source_target_pairs={{0,32},{32,64},{64,96},{96,0},{1,33},{33,65},{65,97},{97,1},{2,34}... | collective-permute-start | bytes 786440 | tf_op jit(solution)/shard_map/ppermute | solution.py:469
  25.1 12.8 %copy-start.11 = (bf16[256,768]{1,0:T(8,128)(2,1)S(1)}, bf16[256,768]{1,0:T(8,128)(2,1)}, u32[]{:S(2)}) copy-start(bf16[256,768]{1,0:T(8,128)(2,1)} %get-tuple-element.65.sc_ref) | copy-start | bytes 1179652
  36.2 5.2 %copy-start.15 = (bf16[4,8,16,1024]{3,2,1,0:T(8,128)(2,1)}, bf16[4,8,16,1024]{3,2,1,0:T(8,128)(2,1)S(1)}, u32[]{:S(2)}) copy-start(bf16[4,8,16,1024]{3,2,1,0:T(8,128)(2,1)S(1)} %pad_maximum_fusion.mine_ref) | copy-start | bytes 3145732
  36.2 4.9 %collective-permute-start.5 = (bf16[4,8,16,1024]{3,2,1,0:T(8,128)(2,1)S(1)}, bf16[4,8,16,1024]{3,2,1,0:T(8,128)(2,1)}, u32[]{:S(2)}, u32[]{:S(2)}) collective-permute-start(bf16[4,8,16,1024]{3,2,1,0:T(8,128)(2,1)S(1)} %pad_maximum_fusion.mine_ref), channel_id=1, source_target_pairs={{0,8},{8,0},{1,9},{9,1},{2,10},{10,2},{3,11},{11,3},{4,12},{12,4},... | collective-permute-start | bytes 3145736 | tf_op jit(solution)/shard_map/ppermute | solution.py:480
  37.9 2.8 %collective-permute-start.4 = (bf16[256,768]{1,0:T(8,128)(2,1)S(1)}, bf16[256,768]{1,0:T(8,128)(2,1)S(1)}, u32[]{:S(2)}, u32[]{:S(2)}) collective-permute-start(bf16[256,768]{1,0:T(8,128)(2,1)S(1)} %copy-done.11), channel_id=1, source_target_pairs={{0,8},{8,0},{1,9},{9,1},{2,10},{10,2},{3,11},{11,3},{4,12},{12,4},... | collective-permute-start | bytes 1179656 | tf_op jit(solution)/shard_map/ppermute | solution.py:476
  38.0 3.1 %collective-permute-start.3 = (bf16[8,64,256]{2,1,0:T(8,128)(2,1)S(1)}, bf16[8,64,256]{2,1,0:T(8,128)(2,1)S(1)}, u32[]{:S(2)}, u32[]{:S(2)}) collective-permute-start(bf16[8,64,256]{2,1,0:T(8,128)(2,1)S(1)} %get-tuple-element.50), channel_id=1, source_target_pairs={{0,8},{8,0},{1,9},{9,1},{2,10},{10,2},{3,11},{11,3},{4,12},{12,4},... | collective-permute-start | bytes 786440 | tf_op jit(solution)/shard_map/ppermute | solution.py:481
  61.4 8.7 %collective-permute-start.6 = (bf16[4,16,64,128]{3,2,1,0:T(8,128)(2,1)}, bf16[4,16,64,128]{3,2,1,0:T(8,128)(2,1)}, u32[]{:S(2)}, u32[]{:S(2)}) collective-permute-start(bf16[4,16,64,128]{3,2,1,0:T(8,128)(2,1)} %get-tuple-element.64), channel_id=1, source_target_pairs={{0,8},{8,0},{1,9},{9,1},{2,10},{10,2},{3,11},{11,3},{4,12},{12,4},... | collective-permute-start | bytes 3145736 | tf_op jit(solution)/shard_map/ppermute | solution.py:491
  64.7 30.9 %all-to-all-start.2 = ((bf16[16,192,256]{2,1,0:T(8,128)(2,1)}), bf16[16,192,256]{2,1,0:T(8,128)(2,1)S(1)}, u32[]{:S(2)}, u32[]{:S(2)}) async-start(bf16[16,192,256]{2,1,0:T(8,128)(2,1)} %get-tuple-element.58), calls=%async_computation.2 | async-start | bytes 3145728 | tf_op jit(solution)/shard_map/all_to_all | solution.py:486
  71.8 10.7 %collective-permute-start.7 = (bf16[16,64,128]{2,1,0:T(8,128)(2,1)S(1)}, bf16[16,64,128]{2,1,0:T(8,128)(2,1)S(1)}, u32[]{:S(2)}, u32[]{:S(2)}) collective-permute-start(bf16[16,64,128]{2,1,0:T(8,128)(2,1)S(1)} %get-tuple-element.100), channel_id=1, source_target_pairs={{0,32},{32,64},{64,96},{96,0},{1,33},{33,65},{65,97},{97,1},{2,34}... | collective-permute-start | bytes 786440 | tf_op jit(solution)/shard_map/ppermute | solution.py:495
  72.3 10.3 %collective-permute-start.9 = (bf16[16,64,128]{2,1,0:T(8,128)(2,1)S(1)}, bf16[16,64,128]{2,1,0:T(8,128)(2,1)S(1)}, u32[]{:S(2)}, u32[]{:S(2)}) collective-permute-start(bf16[16,64,128]{2,1,0:T(8,128)(2,1)S(1)} %get-tuple-element.101), channel_id=1, source_target_pairs={{0,96},{32,0},{64,32},{96,64},{1,97},{33,1},{65,33},{97,65},{2,98}... | collective-permute-start | bytes 786440 | tf_op jit(solution)/shard_map/ppermute | solution.py:495
  73.4 12.6 %collective-permute-start.8 = (bf16[16,64,128]{2,1,0:T(8,128)(2,1)S(1)}, bf16[16,64,128]{2,1,0:T(8,128)(2,1)S(1)}, u32[]{:S(2)}, u32[]{:S(2)}) collective-permute-start(bf16[16,64,128]{2,1,0:T(8,128)(2,1)S(1)} %get-tuple-element.102), channel_id=1, source_target_pairs={{0,64},{32,96},{64,0},{96,32},{1,65},{33,97},{65,1},{97,33},{2,66}... | collective-permute-start | bytes 786440 | tf_op jit(solution)/shard_map/ppermute | solution.py:495
  74.5 2.3 %copy-start = (bf16[768,3072]{1,0:T(8,128)(2,1)S(1)}, bf16[768,3072]{1,0:T(8,128)(2,1)}, u32[]{:S(2)}) copy-start(bf16[768,3072]{1,0:T(8,128)(2,1)} %w_ref.5) | copy-start | bytes 14155780
  79.4 1.5 copy-start.3
  80.9 0.9 copy-start.6
  81.8 0.8 copy-start.9
  82.6 13.0 %copy-start.8 = (f32[768,256]{1,0:T(8,128)S(1)}, f32[768,256]{1,0:T(8,128)}, u32[]{:S(2)}) copy-start(f32[768,256]{1,0:T(8,128)} %get-tuple-element.73.gate_ref) | copy-start | bytes 2359300
  82.6 13.0 %copy-start.12 = (bf16[768,256]{1,0:T(8,128)(2,1)S(1)}, bf16[768,256]{1,0:T(8,128)(2,1)}, u32[]{:S(2)}) copy-start(bf16[768,256]{1,0:T(8,128)(2,1)} %get-tuple-element.74.gg_ref) | copy-start | bytes 1179652
  95.5 7.8 %copy-start.1 = (bf16[16,192,256]{2,1,0:T(8,128)(2,1)}, bf16[16,192,256]{2,1,0:T(8,128)(2,1)S(1)}, u32[]{:S(2)}) copy-start(bf16[16,192,256]{2,1,0:T(8,128)(2,1)S(1)} %all-to-all-done.2.back_ref) | copy-start | bytes 4718596
  95.5 7.8 %copy-start.13 = (f32[768]{0:T(1024)S(1)}, f32[768]{0:T(1024)}, u32[]{:S(2)}) copy-start(f32[768]{0:T(1024)} %gain_ref.5) | copy-start | bytes 9220
  97.1 12.7 %copy-start.5 = (bf16[4,192,256]{2,1,0:T(8,128)(2,1)}, bf16[4,192,256]{2,1,0:T(8,128)(2,1)S(1)}, u32[]{:S(2)}) copy-start(bf16[4,192,256]{2,1,0:T(8,128)(2,1)S(1)} %get-tuple-element.83.ggate_ref) | copy-start | bytes 1179652
  97.1 6.3 %collective-permute-start.10 = (bf16[12,192,256]{2,1,0:T(8,128)(2,1)}, bf16[12,192,256]{2,1,0:T(8,128)(2,1)S(1)}, u32[]{:S(2)}, u32[]{:S(2)}) collective-permute-start(bf16[12,192,256]{2,1,0:T(8,128)(2,1)} %get-tuple-element.76), channel_id=1, source_target_pairs={{0,8},{8,0},{1,9},{9,1},{2,10},{10,2},{3,11},{11,3},{4,12},{12,4},... | collective-permute-start | bytes 3538952 | tf_op jit(solution)/shard_map/ppermute | solution.py:501
  97.8 13.6 %all-to-all-start.3 = ((bf16[16,64,128]{2,1,0:T(8,128)(2,1)}), bf16[16,64,128]{2,1,0:T(8,128)(2,1)}, u32[]{:S(2)}, u32[]{:S(2)}) async-start(bf16[16,64,128]{2,1,0:T(8,128)(2,1)} %fusion.2), calls=%async_computation.3 | async-start | bytes 524288 | tf_op jit(solution)/shard_map/all_to_all | solution.py:498
  103.3 1.7 copy-start.4
  105.0 1.1 copy-start.7
  106.1 1.0 copy-start.10
  109.7 1.7 copy-start.2
  111.4 57.0 %all-to-all-start.4 = ((bf16[64,32,768]{2,1,0:T(8,128)(2,1)}), bf16[64,32,768]{2,1,0:T(8,128)(2,1)S(1)}, u32[]{:S(2)}, u32[]{:S(2)}) async-start(bf16[64,32,768]{2,1,0:T(8,128)(2,1)} %copy-done.2), calls=%async_computation.4 | async-start | bytes 6291456 | tf_op jit(solution)/shard_map/all_to_all | solution.py:511
  169.5 1.3 collective-permute-start.11

commit v9 on v8

--- a/solution.py
+++ b/solution.py
@@ -126,6 +126,7 @@
                 mine = mine_ref[(own_x - x + 4) % 4, t]
                 other = other_ref[(own_x - x + 4) % 4, t]
                 pieces += [jnp.where(core == 0, mine, other), jnp.where(core == 0, other, mine)]
+            gb_s[t * TOK : (t + 1) * TOK] = jnp.zeros((TOK, KEYS), F32)
             bias_s[t * TOK : (t + 1) * TOK] = jnp.concatenate(pieces, axis=0).astype(F32) * LOG2E
 
     whole = jnp.concatenate([x_ref[t] for t in range(8)], axis=1)
@@ -165,20 +166,13 @@
     dscores = [e * dot(l, va_s[...]) for e, l in zip(expd, left)]
     dscores_low = [d.astype(BF) for d in dscores]
 
-    @pl.when(sample == 0)
+    for p, d in zip(every, dscores):
+        gb_s[p] = gb_s[p] + d
+
+    @pl.when(sample == 3)
     def _():
         for p, d in zip(every, dscores):
-            gb_s[p] = d
-
-    @pl.when((sample > 0) & (sample < 3))
-    def _():
-        for p, d in zip(every, dscores):
-            gb_s[p] = gb_s[p] + d
-
-    @pl.when(sample == 3)
-    def _():
-        for p, d in zip(every, dscores):
-            total = (gb_s[p] + d).astype(BF)
+            total = gb_s[p].astype(BF)
             for t in range(rows // TOK):
                 for n in range(8):
                     tile = total[t * TOK : (t + 1) * TOK, n * TOK : (n + 1) * TOK]

time: 172 us -> 172 us (level)
  no operation moved by 1% of the time
where the time goes in v9:
time: 172 us; the launch traced here: 171 us
  waiting for transfers between devices  58.7 us (34%)
  starting transfers between devices  45.2 us (26%)
  Pallas kernels  39.1 us (23%)
  local copies, waits for them, and re-layouts  17.9 us (10%)
  other arithmetic  6.48 us (4%)
  matrix products  2.52 us (1%)
    all_to_all x1, waiting for transfers between devices, per_device(): chunks = lax.all_to_all(chunks, ('x', 'zh', 'zl', 'y'), 0, 0, tiled=True)  34.1 us
    pallas_call x1, Pallas kernels, attention(): pl.pallas_call(functools.partial(attention_kernel, blocks=blocks), grid_s...  19.3 us
    unnamed x33, local copies, waits for them, and re-layouts  13.3 us
    ppermute x3, waiting for transfers between devices, per_device(): pieces = [bias] + [lax.ppermute(bias, 'x', turn(s)) for s in (1, 2, 3)]  10.9 us
    all_to_all x1, starting transfers between devices, per_device(): chunks = lax.all_to_all(chunks, ('x', 'zh', 'zl', 'y'), 0, 0, tiled=True)  9.86 us
    all_to_all x1, waiting for transfers between devices, per_device(): back = lax.all_to_all(result, PLANE, 0, 0, tiled=True)  7.59 us
    pallas_call x1, Pallas kernels, front(): pl.pallas_call(front_kernel, grid=(4,), in_specs=[whole((flat, C)), whole...  7.25 us
    all_to_all x1, starting transfers between devices, per_device(): received = lax.all_to_all(send, PLANE, 0, 0, tiled=True)  6.52 us
  transfers between devices with their start and end apart: 17, of which 10 were waited for; matrix products, arithmetic and copies ran while one was open for 7% of the time, Pallas kernels for 11%

profile of v9, /device:TPU:103, one launch (start us, length us, event | category | flops | bytes accessed | tf_op | source)
XLA Modules:
  0.0 170.7 jit_solution(4045765704071405328)
XLA Ops:
  0.6 1.7 constant_dynamic-slice_fusion
  2.3 5.4 %all-to-all-start = ((bf16[8,16,1024]{2,1,0:T(8,128)(2,1)}), bf16[8,16,1024]{2,1,0:T(8,128)(2,1)S(1)}, u32[]{:S(2)}, u32[]{:S(2)}) async-start(bf16[8,16,1024]{2,1,0:T(8,128)(2,1)} %constant_dynamic-slice_fusion), calls=%async_computation | async-start | bytes 524288 | tf_op jit(solution)/shard_map/all_to_all | solution.py:455
  7.7 7.2 %front.1 = (bf16[256,768]{1,0:T(8,128)(2,1)}, f32[256,1]{1,0:T(8,128)}, f32[256,1]{1,0:T(8,128)}, bf16[16,192,256]{2,1,0:T(8,128)(2,1)}, f32[768,256]{1,0:T(8,128)}, /*index=5*/bf16[768,256]{1,0:T(8,128)(2,1)}) custom-call(bf16[256,768]{1,0:T(8,128)(2,1)} %bitcast.35, f32[768]{0:T(1024)} %gain_ref.5, bf16[768,3072]{1,0:T(8,128)(2,1)} %w_ref.5, ...), custom_call_target="tpu_custom_call" | custom-call | flops 1509949440 | bytes 11534336 | tf_op jit(solution)/shard_map/front/pallas_call | solution.py:93
  15.0 6.5 %all-to-all-start.1 = ((bf16[16,192,256]{2,1,0:T(8,128)(2,1)}), bf16[16,192,256]{2,1,0:T(8,128)(2,1)}, u32[]{:S(2)}, u32[]{:S(2)}) async-start(bf16[16,192,256]{2,1,0:T(8,128)(2,1)} %get-tuple-element.48), calls=%async_computation.1 | async-start | bytes 3145728 | tf_op jit(solution)/shard_map/all_to_all | solution.py:464
  21.5 0.5 collective-permute-start.2
  22.0 0.8 collective-permute-start.1
  22.9 1.8 %collective-permute-start = (bf16[8,16,1024]{2,1,0:T(8,128)(2,1)S(1)}, bf16[8,16,1024]{2,1,0:T(8,128)(2,1)S(1)}, u32[]{:S(2)}, u32[]{:S(2)}) collective-permute-start(bf16[8,16,1024]{2,1,0:T(8,128)(2,1)S(1)} %all-to-all-done), channel_id=1, source_target_pairs={{0,32},{32,64},{64,96},{96,0},{1,33},{33,65},{65,97},{97,1},{2,34}... | collective-permute-start | bytes 786440 | tf_op jit(solution)/shard_map/ppermute | solution.py:463
  25.2 5.2 %collective-permute-done.2 = bf16[8,16,1024]{2,1,0:T(8,128)(2,1)S(1)} collective-permute-done((bf16[8,16,1024]{2,1,0:T(8,128)(2,1)S(1)}, bf16[8,16,1024]{2,1,0:T(8,128)(2,1)S(1)}, u32[]{:S(2)}, u32[]{:S(2)}) %collective-permute-start.2) | collective-permute-done | bytes 262176 | tf_op jit(solution)/shard_map/ppermute | solution.py:463
  30.3 2.8 %collective-permute-done.1 = bf16[8,16,1024]{2,1,0:T(8,128)(2,1)S(1)} collective-permute-done((bf16[8,16,1024]{2,1,0:T(8,128)(2,1)S(1)}, bf16[8,16,1024]{2,1,0:T(8,128)(2,1)S(1)}, u32[]{:S(2)}, u32[]{:S(2)}) %collective-permute-start.1) | collective-permute-done | bytes 262176 | tf_op jit(solution)/shard_map/ppermute | solution.py:463
  33.2 2.9 %collective-permute-done = bf16[8,16,1024]{2,1,0:T(8,128)(2,1)S(1)} collective-permute-done((bf16[8,16,1024]{2,1,0:T(8,128)(2,1)S(1)}, bf16[8,16,1024]{2,1,0:T(8,128)(2,1)S(1)}, u32[]{:S(2)}, u32[]{:S(2)}) %collective-permute-start) | collective-permute-done | bytes 262176 | tf_op jit(solution)/shard_map/ppermute | solution.py:463
  36.2 1.6 collective-permute-start.5
  38.4 0.6 pad_add_fusion.place_ref
  39.0 1.8 %collective-permute-done.4.sco_ref = bf16[256,768]{1,0:T(8,128)(2,1)S(1)} collective-permute-done((bf16[256,768]{1,0:T(8,128)(2,1)S(1)}, bf16[256,768]{1,0:T(8,128)(2,1)S(1)}, u32[]{:S(2)}, u32[]{:S(2)}) %collective-permute-start.4) | collective-permute-done | bytes 393248 | tf_op jit(solution)/shard_map/ppermute | solution.py:470
  41.4 19.3 %attention.1 = (bf16[16,192,256]{2,1,0:T(8,128)(2,1)}, bf16[4,16,64,128]{3,2,1,0:T(8,128)(2,1)}, bf16[4,16,64,128]{3,2,1,0:T(8,128)(2,1)}) custom-call(s32[2]{0:T(128)} %pad_add_fusion.place_ref, bf16[16,192,256]{2,1,0:T(8,128)(2,1)} %all-to-all-done.1.x_ref, bf16[4,8,16,1024]{3,2,1,0:T(8,128)(2,1)} %copy-done.15, ...), custom_call_target="tpu_custom_call" | custom-call | flops 12884901888 | bytes 8388608 | tf_op jit(solution)/shard_map/attention/pallas_call | solution.py:204
  60.7 3.3 %collective-permute-start.6 = (bf16[4,16,64,128]{3,2,1,0:T(8,128)(2,1)}, bf16[4,16,64,128]{3,2,1,0:T(8,128)(2,1)}, u32[]{:S(2)}, u32[]{:S(2)}) collective-permute-start(bf16[4,16,64,128]{3,2,1,0:T(8,128)(2,1)} %get-tuple-element.64), channel_id=1, source_target_pairs={{0,8},{8,0},{1,9},{9,1},{2,10},{10,2},{3,11},{11,3},{4,12},{12,4},... | collective-permute-start | bytes 3145736 | tf_op jit(solution)/shard_map/ppermute | solution.py:485
  64.0 5.5 %all-to-all-start.2 = ((bf16[16,192,256]{2,1,0:T(8,128)(2,1)}), bf16[16,192,256]{2,1,0:T(8,128)(2,1)S(1)}, u32[]{:S(2)}, u32[]{:S(2)}) async-start(bf16[16,192,256]{2,1,0:T(8,128)(2,1)} %get-tuple-element.58), calls=%async_computation.2 | async-start | bytes 3145728 | tf_op jit(solution)/shard_map/all_to_all | solution.py:480
  69.4 1.7 fusion.4
  71.1 0.4 collective-permute-start.7
  71.6 1.1 collective-permute-start.9
  72.7 1.1 collective-permute-start.8
  73.8 2.3 %copy-done = bf16[768,3072]{1,0:T(8,128)(2,1)S(1)} copy-done((bf16[768,3072]{1,0:T(8,128)(2,1)S(1)}, bf16[768,3072]{1,0:T(8,128)(2,1)}, u32[]{:S(2)}) %copy-start) | copy-done | bytes 4718616
  76.1 2.6 %stage.1 = (bf16[8,192,768]{2,1,0:T(8,128)(2,1)S(1)}, bf16[512,768]{1,0:T(8,128)(2,1)S(1)}, bf16[8,64,512]{2,1,0:T(8,128)(2,1)S(1)}) custom-call(s32[1]{0:T(128)} %bitcast.core_ref, bf16[768,3072]{1,0:T(8,128)(2,1)S(1)} %copy-done, bf16[256,768]{1,0:T(8,128)(2,1)S(1)} %copy-done.11, bf16[256,768]{1,0:T(8,128)(2,1)S(1)} %collective-permute-done.4.sco_ref, ...), custom_call_target="tpu_custom_call" | custom-call | flops 4718592 | bytes 7340032 | tf_op jit(solution)/shard_map/stage/pallas_call | solution.py:256
  78.7 1.4 copy-done.3
  80.2 0.9 copy-done.6
  81.1 0.8 copy-done.9
  81.9 3.4 %collective-permute-done.8 = bf16[16,64,128]{2,1,0:T(8,128)(2,1)S(1)} collective-permute-done((bf16[16,64,128]{2,1,0:T(8,128)(2,1)S(1)}, bf16[16,64,128]{2,1,0:T(8,128)(2,1)S(1)}, u32[]{:S(2)}, u32[]{:S(2)}) %collective-permute-start.8) | collective-permute-done | bytes 262176 | tf_op jit(solution)/shard_map/ppermute | solution.py:489
  85.3 1.9 %fusion.2 = bf16[16,64,128]{2,1,0:T(8,128)(2,1)} fusion(bf16[16,64,128]{2,1,0:T(8,128)(2,1)S(1)} %collective-permute-done.9, bf16[16,64,128]{2,1,0:T(8,128)(2,1)S(1)} %collective-permute-done.8, bf16[16,64,128]{2,1,0:T(8,128)(2,1)S(1)} %collective-permute-done.7, bf16[4,16,64,128]{3,2,1,0:T(8,128)(2,1)} %collective-permute-done.6, ...), kind=kLoop, calls=%fused_computation.7 | loop fusion | flops 1572864 | bytes 1572864 | tf_op jit(solution)/shard_map/convert_element_type | solution.py:491
  87.2 7.6 %all-to-all-done.2.back_ref = bf16[16,192,256]{2,1,0:T(8,128)(2,1)S(1)} async-done(((bf16[16,192,256]{2,1,0:T(8,128)(2,1)}), bf16[16,192,256]{2,1,0:T(8,128)(2,1)S(1)}, u32[]{:S(2)}, u32[]{:S(2)}) %all-to-all-start.2) | async-done | bytes 1572896 | tf_op jit(solution)/shard_map/all_to_all | solution.py:480
  94.8 1.5 gate.1
  96.3 0.8 collective-permute-start.10
  97.1 5.5 %all-to-all-start.3 = ((bf16[16,64,128]{2,1,0:T(8,128)(2,1)}), bf16[16,64,128]{2,1,0:T(8,128)(2,1)}, u32[]{:S(2)}, u32[]{:S(2)}) async-start(bf16[16,64,128]{2,1,0:T(8,128)(2,1)} %fusion.2), calls=%async_computation.3 | async-start | bytes 524288 | tf_op jit(solution)/shard_map/all_to_all | solution.py:492
  102.6 1.7 copy-done.4
  104.3 1.1 copy-done.7
  105.4 1.0 copy-done.10
  106.5 2.5 %weight_grads.1 = bf16[64,32,768]{2,1,0:T(8,128)(2,1)S(1)} custom-call(s32[1]{0:T(128)} %bitcast.core_ref, bf16[16,192,256]{2,1,0:T(8,128)(2,1)S(1)} %all-to-all-done.2.back_ref, bf16[4,192,256]{2,1,0:T(8,128)(2,1)S(1)} %get-tuple-element.83.ggate_ref, bf16[12,192,256]{2,1,0:T(8,128)(2,1)S(1)} %collective-permute-done.10.o_ref, ...), custom_call_target="tpu_custom_call" | custom-call | flops 1610612736 | bytes 8388608 | tf_op jit(solution)/shard_map/weight_grads/pallas_call | solution.py:424
  109.0 1.7 copy-done.2
  110.7 9.9 %all-to-all-start.4 = ((bf16[64,32,768]{2,1,0:T(8,128)(2,1)}), bf16[64,32,768]{2,1,0:T(8,128)(2,1)S(1)}, u32[]{:S(2)}, u32[]{:S(2)}) async-start(bf16[64,32,768]{2,1,0:T(8,128)(2,1)} %copy-done.2), calls=%async_computation.4 | async-start | bytes 6291456 | tf_op jit(solution)/shard_map/all_to_all | solution.py:505
  120.6 1.2 fusion.8
  121.8 1.1 pad_maximum_fusion.1
  122.8 2.3 %copy.14 = f32[16,128,64]{1,2,0:T(8,128)} copy(f32[16,128,64]{2,1,0:T(8,128)} %pad_maximum_fusion.1) | data formatting | bytes 1048576
  125.2 5.9 %input_grad.1 = bf16[256,768]{1,0:T(8,128)(2,1)} custom-call(bf16[16,192,256]{2,1,0:T(8,128)(2,1)} %copy-done.1, bf16[4,192,256]{2,1,0:T(8,128)(2,1)} %copy-done.5, bf16[768,3072]{1,0:T(8,128)(2,1)} %w_ref.5, bf16[256,768]{1,0:T(8,128)(2,1)} %bitcast.36, f32[256,1]{1,0:T(8,128)} %get-tuple-element.84.mean_ref, f32[256,1]{1,0:T(8,128)} %get-tuple-element.85.inv_ref, ...), custom_call_target="tpu_custom_call" | custom-call | flops 1207959552 | bytes 8388608 | tf_op jit(solution)/shard_map/input_grad/pallas_call | solution.py:355
  131.1 2.5 %convolution_convert_fusion = bf16[256,768]{1,0:T(8,128)(2,1)} fusion(bf16[768,256]{1,0:T(8,128)(2,1)S(1)} %get-tuple-element.82.gated_ref, bf16[768,768]{1,0:T(8,128)(2,1)} %wout_ref.1), kind=kOutput, calls=%fused_computation.1 | convolution fusion | flops 302186496 | bytes 1966080 | tf_op jit(solution)/shard_map/cr,cd->rd/dot_general | solution.py:504
  133.6 34.1 %all-to-all-done.4 = bf16[64,32,768]{2,1,0:T(8,128)(2,1)S(1)} async-done(((bf16[64,32,768]{2,1,0:T(8,128)(2,1)}), bf16[64,32,768]{2,1,0:T(8,128)(2,1)S(1)}, u32[]{:S(2)}, u32[]{:S(2)}) %all-to-all-start.4) | async-done | bytes 3145760 | tf_op jit(solution)/shard_map/all_to_all | solution.py:505
  167.7 0.5 convert_reduce_fusion
  168.2 0.6 slice_bitcast_fusion
  168.8 0.5 collective-permute-start.11
  169.3 0.6 slice_bitcast_fusion.1
  170.1 0.6 add.67
  (42 shorter events, 2.1 us)
Async XLA Ops:
  2.3 12.6 %all-to-all-start = ((bf16[8,16,1024]{2,1,0:T(8,128)(2,1)}), bf16[8,16,1024]{2,1,0:T(8,128)(2,1)S(1)}, u32[]{:S(2)}, u32[]{:S(2)}) async-start(bf16[8,16,1024]{2,1,0:T(8,128)(2,1)} %constant_dynamic-slice_fusion), calls=%async_computation | async-start | bytes 524288 | tf_op jit(solution)/shard_map/all_to_all | solution.py:455
  14.9 9.7 %copy-start.14 = (bf16[2,128,768]{2,1,0:T(8,128)(2,1)S(1)}, bf16[2,128,768]{2,1,0:T(8,128)(2,1)}, u32[]{:S(2)}) copy-start(bf16[2,128,768]{2,1,0:T(8,128)(2,1)} %param.11) | copy-start | bytes 1179652
  15.0 26.4 %all-to-all-start.1 = ((bf16[16,192,256]{2,1,0:T(8,128)(2,1)}), bf16[16,192,256]{2,1,0:T(8,128)(2,1)}, u32[]{:S(2)}, u32[]{:S(2)}) async-start(bf16[16,192,256]{2,1,0:T(8,128)(2,1)} %get-tuple-element.48), calls=%async_computation.1 | async-start | bytes 3145728 | tf_op jit(solution)/shard_map/all_to_all | solution.py:464
  21.5 8.9 %collective-permute-start.2 = (bf16[8,16,1024]{2,1,0:T(8,128)(2,1)S(1)}, bf16[8,16,1024]{2,1,0:T(8,128)(2,1)S(1)}, u32[]{:S(2)}, u32[]{:S(2)}) collective-permute-start(bf16[8,16,1024]{2,1,0:T(8,128)(2,1)S(1)} %all-to-all-done), channel_id=1, source_target_pairs={{0,96},{32,0},{64,32},{96,64},{1,97},{33,1},{65,33},{97,65},{2,98}... | collective-permute-start | bytes 786440 | tf_op jit(solution)/shard_map/ppermute | solution.py:463
  22.0 11.1 %collective-permute-start.1 = (bf16[8,16,1024]{2,1,0:T(8,128)(2,1)S(1)}, bf16[8,16,1024]{2,1,0:T(8,128)(2,1)S(1)}, u32[]{:S(2)}, u32[]{:S(2)}) collective-permute-start(bf16[8,16,1024]{2,1,0:T(8,128)(2,1)S(1)} %all-to-all-done), channel_id=1, source_target_pairs={{0,64},{32,96},{64,0},{96,32},{1,65},{33,97},{65,1},{97,33},{2,66}... | collective-permute-start | bytes 786440 | tf_op jit(solution)/shard_map/ppermute | solution.py:463
  22.9 13.2 %collective-permute-start = (bf16[8,16,1024]{2,1,0:T(8,128)(2,1)S(1)}, bf16[8,16,1024]{2,1,0:T(8,128)(2,1)S(1)}, u32[]{:S(2)}, u32[]{:S(2)}) collective-permute-start(bf16[8,16,1024]{2,1,0:T(8,128)(2,1)S(1)} %all-to-all-done), channel_id=1, source_target_pairs={{0,32},{32,64},{64,96},{96,0},{1,33},{33,65},{65,97},{97,1},{2,34}... | collective-permute-start | bytes 786440 | tf_op jit(solution)/shard_map/ppermute | solution.py:463
  25.1 12.8 %copy-start.11 = (bf16[256,768]{1,0:T(8,128)(2,1)S(1)}, bf16[256,768]{1,0:T(8,128)(2,1)}, u32[]{:S(2)}) copy-start(bf16[256,768]{1,0:T(8,128)(2,1)} %get-tuple-element.65.sc_ref) | copy-start | bytes 1179652
  36.2 5.2 %copy-start.15 = (bf16[4,8,16,1024]{3,2,1,0:T(8,128)(2,1)}, bf16[4,8,16,1024]{3,2,1,0:T(8,128)(2,1)S(1)}, u32[]{:S(2)}) copy-start(bf16[4,8,16,1024]{3,2,1,0:T(8,128)(2,1)S(1)} %pad_maximum_fusion.mine_ref) | copy-start | bytes 3145732
  36.2 4.9 %collective-permute-start.5 = (bf16[4,8,16,1024]{3,2,1,0:T(8,128)(2,1)S(1)}, bf16[4,8,16,1024]{3,2,1,0:T(8,128)(2,1)}, u32[]{:S(2)}, u32[]{:S(2)}) collective-permute-start(bf16[4,8,16,1024]{3,2,1,0:T(8,128)(2,1)S(1)} %pad_maximum_fusion.mine_ref), channel_id=1, source_target_pairs={{0,8},{8,0},{1,9},{9,1},{2,10},{10,2},{3,11},{11,3},{4,12},{12,4},... | collective-permute-start | bytes 3145736 | tf_op jit(solution)/shard_map/ppermute | solution.py:474
  37.9 2.8 %collective-permute-start.4 = (bf16[256,768]{1,0:T(8,128)(2,1)S(1)}, bf16[256,768]{1,0:T(8,128)(2,1)S(1)}, u32[]{:S(2)}, u32[]{:S(2)}) collective-permute-start(bf16[256,768]{1,0:T(8,128)(2,1)S(1)} %copy-done.11), channel_id=1, source_target_pairs={{0,8},{8,0},{1,9},{9,1},{2,10},{10,2},{3,11},{11,3},{4,12},{12,4},... | collective-permute-start | bytes 1179656 | tf_op jit(solution)/shard_map/ppermute | solution.py:470
  38.0 3.1 %collective-permute-start.3 = (bf16[8,64,256]{2,1,0:T(8,128)(2,1)S(1)}, bf16[8,64,256]{2,1,0:T(8,128)(2,1)S(1)}, u32[]{:S(2)}, u32[]{:S(2)}) collective-permute-start(bf16[8,64,256]{2,1,0:T(8,128)(2,1)S(1)} %get-tuple-element.50), channel_id=1, source_target_pairs={{0,8},{8,0},{1,9},{9,1},{2,10},{10,2},{3,11},{11,3},{4,12},{12,4},... | collective-permute-start | bytes 786440 | tf_op jit(solution)/shard_map/ppermute | solution.py:475
  60.7 8.7 %collective-permute-start.6 = (bf16[4,16,64,128]{3,2,1,0:T(8,128)(2,1)}, bf16[4,16,64,128]{3,2,1,0:T(8,128)(2,1)}, u32[]{:S(2)}, u32[]{:S(2)}) collective-permute-start(bf16[4,16,64,128]{3,2,1,0:T(8,128)(2,1)} %get-tuple-element.64), channel_id=1, source_target_pairs={{0,8},{8,0},{1,9},{9,1},{2,10},{10,2},{3,11},{11,3},{4,12},{12,4},... | collective-permute-start | bytes 3145736 | tf_op jit(solution)/shard_map/ppermute | solution.py:485
  64.0 30.9 %all-to-all-start.2 = ((bf16[16,192,256]{2,1,0:T(8,128)(2,1)}), bf16[16,192,256]{2,1,0:T(8,128)(2,1)S(1)}, u32[]{:S(2)}, u32[]{:S(2)}) async-start(bf16[16,192,256]{2,1,0:T(8,128)(2,1)} %get-tuple-element.58), calls=%async_computation.2 | async-start | bytes 3145728 | tf_op jit(solution)/shard_map/all_to_all | solution.py:480
  71.1 10.7 %collective-permute-start.7 = (bf16[16,64,128]{2,1,0:T(8,128)(2,1)S(1)}, bf16[16,64,128]{2,1,0:T(8,128)(2,1)S(1)}, u32[]{:S(2)}, u32[]{:S(2)}) collective-permute-start(bf16[16,64,128]{2,1,0:T(8,128)(2,1)S(1)} %get-tuple-element.100), channel_id=1, source_target_pairs={{0,32},{32,64},{64,96},{96,0},{1,33},{33,65},{65,97},{97,1},{2,34}... | collective-permute-start | bytes 786440 | tf_op jit(solution)/shard_map/ppermute | solution.py:489
  71.6 10.3 %collective-permute-start.9 = (bf16[16,64,128]{2,1,0:T(8,128)(2,1)S(1)}, bf16[16,64,128]{2,1,0:T(8,128)(2,1)S(1)}, u32[]{:S(2)}, u32[]{:S(2)}) collective-permute-start(bf16[16,64,128]{2,1,0:T(8,128)(2,1)S(1)} %get-tuple-element.101), channel_id=1, source_target_pairs={{0,96},{32,0},{64,32},{96,64},{1,97},{33,1},{65,33},{97,65},{2,98}... | collective-permute-start | bytes 786440 | tf_op jit(solution)/shard_map/ppermute | solution.py:489
  72.7 12.6 %collective-permute-start.8 = (bf16[16,64,128]{2,1,0:T(8,128)(2,1)S(1)}, bf16[16,64,128]{2,1,0:T(8,128)(2,1)S(1)}, u32[]{:S(2)}, u32[]{:S(2)}) collective-permute-start(bf16[16,64,128]{2,1,0:T(8,128)(2,1)S(1)} %get-tuple-element.102), channel_id=1, source_target_pairs={{0,64},{32,96},{64,0},{96,32},{1,65},{33,97},{65,1},{97,33},{2,66}... | collective-permute-start | bytes 786440 | tf_op jit(solution)/shard_map/ppermute | solution.py:489
  73.8 2.3 %copy-start = (bf16[768,3072]{1,0:T(8,128)(2,1)S(1)}, bf16[768,3072]{1,0:T(8,128)(2,1)}, u32[]{:S(2)}) copy-start(bf16[768,3072]{1,0:T(8,128)(2,1)} %w_ref.5) | copy-start | bytes 14155780
  78.7 1.5 copy-start.3
  80.2 0.9 copy-start.6
  81.1 0.8 copy-start.9
  81.9 13.0 %copy-start.8 = (f32[768,256]{1,0:T(8,128)S(1)}, f32[768,256]{1,0:T(8,128)}, u32[]{:S(2)}) copy-start(f32[768,256]{1,0:T(8,128)} %get-tuple-element.73.gate_ref) | copy-start | bytes 2359300
  81.9 13.0 %copy-start.12 = (bf16[768,256]{1,0:T(8,128)(2,1)S(1)}, bf16[768,256]{1,0:T(8,128)(2,1)}, u32[]{:S(2)}) copy-start(bf16[768,256]{1,0:T(8,128)(2,1)} %get-tuple-element.74.gg_ref) | copy-start | bytes 1179652
  94.8 7.8 %copy-start.1 = (bf16[16,192,256]{2,1,0:T(8,128)(2,1)}, bf16[16,192,256]{2,1,0:T(8,128)(2,1)S(1)}, u32[]{:S(2)}) copy-start(bf16[16,192,256]{2,1,0:T(8,128)(2,1)S(1)} %all-to-all-done.2.back_ref) | copy-start | bytes 4718596
  94.8 7.8 %copy-start.13 = (f32[768]{0:T(1024)S(1)}, f32[768]{0:T(1024)}, u32[]{:S(2)}) copy-start(f32[768]{0:T(1024)} %gain_ref.5) | copy-start | bytes 9220
  96.3 12.7 %copy-start.5 = (bf16[4,192,256]{2,1,0:T(8,128)(2,1)}, bf16[4,192,256]{2,1,0:T(8,128)(2,1)S(1)}, u32[]{:S(2)}) copy-start(bf16[4,192,256]{2,1,0:T(8,128)(2,1)S(1)} %get-tuple-element.83.ggate_ref) | copy-start | bytes 1179652
  96.3 6.3 %collective-permute-start.10 = (bf16[12,192,256]{2,1,0:T(8,128)(2,1)}, bf16[12,192,256]{2,1,0:T(8,128)(2,1)S(1)}, u32[]{:S(2)}, u32[]{:S(2)}) collective-permute-start(bf16[12,192,256]{2,1,0:T(8,128)(2,1)} %get-tuple-element.76), channel_id=1, source_target_pairs={{0,8},{8,0},{1,9},{9,1},{2,10},{10,2},{3,11},{11,3},{4,12},{12,4},... | collective-permute-start | bytes 3538952 | tf_op jit(solution)/shard_map/ppermute | solution.py:495
  97.1 13.6 %all-to-all-start.3 = ((bf16[16,64,128]{2,1,0:T(8,128)(2,1)}), bf16[16,64,128]{2,1,0:T(8,128)(2,1)}, u32[]{:S(2)}, u32[]{:S(2)}) async-start(bf16[16,64,128]{2,1,0:T(8,128)(2,1)} %fusion.2), calls=%async_computation.3 | async-start | bytes 524288 | tf_op jit(solution)/shard_map/all_to_all | solution.py:492
  102.6 1.7 copy-start.4
  104.3 1.1 copy-start.7
  105.4 1.0 copy-start.10
  109.0 1.7 copy-start.2
  110.7 57.0 %all-to-all-start.4 = ((bf16[64,32,768]{2,1,0:T(8,128)(2,1)}), bf16[64,32,768]{2,1,0:T(8,128)(2,1)S(1)}, u32[]{:S(2)}, u32[]{:S(2)}) async-start(bf16[64,32,768]{2,1,0:T(8,128)(2,1)} %copy-done.2), calls=%async_computation.4 | async-start | bytes 6291456 | tf_op jit(solution)/shard_map/all_to_all | solution.py:505
  168.8 1.3 collective-permute-start.11

commit v10 on v9

--- a/solution.py
+++ b/solution.py
@@ -159,10 +159,11 @@
     left = []
     for o, g in zip(out, gscaled):
         delta = jnp.sum(o * g, axis=1, keepdims=True)
-        delta_hi = delta.astype(BF).astype(F32)
-        left.append(
-            jnp.where(lane == DH, -delta_hi, jnp.where(lane == DH + 1, delta_hi - delta, g)).astype(BF)
-        )
+        high = delta.astype(BF).astype(F32)
+        middle = (delta - high).astype(BF).astype(F32)
+        low = delta - high - middle
+        tail = jnp.where(lane == DH, high, jnp.where(lane == DH + 1, middle, low))
+        left.append(jnp.where((lane >= DH) & (lane <= DH + 2), -tail, g).astype(BF))
     dscores = [e * dot(l, va_s[...]) for e, l in zip(expd, left)]
     dscores_low = [d.astype(BF) for d in dscores]
 

time: 172 us -> 172 us (level)
  no operation moved by 1% of the time
where the time goes in v10:
time: 172 us; the launch traced here: 171 us
  waiting for transfers between devices  58.7 us (34%)
  starting transfers between devices  45.2 us (26%)
  Pallas kernels  39.3 us (23%)
  local copies, waits for them, and re-layouts  17.9 us (10%)
  other arithmetic  6.48 us (4%)
  matrix products  2.52 us (1%)
    all_to_all x1, waiting for transfers between devices, per_device(): chunks = lax.all_to_all(chunks, ('x', 'zh', 'zl', 'y'), 0, 0, tiled=True)  34.1 us
    pallas_call x1, Pallas kernels, attention(): pl.pallas_call(functools.partial(attention_kernel, blocks=blocks), grid_s...  19.5 us
    unnamed x33, local copies, waits for them, and re-layouts  13.3 us
    ppermute x3, waiting for transfers between devices, per_device(): pieces = [bias] + [lax.ppermute(bias, 'x', turn(s)) for s in (1, 2, 3)]  10.9 us
    all_to_all x1, starting transfers between devices, per_device(): chunks = lax.all_to_all(chunks, ('x', 'zh', 'zl', 'y'), 0, 0, tiled=True)  9.84 us
    all_to_all x1, waiting for transfers between devices, per_device(): back = lax.all_to_all(result, PLANE, 0, 0, tiled=True)  7.62 us
    pallas_call x1, Pallas kernels, front(): pl.pallas_call(front_kernel, grid=(4,), in_specs=[whole((flat, C)), whole...  7.25 us
    all_to_all x1, starting transfers between devices, per_device(): received = lax.all_to_all(send, PLANE, 0, 0, tiled=True)  6.52 us
  transfers between devices with their start and end apart: 17, of which 10 were waited for; matrix products, arithmetic and copies ran while one was open for 7% of the time, Pallas kernels for 11%

profile of v10, /device:TPU:103, one launch (start us, length us, event | category | flops | bytes accessed | tf_op | source)
XLA Modules:
  0.0 171.0 jit_solution(6628166036419725142)
XLA Ops:
  0.6 1.7 constant_dynamic-slice_fusion
  2.3 5.4 %all-to-all-start = ((bf16[8,16,1024]{2,1,0:T(8,128)(2,1)}), bf16[8,16,1024]{2,1,0:T(8,128)(2,1)S(1)}, u32[]{:S(2)}, u32[]{:S(2)}) async-start(bf16[8,16,1024]{2,1,0:T(8,128)(2,1)} %constant_dynamic-slice_fusion), calls=%async_computation | async-start | bytes 524288 | tf_op jit(solution)/shard_map/all_to_all | solution.py:456
  7.7 7.2 %front.1 = (bf16[256,768]{1,0:T(8,128)(2,1)}, f32[256,1]{1,0:T(8,128)}, f32[256,1]{1,0:T(8,128)}, bf16[16,192,256]{2,1,0:T(8,128)(2,1)}, f32[768,256]{1,0:T(8,128)}, /*index=5*/bf16[768,256]{1,0:T(8,128)(2,1)}) custom-call(bf16[256,768]{1,0:T(8,128)(2,1)} %bitcast.35, f32[768]{0:T(1024)} %gain_ref.5, bf16[768,3072]{1,0:T(8,128)(2,1)} %w_ref.5, ...), custom_call_target="tpu_custom_call" | custom-call | flops 1509949440 | bytes 11534336 | tf_op jit(solution)/shard_map/front/pallas_call | solution.py:93
  15.0 6.5 %all-to-all-start.1 = ((bf16[16,192,256]{2,1,0:T(8,128)(2,1)}), bf16[16,192,256]{2,1,0:T(8,128)(2,1)}, u32[]{:S(2)}, u32[]{:S(2)}) async-start(bf16[16,192,256]{2,1,0:T(8,128)(2,1)} %get-tuple-element.48), calls=%async_computation.1 | async-start | bytes 3145728 | tf_op jit(solution)/shard_map/all_to_all | solution.py:465
  21.5 0.5 collective-permute-start.2
  22.0 0.8 collective-permute-start.1
  22.9 1.8 %collective-permute-start = (bf16[8,16,1024]{2,1,0:T(8,128)(2,1)S(1)}, bf16[8,16,1024]{2,1,0:T(8,128)(2,1)S(1)}, u32[]{:S(2)}, u32[]{:S(2)}) collective-permute-start(bf16[8,16,1024]{2,1,0:T(8,128)(2,1)S(1)} %all-to-all-done), channel_id=1, source_target_pairs={{0,32},{32,64},{64,96},{96,0},{1,33},{33,65},{65,97},{97,1},{2,34}... | collective-permute-start | bytes 786440 | tf_op jit(solution)/shard_map/ppermute | solution.py:464
  25.2 5.2 %collective-permute-done.2 = bf16[8,16,1024]{2,1,0:T(8,128)(2,1)S(1)} collective-permute-done((bf16[8,16,1024]{2,1,0:T(8,128)(2,1)S(1)}, bf16[8,16,1024]{2,1,0:T(8,128)(2,1)S(1)}, u32[]{:S(2)}, u32[]{:S(2)}) %collective-permute-start.2) | collective-permute-done | bytes 262176 | tf_op jit(solution)/shard_map/ppermute | solution.py:464
  30.3 2.8 %collective-permute-done.1 = bf16[8,16,1024]{2,1,0:T(8,128)(2,1)S(1)} collective-permute-done((bf16[8,16,1024]{2,1,0:T(8,128)(2,1)S(1)}, bf16[8,16,1024]{2,1,0:T(8,128)(2,1)S(1)}, u32[]{:S(2)}, u32[]{:S(2)}) %collective-permute-start.1) | collective-permute-done | bytes 262176 | tf_op jit(solution)/shard_map/ppermute | solution.py:464
  33.2 2.9 %collective-permute-done = bf16[8,16,1024]{2,1,0:T(8,128)(2,1)S(1)} collective-permute-done((bf16[8,16,1024]{2,1,0:T(8,128)(2,1)S(1)}, bf16[8,16,1024]{2,1,0:T(8,128)(2,1)S(1)}, u32[]{:S(2)}, u32[]{:S(2)}) %collective-permute-start) | collective-permute-done | bytes 262176 | tf_op jit(solution)/shard_map/ppermute | solution.py:464
  36.2 1.6 collective-permute-start.5
  38.0 0.4 collective-permute-start.3
  38.4 0.6 pad_add_fusion.place_ref
  39.0 1.8 %collective-permute-done.4.sco_ref = bf16[256,768]{1,0:T(8,128)(2,1)S(1)} collective-permute-done((bf16[256,768]{1,0:T(8,128)(2,1)S(1)}, bf16[256,768]{1,0:T(8,128)(2,1)S(1)}, u32[]{:S(2)}, u32[]{:S(2)}) %collective-permute-start.4) | collective-permute-done | bytes 393248 | tf_op jit(solution)/shard_map/ppermute | solution.py:471
  41.4 19.5 %attention.1 = (bf16[16,192,256]{2,1,0:T(8,128)(2,1)}, bf16[4,16,64,128]{3,2,1,0:T(8,128)(2,1)}, bf16[4,16,64,128]{3,2,1,0:T(8,128)(2,1)}) custom-call(s32[2]{0:T(128)} %pad_add_fusion.place_ref, bf16[16,192,256]{2,1,0:T(8,128)(2,1)} %all-to-all-done.1.x_ref, bf16[4,8,16,1024]{3,2,1,0:T(8,128)(2,1)} %copy-done.15, ...), custom_call_target="tpu_custom_call" | custom-call | flops 12884901888 | bytes 8388608 | tf_op jit(solution)/shard_map/attention/pallas_call | solution.py:205
  60.9 3.3 %collective-permute-start.6 = (bf16[4,16,64,128]{3,2,1,0:T(8,128)(2,1)}, bf16[4,16,64,128]{3,2,1,0:T(8,128)(2,1)}, u32[]{:S(2)}, u32[]{:S(2)}) collective-permute-start(bf16[4,16,64,128]{3,2,1,0:T(8,128)(2,1)} %get-tuple-element.64), channel_id=1, source_target_pairs={{0,8},{8,0},{1,9},{9,1},{2,10},{10,2},{3,11},{11,3},{4,12},{12,4},... | collective-permute-start | bytes 3145736 | tf_op jit(solution)/shard_map/ppermute | solution.py:486
  64.2 5.5 %all-to-all-start.2 = ((bf16[16,192,256]{2,1,0:T(8,128)(2,1)}), bf16[16,192,256]{2,1,0:T(8,128)(2,1)S(1)}, u32[]{:S(2)}, u32[]{:S(2)}) async-start(bf16[16,192,256]{2,1,0:T(8,128)(2,1)} %get-tuple-element.58), calls=%async_computation.2 | async-start | bytes 3145728 | tf_op jit(solution)/shard_map/all_to_all | solution.py:481
  69.7 1.7 fusion.4
  71.8 1.1 collective-permute-start.9
  72.9 1.1 collective-permute-start.8
  74.0 2.3 %copy-done = bf16[768,3072]{1,0:T(8,128)(2,1)S(1)} copy-done((bf16[768,3072]{1,0:T(8,128)(2,1)S(1)}, bf16[768,3072]{1,0:T(8,128)(2,1)}, u32[]{:S(2)}) %copy-start) | copy-done | bytes 4718616
  76.3 2.6 %stage.1 = (bf16[8,192,768]{2,1,0:T(8,128)(2,1)S(1)}, bf16[512,768]{1,0:T(8,128)(2,1)S(1)}, bf16[8,64,512]{2,1,0:T(8,128)(2,1)S(1)}) custom-call(s32[1]{0:T(128)} %bitcast.core_ref, bf16[768,3072]{1,0:T(8,128)(2,1)S(1)} %copy-done, bf16[256,768]{1,0:T(8,128)(2,1)S(1)} %copy-done.11, bf16[256,768]{1,0:T(8,128)(2,1)S(1)} %collective-permute-done.4.sco_ref, ...), custom_call_target="tpu_custom_call" | custom-call | flops 4718592 | bytes 7340032 | tf_op jit(solution)/shard_map/stage/pallas_call | solution.py:257
  79.0 1.4 copy-done.3
  80.4 0.9 copy-done.6
  81.3 0.8 copy-done.9
  82.1 3.4 %collective-permute-done.8 = bf16[16,64,128]{2,1,0:T(8,128)(2,1)S(1)} collective-permute-done((bf16[16,64,128]{2,1,0:T(8,128)(2,1)S(1)}, bf16[16,64,128]{2,1,0:T(8,128)(2,1)S(1)}, u32[]{:S(2)}, u32[]{:S(2)}) %collective-permute-start.8) | collective-permute-done | bytes 262176 | tf_op jit(solution)/shard_map/ppermute | solution.py:490
  85.5 1.9 %fusion.2 = bf16[16,64,128]{2,1,0:T(8,128)(2,1)} fusion(bf16[16,64,128]{2,1,0:T(8,128)(2,1)S(1)} %collective-permute-done.9, bf16[16,64,128]{2,1,0:T(8,128)(2,1)S(1)} %collective-permute-done.8, bf16[16,64,128]{2,1,0:T(8,128)(2,1)S(1)} %collective-permute-done.7, bf16[4,16,64,128]{3,2,1,0:T(8,128)(2,1)} %collective-permute-done.6, ...), kind=kLoop, calls=%fused_computation.7 | loop fusion | flops 1572864 | bytes 1572864 | tf_op jit(solution)/shard_map/convert_element_type | solution.py:492
  87.5 7.6 %all-to-all-done.2.back_ref = bf16[16,192,256]{2,1,0:T(8,128)(2,1)S(1)} async-done(((bf16[16,192,256]{2,1,0:T(8,128)(2,1)}), bf16[16,192,256]{2,1,0:T(8,128)(2,1)S(1)}, u32[]{:S(2)}, u32[]{:S(2)}) %all-to-all-start.2) | async-done | bytes 1572896 | tf_op jit(solution)/shard_map/all_to_all | solution.py:481
  95.1 1.5 gate.1
  96.6 0.8 collective-permute-start.10
  97.4 5.5 %all-to-all-start.3 = ((bf16[16,64,128]{2,1,0:T(8,128)(2,1)}), bf16[16,64,128]{2,1,0:T(8,128)(2,1)}, u32[]{:S(2)}, u32[]{:S(2)}) async-start(bf16[16,64,128]{2,1,0:T(8,128)(2,1)} %fusion.2), calls=%async_computation.3 | async-start | bytes 524288 | tf_op jit(solution)/shard_map/all_to_all | solution.py:493
  102.9 1.7 copy-done.4
  104.5 1.1 copy-done.7
  105.7 1.0 copy-done.10
  106.7 2.5 %weight_grads.1 = bf16[64,32,768]{2,1,0:T(8,128)(2,1)S(1)} custom-call(s32[1]{0:T(128)} %bitcast.core_ref, bf16[16,192,256]{2,1,0:T(8,128)(2,1)S(1)} %all-to-all-done.2.back_ref, bf16[4,192,256]{2,1,0:T(8,128)(2,1)S(1)} %get-tuple-element.83.ggate_ref, bf16[12,192,256]{2,1,0:T(8,128)(2,1)S(1)} %collective-permute-done.10.o_ref, ...), custom_call_target="tpu_custom_call" | custom-call | flops 1610612736 | bytes 8388608 | tf_op jit(solution)/shard_map/weight_grads/pallas_call | solution.py:425
  109.3 1.7 copy-done.2
  110.9 9.8 %all-to-all-start.4 = ((bf16[64,32,768]{2,1,0:T(8,128)(2,1)}), bf16[64,32,768]{2,1,0:T(8,128)(2,1)S(1)}, u32[]{:S(2)}, u32[]{:S(2)}) async-start(bf16[64,32,768]{2,1,0:T(8,128)(2,1)} %copy-done.2), calls=%async_computation.4 | async-start | bytes 6291456 | tf_op jit(solution)/shard_map/all_to_all | solution.py:506
  120.8 1.2 fusion.8
  122.0 1.1 pad_maximum_fusion.1
  123.1 2.3 %copy.14 = f32[16,128,64]{1,2,0:T(8,128)} copy(f32[16,128,64]{2,1,0:T(8,128)} %pad_maximum_fusion.1) | data formatting | bytes 1048576
  125.4 5.9 %input_grad.1 = bf16[256,768]{1,0:T(8,128)(2,1)} custom-call(bf16[16,192,256]{2,1,0:T(8,128)(2,1)} %copy-done.1, bf16[4,192,256]{2,1,0:T(8,128)(2,1)} %copy-done.5, bf16[768,3072]{1,0:T(8,128)(2,1)} %w_ref.5, bf16[256,768]{1,0:T(8,128)(2,1)} %bitcast.36, f32[256,1]{1,0:T(8,128)} %get-tuple-element.84.mean_ref, f32[256,1]{1,0:T(8,128)} %get-tuple-element.85.inv_ref, ...), custom_call_target="tpu_custom_call" | custom-call | flops 1207959552 | bytes 8388608 | tf_op jit(solution)/shard_map/input_grad/pallas_call | solution.py:356
  131.3 2.5 %convolution_convert_fusion = bf16[256,768]{1,0:T(8,128)(2,1)} fusion(bf16[768,256]{1,0:T(8,128)(2,1)S(1)} %get-tuple-element.82.gated_ref, bf16[768,768]{1,0:T(8,128)(2,1)} %wout_ref.1), kind=kOutput, calls=%fused_computation.1 | convolution fusion | flops 302186496 | bytes 1966080 | tf_op jit(solution)/shard_map/cr,cd->rd/dot_general | solution.py:505
  133.8 34.1 %all-to-all-done.4 = bf16[64,32,768]{2,1,0:T(8,128)(2,1)S(1)} async-done(((bf16[64,32,768]{2,1,0:T(8,128)(2,1)}), bf16[64,32,768]{2,1,0:T(8,128)(2,1)S(1)}, u32[]{:S(2)}, u32[]{:S(2)}) %all-to-all-start.4) | async-done | bytes 3145760 | tf_op jit(solution)/shard_map/all_to_all | solution.py:506
  167.9 0.5 convert_reduce_fusion
  168.4 0.6 slice_bitcast_fusion
  169.1 0.5 collective-permute-start.11
  169.6 0.6 slice_bitcast_fusion.1
  170.4 0.6 add.67
  (42 shorter events, 2.1 us)
Async XLA Ops:
  2.3 12.6 %all-to-all-start = ((bf16[8,16,1024]{2,1,0:T(8,128)(2,1)}), bf16[8,16,1024]{2,1,0:T(8,128)(2,1)S(1)}, u32[]{:S(2)}, u32[]{:S(2)}) async-start(bf16[8,16,1024]{2,1,0:T(8,128)(2,1)} %constant_dynamic-slice_fusion), calls=%async_computation | async-start | bytes 524288 | tf_op jit(solution)/shard_map/all_to_all | solution.py:456
  14.9 9.7 %copy-start.14 = (bf16[2,128,768]{2,1,0:T(8,128)(2,1)S(1)}, bf16[2,128,768]{2,1,0:T(8,128)(2,1)}, u32[]{:S(2)}) copy-start(bf16[2,128,768]{2,1,0:T(8,128)(2,1)} %param.11) | copy-start | bytes 1179652
  15.0 26.4 %all-to-all-start.1 = ((bf16[16,192,256]{2,1,0:T(8,128)(2,1)}), bf16[16,192,256]{2,1,0:T(8,128)(2,1)}, u32[]{:S(2)}, u32[]{:S(2)}) async-start(bf16[16,192,256]{2,1,0:T(8,128)(2,1)} %get-tuple-element.48), calls=%async_computation.1 | async-start | bytes 3145728 | tf_op jit(solution)/shard_map/all_to_all | solution.py:465
  21.5 8.9 %collective-permute-start.2 = (bf16[8,16,1024]{2,1,0:T(8,128)(2,1)S(1)}, bf16[8,16,1024]{2,1,0:T(8,128)(2,1)S(1)}, u32[]{:S(2)}, u32[]{:S(2)}) collective-permute-start(bf16[8,16,1024]{2,1,0:T(8,128)(2,1)S(1)} %all-to-all-done), channel_id=1, source_target_pairs={{0,96},{32,0},{64,32},{96,64},{1,97},{33,1},{65,33},{97,65},{2,98}... | collective-permute-start | bytes 786440 | tf_op jit(solution)/shard_map/ppermute | solution.py:464
  22.0 11.1 %collective-permute-start.1 = (bf16[8,16,1024]{2,1,0:T(8,128)(2,1)S(1)}, bf16[8,16,1024]{2,1,0:T(8,128)(2,1)S(1)}, u32[]{:S(2)}, u32[]{:S(2)}) collective-permute-start(bf16[8,16,1024]{2,1,0:T(8,128)(2,1)S(1)} %all-to-all-done), channel_id=1, source_target_pairs={{0,64},{32,96},{64,0},{96,32},{1,65},{33,97},{65,1},{97,33},{2,66}... | collective-permute-start | bytes 786440 | tf_op jit(solution)/shard_map/ppermute | solution.py:464
  22.9 13.2 %collective-permute-start = (bf16[8,16,1024]{2,1,0:T(8,128)(2,1)S(1)}, bf16[8,16,1024]{2,1,0:T(8,128)(2,1)S(1)}, u32[]{:S(2)}, u32[]{:S(2)}) collective-permute-start(bf16[8,16,1024]{2,1,0:T(8,128)(2,1)S(1)} %all-to-all-done), channel_id=1, source_target_pairs={{0,32},{32,64},{64,96},{96,0},{1,33},{33,65},{65,97},{97,1},{2,34}... | collective-permute-start | bytes 786440 | tf_op jit(solution)/shard_map/ppermute | solution.py:464
  25.1 12.8 %copy-start.11 = (bf16[256,768]{1,0:T(8,128)(2,1)S(1)}, bf16[256,768]{1,0:T(8,128)(2,1)}, u32[]{:S(2)}) copy-start(bf16[256,768]{1,0:T(8,128)(2,1)} %get-tuple-element.65.sc_ref) | copy-start | bytes 1179652
  36.2 5.2 %copy-start.15 = (bf16[4,8,16,1024]{3,2,1,0:T(8,128)(2,1)}, bf16[4,8,16,1024]{3,2,1,0:T(8,128)(2,1)S(1)}, u32[]{:S(2)}) copy-start(bf16[4,8,16,1024]{3,2,1,0:T(8,128)(2,1)S(1)} %pad_maximum_fusion.mine_ref) | copy-start | bytes 3145732
  36.2 4.9 %collective-permute-start.5 = (bf16[4,8,16,1024]{3,2,1,0:T(8,128)(2,1)S(1)}, bf16[4,8,16,1024]{3,2,1,0:T(8,128)(2,1)}, u32[]{:S(2)}, u32[]{:S(2)}) collective-permute-start(bf16[4,8,16,1024]{3,2,1,0:T(8,128)(2,1)S(1)} %pad_maximum_fusion.mine_ref), channel_id=1, source_target_pairs={{0,8},{8,0},{1,9},{9,1},{2,10},{10,2},{3,11},{11,3},{4,12},{12,4},... | collective-permute-start | bytes 3145736 | tf_op jit(solution)/shard_map/ppermute | solution.py:475
  37.9 2.8 %collective-permute-start.4 = (bf16[256,768]{1,0:T(8,128)(2,1)S(1)}, bf16[256,768]{1,0:T(8,128)(2,1)S(1)}, u32[]{:S(2)}, u32[]{:S(2)}) collective-permute-start(bf16[256,768]{1,0:T(8,128)(2,1)S(1)} %copy-done.11), channel_id=1, source_target_pairs={{0,8},{8,0},{1,9},{9,1},{2,10},{10,2},{3,11},{11,3},{4,12},{12,4},... | collective-permute-start | bytes 1179656 | tf_op jit(solution)/shard_map/ppermute | solution.py:471
  38.0 3.1 %collective-permute-start.3 = (bf16[8,64,256]{2,1,0:T(8,128)(2,1)S(1)}, bf16[8,64,256]{2,1,0:T(8,128)(2,1)S(1)}, u32[]{:S(2)}, u32[]{:S(2)}) collective-permute-start(bf16[8,64,256]{2,1,0:T(8,128)(2,1)S(1)} %get-tuple-element.50), channel_id=1, source_target_pairs={{0,8},{8,0},{1,9},{9,1},{2,10},{10,2},{3,11},{11,3},{4,12},{12,4},... | collective-permute-start | bytes 786440 | tf_op jit(solution)/shard_map/ppermute | solution.py:476
  60.9 8.8 %collective-permute-start.6 = (bf16[4,16,64,128]{3,2,1,0:T(8,128)(2,1)}, bf16[4,16,64,128]{3,2,1,0:T(8,128)(2,1)}, u32[]{:S(2)}, u32[]{:S(2)}) collective-permute-start(bf16[4,16,64,128]{3,2,1,0:T(8,128)(2,1)} %get-tuple-element.64), channel_id=1, source_target_pairs={{0,8},{8,0},{1,9},{9,1},{2,10},{10,2},{3,11},{11,3},{4,12},{12,4},... | collective-permute-start | bytes 3145736 | tf_op jit(solution)/shard_map/ppermute | solution.py:486
  64.2 30.9 %all-to-all-start.2 = ((bf16[16,192,256]{2,1,0:T(8,128)(2,1)}), bf16[16,192,256]{2,1,0:T(8,128)(2,1)S(1)}, u32[]{:S(2)}, u32[]{:S(2)}) async-start(bf16[16,192,256]{2,1,0:T(8,128)(2,1)} %get-tuple-element.58), calls=%async_computation.2 | async-start | bytes 3145728 | tf_op jit(solution)/shard_map/all_to_all | solution.py:481
  71.4 10.7 %collective-permute-start.7 = (bf16[16,64,128]{2,1,0:T(8,128)(2,1)S(1)}, bf16[16,64,128]{2,1,0:T(8,128)(2,1)S(1)}, u32[]{:S(2)}, u32[]{:S(2)}) collective-permute-start(bf16[16,64,128]{2,1,0:T(8,128)(2,1)S(1)} %get-tuple-element.100), channel_id=1, source_target_pairs={{0,32},{32,64},{64,96},{96,0},{1,33},{33,65},{65,97},{97,1},{2,34}... | collective-permute-start | bytes 786440 | tf_op jit(solution)/shard_map/ppermute | solution.py:490
  71.8 10.3 %collective-permute-start.9 = (bf16[16,64,128]{2,1,0:T(8,128)(2,1)S(1)}, bf16[16,64,128]{2,1,0:T(8,128)(2,1)S(1)}, u32[]{:S(2)}, u32[]{:S(2)}) collective-permute-start(bf16[16,64,128]{2,1,0:T(8,128)(2,1)S(1)} %get-tuple-element.101), channel_id=1, source_target_pairs={{0,96},{32,0},{64,32},{96,64},{1,97},{33,1},{65,33},{97,65},{2,98}... | collective-permute-start | bytes 786440 | tf_op jit(solution)/shard_map/ppermute | solution.py:490
  72.9 12.6 %collective-permute-start.8 = (bf16[16,64,128]{2,1,0:T(8,128)(2,1)S(1)}, bf16[16,64,128]{2,1,0:T(8,128)(2,1)S(1)}, u32[]{:S(2)}, u32[]{:S(2)}) collective-permute-start(bf16[16,64,128]{2,1,0:T(8,128)(2,1)S(1)} %get-tuple-element.102), channel_id=1, source_target_pairs={{0,64},{32,96},{64,0},{96,32},{1,65},{33,97},{65,1},{97,33},{2,66}... | collective-permute-start | bytes 786440 | tf_op jit(solution)/shard_map/ppermute | solution.py:490
  74.0 2.3 %copy-start = (bf16[768,3072]{1,0:T(8,128)(2,1)S(1)}, bf16[768,3072]{1,0:T(8,128)(2,1)}, u32[]{:S(2)}) copy-start(bf16[768,3072]{1,0:T(8,128)(2,1)} %w_ref.5) | copy-start | bytes 14155780
  78.9 1.5 copy-start.3
  80.4 0.9 copy-start.6
  81.3 0.8 copy-start.9
  82.1 13.0 %copy-start.8 = (f32[768,256]{1,0:T(8,128)S(1)}, f32[768,256]{1,0:T(8,128)}, u32[]{:S(2)}) copy-start(f32[768,256]{1,0:T(8,128)} %get-tuple-element.73.gate_ref) | copy-start | bytes 2359300
  82.1 13.0 %copy-start.12 = (bf16[768,256]{1,0:T(8,128)(2,1)S(1)}, bf16[768,256]{1,0:T(8,128)(2,1)}, u32[]{:S(2)}) copy-start(bf16[768,256]{1,0:T(8,128)(2,1)} %get-tuple-element.74.gg_ref) | copy-start | bytes 1179652
  95.1 7.8 %copy-start.1 = (bf16[16,192,256]{2,1,0:T(8,128)(2,1)}, bf16[16,192,256]{2,1,0:T(8,128)(2,1)S(1)}, u32[]{:S(2)}) copy-start(bf16[16,192,256]{2,1,0:T(8,128)(2,1)S(1)} %all-to-all-done.2.back_ref) | copy-start | bytes 4718596
  95.1 7.8 %copy-start.13 = (f32[768]{0:T(1024)S(1)}, f32[768]{0:T(1024)}, u32[]{:S(2)}) copy-start(f32[768]{0:T(1024)} %gain_ref.5) | copy-start | bytes 9220
  96.6 12.7 %copy-start.5 = (bf16[4,192,256]{2,1,0:T(8,128)(2,1)}, bf16[4,192,256]{2,1,0:T(8,128)(2,1)S(1)}, u32[]{:S(2)}) copy-start(bf16[4,192,256]{2,1,0:T(8,128)(2,1)S(1)} %get-tuple-element.83.ggate_ref) | copy-start | bytes 1179652
  96.6 6.3 %collective-permute-start.10 = (bf16[12,192,256]{2,1,0:T(8,128)(2,1)}, bf16[12,192,256]{2,1,0:T(8,128)(2,1)S(1)}, u32[]{:S(2)}, u32[]{:S(2)}) collective-permute-start(bf16[12,192,256]{2,1,0:T(8,128)(2,1)} %get-tuple-element.76), channel_id=1, source_target_pairs={{0,8},{8,0},{1,9},{9,1},{2,10},{10,2},{3,11},{11,3},{4,12},{12,4},... | collective-permute-start | bytes 3538952 | tf_op jit(solution)/shard_map/ppermute | solution.py:496
  97.4 13.6 %all-to-all-start.3 = ((bf16[16,64,128]{2,1,0:T(8,128)(2,1)}), bf16[16,64,128]{2,1,0:T(8,128)(2,1)}, u32[]{:S(2)}, u32[]{:S(2)}) async-start(bf16[16,64,128]{2,1,0:T(8,128)(2,1)} %fusion.2), calls=%async_computation.3 | async-start | bytes 524288 | tf_op jit(solution)/shard_map/all_to_all | solution.py:493
  102.9 1.7 copy-start.4
  104.5 1.1 copy-start.7
  105.7 1.0 copy-start.10
  109.3 1.7 copy-start.2
  110.9 57.0 %all-to-all-start.4 = ((bf16[64,32,768]{2,1,0:T(8,128)(2,1)}), bf16[64,32,768]{2,1,0:T(8,128)(2,1)S(1)}, u32[]{:S(2)}, u32[]{:S(2)}) async-start(bf16[64,32,768]{2,1,0:T(8,128)(2,1)} %copy-done.2), calls=%async_computation.4 | async-start | bytes 6291456 | tf_op jit(solution)/shard_map/all_to_all | solution.py:506
  169.1 1.3 collective-permute-start.11

commit v11 on v10

--- a/solution.py
+++ b/solution.py
@@ -377,44 +377,32 @@
 
 
 def weight_kernel(
-    core_ref, back_ref, ggate_ref, o_ref, gated_ref, scaled_ref, dout_ref, wt_ref, gain_ref, out_ref, gated_s, sum_s
+    core_ref, back_ref, ggate_ref, o_ref, gated_ref, scaled_ref, dout_ref, wt_ref, gain_ref, out_ref, gated_s
 ):
     core = core_ref[0]
-    step = pl.program_id(0)
     flat = gated_ref.shape[1]
-    last = pl.num_programs(0) - 1
-
-    @pl.when(step == 0)
-    def _():
-        gated_s[:flat] = gated_ref[...].T
-        gated_s[flat:] = o_ref[8:12].reshape(C, flat).T
-        sum_s[...] = jnp.zeros_like(sum_s)
-
+    gated_s[:flat] = gated_ref[...].T
+    gated_s[flat:] = o_ref[8:12].reshape(C, flat).T
+    sums = jnp.zeros((8, C), F32)
     for kind in range(4):
-
-        @pl.when(step == kind)
-        def _(kind=kind):
-            blocks = [
-                jnp.concatenate([head_rows(back_ref, ggate_ref, n, core), o_ref[n]], axis=1)
-                for n in (2 * kind, 2 * kind + 1)
-            ]
-            win = dot(jnp.concatenate(blocks, axis=0), scaled_ref[...])
-            wout = dot(dout_ref[2 * kind : 2 * kind + 2].reshape(128, 2 * flat), gated_s[...])
-            weights = wt_ref[2 * kind : 2 * kind + 2].reshape(8 * DH, C).astype(F32)
-            sum_s[...] += jnp.sum((win * weights).reshape(DH, 8, C), axis=0)
-            for k in range(16):
-                out_ref[kind * 16 + k] = jnp.concatenate(
-                    [win[k * 24 : k * 24 + 24], wout[k * 8 : k * 8 + 8]], axis=0
-                ).astype(BF)
-
-    @pl.when(step == last)
-    def _():
-        gain = jnp.sum(sum_s[...], axis=0, keepdims=True) / gain_ref[...].reshape(1, C)
-        gain_hi = gain.astype(BF).astype(F32)
-        row = lax.broadcasted_iota(jnp.int32, (16, C), 0)
-        extra = jnp.where(row == 14, gain_hi, gain - gain_hi).astype(BF)
-        for k in range(64):
-            out_ref[k, 16:] = jnp.where(row >= 14, extra, out_ref[k, 16:])
+        blocks = [
+            jnp.concatenate([head_rows(back_ref, ggate_ref, n, core), o_ref[n]], axis=1)
+            for n in (2 * kind, 2 * kind + 1)
+        ]
+        win = dot(jnp.concatenate(blocks, axis=0), scaled_ref[...])
+        wout = dot(dout_ref[2 * kind : 2 * kind + 2].reshape(128, 2 * flat), gated_s[...])
+        weights = wt_ref[2 * kind : 2 * kind + 2].reshape(8 * DH, C).astype(F32)
+        sums = sums + jnp.sum((win * weights).reshape(DH, 8, C), axis=0)
+        for k in range(16):
+            out_ref[kind * 16 + k] = jnp.concatenate(
+                [win[k * 24 : k * 24 + 24], wout[k * 8 : k * 8 + 8]], axis=0
+            ).astype(BF)
+    gain = jnp.sum(sums, axis=0, keepdims=True) / gain_ref[...].reshape(1, C)
+    gain_hi = gain.astype(BF).astype(F32)
+    row = lax.broadcasted_iota(jnp.int32, (16, C), 0)
+    extra = jnp.where(row == 14, gain_hi, gain - gain_hi).astype(BF)
+    for k in range(64):
+        out_ref[k, 16:] = jnp.where(row >= 14, extra, out_ref[k, 16:])
 
 
 def weight_grads(core, operands):
@@ -426,13 +414,10 @@
         weight_kernel,
         grid_spec=pltpu.PrefetchScalarGridSpec(
             num_scalar_prefetch=1,
-            grid=(4,),
+            grid=(1,),
             in_specs=[whole(o.shape) for o in operands],
             out_specs=whole((64, 32, C)),
-            scratch_shapes=[
-                pltpu.VMEM((2 * flat, C), BF),
-                pltpu.VMEM((8, C), F32),
-            ],
+            scratch_shapes=[pltpu.VMEM((2 * flat, C), BF)],
         ),
         out_shape=jax.ShapeDtypeStruct((64, 32, C), BF),
         compiler_params=params(24),

time: 172 us -> 171 us (level)
  transfers between devices with their start and end apart: 17 -> 17, of which waited for: 10 -> 10; matrix products, arithmetic and copies ran while one was open for 7% -> 7% of each run, Pallas kernels for 11% -> 10%
where the time goes in v11:
time: 171 us; the launch traced here: 170 us
  waiting for transfers between devices  58.7 us (34%)
  starting transfers between devices  45.2 us (26%)
  Pallas kernels  38.7 us (23%)
  local copies, waits for them, and re-layouts  17.9 us (10%)
  other arithmetic  6.48 us (4%)
  matrix products  2.52 us (1%)
    all_to_all x1, waiting for transfers between devices, per_device(): chunks = lax.all_to_all(chunks, ('x', 'zh', 'zl', 'y'), 0, 0, tiled=True)  34.1 us
    pallas_call x1, Pallas kernels, attention(): pl.pallas_call(functools.partial(attention_kernel, blocks=blocks), grid_s...  19.5 us
    unnamed x33, local copies, waits for them, and re-layouts  13.3 us
    ppermute x3, waiting for transfers between devices, per_device(): pieces = [bias] + [lax.ppermute(bias, 'x', turn(s)) for s in (1, 2, 3)]  10.9 us
    all_to_all x1, starting transfers between devices, per_device(): chunks = lax.all_to_all(chunks, ('x', 'zh', 'zl', 'y'), 0, 0, tiled=True)  9.84 us
    all_to_all x1, waiting for transfers between devices, per_device(): back = lax.all_to_all(result, PLANE, 0, 0, tiled=True)  7.62 us
    pallas_call x1, Pallas kernels, front(): pl.pallas_call(front_kernel, grid=(4,), in_specs=[whole((flat, C)), whole...  7.25 us
    all_to_all x1, starting transfers between devices, per_device(): received = lax.all_to_all(send, PLANE, 0, 0, tiled=True)  6.52 us
  transfers between devices with their start and end apart: 17, of which 10 were waited for; matrix products, arithmetic and copies ran while one was open for 7% of the time, Pallas kernels for 10%

profile of v11, /device:TPU:103, one launch (start us, length us, event | category | flops | bytes accessed | tf_op | source)
XLA Modules:
  0.0 170.4 jit_solution(7595083772783102278)
XLA Ops:
  0.6 1.7 constant_dynamic-slice_fusion
  2.3 5.4 %all-to-all-start = ((bf16[8,16,1024]{2,1,0:T(8,128)(2,1)}), bf16[8,16,1024]{2,1,0:T(8,128)(2,1)S(1)}, u32[]{:S(2)}, u32[]{:S(2)}) async-start(bf16[8,16,1024]{2,1,0:T(8,128)(2,1)} %constant_dynamic-slice_fusion), calls=%async_computation | async-start | bytes 524288 | tf_op jit(solution)/shard_map/all_to_all | solution.py:441
  7.7 7.2 %front.1 = (bf16[256,768]{1,0:T(8,128)(2,1)}, f32[256,1]{1,0:T(8,128)}, f32[256,1]{1,0:T(8,128)}, bf16[16,192,256]{2,1,0:T(8,128)(2,1)}, f32[768,256]{1,0:T(8,128)}, /*index=5*/bf16[768,256]{1,0:T(8,128)(2,1)}) custom-call(bf16[256,768]{1,0:T(8,128)(2,1)} %bitcast.35, f32[768]{0:T(1024)} %gain_ref.5, bf16[768,3072]{1,0:T(8,128)(2,1)} %w_ref.5, ...), custom_call_target="tpu_custom_call" | custom-call | flops 1509949440 | bytes 11534336 | tf_op jit(solution)/shard_map/front/pallas_call | solution.py:93
  15.0 6.5 %all-to-all-start.1 = ((bf16[16,192,256]{2,1,0:T(8,128)(2,1)}), bf16[16,192,256]{2,1,0:T(8,128)(2,1)}, u32[]{:S(2)}, u32[]{:S(2)}) async-start(bf16[16,192,256]{2,1,0:T(8,128)(2,1)} %get-tuple-element.48), calls=%async_computation.1 | async-start | bytes 3145728 | tf_op jit(solution)/shard_map/all_to_all | solution.py:450
  21.5 0.5 collective-permute-start.2
  22.0 0.8 collective-permute-start.1
  22.9 1.8 %collective-permute-start = (bf16[8,16,1024]{2,1,0:T(8,128)(2,1)S(1)}, bf16[8,16,1024]{2,1,0:T(8,128)(2,1)S(1)}, u32[]{:S(2)}, u32[]{:S(2)}) collective-permute-start(bf16[8,16,1024]{2,1,0:T(8,128)(2,1)S(1)} %all-to-all-done), channel_id=1, source_target_pairs={{0,32},{32,64},{64,96},{96,0},{1,33},{33,65},{65,97},{97,1},{2,34}... | collective-permute-start | bytes 786440 | tf_op jit(solution)/shard_map/ppermute | solution.py:449
  25.2 5.2 %collective-permute-done.2 = bf16[8,16,1024]{2,1,0:T(8,128)(2,1)S(1)} collective-permute-done((bf16[8,16,1024]{2,1,0:T(8,128)(2,1)S(1)}, bf16[8,16,1024]{2,1,0:T(8,128)(2,1)S(1)}, u32[]{:S(2)}, u32[]{:S(2)}) %collective-permute-start.2) | collective-permute-done | bytes 262176 | tf_op jit(solution)/shard_map/ppermute | solution.py:449
  30.3 2.8 %collective-permute-done.1 = bf16[8,16,1024]{2,1,0:T(8,128)(2,1)S(1)} collective-permute-done((bf16[8,16,1024]{2,1,0:T(8,128)(2,1)S(1)}, bf16[8,16,1024]{2,1,0:T(8,128)(2,1)S(1)}, u32[]{:S(2)}, u32[]{:S(2)}) %collective-permute-start.1) | collective-permute-done | bytes 262176 | tf_op jit(solution)/shard_map/ppermute | solution.py:449
  33.2 2.9 %collective-permute-done = bf16[8,16,1024]{2,1,0:T(8,128)(2,1)S(1)} collective-permute-done((bf16[8,16,1024]{2,1,0:T(8,128)(2,1)S(1)}, bf16[8,16,1024]{2,1,0:T(8,128)(2,1)S(1)}, u32[]{:S(2)}, u32[]{:S(2)}) %collective-permute-start) | collective-permute-done | bytes 262176 | tf_op jit(solution)/shard_map/ppermute | solution.py:449
  36.2 1.6 collective-permute-start.5
  38.0 0.4 collective-permute-start.3
  38.4 0.6 pad_add_fusion.place_ref
  39.0 1.8 %collective-permute-done.4.sco_ref = bf16[256,768]{1,0:T(8,128)(2,1)S(1)} collective-permute-done((bf16[256,768]{1,0:T(8,128)(2,1)S(1)}, bf16[256,768]{1,0:T(8,128)(2,1)S(1)}, u32[]{:S(2)}, u32[]{:S(2)}) %collective-permute-start.4) | collective-permute-done | bytes 393248 | tf_op jit(solution)/shard_map/ppermute | solution.py:456
  41.4 19.5 %attention.1 = (bf16[16,192,256]{2,1,0:T(8,128)(2,1)}, bf16[4,16,64,128]{3,2,1,0:T(8,128)(2,1)}, bf16[4,16,64,128]{3,2,1,0:T(8,128)(2,1)}) custom-call(s32[2]{0:T(128)} %pad_add_fusion.place_ref, bf16[16,192,256]{2,1,0:T(8,128)(2,1)} %all-to-all-done.1.x_ref, bf16[4,8,16,1024]{3,2,1,0:T(8,128)(2,1)} %copy-done.15, ...), custom_call_target="tpu_custom_call" | custom-call | flops 12884901888 | bytes 8388608 | tf_op jit(solution)/shard_map/attention/pallas_call | solution.py:205
  60.9 3.3 %collective-permute-start.6 = (bf16[4,16,64,128]{3,2,1,0:T(8,128)(2,1)}, bf16[4,16,64,128]{3,2,1,0:T(8,128)(2,1)}, u32[]{:S(2)}, u32[]{:S(2)}) collective-permute-start(bf16[4,16,64,128]{3,2,1,0:T(8,128)(2,1)} %get-tuple-element.64), channel_id=1, source_target_pairs={{0,8},{8,0},{1,9},{9,1},{2,10},{10,2},{3,11},{11,3},{4,12},{12,4},... | collective-permute-start | bytes 3145736 | tf_op jit(solution)/shard_map/ppermute | solution.py:471
  64.2 5.5 %all-to-all-start.2 = ((bf16[16,192,256]{2,1,0:T(8,128)(2,1)}), bf16[16,192,256]{2,1,0:T(8,128)(2,1)S(1)}, u32[]{:S(2)}, u32[]{:S(2)}) async-start(bf16[16,192,256]{2,1,0:T(8,128)(2,1)} %get-tuple-element.58), calls=%async_computation.2 | async-start | bytes 3145728 | tf_op jit(solution)/shard_map/all_to_all | solution.py:466
  69.7 1.7 fusion.4
  71.8 1.1 collective-permute-start.9
  72.9 1.1 collective-permute-start.8
  74.0 2.3 %copy-done = bf16[768,3072]{1,0:T(8,128)(2,1)S(1)} copy-done((bf16[768,3072]{1,0:T(8,128)(2,1)S(1)}, bf16[768,3072]{1,0:T(8,128)(2,1)}, u32[]{:S(2)}) %copy-start) | copy-done | bytes 4718616
  76.3 2.6 %stage.1 = (bf16[8,192,768]{2,1,0:T(8,128)(2,1)S(1)}, bf16[512,768]{1,0:T(8,128)(2,1)S(1)}, bf16[8,64,512]{2,1,0:T(8,128)(2,1)S(1)}) custom-call(s32[1]{0:T(128)} %bitcast.core_ref, bf16[768,3072]{1,0:T(8,128)(2,1)S(1)} %copy-done, bf16[256,768]{1,0:T(8,128)(2,1)S(1)} %copy-done.11, bf16[256,768]{1,0:T(8,128)(2,1)S(1)} %collective-permute-done.4.sco_ref, ...), custom_call_target="tpu_custom_call" | custom-call | flops 4718592 | bytes 7340032 | tf_op jit(solution)/shard_map/stage/pallas_call | solution.py:257
  79.0 1.4 copy-done.3
  80.4 0.9 copy-done.6
  81.3 0.8 copy-done.9
  82.1 3.4 %collective-permute-done.8 = bf16[16,64,128]{2,1,0:T(8,128)(2,1)S(1)} collective-permute-done((bf16[16,64,128]{2,1,0:T(8,128)(2,1)S(1)}, bf16[16,64,128]{2,1,0:T(8,128)(2,1)S(1)}, u32[]{:S(2)}, u32[]{:S(2)}) %collective-permute-start.8) | collective-permute-done | bytes 262176 | tf_op jit(solution)/shard_map/ppermute | solution.py:475
  85.5 1.9 %fusion.2 = bf16[16,64,128]{2,1,0:T(8,128)(2,1)} fusion(bf16[16,64,128]{2,1,0:T(8,128)(2,1)S(1)} %collective-permute-done.9, bf16[16,64,128]{2,1,0:T(8,128)(2,1)S(1)} %collective-permute-done.8, bf16[16,64,128]{2,1,0:T(8,128)(2,1)S(1)} %collective-permute-done.7, bf16[4,16,64,128]{3,2,1,0:T(8,128)(2,1)} %collective-permute-done.6, ...), kind=kLoop, calls=%fused_computation.7 | loop fusion | flops 1572864 | bytes 1572864 | tf_op jit(solution)/shard_map/convert_element_type | solution.py:477
  87.5 7.6 %all-to-all-done.2.back_ref = bf16[16,192,256]{2,1,0:T(8,128)(2,1)S(1)} async-done(((bf16[16,192,256]{2,1,0:T(8,128)(2,1)}), bf16[16,192,256]{2,1,0:T(8,128)(2,1)S(1)}, u32[]{:S(2)}, u32[]{:S(2)}) %all-to-all-start.2) | async-done | bytes 1572896 | tf_op jit(solution)/shard_map/all_to_all | solution.py:466
  95.1 1.5 gate.1
  96.6 0.8 collective-permute-start.10
  97.4 5.5 %all-to-all-start.3 = ((bf16[16,64,128]{2,1,0:T(8,128)(2,1)}), bf16[16,64,128]{2,1,0:T(8,128)(2,1)}, u32[]{:S(2)}, u32[]{:S(2)}) async-start(bf16[16,64,128]{2,1,0:T(8,128)(2,1)} %fusion.2), calls=%async_computation.3 | async-start | bytes 524288 | tf_op jit(solution)/shard_map/all_to_all | solution.py:478
  102.9 1.7 copy-done.4
  104.5 1.1 copy-done.7
  105.7 1.0 copy-done.10
  106.7 2.0 %weight_grads.1 = bf16[64,32,768]{2,1,0:T(8,128)(2,1)S(1)} custom-call(s32[1]{0:T(128)} %bitcast.core_ref, bf16[16,192,256]{2,1,0:T(8,128)(2,1)S(1)} %all-to-all-done.2.back_ref, bf16[4,192,256]{2,1,0:T(8,128)(2,1)S(1)} %get-tuple-element.83.ggate_ref, bf16[12,192,256]{2,1,0:T(8,128)(2,1)S(1)} %collective-permute-done.10.o_ref, ...), custom_call_target="tpu_custom_call" | custom-call | flops 1610612736 | bytes 8388608 | tf_op jit(solution)/shard_map/weight_grads/pallas_call | solution.py:413
  108.7 1.7 copy-done.2
  110.4 9.8 %all-to-all-start.4 = ((bf16[64,32,768]{2,1,0:T(8,128)(2,1)}), bf16[64,32,768]{2,1,0:T(8,128)(2,1)S(1)}, u32[]{:S(2)}, u32[]{:S(2)}) async-start(bf16[64,32,768]{2,1,0:T(8,128)(2,1)} %copy-done.2), calls=%async_computation.4 | async-start | bytes 6291456 | tf_op jit(solution)/shard_map/all_to_all | solution.py:491
  120.2 1.2 fusion.8
  121.4 1.1 pad_maximum_fusion.1
  122.5 2.3 %copy.14 = f32[16,128,64]{1,2,0:T(8,128)} copy(f32[16,128,64]{2,1,0:T(8,128)} %pad_maximum_fusion.1) | data formatting | bytes 1048576
  124.8 5.9 %input_grad.1 = bf16[256,768]{1,0:T(8,128)(2,1)} custom-call(bf16[16,192,256]{2,1,0:T(8,128)(2,1)} %copy-done.1, bf16[4,192,256]{2,1,0:T(8,128)(2,1)} %copy-done.5, bf16[768,3072]{1,0:T(8,128)(2,1)} %w_ref.5, bf16[256,768]{1,0:T(8,128)(2,1)} %bitcast.36, f32[256,1]{1,0:T(8,128)} %get-tuple-element.84.mean_ref, f32[256,1]{1,0:T(8,128)} %get-tuple-element.85.inv_ref, ...), custom_call_target="tpu_custom_call" | custom-call | flops 1207959552 | bytes 8388608 | tf_op jit(solution)/shard_map/input_grad/pallas_call | solution.py:356
  130.8 2.5 %convolution_convert_fusion = bf16[256,768]{1,0:T(8,128)(2,1)} fusion(bf16[768,256]{1,0:T(8,128)(2,1)S(1)} %get-tuple-element.82.gated_ref, bf16[768,768]{1,0:T(8,128)(2,1)} %wout_ref.1), kind=kOutput, calls=%fused_computation.1 | convolution fusion | flops 302186496 | bytes 1966080 | tf_op jit(solution)/shard_map/cr,cd->rd/dot_general | solution.py:490
  133.3 34.1 %all-to-all-done.4 = bf16[64,32,768]{2,1,0:T(8,128)(2,1)S(1)} async-done(((bf16[64,32,768]{2,1,0:T(8,128)(2,1)}), bf16[64,32,768]{2,1,0:T(8,128)(2,1)S(1)}, u32[]{:S(2)}, u32[]{:S(2)}) %all-to-all-start.4) | async-done | bytes 3145760 | tf_op jit(solution)/shard_map/all_to_all | solution.py:491
  167.4 0.5 convert_reduce_fusion
  167.9 0.6 slice_bitcast_fusion
  168.5 0.5 collective-permute-start.11
  169.0 0.6 slice_bitcast_fusion.1
  169.8 0.6 add.67
  (42 shorter events, 2.1 us)
Async XLA Ops:
  2.3 12.6 %all-to-all-start = ((bf16[8,16,1024]{2,1,0:T(8,128)(2,1)}), bf16[8,16,1024]{2,1,0:T(8,128)(2,1)S(1)}, u32[]{:S(2)}, u32[]{:S(2)}) async-start(bf16[8,16,1024]{2,1,0:T(8,128)(2,1)} %constant_dynamic-slice_fusion), calls=%async_computation | async-start | bytes 524288 | tf_op jit(solution)/shard_map/all_to_all | solution.py:441
  14.9 9.7 %copy-start.14 = (bf16[2,128,768]{2,1,0:T(8,128)(2,1)S(1)}, bf16[2,128,768]{2,1,0:T(8,128)(2,1)}, u32[]{:S(2)}) copy-start(bf16[2,128,768]{2,1,0:T(8,128)(2,1)} %param.11) | copy-start | bytes 1179652
  15.0 26.4 %all-to-all-start.1 = ((bf16[16,192,256]{2,1,0:T(8,128)(2,1)}), bf16[16,192,256]{2,1,0:T(8,128)(2,1)}, u32[]{:S(2)}, u32[]{:S(2)}) async-start(bf16[16,192,256]{2,1,0:T(8,128)(2,1)} %get-tuple-element.48), calls=%async_computation.1 | async-start | bytes 3145728 | tf_op jit(solution)/shard_map/all_to_all | solution.py:450
  21.5 8.9 %collective-permute-start.2 = (bf16[8,16,1024]{2,1,0:T(8,128)(2,1)S(1)}, bf16[8,16,1024]{2,1,0:T(8,128)(2,1)S(1)}, u32[]{:S(2)}, u32[]{:S(2)}) collective-permute-start(bf16[8,16,1024]{2,1,0:T(8,128)(2,1)S(1)} %all-to-all-done), channel_id=1, source_target_pairs={{0,96},{32,0},{64,32},{96,64},{1,97},{33,1},{65,33},{97,65},{2,98}... | collective-permute-start | bytes 786440 | tf_op jit(solution)/shard_map/ppermute | solution.py:449
  22.0 11.1 %collective-permute-start.1 = (bf16[8,16,1024]{2,1,0:T(8,128)(2,1)S(1)}, bf16[8,16,1024]{2,1,0:T(8,128)(2,1)S(1)}, u32[]{:S(2)}, u32[]{:S(2)}) collective-permute-start(bf16[8,16,1024]{2,1,0:T(8,128)(2,1)S(1)} %all-to-all-done), channel_id=1, source_target_pairs={{0,64},{32,96},{64,0},{96,32},{1,65},{33,97},{65,1},{97,33},{2,66}... | collective-permute-start | bytes 786440 | tf_op jit(solution)/shard_map/ppermute | solution.py:449
  22.9 13.2 %collective-permute-start = (bf16[8,16,1024]{2,1,0:T(8,128)(2,1)S(1)}, bf16[8,16,1024]{2,1,0:T(8,128)(2,1)S(1)}, u32[]{:S(2)}, u32[]{:S(2)}) collective-permute-start(bf16[8,16,1024]{2,1,0:T(8,128)(2,1)S(1)} %all-to-all-done), channel_id=1, source_target_pairs={{0,32},{32,64},{64,96},{96,0},{1,33},{33,65},{65,97},{97,1},{2,34}... | collective-permute-start | bytes 786440 | tf_op jit(solution)/shard_map/ppermute | solution.py:449
  25.1 12.8 %copy-start.11 = (bf16[256,768]{1,0:T(8,128)(2,1)S(1)}, bf16[256,768]{1,0:T(8,128)(2,1)}, u32[]{:S(2)}) copy-start(bf16[256,768]{1,0:T(8,128)(2,1)} %get-tuple-element.65.sc_ref) | copy-start | bytes 1179652
  36.2 5.2 %copy-start.15 = (bf16[4,8,16,1024]{3,2,1,0:T(8,128)(2,1)}, bf16[4,8,16,1024]{3,2,1,0:T(8,128)(2,1)S(1)}, u32[]{:S(2)}) copy-start(bf16[4,8,16,1024]{3,2,1,0:T(8,128)(2,1)S(1)} %pad_maximum_fusion.mine_ref) | copy-start | bytes 3145732
  36.2 4.9 %collective-permute-start.5 = (bf16[4,8,16,1024]{3,2,1,0:T(8,128)(2,1)S(1)}, bf16[4,8,16,1024]{3,2,1,0:T(8,128)(2,1)}, u32[]{:S(2)}, u32[]{:S(2)}) collective-permute-start(bf16[4,8,16,1024]{3,2,1,0:T(8,128)(2,1)S(1)} %pad_maximum_fusion.mine_ref), channel_id=1, source_target_pairs={{0,8},{8,0},{1,9},{9,1},{2,10},{10,2},{3,11},{11,3},{4,12},{12,4},... | collective-permute-start | bytes 3145736 | tf_op jit(solution)/shard_map/ppermute | solution.py:460
  37.9 2.8 %collective-permute-start.4 = (bf16[256,768]{1,0:T(8,128)(2,1)S(1)}, bf16[256,768]{1,0:T(8,128)(2,1)S(1)}, u32[]{:S(2)}, u32[]{:S(2)}) collective-permute-start(bf16[256,768]{1,0:T(8,128)(2,1)S(1)} %copy-done.11), channel_id=1, source_target_pairs={{0,8},{8,0},{1,9},{9,1},{2,10},{10,2},{3,11},{11,3},{4,12},{12,4},... | collective-permute-start | bytes 1179656 | tf_op jit(solution)/shard_map/ppermute | solution.py:456
  38.0 3.1 %collective-permute-start.3 = (bf16[8,64,256]{2,1,0:T(8,128)(2,1)S(1)}, bf16[8,64,256]{2,1,0:T(8,128)(2,1)S(1)}, u32[]{:S(2)}, u32[]{:S(2)}) collective-permute-start(bf16[8,64,256]{2,1,0:T(8,128)(2,1)S(1)} %get-tuple-element.50), channel_id=1, source_target_pairs={{0,8},{8,0},{1,9},{9,1},{2,10},{10,2},{3,11},{11,3},{4,12},{12,4},... | collective-permute-start | bytes 786440 | tf_op jit(solution)/shard_map/ppermute | solution.py:461
  60.9 8.8 %collective-permute-start.6 = (bf16[4,16,64,128]{3,2,1,0:T(8,128)(2,1)}, bf16[4,16,64,128]{3,2,1,0:T(8,128)(2,1)}, u32[]{:S(2)}, u32[]{:S(2)}) collective-permute-start(bf16[4,16,64,128]{3,2,1,0:T(8,128)(2,1)} %get-tuple-element.64), channel_id=1, source_target_pairs={{0,8},{8,0},{1,9},{9,1},{2,10},{10,2},{3,11},{11,3},{4,12},{12,4},... | collective-permute-start | bytes 3145736 | tf_op jit(solution)/shard_map/ppermute | solution.py:471
  64.2 30.9 %all-to-all-start.2 = ((bf16[16,192,256]{2,1,0:T(8,128)(2,1)}), bf16[16,192,256]{2,1,0:T(8,128)(2,1)S(1)}, u32[]{:S(2)}, u32[]{:S(2)}) async-start(bf16[16,192,256]{2,1,0:T(8,128)(2,1)} %get-tuple-element.58), calls=%async_computation.2 | async-start | bytes 3145728 | tf_op jit(solution)/shard_map/all_to_all | solution.py:466
  71.4 10.7 %collective-permute-start.7 = (bf16[16,64,128]{2,1,0:T(8,128)(2,1)S(1)}, bf16[16,64,128]{2,1,0:T(8,128)(2,1)S(1)}, u32[]{:S(2)}, u32[]{:S(2)}) collective-permute-start(bf16[16,64,128]{2,1,0:T(8,128)(2,1)S(1)} %get-tuple-element.100), channel_id=1, source_target_pairs={{0,32},{32,64},{64,96},{96,0},{1,33},{33,65},{65,97},{97,1},{2,34}... | collective-permute-start | bytes 786440 | tf_op jit(solution)/shard_map/ppermute | solution.py:475
  71.8 10.3 %collective-permute-start.9 = (bf16[16,64,128]{2,1,0:T(8,128)(2,1)S(1)}, bf16[16,64,128]{2,1,0:T(8,128)(2,1)S(1)}, u32[]{:S(2)}, u32[]{:S(2)}) collective-permute-start(bf16[16,64,128]{2,1,0:T(8,128)(2,1)S(1)} %get-tuple-element.101), channel_id=1, source_target_pairs={{0,96},{32,0},{64,32},{96,64},{1,97},{33,1},{65,33},{97,65},{2,98}... | collective-permute-start | bytes 786440 | tf_op jit(solution)/shard_map/ppermute | solution.py:475
  72.9 12.6 %collective-permute-start.8 = (bf16[16,64,128]{2,1,0:T(8,128)(2,1)S(1)}, bf16[16,64,128]{2,1,0:T(8,128)(2,1)S(1)}, u32[]{:S(2)}, u32[]{:S(2)}) collective-permute-start(bf16[16,64,128]{2,1,0:T(8,128)(2,1)S(1)} %get-tuple-element.102), channel_id=1, source_target_pairs={{0,64},{32,96},{64,0},{96,32},{1,65},{33,97},{65,1},{97,33},{2,66}... | collective-permute-start | bytes 786440 | tf_op jit(solution)/shard_map/ppermute | solution.py:475
  74.0 2.3 %copy-start = (bf16[768,3072]{1,0:T(8,128)(2,1)S(1)}, bf16[768,3072]{1,0:T(8,128)(2,1)}, u32[]{:S(2)}) copy-start(bf16[768,3072]{1,0:T(8,128)(2,1)} %w_ref.5) | copy-start | bytes 14155780
  78.9 1.5 copy-start.3
  80.4 0.9 copy-start.6
  81.3 0.8 copy-start.9
  82.1 13.0 %copy-start.8 = (f32[768,256]{1,0:T(8,128)S(1)}, f32[768,256]{1,0:T(8,128)}, u32[]{:S(2)}) copy-start(f32[768,256]{1,0:T(8,128)} %get-tuple-element.73.gate_ref) | copy-start | bytes 2359300
  82.1 13.0 %copy-start.12 = (bf16[768,256]{1,0:T(8,128)(2,1)S(1)}, bf16[768,256]{1,0:T(8,128)(2,1)}, u32[]{:S(2)}) copy-start(bf16[768,256]{1,0:T(8,128)(2,1)} %get-tuple-element.74.gg_ref) | copy-start | bytes 1179652
  95.1 7.8 %copy-start.1 = (bf16[16,192,256]{2,1,0:T(8,128)(2,1)}, bf16[16,192,256]{2,1,0:T(8,128)(2,1)S(1)}, u32[]{:S(2)}) copy-start(bf16[16,192,256]{2,1,0:T(8,128)(2,1)S(1)} %all-to-all-done.2.back_ref) | copy-start | bytes 4718596
  95.1 7.8 %copy-start.13 = (f32[768]{0:T(1024)S(1)}, f32[768]{0:T(1024)}, u32[]{:S(2)}) copy-start(f32[768]{0:T(1024)} %gain_ref.5) | copy-start | bytes 9220
  96.6 12.1 %copy-start.5 = (bf16[4,192,256]{2,1,0:T(8,128)(2,1)}, bf16[4,192,256]{2,1,0:T(8,128)(2,1)S(1)}, u32[]{:S(2)}) copy-start(bf16[4,192,256]{2,1,0:T(8,128)(2,1)S(1)} %get-tuple-element.83.ggate_ref) | copy-start | bytes 1179652
  96.6 6.3 %collective-permute-start.10 = (bf16[12,192,256]{2,1,0:T(8,128)(2,1)}, bf16[12,192,256]{2,1,0:T(8,128)(2,1)S(1)}, u32[]{:S(2)}, u32[]{:S(2)}) collective-permute-start(bf16[12,192,256]{2,1,0:T(8,128)(2,1)} %get-tuple-element.76), channel_id=1, source_target_pairs={{0,8},{8,0},{1,9},{9,1},{2,10},{10,2},{3,11},{11,3},{4,12},{12,4},... | collective-permute-start | bytes 3538952 | tf_op jit(solution)/shard_map/ppermute | solution.py:481
  97.4 13.0 %all-to-all-start.3 = ((bf16[16,64,128]{2,1,0:T(8,128)(2,1)}), bf16[16,64,128]{2,1,0:T(8,128)(2,1)}, u32[]{:S(2)}, u32[]{:S(2)}) async-start(bf16[16,64,128]{2,1,0:T(8,128)(2,1)} %fusion.2), calls=%async_computation.3 | async-start | bytes 524288 | tf_op jit(solution)/shard_map/all_to_all | solution.py:478
  102.9 1.7 copy-start.4
  104.5 1.1 copy-start.7
  105.7 1.0 copy-start.10
  108.7 1.7 copy-start.2
  110.4 57.0 %all-to-all-start.4 = ((bf16[64,32,768]{2,1,0:T(8,128)(2,1)}), bf16[64,32,768]{2,1,0:T(8,128)(2,1)S(1)}, u32[]{:S(2)}, u32[]{:S(2)}) async-start(bf16[64,32,768]{2,1,0:T(8,128)(2,1)} %copy-done.2), calls=%async_computation.4 | async-start | bytes 6291456 | tf_op jit(solution)/shard_map/all_to_all | solution.py:491
  168.5 1.3 collective-permute-start.11

commit v12 on v11

--- a/solution.py
+++ b/solution.py
@@ -384,6 +384,7 @@
     gated_s[:flat] = gated_ref[...].T
     gated_s[flat:] = o_ref[8:12].reshape(C, flat).T
     sums = jnp.zeros((8, C), F32)
+    tails = []
     for kind in range(4):
         blocks = [
             jnp.concatenate([head_rows(back_ref, ggate_ref, n, core), o_ref[n]], axis=1)
@@ -394,15 +395,14 @@
         weights = wt_ref[2 * kind : 2 * kind + 2].reshape(8 * DH, C).astype(F32)
         sums = sums + jnp.sum((win * weights).reshape(DH, 8, C), axis=0)
         for k in range(16):
-            out_ref[kind * 16 + k] = jnp.concatenate(
-                [win[k * 24 : k * 24 + 24], wout[k * 8 : k * 8 + 8]], axis=0
-            ).astype(BF)
+            out_ref[kind * 16 + k, :16] = win[k * 24 : k * 24 + 16].astype(BF)
+            tails.append((win[k * 24 + 16 : k * 24 + 24], wout[k * 8 : k * 8 + 8]))
     gain = jnp.sum(sums, axis=0, keepdims=True) / gain_ref[...].reshape(1, C)
     gain_hi = gain.astype(BF).astype(F32)
-    row = lax.broadcasted_iota(jnp.int32, (16, C), 0)
-    extra = jnp.where(row == 14, gain_hi, gain - gain_hi).astype(BF)
-    for k in range(64):
-        out_ref[k, 16:] = jnp.where(row >= 14, extra, out_ref[k, 16:])
+    row = lax.broadcasted_iota(jnp.int32, (8, C), 0)
+    extra = jnp.where(row == 6, gain_hi, gain - gain_hi)
+    for k, (win, wout) in enumerate(tails):
+        out_ref[k, 16:] = jnp.concatenate([win, jnp.where(row >= 6, extra, wout)], axis=0).astype(BF)
 
 
 def weight_grads(core, operands):

time: 171 us -> 171 us (level)
  no operation moved by 1% of the time
where the time goes in v12:
time: 171 us; the launch traced here: 170 us
  waiting for transfers between devices  58.7 us (34%)
  starting transfers between devices  45.2 us (26%)
  Pallas kernels  38.7 us (23%)
  local copies, waits for them, and re-layouts  17.9 us (10%)
  other arithmetic  6.48 us (4%)
  matrix products  2.52 us (1%)
    all_to_all x1, waiting for transfers between devices, per_device(): chunks = lax.all_to_all(chunks, ('x', 'zh', 'zl', 'y'), 0, 0, tiled=True)  34.1 us
    pallas_call x1, Pallas kernels, attention(): pl.pallas_call(functools.partial(attention_kernel, blocks=blocks), grid_s...  19.5 us
    unnamed x33, local copies, waits for them, and re-layouts  13.3 us
    ppermute x3, waiting for transfers between devices, per_device(): pieces = [bias] + [lax.ppermute(bias, 'x', turn(s)) for s in (1, 2, 3)]  10.9 us
    all_to_all x1, starting transfers between devices, per_device(): chunks = lax.all_to_all(chunks, ('x', 'zh', 'zl', 'y'), 0, 0, tiled=True)  9.83 us
    all_to_all x1, waiting for transfers between devices, per_device(): back = lax.all_to_all(result, PLANE, 0, 0, tiled=True)  7.62 us
    pallas_call x1, Pallas kernels, front(): pl.pallas_call(front_kernel, grid=(4,), in_specs=[whole((flat, C)), whole...  7.25 us
    all_to_all x1, starting transfers between devices, per_device(): received = lax.all_to_all(send, PLANE, 0, 0, tiled=True)  6.52 us
  transfers between devices with their start and end apart: 17, of which 10 were waited for; matrix products, arithmetic and copies ran while one was open for 7% of the time, Pallas kernels for 10%

profile of v12, /device:TPU:103, one launch (start us, length us, event | category | flops | bytes accessed | tf_op | source)
XLA Modules:
  0.0 170.3 jit_solution(12732472704850595653)
XLA Ops:
  0.6 1.7 constant_dynamic-slice_fusion
  2.3 5.4 %all-to-all-start = ((bf16[8,16,1024]{2,1,0:T(8,128)(2,1)}), bf16[8,16,1024]{2,1,0:T(8,128)(2,1)S(1)}, u32[]{:S(2)}, u32[]{:S(2)}) async-start(bf16[8,16,1024]{2,1,0:T(8,128)(2,1)} %constant_dynamic-slice_fusion), calls=%async_computation | async-start | bytes 524288 | tf_op jit(solution)/shard_map/all_to_all | solution.py:441
  7.7 7.2 %front.1 = (bf16[256,768]{1,0:T(8,128)(2,1)}, f32[256,1]{1,0:T(8,128)}, f32[256,1]{1,0:T(8,128)}, bf16[16,192,256]{2,1,0:T(8,128)(2,1)}, f32[768,256]{1,0:T(8,128)}, /*index=5*/bf16[768,256]{1,0:T(8,128)(2,1)}) custom-call(bf16[256,768]{1,0:T(8,128)(2,1)} %bitcast.35, f32[768]{0:T(1024)} %gain_ref.5, bf16[768,3072]{1,0:T(8,128)(2,1)} %w_ref.5, ...), custom_call_target="tpu_custom_call" | custom-call | flops 1509949440 | bytes 11534336 | tf_op jit(solution)/shard_map/front/pallas_call | solution.py:93
  15.0 6.5 %all-to-all-start.1 = ((bf16[16,192,256]{2,1,0:T(8,128)(2,1)}), bf16[16,192,256]{2,1,0:T(8,128)(2,1)}, u32[]{:S(2)}, u32[]{:S(2)}) async-start(bf16[16,192,256]{2,1,0:T(8,128)(2,1)} %get-tuple-element.48), calls=%async_computation.1 | async-start | bytes 3145728 | tf_op jit(solution)/shard_map/all_to_all | solution.py:450
  21.5 0.5 collective-permute-start.2
  22.0 0.8 collective-permute-start.1
  22.9 1.8 %collective-permute-start = (bf16[8,16,1024]{2,1,0:T(8,128)(2,1)S(1)}, bf16[8,16,1024]{2,1,0:T(8,128)(2,1)S(1)}, u32[]{:S(2)}, u32[]{:S(2)}) collective-permute-start(bf16[8,16,1024]{2,1,0:T(8,128)(2,1)S(1)} %all-to-all-done), channel_id=1, source_target_pairs={{0,32},{32,64},{64,96},{96,0},{1,33},{33,65},{65,97},{97,1},{2,34}... | collective-permute-start | bytes 786440 | tf_op jit(solution)/shard_map/ppermute | solution.py:449
  25.2 5.2 %collective-permute-done.2 = bf16[8,16,1024]{2,1,0:T(8,128)(2,1)S(1)} collective-permute-done((bf16[8,16,1024]{2,1,0:T(8,128)(2,1)S(1)}, bf16[8,16,1024]{2,1,0:T(8,128)(2,1)S(1)}, u32[]{:S(2)}, u32[]{:S(2)}) %collective-permute-start.2) | collective-permute-done | bytes 262176 | tf_op jit(solution)/shard_map/ppermute | solution.py:449
  30.3 2.8 %collective-permute-done.1 = bf16[8,16,1024]{2,1,0:T(8,128)(2,1)S(1)} collective-permute-done((bf16[8,16,1024]{2,1,0:T(8,128)(2,1)S(1)}, bf16[8,16,1024]{2,1,0:T(8,128)(2,1)S(1)}, u32[]{:S(2)}, u32[]{:S(2)}) %collective-permute-start.1) | collective-permute-done | bytes 262176 | tf_op jit(solution)/shard_map/ppermute | solution.py:449
  33.2 2.9 %collective-permute-done = bf16[8,16,1024]{2,1,0:T(8,128)(2,1)S(1)} collective-permute-done((bf16[8,16,1024]{2,1,0:T(8,128)(2,1)S(1)}, bf16[8,16,1024]{2,1,0:T(8,128)(2,1)S(1)}, u32[]{:S(2)}, u32[]{:S(2)}) %collective-permute-start) | collective-permute-done | bytes 262176 | tf_op jit(solution)/shard_map/ppermute | solution.py:449
  36.2 1.6 collective-permute-start.5
  38.0 0.4 collective-permute-start.3
  38.4 0.6 pad_add_fusion.place_ref
  39.0 1.8 %collective-permute-done.4.sco_ref = bf16[256,768]{1,0:T(8,128)(2,1)S(1)} collective-permute-done((bf16[256,768]{1,0:T(8,128)(2,1)S(1)}, bf16[256,768]{1,0:T(8,128)(2,1)S(1)}, u32[]{:S(2)}, u32[]{:S(2)}) %collective-permute-start.4) | collective-permute-done | bytes 393248 | tf_op jit(solution)/shard_map/ppermute | solution.py:456
  41.4 19.5 %attention.1 = (bf16[16,192,256]{2,1,0:T(8,128)(2,1)}, bf16[4,16,64,128]{3,2,1,0:T(8,128)(2,1)}, bf16[4,16,64,128]{3,2,1,0:T(8,128)(2,1)}) custom-call(s32[2]{0:T(128)} %pad_add_fusion.place_ref, bf16[16,192,256]{2,1,0:T(8,128)(2,1)} %all-to-all-done.1.x_ref, bf16[4,8,16,1024]{3,2,1,0:T(8,128)(2,1)} %copy-done.15, ...), custom_call_target="tpu_custom_call" | custom-call | flops 12884901888 | bytes 8388608 | tf_op jit(solution)/shard_map/attention/pallas_call | solution.py:205
  60.9 3.3 %collective-permute-start.6 = (bf16[4,16,64,128]{3,2,1,0:T(8,128)(2,1)}, bf16[4,16,64,128]{3,2,1,0:T(8,128)(2,1)}, u32[]{:S(2)}, u32[]{:S(2)}) collective-permute-start(bf16[4,16,64,128]{3,2,1,0:T(8,128)(2,1)} %get-tuple-element.64), channel_id=1, source_target_pairs={{0,8},{8,0},{1,9},{9,1},{2,10},{10,2},{3,11},{11,3},{4,12},{12,4},... | collective-permute-start | bytes 3145736 | tf_op jit(solution)/shard_map/ppermute | solution.py:471
  64.2 5.5 %all-to-all-start.2 = ((bf16[16,192,256]{2,1,0:T(8,128)(2,1)}), bf16[16,192,256]{2,1,0:T(8,128)(2,1)S(1)}, u32[]{:S(2)}, u32[]{:S(2)}) async-start(bf16[16,192,256]{2,1,0:T(8,128)(2,1)} %get-tuple-element.58), calls=%async_computation.2 | async-start | bytes 3145728 | tf_op jit(solution)/shard_map/all_to_all | solution.py:466
  69.7 1.7 fusion.4
  71.8 1.1 collective-permute-start.9
  72.9 1.1 collective-permute-start.8
  74.0 2.3 %copy-done = bf16[768,3072]{1,0:T(8,128)(2,1)S(1)} copy-done((bf16[768,3072]{1,0:T(8,128)(2,1)S(1)}, bf16[768,3072]{1,0:T(8,128)(2,1)}, u32[]{:S(2)}) %copy-start) | copy-done | bytes 4718616
  76.3 2.6 %stage.1 = (bf16[8,192,768]{2,1,0:T(8,128)(2,1)S(1)}, bf16[512,768]{1,0:T(8,128)(2,1)S(1)}, bf16[8,64,512]{2,1,0:T(8,128)(2,1)S(1)}) custom-call(s32[1]{0:T(128)} %bitcast.core_ref, bf16[768,3072]{1,0:T(8,128)(2,1)S(1)} %copy-done, bf16[256,768]{1,0:T(8,128)(2,1)S(1)} %copy-done.11, bf16[256,768]{1,0:T(8,128)(2,1)S(1)} %collective-permute-done.4.sco_ref, ...), custom_call_target="tpu_custom_call" | custom-call | flops 4718592 | bytes 7340032 | tf_op jit(solution)/shard_map/stage/pallas_call | solution.py:257
  79.0 1.4 copy-done.3
  80.4 0.9 copy-done.6
  81.3 0.8 copy-done.9
  82.1 3.4 %collective-permute-done.8 = bf16[16,64,128]{2,1,0:T(8,128)(2,1)S(1)} collective-permute-done((bf16[16,64,128]{2,1,0:T(8,128)(2,1)S(1)}, bf16[16,64,128]{2,1,0:T(8,128)(2,1)S(1)}, u32[]{:S(2)}, u32[]{:S(2)}) %collective-permute-start.8) | collective-permute-done | bytes 262176 | tf_op jit(solution)/shard_map/ppermute | solution.py:475
  85.5 1.9 %fusion.2 = bf16[16,64,128]{2,1,0:T(8,128)(2,1)} fusion(bf16[16,64,128]{2,1,0:T(8,128)(2,1)S(1)} %collective-permute-done.9, bf16[16,64,128]{2,1,0:T(8,128)(2,1)S(1)} %collective-permute-done.8, bf16[16,64,128]{2,1,0:T(8,128)(2,1)S(1)} %collective-permute-done.7, bf16[4,16,64,128]{3,2,1,0:T(8,128)(2,1)} %collective-permute-done.6, ...), kind=kLoop, calls=%fused_computation.7 | loop fusion | flops 1572864 | bytes 1572864 | tf_op jit(solution)/shard_map/convert_element_type | solution.py:477
  87.5 7.6 %all-to-all-done.2.back_ref = bf16[16,192,256]{2,1,0:T(8,128)(2,1)S(1)} async-done(((bf16[16,192,256]{2,1,0:T(8,128)(2,1)}), bf16[16,192,256]{2,1,0:T(8,128)(2,1)S(1)}, u32[]{:S(2)}, u32[]{:S(2)}) %all-to-all-start.2) | async-done | bytes 1572896 | tf_op jit(solution)/shard_map/all_to_all | solution.py:466
  95.1 1.5 gate.1
  96.6 0.8 collective-permute-start.10
  97.4 5.5 %all-to-all-start.3 = ((bf16[16,64,128]{2,1,0:T(8,128)(2,1)}), bf16[16,64,128]{2,1,0:T(8,128)(2,1)}, u32[]{:S(2)}, u32[]{:S(2)}) async-start(bf16[16,64,128]{2,1,0:T(8,128)(2,1)} %fusion.2), calls=%async_computation.3 | async-start | bytes 524288 | tf_op jit(solution)/shard_map/all_to_all | solution.py:478
  102.9 1.7 copy-done.4
  104.5 1.1 copy-done.7
  105.7 1.0 copy-done.10
  106.7 1.9 %weight_grads.1 = bf16[64,32,768]{2,1,0:T(8,128)(2,1)S(1)} custom-call(s32[1]{0:T(128)} %bitcast.core_ref, bf16[16,192,256]{2,1,0:T(8,128)(2,1)S(1)} %all-to-all-done.2.back_ref, bf16[4,192,256]{2,1,0:T(8,128)(2,1)S(1)} %get-tuple-element.83.ggate_ref, bf16[12,192,256]{2,1,0:T(8,128)(2,1)S(1)} %collective-permute-done.10.o_ref, ...), custom_call_target="tpu_custom_call" | custom-call | flops 1610612736 | bytes 8388608 | tf_op jit(solution)/shard_map/weight_grads/pallas_call | solution.py:413
  108.7 1.7 copy-done.2
  110.3 9.8 %all-to-all-start.4 = ((bf16[64,32,768]{2,1,0:T(8,128)(2,1)}), bf16[64,32,768]{2,1,0:T(8,128)(2,1)S(1)}, u32[]{:S(2)}, u32[]{:S(2)}) async-start(bf16[64,32,768]{2,1,0:T(8,128)(2,1)} %copy-done.2), calls=%async_computation.4 | async-start | bytes 6291456 | tf_op jit(solution)/shard_map/all_to_all | solution.py:491
  120.2 1.2 fusion.8
  121.4 1.1 pad_maximum_fusion.1
  122.4 2.3 %copy.14 = f32[16,128,64]{1,2,0:T(8,128)} copy(f32[16,128,64]{2,1,0:T(8,128)} %pad_maximum_fusion.1) | data formatting | bytes 1048576
  124.8 5.9 %input_grad.1 = bf16[256,768]{1,0:T(8,128)(2,1)} custom-call(bf16[16,192,256]{2,1,0:T(8,128)(2,1)} %copy-done.1, bf16[4,192,256]{2,1,0:T(8,128)(2,1)} %copy-done.5, bf16[768,3072]{1,0:T(8,128)(2,1)} %w_ref.5, bf16[256,768]{1,0:T(8,128)(2,1)} %bitcast.36, f32[256,1]{1,0:T(8,128)} %get-tuple-element.84.mean_ref, f32[256,1]{1,0:T(8,128)} %get-tuple-element.85.inv_ref, ...), custom_call_target="tpu_custom_call" | custom-call | flops 1207959552 | bytes 8388608 | tf_op jit(solution)/shard_map/input_grad/pallas_call | solution.py:356
  130.7 2.5 %convolution_convert_fusion = bf16[256,768]{1,0:T(8,128)(2,1)} fusion(bf16[768,256]{1,0:T(8,128)(2,1)S(1)} %get-tuple-element.82.gated_ref, bf16[768,768]{1,0:T(8,128)(2,1)} %wout_ref.1), kind=kOutput, calls=%fused_computation.1 | convolution fusion | flops 302186496 | bytes 1966080 | tf_op jit(solution)/shard_map/cr,cd->rd/dot_general | solution.py:490
  133.2 34.1 %all-to-all-done.4 = bf16[64,32,768]{2,1,0:T(8,128)(2,1)S(1)} async-done(((bf16[64,32,768]{2,1,0:T(8,128)(2,1)}), bf16[64,32,768]{2,1,0:T(8,128)(2,1)S(1)}, u32[]{:S(2)}, u32[]{:S(2)}) %all-to-all-start.4) | async-done | bytes 3145760 | tf_op jit(solution)/shard_map/all_to_all | solution.py:491
  167.3 0.5 convert_reduce_fusion
  167.8 0.6 slice_bitcast_fusion
  168.4 0.5 collective-permute-start.11
  168.9 0.6 slice_bitcast_fusion.1
  169.8 0.6 add.67
  (42 shorter events, 2.1 us)
Async XLA Ops:
  2.3 12.6 %all-to-all-start = ((bf16[8,16,1024]{2,1,0:T(8,128)(2,1)}), bf16[8,16,1024]{2,1,0:T(8,128)(2,1)S(1)}, u32[]{:S(2)}, u32[]{:S(2)}) async-start(bf16[8,16,1024]{2,1,0:T(8,128)(2,1)} %constant_dynamic-slice_fusion), calls=%async_computation | async-start | bytes 524288 | tf_op jit(solution)/shard_map/all_to_all | solution.py:441
  14.9 9.7 %copy-start.14 = (bf16[2,128,768]{2,1,0:T(8,128)(2,1)S(1)}, bf16[2,128,768]{2,1,0:T(8,128)(2,1)}, u32[]{:S(2)}) copy-start(bf16[2,128,768]{2,1,0:T(8,128)(2,1)} %param.11) | copy-start | bytes 1179652
  15.0 26.4 %all-to-all-start.1 = ((bf16[16,192,256]{2,1,0:T(8,128)(2,1)}), bf16[16,192,256]{2,1,0:T(8,128)(2,1)}, u32[]{:S(2)}, u32[]{:S(2)}) async-start(bf16[16,192,256]{2,1,0:T(8,128)(2,1)} %get-tuple-element.48), calls=%async_computation.1 | async-start | bytes 3145728 | tf_op jit(solution)/shard_map/all_to_all | solution.py:450
  21.5 8.9 %collective-permute-start.2 = (bf16[8,16,1024]{2,1,0:T(8,128)(2,1)S(1)}, bf16[8,16,1024]{2,1,0:T(8,128)(2,1)S(1)}, u32[]{:S(2)}, u32[]{:S(2)}) collective-permute-start(bf16[8,16,1024]{2,1,0:T(8,128)(2,1)S(1)} %all-to-all-done), channel_id=1, source_target_pairs={{0,96},{32,0},{64,32},{96,64},{1,97},{33,1},{65,33},{97,65},{2,98}... | collective-permute-start | bytes 786440 | tf_op jit(solution)/shard_map/ppermute | solution.py:449
  22.0 11.1 %collective-permute-start.1 = (bf16[8,16,1024]{2,1,0:T(8,128)(2,1)S(1)}, bf16[8,16,1024]{2,1,0:T(8,128)(2,1)S(1)}, u32[]{:S(2)}, u32[]{:S(2)}) collective-permute-start(bf16[8,16,1024]{2,1,0:T(8,128)(2,1)S(1)} %all-to-all-done), channel_id=1, source_target_pairs={{0,64},{32,96},{64,0},{96,32},{1,65},{33,97},{65,1},{97,33},{2,66}... | collective-permute-start | bytes 786440 | tf_op jit(solution)/shard_map/ppermute | solution.py:449
  22.9 13.2 %collective-permute-start = (bf16[8,16,1024]{2,1,0:T(8,128)(2,1)S(1)}, bf16[8,16,1024]{2,1,0:T(8,128)(2,1)S(1)}, u32[]{:S(2)}, u32[]{:S(2)}) collective-permute-start(bf16[8,16,1024]{2,1,0:T(8,128)(2,1)S(1)} %all-to-all-done), channel_id=1, source_target_pairs={{0,32},{32,64},{64,96},{96,0},{1,33},{33,65},{65,97},{97,1},{2,34}... | collective-permute-start | bytes 786440 | tf_op jit(solution)/shard_map/ppermute | solution.py:449
  25.1 12.8 %copy-start.11 = (bf16[256,768]{1,0:T(8,128)(2,1)S(1)}, bf16[256,768]{1,0:T(8,128)(2,1)}, u32[]{:S(2)}) copy-start(bf16[256,768]{1,0:T(8,128)(2,1)} %get-tuple-element.65.sc_ref) | copy-start | bytes 1179652
  36.2 5.2 %copy-start.15 = (bf16[4,8,16,1024]{3,2,1,0:T(8,128)(2,1)}, bf16[4,8,16,1024]{3,2,1,0:T(8,128)(2,1)S(1)}, u32[]{:S(2)}) copy-start(bf16[4,8,16,1024]{3,2,1,0:T(8,128)(2,1)S(1)} %pad_maximum_fusion.mine_ref) | copy-start | bytes 3145732
  36.2 4.9 %collective-permute-start.5 = (bf16[4,8,16,1024]{3,2,1,0:T(8,128)(2,1)S(1)}, bf16[4,8,16,1024]{3,2,1,0:T(8,128)(2,1)}, u32[]{:S(2)}, u32[]{:S(2)}) collective-permute-start(bf16[4,8,16,1024]{3,2,1,0:T(8,128)(2,1)S(1)} %pad_maximum_fusion.mine_ref), channel_id=1, source_target_pairs={{0,8},{8,0},{1,9},{9,1},{2,10},{10,2},{3,11},{11,3},{4,12},{12,4},... | collective-permute-start | bytes 3145736 | tf_op jit(solution)/shard_map/ppermute | solution.py:460
  37.9 2.8 %collective-permute-start.4 = (bf16[256,768]{1,0:T(8,128)(2,1)S(1)}, bf16[256,768]{1,0:T(8,128)(2,1)S(1)}, u32[]{:S(2)}, u32[]{:S(2)}) collective-permute-start(bf16[256,768]{1,0:T(8,128)(2,1)S(1)} %copy-done.11), channel_id=1, source_target_pairs={{0,8},{8,0},{1,9},{9,1},{2,10},{10,2},{3,11},{11,3},{4,12},{12,4},... | collective-permute-start | bytes 1179656 | tf_op jit(solution)/shard_map/ppermute | solution.py:456
  38.0 3.1 %collective-permute-start.3 = (bf16[8,64,256]{2,1,0:T(8,128)(2,1)S(1)}, bf16[8,64,256]{2,1,0:T(8,128)(2,1)S(1)}, u32[]{:S(2)}, u32[]{:S(2)}) collective-permute-start(bf16[8,64,256]{2,1,0:T(8,128)(2,1)S(1)} %get-tuple-element.50), channel_id=1, source_target_pairs={{0,8},{8,0},{1,9},{9,1},{2,10},{10,2},{3,11},{11,3},{4,12},{12,4},... | collective-permute-start | bytes 786440 | tf_op jit(solution)/shard_map/ppermute | solution.py:461
  60.9 8.8 %collective-permute-start.6 = (bf16[4,16,64,128]{3,2,1,0:T(8,128)(2,1)}, bf16[4,16,64,128]{3,2,1,0:T(8,128)(2,1)}, u32[]{:S(2)}, u32[]{:S(2)}) collective-permute-start(bf16[4,16,64,128]{3,2,1,0:T(8,128)(2,1)} %get-tuple-element.64), channel_id=1, source_target_pairs={{0,8},{8,0},{1,9},{9,1},{2,10},{10,2},{3,11},{11,3},{4,12},{12,4},... | collective-permute-start | bytes 3145736 | tf_op jit(solution)/shard_map/ppermute | solution.py:471
  64.2 30.9 %all-to-all-start.2 = ((bf16[16,192,256]{2,1,0:T(8,128)(2,1)}), bf16[16,192,256]{2,1,0:T(8,128)(2,1)S(1)}, u32[]{:S(2)}, u32[]{:S(2)}) async-start(bf16[16,192,256]{2,1,0:T(8,128)(2,1)} %get-tuple-element.58), calls=%async_computation.2 | async-start | bytes 3145728 | tf_op jit(solution)/shard_map/all_to_all | solution.py:466
  71.4 10.7 %collective-permute-start.7 = (bf16[16,64,128]{2,1,0:T(8,128)(2,1)S(1)}, bf16[16,64,128]{2,1,0:T(8,128)(2,1)S(1)}, u32[]{:S(2)}, u32[]{:S(2)}) collective-permute-start(bf16[16,64,128]{2,1,0:T(8,128)(2,1)S(1)} %get-tuple-element.100), channel_id=1, source_target_pairs={{0,32},{32,64},{64,96},{96,0},{1,33},{33,65},{65,97},{97,1},{2,34}... | collective-permute-start | bytes 786440 | tf_op jit(solution)/shard_map/ppermute | solution.py:475
  71.8 10.3 %collective-permute-start.9 = (bf16[16,64,128]{2,1,0:T(8,128)(2,1)S(1)}, bf16[16,64,128]{2,1,0:T(8,128)(2,1)S(1)}, u32[]{:S(2)}, u32[]{:S(2)}) collective-permute-start(bf16[16,64,128]{2,1,0:T(8,128)(2,1)S(1)} %get-tuple-element.101), channel_id=1, source_target_pairs={{0,96},{32,0},{64,32},{96,64},{1,97},{33,1},{65,33},{97,65},{2,98}... | collective-permute-start | bytes 786440 | tf_op jit(solution)/shard_map/ppermute | solution.py:475
  72.9 12.6 %collective-permute-start.8 = (bf16[16,64,128]{2,1,0:T(8,128)(2,1)S(1)}, bf16[16,64,128]{2,1,0:T(8,128)(2,1)S(1)}, u32[]{:S(2)}, u32[]{:S(2)}) collective-permute-start(bf16[16,64,128]{2,1,0:T(8,128)(2,1)S(1)} %get-tuple-element.102), channel_id=1, source_target_pairs={{0,64},{32,96},{64,0},{96,32},{1,65},{33,97},{65,1},{97,33},{2,66}... | collective-permute-start | bytes 786440 | tf_op jit(solution)/shard_map/ppermute | solution.py:475
  74.0 2.3 %copy-start = (bf16[768,3072]{1,0:T(8,128)(2,1)S(1)}, bf16[768,3072]{1,0:T(8,128)(2,1)}, u32[]{:S(2)}) copy-start(bf16[768,3072]{1,0:T(8,128)(2,1)} %w_ref.5) | copy-start | bytes 14155780
  78.9 1.5 copy-start.3
  80.4 0.9 copy-start.6
  81.3 0.8 copy-start.9
  82.1 13.0 %copy-start.8 = (f32[768,256]{1,0:T(8,128)S(1)}, f32[768,256]{1,0:T(8,128)}, u32[]{:S(2)}) copy-start(f32[768,256]{1,0:T(8,128)} %get-tuple-element.73.gate_ref) | copy-start | bytes 2359300
  82.1 13.0 %copy-start.12 = (bf16[768,256]{1,0:T(8,128)(2,1)S(1)}, bf16[768,256]{1,0:T(8,128)(2,1)}, u32[]{:S(2)}) copy-start(bf16[768,256]{1,0:T(8,128)(2,1)} %get-tuple-element.74.gg_ref) | copy-start | bytes 1179652
  95.1 7.8 %copy-start.1 = (bf16[16,192,256]{2,1,0:T(8,128)(2,1)}, bf16[16,192,256]{2,1,0:T(8,128)(2,1)S(1)}, u32[]{:S(2)}) copy-start(bf16[16,192,256]{2,1,0:T(8,128)(2,1)S(1)} %all-to-all-done.2.back_ref) | copy-start | bytes 4718596
  95.1 7.8 %copy-start.13 = (f32[768]{0:T(1024)S(1)}, f32[768]{0:T(1024)}, u32[]{:S(2)}) copy-start(f32[768]{0:T(1024)} %gain_ref.5) | copy-start | bytes 9220
  96.6 12.0 %copy-start.5 = (bf16[4,192,256]{2,1,0:T(8,128)(2,1)}, bf16[4,192,256]{2,1,0:T(8,128)(2,1)S(1)}, u32[]{:S(2)}) copy-start(bf16[4,192,256]{2,1,0:T(8,128)(2,1)S(1)} %get-tuple-element.83.ggate_ref) | copy-start | bytes 1179652
  96.6 6.3 %collective-permute-start.10 = (bf16[12,192,256]{2,1,0:T(8,128)(2,1)}, bf16[12,192,256]{2,1,0:T(8,128)(2,1)S(1)}, u32[]{:S(2)}, u32[]{:S(2)}) collective-permute-start(bf16[12,192,256]{2,1,0:T(8,128)(2,1)} %get-tuple-element.76), channel_id=1, source_target_pairs={{0,8},{8,0},{1,9},{9,1},{2,10},{10,2},{3,11},{11,3},{4,12},{12,4},... | collective-permute-start | bytes 3538952 | tf_op jit(solution)/shard_map/ppermute | solution.py:481
  97.4 12.9 %all-to-all-start.3 = ((bf16[16,64,128]{2,1,0:T(8,128)(2,1)}), bf16[16,64,128]{2,1,0:T(8,128)(2,1)}, u32[]{:S(2)}, u32[]{:S(2)}) async-start(bf16[16,64,128]{2,1,0:T(8,128)(2,1)} %fusion.2), calls=%async_computation.3 | async-start | bytes 524288 | tf_op jit(solution)/shard_map/all_to_all | solution.py:478
  102.9 1.7 copy-start.4
  104.5 1.1 copy-start.7
  105.7 1.0 copy-start.10
  108.6 1.7 copy-start.2
  110.3 57.0 %all-to-all-start.4 = ((bf16[64,32,768]{2,1,0:T(8,128)(2,1)}), bf16[64,32,768]{2,1,0:T(8,128)(2,1)S(1)}, u32[]{:S(2)}, u32[]{:S(2)}) async-start(bf16[64,32,768]{2,1,0:T(8,128)(2,1)} %copy-done.2), calls=%async_computation.4 | async-start | bytes 6291456 | tf_op jit(solution)/shard_map/all_to_all | solution.py:491
  168.4 1.3 collective-permute-start.11
